TPU v7x, 512 devices: a whole 4x8x8 slice. The times are simulated.
512 devices in a mesh: dp: 8 (over y), seq: 64 (over z, x, core).
Axes of the slice: x: 4, y: 8, z: 8, core: 2. Of those that a mesh axis runs over, the one named last changes fastest.
Arguments:
- tokens: bfloat16 [8, 32768, 1024], P('dp', 'seq'), may hold values from -50 to 50
- w_query: bfloat16 [1024, 1024], P(None, 'dp'), may hold values from -0.1875 to 0.1875
- w_key: bfloat16 [1024, 1024], P(None, 'dp'), may hold values from -0.1875 to 0.1875
- w_value: bfloat16 [1024, 1024], P(None, 'dp'), may hold values from -0.1875 to 0.1875
- w_out: bfloat16 [1024, 1024], P('dp'), may hold values from -0.1875 to 0.1875
- norm_gain: float32 [1024], replicated, may hold values from 0.1 to 1.9
Outputs:
- layer_out: bfloat16 [8, 32768, 1024], P('dp', 'seq')
All inputs are finite; a program needn't handle non-finite values.
Results may differ from a plain program's by a relative error of at most 0.017.
Values may be sent and summed in bfloat16 or wider, within the bound.
No kernel may reach another device: no remote copies, remote signals or barrier semaphores. Data moves between devices by JAX's collectives and lax.ppermute only.
A program may use at most 128 MiB of HBM per device.

v0:
```python
import jax
import jax.numpy as jnp
from jax import lax
from jax.sharding import PartitionSpec as P

H = 8
DH = 128


def entering(value, axis, join, neutral):
    place = lax.axis_index(axis)
    gathered = lax.all_gather(value.astype(jnp.bfloat16), axis)
    state = jnp.zeros_like(value) + jnp.asarray(neutral, value.dtype)

    def one(lap, state):
        return join(state, lax.dynamic_index_in_dim(gathered, lap, 0, False).astype(value.dtype))

    return lax.fori_loop(0, place, one, state)


def inner_block(query_heads, key_heads, value_heads):
    length = query_heads.shape[1]
    block = min(length, 512)
    scores = jnp.einsum("hid,hjd->hij", query_heads, key_heads, preferred_element_type=jnp.float32)
    row_ids = jnp.arange(0, block)[:, None]
    col_ids = jnp.arange(block)[None, :]
    scores = jnp.where(col_ids <= row_ids, scores, 0.0).astype(jnp.bfloat16)
    pieces = jnp.einsum("hij,hje->hie", scores, value_heads, preferred_element_type=jnp.float32)
    return pieces


def add_states(earlier, later):
    return earlier + later


def key_value_state(key_heads, value_heads):
    return jnp.einsum("htd,hte->hde", key_heads, value_heads, preferred_element_type=jnp.float32)


def attend(query_heads, key_heads, value_heads, prior):
    within = inner_block(query_heads, key_heads, value_heads)
    carried = jnp.einsum(
        "htd,hde->hte", query_heads, prior.astype(jnp.bfloat16), preferred_element_type=jnp.float32
    )
    return within + carried


def body(tokens, w_query, w_key, w_value, w_out, norm_gain):
    rows = tokens[0]
    length = rows.shape[0]
    full_query, full_key, full_value = (
        lax.all_gather(w_query, "dp", axis=1, tiled=True),
        lax.all_gather(w_key, "dp", axis=1, tiled=True),
        lax.all_gather(w_value, "dp", axis=1, tiled=True),
    )
    query = jnp.dot(rows, full_query, preferred_element_type=jnp.float32).astype(jnp.bfloat16)
    key = jnp.dot(rows, full_key, preferred_element_type=jnp.float32).astype(jnp.bfloat16)
    value = jnp.dot(rows, full_value, preferred_element_type=jnp.float32).astype(jnp.bfloat16)
    query_heads = query.reshape(length, H, DH).transpose(1, 0, 2)
    key_heads = key.reshape(length, H, DH).transpose(1, 0, 2)
    value_heads = value.reshape(length, H, DH).transpose(1, 0, 2)
    local_state = key_value_state(key_heads, value_heads)
    empty_state = jnp.zeros((H, DH, DH), jnp.float32)
    prior = entering(local_state, "seq", add_states, empty_state)
    mixed_raw = attend(query_heads, key_heads, value_heads, prior)
    scale = lax.rsqrt(jnp.mean(mixed_raw * mixed_raw, axis=-1, keepdims=True) + 1e-05)
    normed = (mixed_raw * scale * norm_gain.reshape(H, 1, DH)).astype(jnp.bfloat16)
    normed = normed.transpose(1, 0, 2).reshape(length, H * DH)
    result = jnp.dot(
        normed, lax.all_gather(w_out, "dp", axis=0, tiled=True), preferred_element_type=jnp.float32
    )
    return result.astype(jnp.bfloat16)[None]


def solution(mesh):
    in_specs = (
        P("dp", "seq", None),
        P(None, "dp"),
        P(None, "dp"),
        P(None, "dp"),
        P("dp", None),
        P(),
    )
    out_specs = P("dp", "seq", None)
    return jax.shard_map(body, mesh=mesh, in_specs=in_specs, out_specs=out_specs, check_vma=False)
```

profile of v0, /device:TPU:455, one launch (start us, length us, event | category | flops | bytes accessed | tf_op | source)
XLA Modules:
  0.0 347.7 jit_solution(2035250541791715043)
XLA Ops:
  8.8 46.0 %all-gather.9.cloned.1.call-done = bf16[1024,1024]{1,0:T(8,128)(2,1)} async-done(((bf16[1024,128]{1,0:T(8,128)(2,1)}), bf16[1024,1024]{1,0:T(8,128)(2,1)}) %all-gather.9.cloned.1.call-update) | async-done | bytes 2097168 | tf_op jit(solution)/shard_map/all_gather | solution.py:53
  54.8 2.8 convolution_convert_fusion.2
  58.2 47.8 %all-gather.11.cloned.1.call-done = bf16[1024,1024]{1,0:T(8,128)(2,1)} async-done(((bf16[1024,128]{1,0:T(8,128)(2,1)}), bf16[1024,1024]{1,0:T(8,128)(2,1)}) %all-gather.11.cloned.1.call-update) | async-done | bytes 2097168 | tf_op jit(solution)/shard_map/all_gather | solution.py:54
  106.0 2.8 convolution_convert_fusion.1
  108.8 1.2 convolution_convert_fusion.4
  110.8 1.2 copy.24
  112.0 45.2 %all-gather.7.cloned.1.call-done = bf16[1024,1024]{1,0:T(8,128)(2,1)} async-done(((bf16[1024,128]{1,0:T(8,128)(2,1)}), bf16[1024,1024]{1,0:T(8,128)(2,1)}) %all-gather.7.cloned.1.call-update) | async-done | bytes 2097168 | tf_op jit(solution)/shard_map/all_gather | solution.py:52
  157.2 3.8 %fusion.7 = bf16[64,8,8,128]{3,2,1,0:T(8,128)(2,1)} fusion(bf16[1024,1024]{1,0:T(8,128)(2,1)} %all-gather.7.cloned.1.call-done, bf16[1,512,1024]{2,1,0:T(8,128)(2,1)S(1)} %copy-done), kind=kOutput, calls=%fused_computation.15 | convolution fusion | flops 1074266112 | bytes 4194304 | tf_op jit(solution)/shard_map/dot_general | solution.py:56
  161.0 5.1 %fusion = f32[8,512,128]{1,2,0:T(8,128)} fusion(pred[512,512]{1,0:T(8,128)(4,1)S(1)} %iota_compare_fusion, bf16[8,512,128]{1,2,0:T(8,128)(2,1)S(1)} %bitcast.67, bf16[8,512,128]{2,0,1:T(8,128)(2,1)S(1)} %bitcast.69, bf16[64,8,8,128]{3,2,1,0:T(8,128)(2,1)} %fusion.7), kind=kOutput, calls=%fused_computation.2 | convolution fusion | flops 1077936128 | bytes 5505024 | tf_op jit(solution)/shard_map/hij,hje->hie/dot_general | solution.py:28
  166.1 99.4 %all-gather.15.cloned.1.call-done = bf16[512,128,128]{2,1,0:T(8,128)(2,1)} async-done(((bf16[8,128,128]{2,1,0:T(8,128)(2,1)}), bf16[512,128,128]{2,1,0:T(8,128)(2,1)}) %all-gather.15.cloned.1.call-update) | async-done | bytes 16777232 | tf_op jit(solution)/shard_map/all_gather | solution.py:12
  265.6 69.2 %while.10 = (s32[]{:T(128)}, f32[8,128,128]{2,1,0:T(8,128)S(1)}, s32[]{:T(128)}, bf16[64,8,128,128]{3,2,1,0:T(8,128)(2,1)}, s32[]{:T(128)}, /*index=5*/s32[]{:T(128)}, s32[]{:T(128)}) while((s32[]{:T(128)}, f32[8,128,128]{2,1,0:T(8,128)S(1)}, s32[]{:T(128)}, bf16[64,8,128,128]{3,2,1,0:T(8,128)(2,1)}, s32[]{:T(128)}, /*index=5*/s32[]{:T(128)}, ...), condition=%wide.region_1.2_spmd, body=%wide.region_0.1_spmd.sunk | while | flops 262149 | bytes 1310835 | solution.py:18
  265.6 1.2 convert_add_fusion.2
  282.2 1.1 convert_add_fusion.2
  288.7 1.1 convert_add_fusion.2
  292.0 1.1 convert_add_fusion.2
  295.3 1.1 convert_add_fusion.2
  296.4 1.1 convert_add_fusion.2
  297.5 1.1 convert_add_fusion.2
  298.6 1.1 convert_add_fusion.2
  300.8 1.1 convert_add_fusion.2
  301.9 1.1 convert_add_fusion.2
  303.0 1.1 convert_add_fusion.2
  334.8 2.1 multiply_reduce_fusion
  337.4 3.8 %fusion.8 = bf16[1,512,1024]{2,1,0:T(8,128)(2,1)} fusion(bf16[512,1024]{0,1:T(8,128)(2,1)S(1)} %bitcast.65, bf16[1024,1024]{1,0:T(8,128)(2,1)} %all-gather.13.cloned.1.call-done), kind=kOutput, calls=%fused_computation.16 | convolution fusion | flops 1074266112 | bytes 4194304 | tf_op jit(solution)/shard_map/dot_general | solution.py:69
  (76 shorter events, 59.4 us)
Async XLA Ops:
  6.5 48.3 %copy-start = (bf16[1,512,1024]{2,1,0:T(8,128)(2,1)S(1)}, bf16[1,512,1024]{2,1,0:T(8,128)(2,1)}, u32[]{:S(2)}) copy-start(bf16[1,512,1024]{2,1,0:T(8,128)(2,1)} %param.8) | copy-start | bytes 3145732
  6.5 48.3 %all-gather.9.cloned.1.call-start = ((), (), s32[]{:S(2)}) async-start(), calls=%async_computation.1 | async-start | bytes 2359296 | tf_op jit(solution)/shard_map/all_gather | solution.py:53
  7.3 98.7 %all-gather.11.cloned.1.call-start = ((), (), s32[]{:S(2)}) async-start(), calls=%async_computation.2 | async-start | bytes 2359296 | tf_op jit(solution)/shard_map/all_gather | solution.py:54
  8.0 149.2 %all-gather.7.cloned.1.call-start = ((), (), s32[]{:S(2)}) async-start(), calls=%async_computation | async-start | bytes 2359296 | tf_op jit(solution)/shard_map/all_gather | solution.py:52
  8.7 256.8 %all-gather.15.cloned.1.call-start = ((), (), s32[]{:S(2)}) async-start(), calls=%async_computation.4 | async-start | bytes 17039360 | tf_op jit(solution)/shard_map/all_gather | solution.py:12
  110.1 227.3 %all-gather.13.cloned.1.call-start = ((), (), s32[]{:S(2)}) async-start(), calls=%async_computation.3 | async-start | bytes 2359296 | tf_op jit(solution)/shard_map/all_gather | solution.py:70
  112.0 49.0 %copy-start.1 = (bf16[64,8,8,128]{3,2,1,0:T(8,128)(2,1)S(1)}, bf16[64,8,8,128]{3,2,1,0:T(8,128)(2,1)}, u32[]{:S(2)}) copy-start(bf16[64,8,8,128]{3,2,1,0:T(8,128)(2,1)} %copy.24) | copy-start | bytes 3145732
  265.6 69.2 %copy-start.2 = (bf16[64,8,8,128]{3,2,1,0:T(8,128)(2,1)S(1)}, bf16[64,8,8,128]{3,2,1,0:T(8,128)(2,1)}, u32[]{:S(2)}) copy-start(bf16[64,8,8,128]{3,2,1,0:T(8,128)(2,1)} %fusion.7) | copy-start | bytes 3145732
  334.8 2.2 copy-start.3
Sparse Core Ops, SparseCore 0:
  9.4 45.3 all-gather.8
  56.8 49.1 all-gather.10
  108.0 49.1 all-gather.6
  160.4 105.0 all-gather.14
  267.5 40.4 all-gather.12
where the time goes:
time: 350 us; the launch traced here: 348 us
  waiting for transfers between devices  241 us (69%)
  other arithmetic  67.9 us (19%)
  matrix products  21.8 us (6%)
  between operations  13.2 us (4%)
    all_gather x1, waiting for transfers between devices, entering(): gathered = lax.all_gather(value.astype(jnp.bfloat16), axis)  99.4 us
    add x63, other arithmetic, add_states(): return earlier + later  67.5 us
    all_gather x1, waiting for transfers between devices, body(): lax.all_gather(w_value, 'dp', axis=1, tiled=True)  47.8 us
    all_gather x1, waiting for transfers between devices, body(): lax.all_gather(w_key, 'dp', axis=1, tiled=True)  46 us
    all_gather x1, waiting for transfers between devices, body(): lax.all_gather(w_query, 'dp', axis=1, tiled=True)  45.2 us
  transfers between devices with their start and end apart: 5, of which 4 were waited for; matrix products, arithmetic and copies ran while one was open for 25% of the time, Pallas kernels for 0%

commit v1 on v0

v1 whole, which is shorter than its diff:
```python
import jax
import jax.numpy as jnp
from jax import lax
from jax.experimental import pallas as pl
from jax.experimental.pallas import tpu as pltpu
from jax.sharding import Mesh
from jax.sharding import PartitionSpec as P


DP, ZN, XN = 8, 8, 4
CHIPS = ZN * XN
TOK = 512
D = 1024
DH = 128
SLOTS = 4
F32 = jnp.float32
BF16 = jnp.bfloat16
SWAP = [(0, 1), (1, 0)]
VMEM = pl.BlockSpec(memory_space=pltpu.VMEM)
HBM = pl.BlockSpec(memory_space=pl.ANY)


def toward(distance):
    pairs = []
    for y in range(DP):
        for place in range(2 * CHIPS):
            step = -distance if place % 2 == 0 else distance
            pairs.append((y * 2 * CHIPS + place, (y + step) % DP * 2 * CHIPS + place))
    return pairs


def hop(weight, distance):
    return lax.ppermute(weight, ("dp", "z", "x", "core"), toward(distance))


def call(kernel, outs, flops, moved, specs=None, scratch=(), count=None):
    return pl.pallas_call(
        kernel,
        out_shape=outs,
        in_specs=specs if specs is not None else [VMEM] * count,
        out_specs=jax.tree.map(lambda _: VMEM, outs),
        scratch_shapes=list(scratch),
        compiler_params=pltpu.CompilerParams(vmem_limit_bytes=32 * 1024 * 1024),
        cost_estimate=pl.CostEstimate(flops=flops, bytes_accessed=moved, transcendentals=0),
    )


def shape(dims, kind):
    return jax.ShapeDtypeStruct(dims, kind)


def mm(a, b):
    return jnp.dot(a, b, preferred_element_type=F32)


def mm_t(a, b):
    return lax.dot_general(a, b, (((1,), (1,)), ((), ())), preferred_element_type=F32)


def t_mm(a, b):
    return lax.dot_general(a, b, (((0,), (0,)), ((), ())), preferred_element_type=F32)


def project(tokens_refs, weight, key_ref, value_ref, state_ref):
    for block, tokens_ref in enumerate(tokens_refs):
        both = mm(tokens_ref[...], weight).astype(BF16)
        key, value = both[:, :DH], both[:, DH:]
        key_ref[block] = key
        value_ref[block] = value
        state_ref[block] = t_mm(key, value)


def key_value_kernel(own_ref, other_ref, wk_ref, wv_ref, key_ref, value_ref, state_ref):
    weight = jnp.concatenate([wk_ref[...], wv_ref[...]], axis=1)
    project((own_ref, other_ref), weight, key_ref, value_ref, state_ref)


def last_key_value_kernel(
    own_ref, other_ref, wk_ref, wv_ref, wk_far_ref, wv_far_ref, s0, s1, s2, key_ref, value_ref, state_ref, total_ref
):
    first = lax.axis_index("core") == 0
    wk = jnp.where(first, wk_ref[...], wk_far_ref[...])
    wv = jnp.where(first, wv_ref[...], wv_far_ref[...])
    project((own_ref, other_ref), jnp.concatenate([wk, wv], axis=1), key_ref, value_ref, state_ref)
    for slot, ref in enumerate((s0, s1, s2, state_ref)):
        total_ref[slot] = (ref[0] + ref[1]).astype(BF16)


def within_kernel(own_ref, other_ref, q0, q1, q2, q_own, q_far, k0, k1, k2, k3, v0, v1, v2, v3, query_ref, within_ref):
    first = lax.axis_index("core") == 0
    wq3 = jnp.where(first, q_own[...], q_far[...])
    weights = (
        jnp.concatenate([q0[...], q1[...]], axis=1),
        jnp.concatenate([q2[...], wq3], axis=1),
    )
    keys, values = (k0, k1, k2, k3), (v0, v1, v2, v3)
    half = TOK // 2
    rows = lax.broadcasted_iota(jnp.int32, (half, half), 0)
    cols = lax.broadcasted_iota(jnp.int32, (half, half), 1)
    keep = cols <= rows
    for block, tokens_ref in enumerate((own_ref, other_ref)):
        for pair in range(2):
            both = mm(tokens_ref[...], weights[pair]).astype(BF16)
            for side in range(2):
                slot = 2 * pair + side
                query = both[:, side * DH : (side + 1) * DH]
                query_ref[slot, block] = query
                key, value = keys[slot][block], values[slot][block]
                top = jnp.where(keep, mm_t(query[:half], key[:half]), 0.0).astype(BF16)
                within_ref[slot, block, :half] = mm(top, value[:half])
                left = mm_t(query[half:], key[:half]).astype(BF16)
                right = jnp.where(keep, mm_t(query[half:], key[half:]), 0.0).astype(BF16)
                within_ref[slot, block, half:] = mm(left, value[:half]) + mm(right, value[half:])


def prefix_kernel(chunk_ref, prior_ref):
    total = jnp.zeros(chunk_ref.shape[1:], F32)
    for chip in range(CHIPS):
        prior_ref[chip] = total.astype(BF16)
        total = total + chunk_ref[chip].astype(F32)


def head_of(y, core, slot):
    if slot == 3:
        return lax.rem(y + 4 * core, DP)
    return lax.rem(y + DP + (slot + 1) * (1 - 2 * core), DP)


def norm_kernel(query_ref, within_ref, prior_ref, s0, s1, s2, s3, gain_ref, own_ref, other_ref):
    core = lax.axis_index("core")
    y = lax.axis_index("dp")
    shares = (core.astype(F32), 1.0 - core.astype(F32))
    for slot, state_ref in enumerate((s0, s1, s2, s3)):
        gain = gain_ref[pl.ds(head_of(y, core, slot), 1), :]
        for block, out_ref in enumerate((own_ref, other_ref)):
            prior = (prior_ref[slot].astype(F32) + shares[block] * state_ref[1 - block]).astype(BF16)
            mixed = within_ref[slot, block] + mm(query_ref[slot, block], prior)
            scale = lax.rsqrt(jnp.mean(mixed * mixed, axis=-1, keepdims=True) + 1e-05)
            out_ref[:, slot * DH : (slot + 1) * DH] = (mixed * scale * gain).astype(BF16)


def out_kernel(own_ref, got_ref, weight_hbm, out_ref, mine, theirs, sems):
    core = lax.axis_index("core")
    y = lax.axis_index("dp")
    copies = []
    for side, (place, buffer) in enumerate(((core, mine), (1 - core, theirs))):
        for slot in range(SLOTS):
            begin = pl.multiple_of(head_of(y, place, slot) * DH, DH)
            copy = pltpu.make_async_copy(
                weight_hbm.at[pl.ds(begin, DH), :], buffer.at[pl.ds(slot * DH, DH), :], sems.at[side * SLOTS + slot]
            )
            copy.start()
            copies.append(copy)
    for copy in copies:
        copy.wait()
    for begin in range(0, D, 256):
        cols = pl.ds(begin, 256)
        out_ref[0, :, cols] = (mm(own_ref[...], mine[:, cols]) + mm(got_ref[...], theirs[:, cols])).astype(BF16)


def body(tokens, w_query, w_key, w_value, w_out, norm_gain):
    own = tokens[0]
    full_out = lax.all_gather(w_out, "dp", axis=0, tiled=True)

    key_1, value_1 = hop(w_key, 1), hop(w_value, 1)
    key_2, value_2 = hop(w_key, 2), hop(w_value, 2)
    other = lax.ppermute(own, "core", SWAP)
    key_3, value_3 = hop(key_2, 1), hop(value_2, 1)
    key_4, value_4 = hop(key_3, 1), hop(value_3, 1)
    w_query, key_1 = lax.optimization_barrier((w_query, key_1))
    query_1, query_2 = hop(w_query, 1), hop(w_query, 2)
    query_3 = hop(query_2, 1)
    query_4 = hop(query_3, 1)

    piece = shape((2, TOK, DH), BF16)
    state = shape((2, DH, DH), F32)
    flops = 2 * 2 * TOK * D * 2 * DH
    one = call(key_value_kernel, (piece, piece, state), flops, 3 << 20, count=4)
    last = call(last_key_value_kernel, (piece, piece, state, shape((SLOTS, DH, DH), BF16)), flops, 3 << 20, count=9)
    k0, v0, s0 = one(own, other, key_1, value_1)
    k1, v1, s1 = one(own, other, key_2, value_2)
    k2, v2, s2 = one(own, other, key_3, value_3)
    k3, v3, s3, total = last(own, other, w_key, w_value, key_4, value_4, s0, s1, s2)

    chunks = total.reshape(CHIPS, SLOTS * DH // CHIPS, DH)
    chunks = lax.all_to_all(chunks, ("z", "x"), 0, 0, tiled=True)
    priors = call(prefix_kernel, shape(chunks.shape, BF16), 1 << 16, 1 << 18, count=1)(chunks)
    prior = lax.all_to_all(priors, ("z", "x"), 0, 0, tiled=True).reshape(SLOTS, DH, DH)

    query, within = call(
        within_kernel,
        (shape((SLOTS, 2, TOK, DH), BF16), shape((SLOTS, 2, TOK, DH), F32)),
        3 * 2 * TOK * D * SLOTS * DH,
        8 << 20,
        count=15,
    )(own, other, query_1, query_2, query_3, w_query, query_4, k0, k1, k2, k3, v0, v1, v2, v3)

    half = shape((TOK, SLOTS * DH), BF16)
    normed_own, normed_other = call(norm_kernel, (half, half), 1 << 28, 4 << 20, count=8)(
        query, within, prior, s0, s1, s2, s3, norm_gain.reshape(DP, DH)
    )
    got = lax.ppermute(normed_other, "core", SWAP)
    weight = pltpu.VMEM((SLOTS * DH, D), BF16)
    return call(
        out_kernel,
        shape((1, TOK, D), BF16),
        1 << 30,
        5 << 20,
        specs=[VMEM, VMEM, HBM],
        scratch=[weight, weight, pltpu.SemaphoreType.DMA((2 * SLOTS,))],
    )(normed_own, got, full_out)


def solution(mesh):
    fine = Mesh(mesh.devices.reshape(DP, ZN, XN, 2), ("dp", "z", "x", "core"))
    seq = ("z", "x", "core")
    in_specs = (
        P("dp", seq, None),
        P(None, "dp"),
        P(None, "dp"),
        P(None, "dp"),
        P("dp", None),
        P(),
    )
    return jax.shard_map(body, mesh=fine, in_specs=in_specs, out_specs=P("dp", seq, None), check_vma=False)
```

time: 350 us -> 151 us (0.43)
  the two profiles are of different devices: /device:TPU:455 before, /device:TPU:1 now
where the time goes in v1:
time: 151 us; the launch traced here: 150 us
  starting transfers between devices  56.5 us (37%)
  waiting for transfers between devices  37.6 us (25%)
  local copies, waits for them, and re-layouts  23.4 us (15%)
  Pallas kernels  18.8 us (12%)
  between operations  13.7 us (9%)
    ppermute x12, waiting for transfers between devices, hop(): return lax.ppermute(weight, ('dp', 'z', 'x', 'core'), toward(distance))  31.6 us
    ppermute x12, starting transfers between devices, hop(): return lax.ppermute(weight, ('dp', 'z', 'x', 'core'), toward(distance))  26 us
    unnamed x64, local copies, waits for them, and re-layouts  23.4 us
    all_to_all x1, starting transfers between devices, body(): chunks = lax.all_to_all(chunks, ('z', 'x'), 0, 0, tiled=True)  10.3 us
    ppermute x1, starting transfers between devices, body(): other = lax.ppermute(own, 'core', SWAP)  8.79 us
    pallas_call x1, Pallas kernels, body(): call(within_kernel, (shape((SLOTS, 2, TOK, DH), BF16), shape((SLOTS, 2, T...  6.83 us
    ppermute x1, starting transfers between devices, body(): got = lax.ppermute(normed_other, 'core', SWAP)  5.83 us
    all_to_all x1, starting transfers between devices, body(): lax.all_to_all(priors, ('z', 'x'), 0, 0, tiled=True).reshape(SLOTS, DH, DH)  5.59 us
  transfers between devices with their start and end apart: 17, of which 8 were waited for; matrix products, arithmetic and copies ran while one was open for 0% of the time, Pallas kernels for 11%

profile of v1, /device:TPU:1, one launch (start us, length us, event | category | flops | bytes accessed | tf_op | source)
XLA Modules:
  0.0 150.0 jit_solution(3898567255843741196)
XLA Ops:
  7.3 8.8 %collective-permute-start = (bf16[512,1024]{1,0:T(8,128)(2,1)}, bf16[512,1024]{1,0:T(8,128)(2,1)S(1)}, u32[]{:S(2)}, u32[]{:S(2)}) collective-permute-start(bf16[512,1024]{1,0:T(8,128)(2,1)} %bitcast.4), channel_id=1, source_target_pairs={{0,1},{1,0},{2,3},{3,2},{4,5},{5,4},{6,7},{7,6},{8,9},{9,8},{10,11... | collective-permute-start | bytes 3145736 | tf_op jit(solution)/shard_map/ppermute | solution.py:167
  16.1 1.9 %collective-permute-start.7 = (bf16[1024,128]{1,0:T(8,128)(2,1)}, bf16[1024,128]{1,0:T(8,128)(2,1)S(1)}, u32[]{:S(2)}, u32[]{:S(2)}) collective-permute-start(bf16[1024,128]{1,0:T(8,128)(2,1)} %wk_ref.1), channel_id=1, source_target_pairs={{0,384},{1,129},{2,386},{3,131},{4,388},{5,133},{6,390},{7,135},{8... | collective-permute-start | bytes 786440 | tf_op jit(solution)/shard_map/ppermute | solution.py:33
  18.0 2.4 %collective-permute-start.8 = (bf16[1024,128]{1,0:T(8,128)(2,1)}, bf16[1024,128]{1,0:T(8,128)(2,1)S(1)}, u32[]{:S(2)}, u32[]{:S(2)}) collective-permute-start(bf16[1024,128]{1,0:T(8,128)(2,1)} %wv_ref.1), channel_id=1, source_target_pairs={{0,384},{1,129},{2,386},{3,131},{4,388},{5,133},{6,390},{7,135},{8... | collective-permute-start | bytes 786440 | tf_op jit(solution)/shard_map/ppermute | solution.py:33
  20.3 2.3 %collective-permute-start.1 = (bf16[1024,128]{1,0:T(8,128)(2,1)}, bf16[1024,128]{1,0:T(8,128)(2,1)S(1)}, u32[]{:S(2)}, u32[]{:S(2)}) collective-permute-start(bf16[1024,128]{1,0:T(8,128)(2,1)} %wk_ref.1), channel_id=1, source_target_pairs={{0,448},{1,65},{2,450},{3,67},{4,452},{5,69},{6,454},{7,71},{8,456... | collective-permute-start | bytes 786440 | tf_op jit(solution)/shard_map/ppermute | solution.py:33
  22.7 6.9 %collective-permute-done.7.wk_ref = bf16[1024,128]{1,0:T(8,128)(2,1)S(1)} collective-permute-done((bf16[1024,128]{1,0:T(8,128)(2,1)}, bf16[1024,128]{1,0:T(8,128)(2,1)S(1)}, u32[]{:S(2)}, u32[]{:S(2)}) %collective-permute-start.7) | collective-permute-done | bytes 262176 | tf_op jit(solution)/shard_map/ppermute | solution.py:33
  29.5 1.9 %collective-permute-start.9 = (bf16[1024,128]{1,0:T(8,128)(2,1)S(1)}, bf16[1024,128]{1,0:T(8,128)(2,1)S(1)}, u32[]{:S(2)}, u32[]{:S(2)}) collective-permute-start(bf16[1024,128]{1,0:T(8,128)(2,1)S(1)} %collective-permute-done.7.wk_ref), channel_id=1, source_target_pairs={{0,448},{1,65},{2,450},{3,67},{4,452},{5,69},{6,454},{7,71},{8,456... | collective-permute-start | bytes 786440 | tf_op jit(solution)/shard_map/ppermute | solution.py:33
  32.4 1.9 %collective-permute-start.10 = (bf16[1024,128]{1,0:T(8,128)(2,1)S(1)}, bf16[1024,128]{1,0:T(8,128)(2,1)S(1)}, u32[]{:S(2)}, u32[]{:S(2)}) collective-permute-start(bf16[1024,128]{1,0:T(8,128)(2,1)S(1)} %collective-permute-done.8.wv_ref), channel_id=1, source_target_pairs={{0,448},{1,65},{2,450},{3,67},{4,452},{5,69},{6,454},{7,71},{8,456... | collective-permute-start | bytes 786440 | tf_op jit(solution)/shard_map/ppermute | solution.py:33
  34.3 2.2 %collective-permute-done.1.wk_ref = bf16[1024,128]{1,0:T(8,128)(2,1)S(1)} collective-permute-done((bf16[1024,128]{1,0:T(8,128)(2,1)}, bf16[1024,128]{1,0:T(8,128)(2,1)S(1)}, u32[]{:S(2)}, u32[]{:S(2)}) %collective-permute-start.1) | collective-permute-done | bytes 262176 | tf_op jit(solution)/shard_map/ppermute | solution.py:33
  36.5 2.4 %collective-permute-start.3 = (bf16[1024,128]{1,0:T(8,128)(2,1)}, bf16[1024,128]{1,0:T(8,128)(2,1)}, u32[]{:S(2)}, u32[]{:S(2)}) collective-permute-start(bf16[1024,128]{1,0:T(8,128)(2,1)} %q_own), channel_id=1, source_target_pairs={{0,384},{1,129},{2,386},{3,131},{4,388},{5,133},{6,390},{7,135},{8... | collective-permute-start | bytes 786440 | tf_op jit(solution)/shard_map/ppermute | solution.py:33
  38.9 1.9 %collective-permute-start.6 = (bf16[1024,128]{1,0:T(8,128)(2,1)}, bf16[1024,128]{1,0:T(8,128)(2,1)S(1)}, u32[]{:S(2)}, u32[]{:S(2)}) collective-permute-start(bf16[1024,128]{1,0:T(8,128)(2,1)} %wv_ref.1), channel_id=1, source_target_pairs={{0,448},{1,65},{2,450},{3,67},{4,452},{5,69},{6,454},{7,71},{8,456... | collective-permute-start | bytes 786440 | tf_op jit(solution)/shard_map/ppermute | solution.py:33
  40.8 4.1 %collective-permute-done.9.wk_ref = bf16[1024,128]{1,0:T(8,128)(2,1)S(1)} collective-permute-done((bf16[1024,128]{1,0:T(8,128)(2,1)S(1)}, bf16[1024,128]{1,0:T(8,128)(2,1)S(1)}, u32[]{:S(2)}, u32[]{:S(2)}) %collective-permute-start.9) | collective-permute-done | bytes 262176 | tf_op jit(solution)/shard_map/ppermute | solution.py:33
  44.9 1.9 %collective-permute-start.11 = (bf16[1024,128]{1,0:T(8,128)(2,1)S(1)}, bf16[1024,128]{1,0:T(8,128)(2,1)S(1)}, u32[]{:S(2)}, u32[]{:S(2)}) collective-permute-start(bf16[1024,128]{1,0:T(8,128)(2,1)S(1)} %collective-permute-done.9.wk_ref), channel_id=1, source_target_pairs={{0,448},{1,65},{2,450},{3,67},{4,452},{5,69},{6,454},{7,71},{8,456... | collective-permute-start | bytes 786440 | tf_op jit(solution)/shard_map/ppermute | solution.py:33
  46.8 6.4 %collective-permute-done.10.wv_ref = bf16[1024,128]{1,0:T(8,128)(2,1)S(1)} collective-permute-done((bf16[1024,128]{1,0:T(8,128)(2,1)S(1)}, bf16[1024,128]{1,0:T(8,128)(2,1)S(1)}, u32[]{:S(2)}, u32[]{:S(2)}) %collective-permute-start.10) | collective-permute-done | bytes 262176 | tf_op jit(solution)/shard_map/ppermute | solution.py:33
  55.2 11.1 %collective-permute-done.3.q1 = bf16[1024,128]{1,0:T(8,128)(2,1)} collective-permute-done((bf16[1024,128]{1,0:T(8,128)(2,1)}, bf16[1024,128]{1,0:T(8,128)(2,1)}, u32[]{:S(2)}, u32[]{:S(2)}) %collective-permute-start.3) | collective-permute-done | bytes 262176 | tf_op jit(solution)/shard_map/ppermute | solution.py:33
  66.2 1.9 %collective-permute-start.4 = (bf16[1024,128]{1,0:T(8,128)(2,1)}, bf16[1024,128]{1,0:T(8,128)(2,1)}, u32[]{:S(2)}, u32[]{:S(2)}) collective-permute-start(bf16[1024,128]{1,0:T(8,128)(2,1)} %collective-permute-done.3.q1), channel_id=1, source_target_pairs={{0,448},{1,65},{2,450},{3,67},{4,452},{5,69},{6,454},{7,71},{8,456... | collective-permute-start | bytes 786440 | tf_op jit(solution)/shard_map/ppermute | solution.py:33
  77.1 2.3 %shard_map.67 = (bf16[2,512,128]{2,1,0:T(8,128)(2,1)S(1)}, bf16[2,512,128]{2,1,0:T(8,128)(2,1)S(1)}, f32[2,128,128]{2,1,0:T(8,128)S(1)}, bf16[4,128,128]{2,1,0:T(8,128)(2,1)}) custom-call(bf16[512,1024]{1,0:T(8,128)(2,1)S(1)} %bitcast.8, bf16[512,1024]{1,0:T(8,128)(2,1)S(1)} %collective-permute-done.other_ref, bf16[1024,128]{1,0:T(8,128)(2,1)S(1)} %copy-done.5, ...), custom_call_target="tpu_custom_call" | custom-call | flops 536870912 | bytes 3145728 | tf_op jit(solution)/shard_map/pallas_call | solution.py:183
  81.5 10.3 %all-to-all-start = ((bf16[32,16,128]{2,1,0:T(8,128)(2,1)}), bf16[32,16,128]{2,1,0:T(8,128)(2,1)S(1)}, u32[]{:S(2)}, u32[]{:S(2)}) async-start(bf16[32,16,128]{2,1,0:T(8,128)(2,1)} %bitcast.1), calls=%async_computation | async-start | bytes 262144 | tf_op jit(solution)/shard_map/all_to_all | solution.py:186
  91.8 3.6 %collective-permute-start.2 = (bf16[1024,128]{1,0:T(8,128)(2,1)S(1)}, bf16[1024,128]{1,0:T(8,128)(2,1)S(1)}, u32[]{:S(2)}, u32[]{:S(2)}) collective-permute-start(bf16[1024,128]{1,0:T(8,128)(2,1)S(1)} %copy-done.10), channel_id=1, source_target_pairs={{0,448},{1,65},{2,450},{3,67},{4,452},{5,69},{6,454},{7,71},{8,456... | collective-permute-start | bytes 786440 | tf_op jit(solution)/shard_map/ppermute | solution.py:33
  95.4 1.9 %collective-permute-start.5 = (bf16[1024,128]{1,0:T(8,128)(2,1)}, bf16[1024,128]{1,0:T(8,128)(2,1)S(1)}, u32[]{:S(2)}, u32[]{:S(2)}) collective-permute-start(bf16[1024,128]{1,0:T(8,128)(2,1)} %collective-permute-done.4.q2), channel_id=1, source_target_pairs={{0,448},{1,65},{2,450},{3,67},{4,452},{5,69},{6,454},{7,71},{8,456... | collective-permute-start | bytes 786440 | tf_op jit(solution)/shard_map/ppermute | solution.py:33
  97.4 3.8 %all-to-all-done.chunk_ref = bf16[32,16,128]{2,1,0:T(8,128)(2,1)S(1)} async-done(((bf16[32,16,128]{2,1,0:T(8,128)(2,1)}), bf16[32,16,128]{2,1,0:T(8,128)(2,1)S(1)}, u32[]{:S(2)}, u32[]{:S(2)}) %all-to-all-start) | async-done | bytes 131104 | tf_op jit(solution)/shard_map/all_to_all | solution.py:186
  101.8 5.6 %all-to-all-start.1 = ((bf16[32,16,128]{2,1,0:T(8,128)(2,1)}), bf16[32,16,128]{2,1,0:T(8,128)(2,1)}, u32[]{:S(2)}, u32[]{:S(2)}) async-start(bf16[32,16,128]{2,1,0:T(8,128)(2,1)} %shard_map.69), calls=%async_computation.1 | async-start | bytes 262144 | tf_op jit(solution)/shard_map/all_to_all | solution.py:188
  119.3 6.8 %shard_map.68 = (bf16[4,2,512,128]{3,2,1,0:T(8,128)(2,1)S(1)}, f32[4,2,512,128]{3,2,1,0:T(8,128)S(1)}) custom-call(bf16[512,1024]{1,0:T(8,128)(2,1)S(1)} %bitcast.9, bf16[512,1024]{1,0:T(8,128)(2,1)S(1)} %collective-permute-done.other_ref, bf16[1024,128]{1,0:T(8,128)(2,1)S(1)} %copy-done.29, bf16[1024,128]{1,0:T(8,128)(2,1)} %collective-permute-done.3.q1, ...), custom_call_target="tpu_custom_call" | custom-call | flops 1610612736 | bytes 8388608 | tf_op jit(solution)/shard_map/pallas_call | solution.py:190
  131.7 5.8 %collective-permute-start.13 = (bf16[512,512]{1,0:T(8,128)(2,1)S(1)}, bf16[512,512]{1,0:T(8,128)(2,1)S(1)}, u32[]{:S(2)}, u32[]{:S(2)}) collective-permute-start(bf16[512,512]{1,0:T(8,128)(2,1)S(1)} %get-tuple-element.42), channel_id=1, source_target_pairs={{0,1},{1,0},{2,3},{3,2},{4,5},{5,4},{6,7},{7,6},{8,9},{9,8},{10,11... | collective-permute-start | bytes 1572872 | tf_op jit(solution)/shard_map/ppermute | solution.py:202
  140.7 2.5 %shard_map.71 = bf16[1,512,1024]{2,1,0:T(8,128)(2,1)} custom-call(bf16[512,512]{1,0:T(8,128)(2,1)S(1)} %get-tuple-element.41.own_ref, bf16[512,512]{1,0:T(8,128)(2,1)S(1)} %collective-permute-done.13.got_ref, bf16[1024,1024]{1,0:T(8,128)(2,1)S(1)} %copy-done.2), custom_call_target="tpu_custom_call" | custom-call | flops 1073741824 | bytes 5242880 | tf_op jit(solution)/shard_map/pallas_call | solution.py:204
  (83 shorter events, 35.7 us)
Async XLA Ops:
  6.5 132.6 %all-gather.2.cloned.1.call-start = ((), (), s32[]{:S(2)}) async-start(), calls=%async_computation.2 | async-start | bytes 2359296 | tf_op jit(solution)/shard_map/all_gather | solution.py:163
  7.3 60.9 %collective-permute-start = (bf16[512,1024]{1,0:T(8,128)(2,1)}, bf16[512,1024]{1,0:T(8,128)(2,1)S(1)}, u32[]{:S(2)}, u32[]{:S(2)}) collective-permute-start(bf16[512,1024]{1,0:T(8,128)(2,1)} %bitcast.4), channel_id=1, source_target_pairs={{0,1},{1,0},{2,3},{3,2},{4,5},{5,4},{6,7},{7,6},{8,9},{9,8},{10,11... | collective-permute-start | bytes 3145736 | tf_op jit(solution)/shard_map/ppermute | solution.py:167
  16.1 13.5 %collective-permute-start.7 = (bf16[1024,128]{1,0:T(8,128)(2,1)}, bf16[1024,128]{1,0:T(8,128)(2,1)S(1)}, u32[]{:S(2)}, u32[]{:S(2)}) collective-permute-start(bf16[1024,128]{1,0:T(8,128)(2,1)} %wk_ref.1), channel_id=1, source_target_pairs={{0,384},{1,129},{2,386},{3,131},{4,388},{5,133},{6,390},{7,135},{8... | collective-permute-start | bytes 786440 | tf_op jit(solution)/shard_map/ppermute | solution.py:33
  18.0 14.4 %collective-permute-start.8 = (bf16[1024,128]{1,0:T(8,128)(2,1)}, bf16[1024,128]{1,0:T(8,128)(2,1)S(1)}, u32[]{:S(2)}, u32[]{:S(2)}) collective-permute-start(bf16[1024,128]{1,0:T(8,128)(2,1)} %wv_ref.1), channel_id=1, source_target_pairs={{0,384},{1,129},{2,386},{3,131},{4,388},{5,133},{6,390},{7,135},{8... | collective-permute-start | bytes 786440 | tf_op jit(solution)/shard_map/ppermute | solution.py:33
  20.3 16.2 %collective-permute-start.1 = (bf16[1024,128]{1,0:T(8,128)(2,1)}, bf16[1024,128]{1,0:T(8,128)(2,1)S(1)}, u32[]{:S(2)}, u32[]{:S(2)}) collective-permute-start(bf16[1024,128]{1,0:T(8,128)(2,1)} %wk_ref.1), channel_id=1, source_target_pairs={{0,448},{1,65},{2,450},{3,67},{4,452},{5,69},{6,454},{7,71},{8,456... | collective-permute-start | bytes 786440 | tf_op jit(solution)/shard_map/ppermute | solution.py:33
  29.5 15.4 %collective-permute-start.9 = (bf16[1024,128]{1,0:T(8,128)(2,1)S(1)}, bf16[1024,128]{1,0:T(8,128)(2,1)S(1)}, u32[]{:S(2)}, u32[]{:S(2)}) collective-permute-start(bf16[1024,128]{1,0:T(8,128)(2,1)S(1)} %collective-permute-done.7.wk_ref), channel_id=1, source_target_pairs={{0,448},{1,65},{2,450},{3,67},{4,452},{5,69},{6,454},{7,71},{8,456... | collective-permute-start | bytes 786440 | tf_op jit(solution)/shard_map/ppermute | solution.py:33
  32.4 20.9 %collective-permute-start.10 = (bf16[1024,128]{1,0:T(8,128)(2,1)S(1)}, bf16[1024,128]{1,0:T(8,128)(2,1)S(1)}, u32[]{:S(2)}, u32[]{:S(2)}) collective-permute-start(bf16[1024,128]{1,0:T(8,128)(2,1)S(1)} %collective-permute-done.8.wv_ref), channel_id=1, source_target_pairs={{0,448},{1,65},{2,450},{3,67},{4,452},{5,69},{6,454},{7,71},{8,456... | collective-permute-start | bytes 786440 | tf_op jit(solution)/shard_map/ppermute | solution.py:33
  36.5 29.7 %collective-permute-start.3 = (bf16[1024,128]{1,0:T(8,128)(2,1)}, bf16[1024,128]{1,0:T(8,128)(2,1)}, u32[]{:S(2)}, u32[]{:S(2)}) collective-permute-start(bf16[1024,128]{1,0:T(8,128)(2,1)} %q_own), channel_id=1, source_target_pairs={{0,384},{1,129},{2,386},{3,131},{4,388},{5,133},{6,390},{7,135},{8... | collective-permute-start | bytes 786440 | tf_op jit(solution)/shard_map/ppermute | solution.py:33
  38.9 35.8 %collective-permute-start.6 = (bf16[1024,128]{1,0:T(8,128)(2,1)}, bf16[1024,128]{1,0:T(8,128)(2,1)S(1)}, u32[]{:S(2)}, u32[]{:S(2)}) collective-permute-start(bf16[1024,128]{1,0:T(8,128)(2,1)} %wv_ref.1), channel_id=1, source_target_pairs={{0,448},{1,65},{2,450},{3,67},{4,452},{5,69},{6,454},{7,71},{8,456... | collective-permute-start | bytes 786440 | tf_op jit(solution)/shard_map/ppermute | solution.py:33
  44.9 32.1 %collective-permute-start.11 = (bf16[1024,128]{1,0:T(8,128)(2,1)S(1)}, bf16[1024,128]{1,0:T(8,128)(2,1)S(1)}, u32[]{:S(2)}, u32[]{:S(2)}) collective-permute-start(bf16[1024,128]{1,0:T(8,128)(2,1)S(1)} %collective-permute-done.9.wk_ref), channel_id=1, source_target_pairs={{0,448},{1,65},{2,450},{3,67},{4,452},{5,69},{6,454},{7,71},{8,456... | collective-permute-start | bytes 786440 | tf_op jit(solution)/shard_map/ppermute | solution.py:33
  53.2 23.8 %collective-permute-start.12 = (bf16[1024,128]{1,0:T(8,128)(2,1)S(1)}, bf16[1024,128]{1,0:T(8,128)(2,1)S(1)}, u32[]{:S(2)}, u32[]{:S(2)}) collective-permute-start(bf16[1024,128]{1,0:T(8,128)(2,1)S(1)} %collective-permute-done.10.wv_ref), channel_id=1, source_target_pairs={{0,448},{1,65},{2,450},{3,67},{4,452},{5,69},{6,454},{7,71},{8,456... | collective-permute-start | bytes 786440 | tf_op jit(solution)/shard_map/ppermute | solution.py:33
  66.2 29.2 %collective-permute-start.4 = (bf16[1024,128]{1,0:T(8,128)(2,1)}, bf16[1024,128]{1,0:T(8,128)(2,1)}, u32[]{:S(2)}, u32[]{:S(2)}) collective-permute-start(bf16[1024,128]{1,0:T(8,128)(2,1)} %collective-permute-done.3.q1), channel_id=1, source_target_pairs={{0,448},{1,65},{2,450},{3,67},{4,452},{5,69},{6,454},{7,71},{8,456... | collective-permute-start | bytes 786440 | tf_op jit(solution)/shard_map/ppermute | solution.py:33
  72.4 4.7 %copy-start.5 = (bf16[1024,128]{1,0:T(8,128)(2,1)S(1)}, bf16[1024,128]{1,0:T(8,128)(2,1)}, u32[]{:S(2)}) copy-start(bf16[1024,128]{1,0:T(8,128)(2,1)} %wk_ref.1) | copy-start | bytes 786436
  72.4 4.7 %copy-start.6 = (bf16[1024,128]{1,0:T(8,128)(2,1)S(1)}, bf16[1024,128]{1,0:T(8,128)(2,1)}, u32[]{:S(2)}) copy-start(bf16[1024,128]{1,0:T(8,128)(2,1)} %wv_ref.1) | copy-start | bytes 786436
  74.7 4.7 %copy-start.16 = (bf16[2,512,128]{2,1,0:T(8,128)(2,1)}, bf16[2,512,128]{2,1,0:T(8,128)(2,1)S(1)}, u32[]{:S(2)}) copy-start(bf16[2,512,128]{2,1,0:T(8,128)(2,1)S(1)} %get-tuple-element.27.k1) | copy-start | bytes 786436
  77.0 4.4 %copy-start.20 = (bf16[2,512,128]{2,1,0:T(8,128)(2,1)}, bf16[2,512,128]{2,1,0:T(8,128)(2,1)S(1)}, u32[]{:S(2)}) copy-start(bf16[2,512,128]{2,1,0:T(8,128)(2,1)S(1)} %get-tuple-element.26.k0) | copy-start | bytes 786436
  77.0 14.7 %copy-start.10 = (bf16[1024,128]{1,0:T(8,128)(2,1)S(1)}, bf16[1024,128]{1,0:T(8,128)(2,1)}, u32[]{:S(2)}) copy-start(bf16[1024,128]{1,0:T(8,128)(2,1)} %q_own) | copy-start | bytes 786436
  77.1 31.8 %copy-start.1 = (bf16[1,512,1024]{2,1,0:T(8,128)(2,1)S(1)}, bf16[1,512,1024]{2,1,0:T(8,128)(2,1)}, u32[]{:S(2)}) copy-start(bf16[1,512,1024]{2,1,0:T(8,128)(2,1)} %param.6) | copy-start | bytes 3145732
  81.5 19.7 %all-to-all-start = ((bf16[32,16,128]{2,1,0:T(8,128)(2,1)}), bf16[32,16,128]{2,1,0:T(8,128)(2,1)S(1)}, u32[]{:S(2)}, u32[]{:S(2)}) async-start(bf16[32,16,128]{2,1,0:T(8,128)(2,1)} %bitcast.1), calls=%async_computation | async-start | bytes 262144 | tf_op jit(solution)/shard_map/all_to_all | solution.py:186
  91.8 15.6 %collective-permute-start.2 = (bf16[1024,128]{1,0:T(8,128)(2,1)S(1)}, bf16[1024,128]{1,0:T(8,128)(2,1)S(1)}, u32[]{:S(2)}, u32[]{:S(2)}) collective-permute-start(bf16[1024,128]{1,0:T(8,128)(2,1)S(1)} %copy-done.10), channel_id=1, source_target_pairs={{0,448},{1,65},{2,450},{3,67},{4,452},{5,69},{6,454},{7,71},{8,456... | collective-permute-start | bytes 786440 | tf_op jit(solution)/shard_map/ppermute | solution.py:33
  95.4 12.7 %collective-permute-start.5 = (bf16[1024,128]{1,0:T(8,128)(2,1)}, bf16[1024,128]{1,0:T(8,128)(2,1)S(1)}, u32[]{:S(2)}, u32[]{:S(2)}) collective-permute-start(bf16[1024,128]{1,0:T(8,128)(2,1)} %collective-permute-done.4.q2), channel_id=1, source_target_pairs={{0,448},{1,65},{2,450},{3,67},{4,452},{5,69},{6,454},{7,71},{8,456... | collective-permute-start | bytes 786440 | tf_op jit(solution)/shard_map/ppermute | solution.py:33
  101.8 25.7 %all-to-all-start.1 = ((bf16[32,16,128]{2,1,0:T(8,128)(2,1)}), bf16[32,16,128]{2,1,0:T(8,128)(2,1)}, u32[]{:S(2)}, u32[]{:S(2)}) async-start(bf16[32,16,128]{2,1,0:T(8,128)(2,1)} %shard_map.69), calls=%async_computation.1 | async-start | bytes 262144 | tf_op jit(solution)/shard_map/all_to_all | solution.py:188
  119.3 8.2 %copy-start.9 = (f32[1024]{0:T(1024)S(1)}, f32[1024]{0:T(1024)}, u32[]{:S(2)}) copy-start(f32[1024]{0:T(1024)} %param.11) | copy-start | bytes 12292
  131.7 7.3 %collective-permute-start.13 = (bf16[512,512]{1,0:T(8,128)(2,1)S(1)}, bf16[512,512]{1,0:T(8,128)(2,1)S(1)}, u32[]{:S(2)}, u32[]{:S(2)}) collective-permute-start(bf16[512,512]{1,0:T(8,128)(2,1)S(1)} %get-tuple-element.42), channel_id=1, source_target_pairs={{0,1},{1,0},{2,3},{3,2},{4,5},{5,4},{6,7},{7,6},{8,9},{9,8},{10,11... | collective-permute-start | bytes 1572872 | tf_op jit(solution)/shard_map/ppermute | solution.py:202
  (25 other events, 23.5 us)
Sparse Core Ops, SparseCore 0:
  9.4 57.5 all-gather.1

commit v2 on v1

v2 whole, which is shorter than its diff:
```python
import jax
import jax.numpy as jnp
from jax import lax
from jax.experimental import pallas as pl
from jax.experimental.pallas import tpu as pltpu
from jax.sharding import Mesh
from jax.sharding import PartitionSpec as P


DP, ZN, XN = 8, 8, 4
CHIPS = ZN * XN
TOK = 512
D = 1024
DH = 128
HALF = D // 2
SLOTS = 4
F32 = jnp.float32
BF16 = jnp.bfloat16
SWAP = [(0, 1), (1, 0)]
VMEM = pl.BlockSpec(memory_space=pltpu.VMEM)
HBM = pl.BlockSpec(memory_space=pl.ANY)
DMA = pltpu.SemaphoreType.DMA


def toward(distance):
    pairs = []
    for y in range(DP):
        for place in range(2 * CHIPS):
            step = -distance if place % 2 == 0 else distance
            pairs.append((y * 2 * CHIPS + place, (y + step) % DP * 2 * CHIPS + place))
    return pairs


def hop(weight, distance):
    return lax.ppermute(weight, ("dp", "z", "x", "core"), toward(distance))


def call(kernel, count, outs, scratch, flops, moved, spec=HBM, limit=56):
    return pl.pallas_call(
        kernel,
        out_shape=outs,
        in_specs=[spec] * count,
        out_specs=jax.tree.map(lambda _: spec, outs),
        scratch_shapes=scratch,
        compiler_params=pltpu.CompilerParams(vmem_limit_bytes=limit * 1024 * 1024),
        cost_estimate=pl.CostEstimate(flops=flops, bytes_accessed=moved, transcendentals=0),
    )


def shape(dims, kind):
    return jax.ShapeDtypeStruct(dims, kind)


def mm(a, b):
    return jnp.dot(a, b, preferred_element_type=F32)


def mm_t(a, b):
    return lax.dot_general(a, b, (((1,), (1,)), ((), ())), preferred_element_type=F32)


def t_mm(a, b):
    return lax.dot_general(a, b, (((0,), (0,)), ((), ())), preferred_element_type=F32)


def begin(source, target, sem):
    copy = pltpu.make_async_copy(source, target, sem)
    copy.start()
    return copy


def head_of(y, core, slot):
    if slot == 3:
        return lax.rem(y + 4 * core, DP)
    return lax.rem(y + DP + (slot + 1) * (1 - 2 * core), DP)


def pack_kernel(wq, wo, part, sems):
    core = lax.axis_index("core")
    start = pl.multiple_of(core * HALF, HALF)
    copies = [begin(wq.at[pl.ds(start, HALF), :], part.at[pl.ds(0, HALF), :], sems.at[0])]
    for c in range(4):
        cols = pl.ds(pl.multiple_of(core * HALF + c * DH, DH), DH)
        copies.append(begin(wo.at[:, cols], part.at[pl.ds(HALF + c * DH, DH), :], sems.at[1 + c]))
    for copy in copies:
        copy.wait()


def project(own, other, loads, kv, state, tokens, weight, kv_out, state_out, sems):
    copies = [begin(ref, tokens.at[block], sems.at[2 + block]) for block, ref in enumerate((own, other))]
    for load in loads:
        load.wait()
    for block in range(2):
        copies[block].wait()
        both = mm(tokens[block], weight[...]).astype(BF16)
        kv_out[block] = both
        state_out[block] = t_mm(both[:, :DH], both[:, DH:])
    return [begin(kv_out, kv, sems.at[4]), begin(state_out, state, sems.at[5])]


def key_value_kernel(own, other, wk, wv, kv, state, tokens, weight, kv_out, state_out, sems):
    loads = [
        begin(wk, weight.at[:, pl.ds(0, DH)], sems.at[0]),
        begin(wv, weight.at[:, pl.ds(DH, DH)], sems.at[1]),
    ]
    for copy in project(own, other, loads, kv, state, tokens, weight, kv_out, state_out, sems):
        copy.wait()


def last_key_value_kernel(
    own, other, wk, wv, wk_far, wv_far, s0, s1, s2, kv, state, total, tokens, weight, kv_out, state_out, sums, total_out, sems
):
    core = lax.axis_index("core")
    left, right = weight.at[:, pl.ds(0, DH)], weight.at[:, pl.ds(DH, DH)]

    @pl.when(core == 0)
    def _():
        begin(wk, left, sems.at[0])
        begin(wv, right, sems.at[1])

    @pl.when(core != 0)
    def _():
        begin(wk_far, left, sems.at[0])
        begin(wv_far, right, sems.at[1])

    loads = [pltpu.make_async_copy(wk, left, sems.at[0]), pltpu.make_async_copy(wv, right, sems.at[1])]
    early = [begin(ref, sums.at[slot], sems.at[6 + slot]) for slot, ref in enumerate((s0, s1, s2))]
    copies = project(own, other, loads, kv, state, tokens, weight, kv_out, state_out, sems)
    for slot in range(3):
        early[slot].wait()
        total_out[slot] = (sums[slot, 0] + sums[slot, 1]).astype(BF16)
    total_out[3] = (state_out[0] + state_out[1]).astype(BF16)
    copies.append(begin(total_out, total, sems.at[9]))
    for copy in copies:
        copy.wait()


def within_kernel(
    own, other, mine, theirs, kv0, kv1, kv2, kv3, query_ref, within_ref, tokens, weight, kv, query, within, sems, out_sems
):
    core = lax.axis_index("core")
    y = lax.axis_index("dp")
    loads = [begin(ref, tokens.at[block], sems.at[block]) for block, ref in enumerate((own, other))]
    weights, pairs = [], []
    for slot in range(SLOTS):
        head = head_of(y, core, slot)
        cols = pl.ds(slot * DH, DH)
        weights.append([])
        for side, (source, place) in enumerate(((mine, core), (theirs, 1 - core))):
            rows = pl.ds(pl.multiple_of(place * HALF, HALF), HALF)
            sem = sems.at[2 + 2 * slot + side]
            weights[slot].append(begin(source.at[head, pl.ds(0, HALF), :], weight.at[rows, cols], sem))
    for slot, ref in enumerate((kv0, kv1, kv2, kv3)):
        pairs.append(begin(ref, kv.at[slot], sems.at[10 + slot]))
    half = TOK // 2
    rows = lax.broadcasted_iota(jnp.int32, (half, half), 0)
    cols = lax.broadcasted_iota(jnp.int32, (half, half), 1)
    keep = cols <= rows
    for load in loads:
        load.wait()
    copies = []
    for pair in range(2):
        for slot in (2 * pair, 2 * pair + 1):
            for load in weights[slot]:
                load.wait()
            pairs[slot].wait()
        for block in range(2):
            both = mm(tokens[block], weight[:, 2 * pair * DH : 2 * (pair + 1) * DH]).astype(BF16)
            for side in range(2):
                slot = 2 * pair + side
                q = both[:, side * DH : (side + 1) * DH]
                query[slot, block] = q
                copies.append(begin(query.at[slot, block], query_ref.at[slot, block], out_sems.at[0, slot, block]))
                key, value = kv[slot, block, :, :DH], kv[slot, block, :, DH:]
                top = jnp.where(keep, mm_t(q[:half], key[:half]), 0.0).astype(BF16)
                within[slot, block, :half] = mm(top, value[:half])
                left = mm_t(q[half:], key[:half]).astype(BF16)
                right = jnp.where(keep, mm_t(q[half:], key[half:]), 0.0).astype(BF16)
                within[slot, block, half:] = mm(left, value[:half]) + mm(right, value[half:])
                copies.append(begin(within.at[slot, block], within_ref.at[slot, block], out_sems.at[1, slot, block]))
    for copy in copies:
        copy.wait()


def prefix_kernel(chunk_ref, prior_ref):
    total = jnp.zeros(chunk_ref.shape[1:], F32)
    for chip in range(CHIPS):
        prior_ref[chip] = total.astype(BF16)
        total = total + chunk_ref[chip].astype(F32)


def norm_kernel(
    query_ref, within_ref, prior_ref, s0, s1, s2, s3, gain_ref, own_ref, other_ref,
    query, within, prior, state, gain, own, other, sems,
):
    core = lax.axis_index("core")
    y = lax.axis_index("dp")
    first = [begin(prior_ref, prior, sems.at[0]), begin(gain_ref, gain, sems.at[1])]
    loads = []
    for slot, ref in enumerate((s0, s1, s2, s3)):
        loads.append(
            [
                begin(ref, state.at[slot], sems.at[2 + 3 * slot]),
                begin(query_ref.at[slot], query.at[slot], sems.at[3 + 3 * slot]),
                begin(within_ref.at[slot], within.at[slot], sems.at[4 + 3 * slot]),
            ]
        )
    for load in first:
        load.wait()
    shares = (core.astype(F32), 1.0 - core.astype(F32))
    for slot in range(SLOTS):
        for load in loads[slot]:
            load.wait()
        g = gain[pl.ds(head_of(y, core, slot), 1), :]
        for block, out in enumerate((own, other)):
            before = (prior[slot].astype(F32) + shares[block] * state[slot, 1 - block]).astype(BF16)
            mixed = within[slot, block] + mm(query[slot, block], before)
            scale = lax.rsqrt(jnp.mean(mixed * mixed, axis=-1, keepdims=True) + 1e-05)
            out[:, slot * DH : (slot + 1) * DH] = (mixed * scale * g).astype(BF16)
    copies = [begin(own, own_ref, sems.at[14]), begin(other, other_ref, sems.at[15])]
    for copy in copies:
        copy.wait()


def out_kernel(own_ref, got_ref, mine, theirs, out_ref, normed, weight, out, sems, out_sems):
    core = lax.axis_index("core")
    y = lax.axis_index("dp")
    loads = [
        begin(own_ref, normed.at[:, pl.ds(0, HALF)], sems.at[0]),
        begin(got_ref, normed.at[:, pl.ds(HALF, HALF)], sems.at[1]),
    ]
    weights = ([], [])
    for side, (source, where) in enumerate(((mine, core), (theirs, 1 - core))):
        for place in range(2):
            for slot in range(SLOTS):
                head = head_of(y, core if place == 0 else 1 - core, slot)
                index = place * SLOTS + slot
                weights[side].append(
                    begin(source.at[head, pl.ds(HALF, HALF), :], weight.at[side, index], sems.at[2 + side * 8 + index])
                )
    for load in loads:
        load.wait()
    copies = []
    for side, where in enumerate((core, 1 - core)):
        for load in weights[side]:
            load.wait()
        for c in range(0, 4, 2):
            w = jnp.concatenate(
                [
                    jnp.concatenate([weight[side, i, (c + k) * DH : (c + k + 1) * DH, :] for i in range(DP)], axis=0)
                    for k in range(2)
                ],
                axis=1,
            )
            out[side, :, c * DH : (c + 2) * DH] = mm(normed[...], w).astype(BF16)
        cols = pl.ds(pl.multiple_of(where * HALF, HALF), HALF)
        copies.append(begin(out.at[side], out_ref.at[0, :, cols], out_sems.at[side]))
    for copy in copies:
        copy.wait()


def body(tokens, w_query, w_key, w_value, w_out, norm_gain):
    own = tokens[0]
    key_1, value_1 = hop(w_key, 1), hop(w_value, 1)
    other = lax.ppermute(own, "core", SWAP)
    key_2, value_2 = hop(w_key, 2), hop(w_value, 2)

    part = call(pack_kernel, 2, shape((D, DH), BF16), [DMA((5,))], 0, 1 << 19)(w_query, w_out)
    mine = lax.all_gather(part, "dp")

    pair = shape((2, TOK, 2 * DH), BF16)
    state = shape((2, DH, DH), F32)
    flops = 2 * 2 * TOK * D * 2 * DH
    room = [
        pltpu.VMEM((2, TOK, D), BF16),
        pltpu.VMEM((D, 2 * DH), BF16),
        pltpu.VMEM((2, TOK, 2 * DH), BF16),
        pltpu.VMEM((2, DH, DH), F32),
    ]
    one = call(key_value_kernel, 4, (pair, state), [*room, DMA((6,))], flops, 3 << 20, HBM, 16)
    last = call(
        last_key_value_kernel,
        9,
        (pair, state, shape((SLOTS, DH, DH), BF16)),
        [*room, pltpu.VMEM((3, 2, DH, DH), F32), pltpu.VMEM((SLOTS, DH, DH), BF16), DMA((10,))],
        flops,
        3 << 20,
        HBM,
        16,
    )
    kv0, s0 = one(own, other, key_1, value_1)
    key_2, value_2, s0 = lax.optimization_barrier((key_2, value_2, s0))
    key_3, value_3 = hop(key_2, 1), hop(value_2, 1)
    kv1, s1 = one(own, other, key_2, value_2)
    key_3, value_3, s1 = lax.optimization_barrier((key_3, value_3, s1))
    key_4, value_4 = hop(key_3, 1), hop(value_3, 1)
    kv2, s2 = one(own, other, key_3, value_3)
    kv3, s3, total = last(own, other, w_key, w_value, key_4, value_4, s0, s1, s2)

    chunks = total.reshape(CHIPS, SLOTS * DH // CHIPS, DH)
    chunks = lax.all_to_all(chunks, ("z", "x"), 0, 0, tiled=True)
    mine, chunks = lax.optimization_barrier((mine, chunks))
    theirs = lax.ppermute(mine, "core", SWAP)
    priors = call(prefix_kernel, 1, shape(chunks.shape, BF16), [], 1 << 16, 1 << 18, VMEM, 4)(chunks)
    prior = lax.all_to_all(priors, ("z", "x"), 0, 0, tiled=True).reshape(SLOTS, DH, DH)

    queries, withins = (SLOTS, 2, TOK, DH), (SLOTS, 2, TOK, DH)
    query, within = call(
        within_kernel,
        8,
        (shape(queries, BF16), shape(withins, F32)),
        [
            pltpu.VMEM((2, TOK, D), BF16),
            pltpu.VMEM((D, SLOTS * DH), BF16),
            pltpu.VMEM((SLOTS, 2, TOK, 2 * DH), BF16),
            pltpu.VMEM(queries, BF16),
            pltpu.VMEM(withins, F32),
            DMA((14,)),
            DMA((2, SLOTS, 2)),
        ],
        3 * 2 * TOK * D * SLOTS * DH,
        8 << 20,
    )(own, other, mine, theirs, kv0, kv1, kv2, kv3)

    normed = (TOK, SLOTS * DH)
    normed_own, normed_other = call(
        norm_kernel,
        8,
        (shape(normed, BF16), shape(normed, BF16)),
        [
            pltpu.VMEM(queries, BF16),
            pltpu.VMEM(withins, F32),
            pltpu.VMEM((SLOTS, DH, DH), BF16),
            pltpu.VMEM((SLOTS, 2, DH, DH), F32),
            pltpu.VMEM((DP, DH), F32),
            pltpu.VMEM(normed, BF16),
            pltpu.VMEM(normed, BF16),
            DMA((16,)),
        ],
        1 << 28,
        4 << 20,
    )(query, within, prior, s0, s1, s2, s3, norm_gain.reshape(DP, DH))
    got = lax.ppermute(normed_other, "core", SWAP)
    return call(
        out_kernel,
        4,
        shape((1, TOK, D), BF16),
        [
            pltpu.VMEM((TOK, D), BF16),
            pltpu.VMEM((2, DP, HALF, DH), BF16),
            pltpu.VMEM((2, TOK, HALF), BF16),
            DMA((18,)),
            DMA((2,)),
        ],
        1 << 30,
        5 << 20,
    )(normed_own, got, mine, theirs)


def solution(mesh):
    fine = Mesh(mesh.devices.reshape(DP, ZN, XN, 2), ("dp", "z", "x", "core"))
    seq = ("z", "x", "core")
    in_specs = (
        P("dp", seq, None),
        P(None, "dp"),
        P(None, "dp"),
        P(None, "dp"),
        P("dp", None),
        P(),
    )
    return jax.shard_map(body, mesh=fine, in_specs=in_specs, out_specs=P("dp", seq, None), check_vma=False)
```

time: 151 us -> 150 us (level)
  blocking collectives: 0 us -> 19.3 us
  starting transfers between devices: 56.5 us -> 38.9 us
  Pallas kernels: 18.8 us -> 36.4 us
  local copies, waits for them, and re-layouts: 23.4 us -> 6.28 us
  waiting for transfers between devices: 37.6 us -> 35.3 us
    all_to_all x0 -> x1, blocking collectives: none -> 19.3 us  [body(): chunks = lax.all_to_all(chunks, ('z', 'x'), 0, 0, tiled=True)]
    unnamed x64 -> x30, local copies, waits for them, and re-layouts: 23.4 us -> 6.28 us
    pallas_call x7 -> x8, Pallas kernels: 16.5 us -> 33.4 us  [the longest x1 9.09 us: body(): call(within_kernel, 8, (shape(queries, BF16), shape(withins, F32)), [pltp...]
    all_to_all x1 -> x0, starting transfers between devices: 10.3 us -> none  [body(): chunks = lax.all_to_all(chunks, ('z', 'x'), 0, 0, tiled=True)]
    ppermute x12 -> x8, starting transfers between devices: 26 us -> 17.1 us  [hop(): return lax.ppermute(weight, ('dp', 'z', 'x', 'core'), toward(distance))]
    ppermute x0 -> x1, starting transfers between devices: none -> 6.18 us  [body(): theirs = lax.ppermute(mine, 'core', SWAP)]
    all_to_all x1 -> x0, waiting for transfers between devices: 3.76 us -> none  [body(): chunks = lax.all_to_all(chunks, ('z', 'x'), 0, 0, tiled=True)]
    ppermute x1, starting transfers between devices: 5.83 us -> 2.71 us  [body(): got = lax.ppermute(normed_other, 'core', SWAP)]
  transfers between devices with their start and end apart: 17 -> 13, of which waited for: 8 -> 8; matrix products, arithmetic and copies ran while one was open for 0% -> 0% of each run, Pallas kernels for 11% -> 13%
where the time goes in v2:
time: 150 us
  starting transfers between devices  38.9 us (26%)
  Pallas kernels  36.4 us (24%)
  waiting for transfers between devices  35.3 us (24%)
  blocking collectives  19.3 us (13%)
  between operations  13.7 us (9%)
  local copies, waits for them, and re-layouts  6.28 us (4%)
    ppermute x8, waiting for transfers between devices, hop(): return lax.ppermute(weight, ('dp', 'z', 'x', 'core'), toward(distance))  33.5 us
    all_to_all x1, blocking collectives, body(): chunks = lax.all_to_all(chunks, ('z', 'x'), 0, 0, tiled=True)  19.3 us
    ppermute x8, starting transfers between devices, hop(): return lax.ppermute(weight, ('dp', 'z', 'x', 'core'), toward(distance))  17.1 us
    pallas_call x1, Pallas kernels, body(): call(within_kernel, 8, (shape(queries, BF16), shape(withins, F32)), [pltp...  9.09 us
    pallas_call x1, Pallas kernels, body(): call(pack_kernel, 2, shape((D, DH), BF16), [DMA((5,))], 0, 1 << 19)  9.08 us
    ppermute x1, starting transfers between devices, body(): other = lax.ppermute(own, 'core', SWAP)  8.79 us
    unnamed x30, local copies, waits for them, and re-layouts  6.28 us
    ppermute x1, starting transfers between devices, body(): theirs = lax.ppermute(mine, 'core', SWAP)  6.18 us
  transfers between devices with their start and end apart: 13, of which 8 were waited for; matrix products, arithmetic and copies ran while one was open for 0% of the time, Pallas kernels for 13%

profile of v2, /device:TPU:1, one launch (start us, length us, event | category | flops | bytes accessed | tf_op | source)
XLA Modules:
  0.0 149.8 jit_solution(6220662770410225000)
XLA Ops:
  6.5 9.1 %shard_map.64 = bf16[1024,128]{1,0:T(8,128)(2,1)} custom-call(bf16[1024,128]{1,0:T(8,128)(2,1)} %wq.1, bf16[128,1024]{1,0:T(8,128)(2,1)} %wo.1), custom_call_target="tpu_custom_call" | custom-call | bytes 524288 | tf_op jit(solution)/shard_map/pallas_call | solution.py:268
  15.7 8.8 %collective-permute-start = (bf16[512,1024]{1,0:T(8,128)(2,1)}, bf16[512,1024]{1,0:T(8,128)(2,1)S(1)}, u32[]{:S(2)}, u32[]{:S(2)}) collective-permute-start(bf16[512,1024]{1,0:T(8,128)(2,1)} %bitcast.5), channel_id=1, source_target_pairs={{0,1},{1,0},{2,3},{3,2},{4,5},{5,4},{6,7},{7,6},{8,9},{9,8},{10,11... | collective-permute-start | bytes 3145736 | tf_op jit(solution)/shard_map/ppermute | solution.py:265
  26.4 1.9 %collective-permute-start.4 = (bf16[1024,128]{1,0:T(8,128)(2,1)}, bf16[1024,128]{1,0:T(8,128)(2,1)S(1)}, u32[]{:S(2)}, u32[]{:S(2)}) collective-permute-start(bf16[1024,128]{1,0:T(8,128)(2,1)} %wv.1), channel_id=1, source_target_pairs={{0,448},{1,65},{2,450},{3,67},{4,452},{5,69},{6,454},{7,71},{8,456... | collective-permute-start | bytes 786440 | tf_op jit(solution)/shard_map/ppermute | solution.py:35
  28.3 2.6 %collective-permute-start.1 = (bf16[1024,128]{1,0:T(8,128)(2,1)}, bf16[1024,128]{1,0:T(8,128)(2,1)S(1)}, u32[]{:S(2)}, u32[]{:S(2)}) collective-permute-start(bf16[1024,128]{1,0:T(8,128)(2,1)} %wk.1), channel_id=1, source_target_pairs={{0,384},{1,129},{2,386},{3,131},{4,388},{5,133},{6,390},{7,135},{8... | collective-permute-start | bytes 786440 | tf_op jit(solution)/shard_map/ppermute | solution.py:35
  30.9 2.4 %collective-permute-start.2 = (bf16[1024,128]{1,0:T(8,128)(2,1)}, bf16[1024,128]{1,0:T(8,128)(2,1)S(1)}, u32[]{:S(2)}, u32[]{:S(2)}) collective-permute-start(bf16[1024,128]{1,0:T(8,128)(2,1)} %wv.1), channel_id=1, source_target_pairs={{0,384},{1,129},{2,386},{3,131},{4,388},{5,133},{6,390},{7,135},{8... | collective-permute-start | bytes 786440 | tf_op jit(solution)/shard_map/ppermute | solution.py:35
  33.4 2.6 %collective-permute-done.4.wv = bf16[1024,128]{1,0:T(8,128)(2,1)S(1)} collective-permute-done((bf16[1024,128]{1,0:T(8,128)(2,1)}, bf16[1024,128]{1,0:T(8,128)(2,1)S(1)}, u32[]{:S(2)}, u32[]{:S(2)}) %collective-permute-start.4) | collective-permute-done | bytes 262176 | tf_op jit(solution)/shard_map/ppermute | solution.py:35
  37.2 2.3 %shard_map.65 = (bf16[2,512,256]{2,1,0:T(8,128)(2,1)S(1)}, f32[2,128,128]{2,1,0:T(8,128)S(1)}) custom-call(bf16[512,1024]{1,0:T(8,128)(2,1)S(1)} %bitcast.7, bf16[512,1024]{1,0:T(8,128)(2,1)S(1)} %collective-permute-done.other, bf16[1024,128]{1,0:T(8,128)(2,1)S(1)} %collective-permute-done.3.wk, bf16[1024,128]{1,0:T(8,128)(2,1)S(1)} %collective-permute-done.4.wv), custom_call_target="tpu_custom_call" | custom-call | flops 536870912 | bytes 3145728 | tf_op jit(solution)/shard_map/pallas_call | solution.py:291
  39.5 7.2 %collective-permute-done.1.wk = bf16[1024,128]{1,0:T(8,128)(2,1)S(1)} collective-permute-done((bf16[1024,128]{1,0:T(8,128)(2,1)}, bf16[1024,128]{1,0:T(8,128)(2,1)S(1)}, u32[]{:S(2)}, u32[]{:S(2)}) %collective-permute-start.1) | collective-permute-done | bytes 262176 | tf_op jit(solution)/shard_map/ppermute | solution.py:35
  46.6 9.3 %collective-permute-done.2.wv = bf16[1024,128]{1,0:T(8,128)(2,1)S(1)} collective-permute-done((bf16[1024,128]{1,0:T(8,128)(2,1)}, bf16[1024,128]{1,0:T(8,128)(2,1)S(1)}, u32[]{:S(2)}, u32[]{:S(2)}) %collective-permute-start.2) | collective-permute-done | bytes 262176 | tf_op jit(solution)/shard_map/ppermute | solution.py:35
  55.9 2.0 %collective-permute-start.5 = (bf16[1024,128]{1,0:T(8,128)(2,1)S(1)}, bf16[1024,128]{1,0:T(8,128)(2,1)S(1)}, u32[]{:S(2)}, u32[]{:S(2)}) collective-permute-start(bf16[1024,128]{1,0:T(8,128)(2,1)S(1)} %collective-permute-done.1.wk), channel_id=1, source_target_pairs={{0,448},{1,65},{2,450},{3,67},{4,452},{5,69},{6,454},{7,71},{8,456... | collective-permute-start | bytes 786440 | tf_op jit(solution)/shard_map/ppermute | solution.py:35
  59.9 2.3 %shard_map.66 = (bf16[2,512,256]{2,1,0:T(8,128)(2,1)S(1)}, f32[2,128,128]{2,1,0:T(8,128)S(1)}) custom-call(bf16[512,1024]{1,0:T(8,128)(2,1)S(1)} %bitcast.8, bf16[512,1024]{1,0:T(8,128)(2,1)S(1)} %collective-permute-done.other, bf16[1024,128]{1,0:T(8,128)(2,1)S(1)} %collective-permute-done.1.wk, bf16[1024,128]{1,0:T(8,128)(2,1)S(1)} %collective-permute-done.2.wv), custom_call_target="tpu_custom_call" | custom-call | flops 536870912 | bytes 3145728 | tf_op jit(solution)/shard_map/pallas_call | solution.py:294
  62.2 7.9 %collective-permute-done.5.wk = bf16[1024,128]{1,0:T(8,128)(2,1)S(1)} collective-permute-done((bf16[1024,128]{1,0:T(8,128)(2,1)S(1)}, bf16[1024,128]{1,0:T(8,128)(2,1)S(1)}, u32[]{:S(2)}, u32[]{:S(2)}) %collective-permute-start.5) | collective-permute-done | bytes 262176 | tf_op jit(solution)/shard_map/ppermute | solution.py:35
  70.1 2.9 %collective-permute-done.6.wv = bf16[1024,128]{1,0:T(8,128)(2,1)S(1)} collective-permute-done((bf16[1024,128]{1,0:T(8,128)(2,1)S(1)}, bf16[1024,128]{1,0:T(8,128)(2,1)S(1)}, u32[]{:S(2)}, u32[]{:S(2)}) %collective-permute-start.6) | collective-permute-done | bytes 262176 | tf_op jit(solution)/shard_map/ppermute | solution.py:35
  73.0 2.4 %collective-permute-start.7 = (bf16[1024,128]{1,0:T(8,128)(2,1)S(1)}, bf16[1024,128]{1,0:T(8,128)(2,1)S(1)}, u32[]{:S(2)}, u32[]{:S(2)}) collective-permute-start(bf16[1024,128]{1,0:T(8,128)(2,1)S(1)} %collective-permute-done.5.wk), channel_id=1, source_target_pairs={{0,448},{1,65},{2,450},{3,67},{4,452},{5,69},{6,454},{7,71},{8,456... | collective-permute-start | bytes 786440 | tf_op jit(solution)/shard_map/ppermute | solution.py:35
  77.3 2.3 %shard_map.67 = (bf16[2,512,256]{2,1,0:T(8,128)(2,1)S(1)}, f32[2,128,128]{2,1,0:T(8,128)S(1)}) custom-call(bf16[512,1024]{1,0:T(8,128)(2,1)S(1)} %bitcast.9, bf16[512,1024]{1,0:T(8,128)(2,1)S(1)} %collective-permute-done.other, bf16[1024,128]{1,0:T(8,128)(2,1)S(1)} %collective-permute-done.5.wk, bf16[1024,128]{1,0:T(8,128)(2,1)S(1)} %collective-permute-done.6.wv), custom_call_target="tpu_custom_call" | custom-call | flops 536870912 | bytes 3145728 | tf_op jit(solution)/shard_map/pallas_call | solution.py:297
  81.3 2.8 %collective-permute-done.8.wv_far = bf16[1024,128]{1,0:T(8,128)(2,1)S(1)} collective-permute-done((bf16[1024,128]{1,0:T(8,128)(2,1)S(1)}, bf16[1024,128]{1,0:T(8,128)(2,1)S(1)}, u32[]{:S(2)}, u32[]{:S(2)}) %collective-permute-start.8) | collective-permute-done | bytes 262176 | tf_op jit(solution)/shard_map/ppermute | solution.py:35
  84.2 3.0 %shard_map.68 = (bf16[2,512,256]{2,1,0:T(8,128)(2,1)S(1)}, f32[2,128,128]{2,1,0:T(8,128)S(1)}, bf16[4,128,128]{2,1,0:T(8,128)(2,1)S(1)}) custom-call(bf16[512,1024]{1,0:T(8,128)(2,1)S(1)} %bitcast.10, bf16[512,1024]{1,0:T(8,128)(2,1)S(1)} %collective-permute-done.other, bf16[1024,128]{1,0:T(8,128)(2,1)S(1)} %copy-done.9, bf16[1024,128]{1,0:T(8,128)(2,1)S(1)} %copy-done.10, ...), custom_call_target="tpu_custom_call" | custom-call | flops 536870912 | bytes 3145728 | tf_op jit(solution)/shard_map/pallas_call | solution.py:298
  88.6 19.3 %all_to_all.10.chunk_ref = bf16[32,16,128]{2,1,0:T(8,128)(2,1)S(1)} all-to-all(bf16[32,16,128]{2,1,0:T(8,128)(2,1)S(1)} %bitcast.11), channel_id=1, replica_groups=mesh['dp'=8,'z'=8,'x'=4,'core'=2] {'z','x'}, dimensions={0} | all-to-all | bytes 262144 | tf_op jit(solution)/shard_map/all_to_all | solution.py:301
  107.9 6.2 %collective-permute-start.9 = (bf16[8,1024,128]{2,1,0:T(8,128)(2,1)}, bf16[8,1024,128]{2,1,0:T(8,128)(2,1)S(1)}, u32[]{:S(2)}, u32[]{:S(2)}) collective-permute-start(bf16[8,1024,128]{2,1,0:T(8,128)(2,1)} %bitcast.12), channel_id=1, source_target_pairs={{0,1},{1,0},{2,3},{3,2},{4,5},{5,4},{6,7},{7,6},{8,9},{9,8},{10,11... | collective-permute-start | bytes 6291464 | tf_op jit(solution)/shard_map/ppermute | solution.py:303
  114.8 4.0 %all-to-all-start.1 = ((bf16[32,16,128]{2,1,0:T(8,128)(2,1)}), bf16[32,16,128]{2,1,0:T(8,128)(2,1)S(1)}, u32[]{:S(2)}, u32[]{:S(2)}) async-start(bf16[32,16,128]{2,1,0:T(8,128)(2,1)} %shard_map.70), calls=%async_computation.1 | async-start | bytes 262144 | tf_op jit(solution)/shard_map/all_to_all | solution.py:305
  120.2 9.1 %shard_map.69 = (bf16[4,2,512,128]{3,2,1,0:T(8,128)(2,1)}, f32[4,2,512,128]{3,2,1,0:T(8,128)}) custom-call(bf16[512,1024]{1,0:T(8,128)(2,1)} %bitcast.6, bf16[512,1024]{1,0:T(8,128)(2,1)} %copy-done.1, bf16[8,1024,128]{2,1,0:T(8,128)(2,1)} %bitcast.13, bf16[8,1024,128]{2,1,0:T(8,128)(2,1)} %copy-done.12, bf16[2,512,256]{2,1,0:T(8,128)(2,1)} %copy-done.5, ...), custom_call_target="tpu_custom_call" | custom-call | flops 1610612736 | bytes 8388608 | tf_op jit(solution)/shard_map/pallas_call | solution.py:308
  129.9 3.9 %shard_map.71 = (bf16[512,512]{1,0:T(8,128)(2,1)}, bf16[512,512]{1,0:T(8,128)(2,1)}) custom-call(bf16[4,2,512,128]{3,2,1,0:T(8,128)(2,1)} %get-tuple-element.41.query_ref, f32[4,2,512,128]{3,2,1,0:T(8,128)} %get-tuple-element.42.within_ref, bf16[4,128,128]{2,1,0:T(8,128)(2,1)} %bitcast.15, f32[2,128,128]{2,1,0:T(8,128)} %copy-done.2, ...), custom_call_target="tpu_custom_call" | custom-call | flops 268435456 | bytes 4194304 | tf_op jit(solution)/shard_map/pallas_call | solution.py:326
  133.8 2.7 %collective-permute-start.10 = (bf16[512,512]{1,0:T(8,128)(2,1)}, bf16[512,512]{1,0:T(8,128)(2,1)S(1)}, u32[]{:S(2)}, u32[]{:S(2)}) collective-permute-start(bf16[512,512]{1,0:T(8,128)(2,1)} %get-tuple-element.46), channel_id=1, source_target_pairs={{0,1},{1,0},{2,3},{3,2},{4,5},{5,4},{6,7},{7,6},{8,9},{9,8},{10,11... | collective-permute-start | bytes 1572872 | tf_op jit(solution)/shard_map/ppermute | solution.py:343
  139.1 3.9 %shard_map.72 = bf16[1,512,1024]{2,1,0:T(8,128)(2,1)} custom-call(bf16[512,512]{1,0:T(8,128)(2,1)} %get-tuple-element.45.own_ref, bf16[512,512]{1,0:T(8,128)(2,1)} %copy-done.13, bf16[8,1024,128]{2,1,0:T(8,128)(2,1)} %bitcast.14, bf16[8,1024,128]{2,1,0:T(8,128)(2,1)} %copy-done.12), custom_call_target="tpu_custom_call" | custom-call | flops 1073741824 | bytes 5242880 | tf_op jit(solution)/shard_map/pallas_call | solution.py:344
  (43 shorter events, 15.4 us)
Async XLA Ops:
  6.5 101.4 %all-gather.3.cloned.1.call-start = ((), (), s32[]{:S(2)}) async-start(), calls=%async_computation.2 | async-start | bytes 2359296 | tf_op jit(solution)/shard_map/all_gather | solution.py:269
  15.7 20.3 %collective-permute-start = (bf16[512,1024]{1,0:T(8,128)(2,1)}, bf16[512,1024]{1,0:T(8,128)(2,1)S(1)}, u32[]{:S(2)}, u32[]{:S(2)}) collective-permute-start(bf16[512,1024]{1,0:T(8,128)(2,1)} %bitcast.5), channel_id=1, source_target_pairs={{0,1},{1,0},{2,3},{3,2},{4,5},{5,4},{6,7},{7,6},{8,9},{9,8},{10,11... | collective-permute-start | bytes 3145736 | tf_op jit(solution)/shard_map/ppermute | solution.py:265
  24.5 8.9 %collective-permute-start.3 = (bf16[1024,128]{1,0:T(8,128)(2,1)}, bf16[1024,128]{1,0:T(8,128)(2,1)S(1)}, u32[]{:S(2)}, u32[]{:S(2)}) collective-permute-start(bf16[1024,128]{1,0:T(8,128)(2,1)} %wk.1), channel_id=1, source_target_pairs={{0,448},{1,65},{2,450},{3,67},{4,452},{5,69},{6,454},{7,71},{8,456... | collective-permute-start | bytes 786440 | tf_op jit(solution)/shard_map/ppermute | solution.py:35
  26.4 9.6 %collective-permute-start.4 = (bf16[1024,128]{1,0:T(8,128)(2,1)}, bf16[1024,128]{1,0:T(8,128)(2,1)S(1)}, u32[]{:S(2)}, u32[]{:S(2)}) collective-permute-start(bf16[1024,128]{1,0:T(8,128)(2,1)} %wv.1), channel_id=1, source_target_pairs={{0,448},{1,65},{2,450},{3,67},{4,452},{5,69},{6,454},{7,71},{8,456... | collective-permute-start | bytes 786440 | tf_op jit(solution)/shard_map/ppermute | solution.py:35
  28.3 18.3 %collective-permute-start.1 = (bf16[1024,128]{1,0:T(8,128)(2,1)}, bf16[1024,128]{1,0:T(8,128)(2,1)S(1)}, u32[]{:S(2)}, u32[]{:S(2)}) collective-permute-start(bf16[1024,128]{1,0:T(8,128)(2,1)} %wk.1), channel_id=1, source_target_pairs={{0,384},{1,129},{2,386},{3,131},{4,388},{5,133},{6,390},{7,135},{8... | collective-permute-start | bytes 786440 | tf_op jit(solution)/shard_map/ppermute | solution.py:35
  30.9 25.0 %collective-permute-start.2 = (bf16[1024,128]{1,0:T(8,128)(2,1)}, bf16[1024,128]{1,0:T(8,128)(2,1)S(1)}, u32[]{:S(2)}, u32[]{:S(2)}) collective-permute-start(bf16[1024,128]{1,0:T(8,128)(2,1)} %wv.1), channel_id=1, source_target_pairs={{0,384},{1,129},{2,386},{3,131},{4,388},{5,133},{6,390},{7,135},{8... | collective-permute-start | bytes 786440 | tf_op jit(solution)/shard_map/ppermute | solution.py:35
  35.9 1.2 copy-start
  37.2 47.0 %copy-start.1 = (bf16[512,1024]{1,0:T(8,128)(2,1)}, bf16[512,1024]{1,0:T(8,128)(2,1)S(1)}, u32[]{:S(2)}) copy-start(bf16[512,1024]{1,0:T(8,128)(2,1)S(1)} %collective-permute-done.other) | copy-start | bytes 3145732
  39.4 40.2 %copy-start.5 = (bf16[2,512,256]{2,1,0:T(8,128)(2,1)}, bf16[2,512,256]{2,1,0:T(8,128)(2,1)S(1)}, u32[]{:S(2)}) copy-start(bf16[2,512,256]{2,1,0:T(8,128)(2,1)S(1)} %get-tuple-element.37.kv0) | copy-start | bytes 1572868
  39.4 44.7 %copy-start.2 = (f32[2,128,128]{2,1,0:T(8,128)}, f32[2,128,128]{2,1,0:T(8,128)S(1)}, u32[]{:S(2)}) copy-start(f32[2,128,128]{2,1,0:T(8,128)S(1)} %get-tuple-element.32.s0) | copy-start | bytes 393220
  55.9 28.2 %copy-start.9 = (bf16[1024,128]{1,0:T(8,128)(2,1)S(1)}, bf16[1024,128]{1,0:T(8,128)(2,1)}, u32[]{:S(2)}) copy-start(bf16[1024,128]{1,0:T(8,128)(2,1)} %wk.1) | copy-start | bytes 786436
  55.9 28.2 %copy-start.10 = (bf16[1024,128]{1,0:T(8,128)(2,1)S(1)}, bf16[1024,128]{1,0:T(8,128)(2,1)}, u32[]{:S(2)}) copy-start(bf16[1024,128]{1,0:T(8,128)(2,1)} %wv.1) | copy-start | bytes 786436
  55.9 14.1 %collective-permute-start.5 = (bf16[1024,128]{1,0:T(8,128)(2,1)S(1)}, bf16[1024,128]{1,0:T(8,128)(2,1)S(1)}, u32[]{:S(2)}, u32[]{:S(2)}) collective-permute-start(bf16[1024,128]{1,0:T(8,128)(2,1)S(1)} %collective-permute-done.1.wk), channel_id=1, source_target_pairs={{0,448},{1,65},{2,450},{3,67},{4,452},{5,69},{6,454},{7,71},{8,456... | collective-permute-start | bytes 786440 | tf_op jit(solution)/shard_map/ppermute | solution.py:35
  58.0 15.0 %collective-permute-start.6 = (bf16[1024,128]{1,0:T(8,128)(2,1)S(1)}, bf16[1024,128]{1,0:T(8,128)(2,1)S(1)}, u32[]{:S(2)}, u32[]{:S(2)}) collective-permute-start(bf16[1024,128]{1,0:T(8,128)(2,1)S(1)} %collective-permute-done.2.wv), channel_id=1, source_target_pairs={{0,448},{1,65},{2,450},{3,67},{4,452},{5,69},{6,454},{7,71},{8,456... | collective-permute-start | bytes 786440 | tf_op jit(solution)/shard_map/ppermute | solution.py:35
  62.2 25.0 %copy-start.3 = (f32[2,128,128]{2,1,0:T(8,128)}, f32[2,128,128]{2,1,0:T(8,128)S(1)}, u32[]{:S(2)}) copy-start(f32[2,128,128]{2,1,0:T(8,128)S(1)} %get-tuple-element.33.s1) | copy-start | bytes 393220
  62.2 25.0 %copy-start.6 = (bf16[2,512,256]{2,1,0:T(8,128)(2,1)}, bf16[2,512,256]{2,1,0:T(8,128)(2,1)S(1)}, u32[]{:S(2)}) copy-start(bf16[2,512,256]{2,1,0:T(8,128)(2,1)S(1)} %get-tuple-element.38.kv1) | copy-start | bytes 1572868
  73.0 8.3 %collective-permute-start.7 = (bf16[1024,128]{1,0:T(8,128)(2,1)S(1)}, bf16[1024,128]{1,0:T(8,128)(2,1)S(1)}, u32[]{:S(2)}, u32[]{:S(2)}) collective-permute-start(bf16[1024,128]{1,0:T(8,128)(2,1)S(1)} %collective-permute-done.5.wk), channel_id=1, source_target_pairs={{0,448},{1,65},{2,450},{3,67},{4,452},{5,69},{6,454},{7,71},{8,456... | collective-permute-start | bytes 786440 | tf_op jit(solution)/shard_map/ppermute | solution.py:35
  75.4 8.7 %collective-permute-start.8 = (bf16[1024,128]{1,0:T(8,128)(2,1)S(1)}, bf16[1024,128]{1,0:T(8,128)(2,1)S(1)}, u32[]{:S(2)}, u32[]{:S(2)}) collective-permute-start(bf16[1024,128]{1,0:T(8,128)(2,1)S(1)} %collective-permute-done.6.wv), channel_id=1, source_target_pairs={{0,448},{1,65},{2,450},{3,67},{4,452},{5,69},{6,454},{7,71},{8,456... | collective-permute-start | bytes 786440 | tf_op jit(solution)/shard_map/ppermute | solution.py:35
  79.6 0.8 copy-start.7
  80.4 34.4 %copy-start.4 = (f32[2,128,128]{2,1,0:T(8,128)}, f32[2,128,128]{2,1,0:T(8,128)S(1)}, u32[]{:S(2)}) copy-start(f32[2,128,128]{2,1,0:T(8,128)S(1)} %get-tuple-element.34.s2) | copy-start | bytes 393220
  107.9 10.9 %collective-permute-start.9 = (bf16[8,1024,128]{2,1,0:T(8,128)(2,1)}, bf16[8,1024,128]{2,1,0:T(8,128)(2,1)S(1)}, u32[]{:S(2)}, u32[]{:S(2)}) collective-permute-start(bf16[8,1024,128]{2,1,0:T(8,128)(2,1)} %bitcast.12), channel_id=1, source_target_pairs={{0,1},{1,0},{2,3},{3,2},{4,5},{5,4},{6,7},{7,6},{8,9},{9,8},{10,11... | collective-permute-start | bytes 6291464 | tf_op jit(solution)/shard_map/ppermute | solution.py:303
  114.8 14.5 %all-to-all-start.1 = ((bf16[32,16,128]{2,1,0:T(8,128)(2,1)}), bf16[32,16,128]{2,1,0:T(8,128)(2,1)S(1)}, u32[]{:S(2)}, u32[]{:S(2)}) async-start(bf16[32,16,128]{2,1,0:T(8,128)(2,1)} %shard_map.70), calls=%async_computation.1 | async-start | bytes 262144 | tf_op jit(solution)/shard_map/all_to_all | solution.py:305
  118.8 1.3 copy-start.12
  133.8 4.4 %collective-permute-start.10 = (bf16[512,512]{1,0:T(8,128)(2,1)}, bf16[512,512]{1,0:T(8,128)(2,1)S(1)}, u32[]{:S(2)}, u32[]{:S(2)}) collective-permute-start(bf16[512,512]{1,0:T(8,128)(2,1)} %get-tuple-element.46), channel_id=1, source_target_pairs={{0,1},{1,0},{2,3},{3,2},{4,5},{5,4},{6,7},{7,6},{8,9},{9,8},{10,11... | collective-permute-start | bytes 1572872 | tf_op jit(solution)/shard_map/ppermute | solution.py:343
  (4 other events, 2.9 us)
Sparse Core Ops, SparseCore 0:
  15.8 54.7 all-gather.2

commit v3 on v2

--- a/solution.py
+++ b/solution.py
@@ -22,17 +22,13 @@
 DMA = pltpu.SemaphoreType.DMA
 
 
-def toward(distance):
+def hop(weight):
     pairs = []
     for y in range(DP):
         for place in range(2 * CHIPS):
-            step = -distance if place % 2 == 0 else distance
+            step = -1 if place % 2 == 0 else 1
             pairs.append((y * 2 * CHIPS + place, (y + step) % DP * 2 * CHIPS + place))
-    return pairs
-
-
-def hop(weight, distance):
-    return lax.ppermute(weight, ("dp", "z", "x", "core"), toward(distance))
+    return lax.ppermute(weight, ("dp", "z", "x", "core"), pairs)
 
 
 def call(kernel, count, outs, scratch, flops, moved, spec=HBM, limit=56):
@@ -75,17 +71,6 @@
     return lax.rem(y + DP + (slot + 1) * (1 - 2 * core), DP)
 
 
-def pack_kernel(wq, wo, part, sems):
-    core = lax.axis_index("core")
-    start = pl.multiple_of(core * HALF, HALF)
-    copies = [begin(wq.at[pl.ds(start, HALF), :], part.at[pl.ds(0, HALF), :], sems.at[0])]
-    for c in range(4):
-        cols = pl.ds(pl.multiple_of(core * HALF + c * DH, DH), DH)
-        copies.append(begin(wo.at[:, cols], part.at[pl.ds(HALF + c * DH, DH), :], sems.at[1 + c]))
-    for copy in copies:
-        copy.wait()
-
-
 def project(own, other, loads, kv, state, tokens, weight, kv_out, state_out, sems):
     copies = [begin(ref, tokens.at[block], sems.at[2 + block]) for block, ref in enumerate((own, other))]
     for load in loads:
@@ -136,20 +121,25 @@
 
 
 def within_kernel(
-    own, other, mine, theirs, kv0, kv1, kv2, kv3, query_ref, within_ref, tokens, weight, kv, query, within, sems, out_sems
+    own, other, q0, q1, q2, q_own, q_far, kv0, kv1, kv2, kv3, query_ref, within_ref,
+    tokens, weight, kv, query, within, sems, out_sems,
 ):
     core = lax.axis_index("core")
-    y = lax.axis_index("dp")
     loads = [begin(ref, tokens.at[block], sems.at[block]) for block, ref in enumerate((own, other))]
     weights, pairs = [], []
-    for slot in range(SLOTS):
-        head = head_of(y, core, slot)
-        cols = pl.ds(slot * DH, DH)
-        weights.append([])
-        for side, (source, place) in enumerate(((mine, core), (theirs, 1 - core))):
-            rows = pl.ds(pl.multiple_of(place * HALF, HALF), HALF)
-            sem = sems.at[2 + 2 * slot + side]
-            weights[slot].append(begin(source.at[head, pl.ds(0, HALF), :], weight.at[rows, cols], sem))
+    for slot, ref in enumerate((q0, q1, q2)):
+        weights.append(begin(ref, weight.at[:, pl.ds(slot * DH, DH)], sems.at[2 + slot]))
+    final = weight.at[:, pl.ds(3 * DH, DH)]
+
+    @pl.when(core == 0)
+    def _():
+        begin(q_own, final, sems.at[5])
+
+    @pl.when(core != 0)
+    def _():
+        begin(q_far, final, sems.at[5])
+
+    weights.append(pltpu.make_async_copy(q_own, final, sems.at[5]))
     for slot, ref in enumerate((kv0, kv1, kv2, kv3)):
         pairs.append(begin(ref, kv.at[slot], sems.at[10 + slot]))
     half = TOK // 2
@@ -161,8 +151,7 @@
     copies = []
     for pair in range(2):
         for slot in (2 * pair, 2 * pair + 1):
-            for load in weights[slot]:
-                load.wait()
+            weights[slot].wait()
             pairs[slot].wait()
         for block in range(2):
             both = mm(tokens[block], weight[:, 2 * pair * DH : 2 * (pair + 1) * DH]).astype(BF16)
@@ -222,51 +211,33 @@
         copy.wait()
 
 
-def out_kernel(own_ref, got_ref, mine, theirs, out_ref, normed, weight, out, sems, out_sems):
+def out_kernel(own_ref, got_ref, weight_ref, out_ref, normed, weight, out, sems, out_sems):
     core = lax.axis_index("core")
     y = lax.axis_index("dp")
     loads = [
         begin(own_ref, normed.at[:, pl.ds(0, HALF)], sems.at[0]),
         begin(got_ref, normed.at[:, pl.ds(HALF, HALF)], sems.at[1]),
     ]
-    weights = ([], [])
-    for side, (source, where) in enumerate(((mine, core), (theirs, 1 - core))):
-        for place in range(2):
-            for slot in range(SLOTS):
-                head = head_of(y, core if place == 0 else 1 - core, slot)
-                index = place * SLOTS + slot
-                weights[side].append(
-                    begin(source.at[head, pl.ds(HALF, HALF), :], weight.at[side, index], sems.at[2 + side * 8 + index])
-                )
+    for place in range(2):
+        for slot in range(SLOTS):
+            rows = pl.ds(pl.multiple_of(head_of(y, core if place == 0 else 1 - core, slot) * DH, DH), DH)
+            index = place * SLOTS + slot
+            loads.append(begin(weight_ref.at[rows, :], weight.at[pl.ds(index * DH, DH), :], sems.at[2 + index]))
     for load in loads:
         load.wait()
     copies = []
-    for side, where in enumerate((core, 1 - core)):
-        for load in weights[side]:
-            load.wait()
-        for c in range(0, 4, 2):
-            w = jnp.concatenate(
-                [
-                    jnp.concatenate([weight[side, i, (c + k) * DH : (c + k + 1) * DH, :] for i in range(DP)], axis=0)
-                    for k in range(2)
-                ],
-                axis=1,
-            )
-            out[side, :, c * DH : (c + 2) * DH] = mm(normed[...], w).astype(BF16)
-        cols = pl.ds(pl.multiple_of(where * HALF, HALF), HALF)
-        copies.append(begin(out.at[side], out_ref.at[0, :, cols], out_sems.at[side]))
+    for c in range(4):
+        cols = pl.ds(c * 2 * DH, 2 * DH)
+        out[:, cols] = mm(normed[...], weight[:, cols]).astype(BF16)
+        copies.append(begin(out.at[:, cols], out_ref.at[0, :, cols], out_sems.at[c]))
     for copy in copies:
         copy.wait()
 
 
 def body(tokens, w_query, w_key, w_value, w_out, norm_gain):
     own = tokens[0]
-    key_1, value_1 = hop(w_key, 1), hop(w_value, 1)
+    key_1, value_1, query_1 = hop(w_key), hop(w_value), hop(w_query)
     other = lax.ppermute(own, "core", SWAP)
-    key_2, value_2 = hop(w_key, 2), hop(w_value, 2)
-
-    part = call(pack_kernel, 2, shape((D, DH), BF16), [DMA((5,))], 0, 1 << 19)(w_query, w_out)
-    mine = lax.all_gather(part, "dp")
 
     pair = shape((2, TOK, 2 * DH), BF16)
     state = shape((2, DH, DH), F32)
@@ -289,25 +260,26 @@
         16,
     )
     kv0, s0 = one(own, other, key_1, value_1)
+    key_2, value_2, query_2 = hop(key_1), hop(value_1), hop(query_1)
     key_2, value_2, s0 = lax.optimization_barrier((key_2, value_2, s0))
-    key_3, value_3 = hop(key_2, 1), hop(value_2, 1)
     kv1, s1 = one(own, other, key_2, value_2)
+    w_out, key_2 = lax.optimization_barrier((w_out, key_2))
+    full_out = lax.all_gather(w_out, "dp", axis=0, tiled=True)
+    key_3, value_3, query_3 = hop(key_2), hop(value_2), hop(query_2)
     key_3, value_3, s1 = lax.optimization_barrier((key_3, value_3, s1))
-    key_4, value_4 = hop(key_3, 1), hop(value_3, 1)
     kv2, s2 = one(own, other, key_3, value_3)
+    key_4, value_4, query_4 = hop(key_3), hop(value_3), hop(query_3)
     kv3, s3, total = last(own, other, w_key, w_value, key_4, value_4, s0, s1, s2)
 
     chunks = total.reshape(CHIPS, SLOTS * DH // CHIPS, DH)
     chunks = lax.all_to_all(chunks, ("z", "x"), 0, 0, tiled=True)
-    mine, chunks = lax.optimization_barrier((mine, chunks))
-    theirs = lax.ppermute(mine, "core", SWAP)
     priors = call(prefix_kernel, 1, shape(chunks.shape, BF16), [], 1 << 16, 1 << 18, VMEM, 4)(chunks)
     prior = lax.all_to_all(priors, ("z", "x"), 0, 0, tiled=True).reshape(SLOTS, DH, DH)
 
     queries, withins = (SLOTS, 2, TOK, DH), (SLOTS, 2, TOK, DH)
     query, within = call(
         within_kernel,
-        8,
+        11,
         (shape(queries, BF16), shape(withins, F32)),
         [
             pltpu.VMEM((2, TOK, D), BF16),
@@ -320,7 +292,7 @@
         ],
         3 * 2 * TOK * D * SLOTS * DH,
         8 << 20,
-    )(own, other, mine, theirs, kv0, kv1, kv2, kv3)
+    )(own, other, query_1, query_2, query_3, w_query, query_4, kv0, kv1, kv2, kv3)
 
     normed = (TOK, SLOTS * DH)
     normed_own, normed_other = call(
@@ -343,18 +315,18 @@
     got = lax.ppermute(normed_other, "core", SWAP)
     return call(
         out_kernel,
-        4,
+        3,
         shape((1, TOK, D), BF16),
         [
             pltpu.VMEM((TOK, D), BF16),
-            pltpu.VMEM((2, DP, HALF, DH), BF16),
-            pltpu.VMEM((2, TOK, HALF), BF16),
-            DMA((18,)),
-            DMA((2,)),
+            pltpu.VMEM((D, D), BF16),
+            pltpu.VMEM((TOK, D), BF16),
+            DMA((10,)),
+            DMA((4,)),
         ],
         1 << 30,
         5 << 20,
-    )(normed_own, got, mine, theirs)
+    )(normed_own, got, full_out)
 
 
 def solution(mesh):

time: 150 us -> 141 us (0.940)
  starting transfers between devices: 38.9 us -> 62.7 us
  blocking collectives: 19.3 us -> 0 us
  Pallas kernels: 36.4 us -> 27.9 us
  waiting for transfers between devices: 35.3 us -> 29.9 us
    all_to_all x1 -> x0, blocking collectives: 19.3 us -> none  [body(): chunks = lax.all_to_all(chunks, ('z', 'x'), 0, 0, tiled=True)]
    all_to_all x0 -> x1, starting transfers between devices: none -> 11.8 us  [body(): chunks = lax.all_to_all(chunks, ('z', 'x'), 0, 0, tiled=True)]
    ppermute x9 -> x12, waiting for transfers between devices: 33.6 us -> 22.2 us  [hop(): return lax.ppermute(weight, ('dp', 'z', 'x', 'core'), pairs)]
    pallas_call x3 -> x2, Pallas kernels: 22.1 us -> 13.1 us  [the longest x1 9.09 us: body(): call(within_kernel, 11, (shape(queries, BF16), shape(withins, F32)), [plt...]
    ppermute x1, starting transfers between devices: 2.71 us -> 11.5 us  [body(): got = lax.ppermute(normed_other, 'core', SWAP)]
    all_to_all x0 -> x1, waiting for transfers between devices: none -> 5.94 us  [body(): chunks = lax.all_to_all(chunks, ('z', 'x'), 0, 0, tiled=True)]
    ppermute x9 -> x12, starting transfers between devices: 23.3 us -> 26.7 us  [hop(): return lax.ppermute(weight, ('dp', 'z', 'x', 'core'), pairs)]
    unnamed x30 -> x40, local copies, waits for them, and re-layouts: 6.28 us -> 6.45 us
  transfers between devices with their start and end apart: 13 -> 17, of which waited for: 8 -> 9; matrix products, arithmetic and copies ran while one was open for 0% -> 0% of each run, Pallas kernels for 13% -> 17%
where the time goes in v3:
time: 141 us
  starting transfers between devices  62.7 us (44%)
  waiting for transfers between devices  29.9 us (21%)
  Pallas kernels  27.9 us (20%)
  between operations  13.8 us (10%)
  local copies, waits for them, and re-layouts  6.45 us (5%)
    ppermute x12, starting transfers between devices, hop(): return lax.ppermute(weight, ('dp', 'z', 'x', 'core'), pairs)  26.7 us
    ppermute x12, waiting for transfers between devices, hop(): return lax.ppermute(weight, ('dp', 'z', 'x', 'core'), pairs)  22.2 us
    all_to_all x1, starting transfers between devices, body(): chunks = lax.all_to_all(chunks, ('z', 'x'), 0, 0, tiled=True)  11.8 us
    ppermute x1, starting transfers between devices, body(): got = lax.ppermute(normed_other, 'core', SWAP)  11.5 us
    pallas_call x1, Pallas kernels, body(): call(within_kernel, 11, (shape(queries, BF16), shape(withins, F32)), [plt...  9.09 us
    ppermute x1, starting transfers between devices, body(): other = lax.ppermute(own, 'core', SWAP)  8.78 us
    unnamed x40, local copies, waits for them, and re-layouts  6.45 us
    all_to_all x1, waiting for transfers between devices, body(): chunks = lax.all_to_all(chunks, ('z', 'x'), 0, 0, tiled=True)  5.94 us
  transfers between devices with their start and end apart: 17, of which 9 were waited for; matrix products, arithmetic and copies ran while one was open for 0% of the time, Pallas kernels for 17%

profile of v3, /device:TPU:1, one launch (start us, length us, event | category | flops | bytes accessed | tf_op | source)
XLA Modules:
  0.0 140.8 jit_solution(17109155981788159158)
XLA Ops:
  6.5 8.8 %collective-permute-start = (bf16[512,1024]{1,0:T(8,128)(2,1)}, bf16[512,1024]{1,0:T(8,128)(2,1)S(1)}, u32[]{:S(2)}, u32[]{:S(2)}) collective-permute-start(bf16[512,1024]{1,0:T(8,128)(2,1)} %bitcast.4), channel_id=1, source_target_pairs={{0,1},{1,0},{2,3},{3,2},{4,5},{5,4},{6,7},{7,6},{8,9},{9,8},{10,11... | collective-permute-start | bytes 3145736 | tf_op jit(solution)/shard_map/ppermute | solution.py:240
  15.3 1.9 %collective-permute-start.5 = (bf16[1024,128]{1,0:T(8,128)(2,1)}, bf16[1024,128]{1,0:T(8,128)(2,1)S(1)}, u32[]{:S(2)}, u32[]{:S(2)}) collective-permute-start(bf16[1024,128]{1,0:T(8,128)(2,1)} %wk.1), channel_id=1, source_target_pairs={{0,448},{1,65},{2,450},{3,67},{4,452},{5,69},{6,454},{7,71},{8,456... | collective-permute-start | bytes 786440 | tf_op jit(solution)/shard_map/ppermute | solution.py:31
  17.3 1.9 %collective-permute-start.6 = (bf16[1024,128]{1,0:T(8,128)(2,1)}, bf16[1024,128]{1,0:T(8,128)(2,1)S(1)}, u32[]{:S(2)}, u32[]{:S(2)}) collective-permute-start(bf16[1024,128]{1,0:T(8,128)(2,1)} %wv.1), channel_id=1, source_target_pairs={{0,448},{1,65},{2,450},{3,67},{4,452},{5,69},{6,454},{7,71},{8,456... | collective-permute-start | bytes 786440 | tf_op jit(solution)/shard_map/ppermute | solution.py:31
  19.2 4.7 %collective-permute-done.5.wk = bf16[1024,128]{1,0:T(8,128)(2,1)S(1)} collective-permute-done((bf16[1024,128]{1,0:T(8,128)(2,1)}, bf16[1024,128]{1,0:T(8,128)(2,1)S(1)}, u32[]{:S(2)}, u32[]{:S(2)}) %collective-permute-start.5) | collective-permute-done | bytes 262176 | tf_op jit(solution)/shard_map/ppermute | solution.py:31
  29.8 2.3 %shard_map.64 = (bf16[2,512,256]{2,1,0:T(8,128)(2,1)S(1)}, f32[2,128,128]{2,1,0:T(8,128)S(1)}) custom-call(bf16[512,1024]{1,0:T(8,128)(2,1)S(1)} %bitcast.6, bf16[512,1024]{1,0:T(8,128)(2,1)S(1)} %collective-permute-done.other, bf16[1024,128]{1,0:T(8,128)(2,1)S(1)} %collective-permute-done.5.wk, bf16[1024,128]{1,0:T(8,128)(2,1)S(1)} %collective-permute-done.6.wv), custom_call_target="tpu_custom_call" | custom-call | flops 536870912 | bytes 3145728 | tf_op jit(solution)/shard_map/pallas_call | solution.py:262
  32.9 2.1 %collective-permute-done.8.wv = bf16[1024,128]{1,0:T(8,128)(2,1)S(1)} collective-permute-done((bf16[1024,128]{1,0:T(8,128)(2,1)S(1)}, bf16[1024,128]{1,0:T(8,128)(2,1)S(1)}, u32[]{:S(2)}, u32[]{:S(2)}) %collective-permute-start.8) | collective-permute-done | bytes 262176 | tf_op jit(solution)/shard_map/ppermute | solution.py:31
  35.0 2.1 %collective-permute-start.1 = (bf16[1024,128]{1,0:T(8,128)(2,1)S(1)}, bf16[1024,128]{1,0:T(8,128)(2,1)S(1)}, u32[]{:S(2)}, u32[]{:S(2)}) collective-permute-start(bf16[1024,128]{1,0:T(8,128)(2,1)S(1)} %copy-done.15), channel_id=1, source_target_pairs={{0,448},{1,65},{2,450},{3,67},{4,452},{5,69},{6,454},{7,71},{8,456... | collective-permute-start | bytes 786440 | tf_op jit(solution)/shard_map/ppermute | solution.py:31
  37.1 1.9 %collective-permute-start.9 = (bf16[1024,128]{1,0:T(8,128)(2,1)S(1)}, bf16[1024,128]{1,0:T(8,128)(2,1)S(1)}, u32[]{:S(2)}, u32[]{:S(2)}) collective-permute-start(bf16[1024,128]{1,0:T(8,128)(2,1)S(1)} %collective-permute-done.7.wk), channel_id=1, source_target_pairs={{0,448},{1,65},{2,450},{3,67},{4,452},{5,69},{6,454},{7,71},{8,456... | collective-permute-start | bytes 786440 | tf_op jit(solution)/shard_map/ppermute | solution.py:31
  41.0 2.5 %collective-permute-done.1.q0 = bf16[1024,128]{1,0:T(8,128)(2,1)S(1)} collective-permute-done((bf16[1024,128]{1,0:T(8,128)(2,1)S(1)}, bf16[1024,128]{1,0:T(8,128)(2,1)S(1)}, u32[]{:S(2)}, u32[]{:S(2)}) %collective-permute-start.1) | collective-permute-done | bytes 262176 | tf_op jit(solution)/shard_map/ppermute | solution.py:31
  45.4 2.3 %shard_map.65 = (bf16[2,512,256]{2,1,0:T(8,128)(2,1)S(1)}, f32[2,128,128]{2,1,0:T(8,128)S(1)}) custom-call(bf16[512,1024]{1,0:T(8,128)(2,1)S(1)} %bitcast.7, bf16[512,1024]{1,0:T(8,128)(2,1)S(1)} %collective-permute-done.other, bf16[1024,128]{1,0:T(8,128)(2,1)S(1)} %collective-permute-done.7.wk, bf16[1024,128]{1,0:T(8,128)(2,1)S(1)} %collective-permute-done.8.wv), custom_call_target="tpu_custom_call" | custom-call | flops 536870912 | bytes 3145728 | tf_op jit(solution)/shard_map/pallas_call | solution.py:265
  51.0 2.9 %collective-permute-start.12 = (bf16[1024,128]{1,0:T(8,128)(2,1)S(1)}, bf16[1024,128]{1,0:T(8,128)(2,1)S(1)}, u32[]{:S(2)}, u32[]{:S(2)}) collective-permute-start(bf16[1024,128]{1,0:T(8,128)(2,1)S(1)} %collective-permute-done.10.wv), channel_id=1, source_target_pairs={{0,448},{1,65},{2,450},{3,67},{4,452},{5,69},{6,454},{7,71},{8,456... | collective-permute-start | bytes 786440 | tf_op jit(solution)/shard_map/ppermute | solution.py:31
  53.9 3.1 %collective-permute-start.3 = (bf16[1024,128]{1,0:T(8,128)(2,1)S(1)}, bf16[1024,128]{1,0:T(8,128)(2,1)S(1)}, u32[]{:S(2)}, u32[]{:S(2)}) collective-permute-start(bf16[1024,128]{1,0:T(8,128)(2,1)S(1)} %collective-permute-done.2.q1), channel_id=1, source_target_pairs={{0,448},{1,65},{2,450},{3,67},{4,452},{5,69},{6,454},{7,71},{8,456... | collective-permute-start | bytes 786440 | tf_op jit(solution)/shard_map/ppermute | solution.py:31
  57.0 2.3 %shard_map.66 = (bf16[2,512,256]{2,1,0:T(8,128)(2,1)S(1)}, f32[2,128,128]{2,1,0:T(8,128)S(1)}) custom-call(bf16[512,1024]{1,0:T(8,128)(2,1)S(1)} %bitcast.8, bf16[512,1024]{1,0:T(8,128)(2,1)S(1)} %collective-permute-done.other, bf16[1024,128]{1,0:T(8,128)(2,1)S(1)} %collective-permute-done.9.wk, bf16[1024,128]{1,0:T(8,128)(2,1)S(1)} %collective-permute-done.10.wv), custom_call_target="tpu_custom_call" | custom-call | flops 536870912 | bytes 3145728 | tf_op jit(solution)/shard_map/pallas_call | solution.py:270
  59.3 3.4 %collective-permute-done.11.wk_far = bf16[1024,128]{1,0:T(8,128)(2,1)S(1)} collective-permute-done((bf16[1024,128]{1,0:T(8,128)(2,1)S(1)}, bf16[1024,128]{1,0:T(8,128)(2,1)S(1)}, u32[]{:S(2)}, u32[]{:S(2)}) %collective-permute-start.11) | collective-permute-done | bytes 262176 | tf_op jit(solution)/shard_map/ppermute | solution.py:31
  62.7 8.0 %collective-permute-done.12.wv_far = bf16[1024,128]{1,0:T(8,128)(2,1)S(1)} collective-permute-done((bf16[1024,128]{1,0:T(8,128)(2,1)S(1)}, bf16[1024,128]{1,0:T(8,128)(2,1)S(1)}, u32[]{:S(2)}, u32[]{:S(2)}) %collective-permute-start.12) | collective-permute-done | bytes 262176 | tf_op jit(solution)/shard_map/ppermute | solution.py:31
  70.7 3.5 %shard_map.67 = (bf16[2,512,256]{2,1,0:T(8,128)(2,1)S(1)}, f32[2,128,128]{2,1,0:T(8,128)S(1)}, bf16[4,128,128]{2,1,0:T(8,128)(2,1)}) custom-call(bf16[512,1024]{1,0:T(8,128)(2,1)S(1)} %bitcast.9, bf16[512,1024]{1,0:T(8,128)(2,1)S(1)} %collective-permute-done.other, bf16[1024,128]{1,0:T(8,128)(2,1)S(1)} %copy-done.6, bf16[1024,128]{1,0:T(8,128)(2,1)S(1)} %copy-done.7, ...), custom_call_target="tpu_custom_call" | custom-call | flops 536870912 | bytes 3145728 | tf_op jit(solution)/shard_map/pallas_call | solution.py:272
  75.7 11.8 %all-to-all-start = ((bf16[32,16,128]{2,1,0:T(8,128)(2,1)}), bf16[32,16,128]{2,1,0:T(8,128)(2,1)S(1)}, u32[]{:S(2)}, u32[]{:S(2)}) async-start(bf16[32,16,128]{2,1,0:T(8,128)(2,1)} %bitcast.1), calls=%async_computation | async-start | bytes 262144 | tf_op jit(solution)/shard_map/all_to_all | solution.py:275
  87.5 3.4 %collective-permute-start.4 = (bf16[1024,128]{1,0:T(8,128)(2,1)S(1)}, bf16[1024,128]{1,0:T(8,128)(2,1)S(1)}, u32[]{:S(2)}, u32[]{:S(2)}) collective-permute-start(bf16[1024,128]{1,0:T(8,128)(2,1)S(1)} %collective-permute-done.3.q2), channel_id=1, source_target_pairs={{0,448},{1,65},{2,450},{3,67},{4,452},{5,69},{6,454},{7,71},{8,456... | collective-permute-start | bytes 786440 | tf_op jit(solution)/shard_map/ppermute | solution.py:31
  90.9 5.9 %all-to-all-done.chunk_ref = bf16[32,16,128]{2,1,0:T(8,128)(2,1)S(1)} async-done(((bf16[32,16,128]{2,1,0:T(8,128)(2,1)}), bf16[32,16,128]{2,1,0:T(8,128)(2,1)S(1)}, u32[]{:S(2)}, u32[]{:S(2)}) %all-to-all-start) | async-done | bytes 131104 | tf_op jit(solution)/shard_map/all_to_all | solution.py:275
  97.5 4.0 %all-to-all-start.1 = ((bf16[32,16,128]{2,1,0:T(8,128)(2,1)}), bf16[32,16,128]{2,1,0:T(8,128)(2,1)S(1)}, u32[]{:S(2)}, u32[]{:S(2)}) async-start(bf16[32,16,128]{2,1,0:T(8,128)(2,1)} %shard_map.69), calls=%async_computation.1 | async-start | bytes 262144 | tf_op jit(solution)/shard_map/all_to_all | solution.py:277
  102.2 9.1 %shard_map.68 = (bf16[4,2,512,128]{3,2,1,0:T(8,128)(2,1)}, f32[4,2,512,128]{3,2,1,0:T(8,128)}) custom-call(bf16[512,1024]{1,0:T(8,128)(2,1)} %bitcast.5, bf16[512,1024]{1,0:T(8,128)(2,1)} %copy-done.2, bf16[1024,128]{1,0:T(8,128)(2,1)} %copy-done.16, bf16[1024,128]{1,0:T(8,128)(2,1)} %copy-done.17, bf16[1024,128]{1,0:T(8,128)(2,1)} %copy-done.18, ...), custom_call_target="tpu_custom_call" | custom-call | flops 1610612736 | bytes 8388608 | tf_op jit(solution)/shard_map/pallas_call | solution.py:280
  112.0 3.9 %shard_map.70 = (bf16[512,512]{1,0:T(8,128)(2,1)}, bf16[512,512]{1,0:T(8,128)(2,1)}) custom-call(bf16[4,2,512,128]{3,2,1,0:T(8,128)(2,1)} %get-tuple-element.40.query_ref, f32[4,2,512,128]{3,2,1,0:T(8,128)} %get-tuple-element.41.within_ref, bf16[4,128,128]{2,1,0:T(8,128)(2,1)} %bitcast.10, f32[2,128,128]{2,1,0:T(8,128)} %copy-done.3, ...), custom_call_target="tpu_custom_call" | custom-call | flops 268435456 | bytes 4194304 | tf_op jit(solution)/shard_map/pallas_call | solution.py:298
  115.8 11.5 %collective-permute-start.13 = (bf16[512,512]{1,0:T(8,128)(2,1)}, bf16[512,512]{1,0:T(8,128)(2,1)S(1)}, u32[]{:S(2)}, u32[]{:S(2)}) collective-permute-start(bf16[512,512]{1,0:T(8,128)(2,1)} %get-tuple-element.45), channel_id=1, source_target_pairs={{0,1},{1,0},{2,3},{3,2},{4,5},{5,4},{6,7},{7,6},{8,9},{9,8},{10,11... | collective-permute-start | bytes 1572872 | tf_op jit(solution)/shard_map/ppermute | solution.py:315
  129.9 4.0 %shard_map.71 = bf16[1,512,1024]{2,1,0:T(8,128)(2,1)} custom-call(bf16[512,512]{1,0:T(8,128)(2,1)} %get-tuple-element.44.own_ref, bf16[512,512]{1,0:T(8,128)(2,1)} %copy-done.14, bf16[1024,1024]{1,0:T(8,128)(2,1)} %all-gather.2.cloned.1.call-done.weight_ref), custom_call_target="tpu_custom_call" | custom-call | flops 1073741824 | bytes 5242880 | tf_op jit(solution)/shard_map/pallas_call | solution.py:316
  (59 shorter events, 20.0 us)
Async XLA Ops:
  6.5 122.5 %all-gather.2.cloned.1.call-start = ((), (), s32[]{:S(2)}) async-start(), calls=%async_computation.2 | async-start | bytes 2359296 | tf_op jit(solution)/shard_map/all_gather | solution.py:267
  6.5 22.1 %collective-permute-start = (bf16[512,1024]{1,0:T(8,128)(2,1)}, bf16[512,1024]{1,0:T(8,128)(2,1)S(1)}, u32[]{:S(2)}, u32[]{:S(2)}) collective-permute-start(bf16[512,1024]{1,0:T(8,128)(2,1)} %bitcast.4), channel_id=1, source_target_pairs={{0,1},{1,0},{2,3},{3,2},{4,5},{5,4},{6,7},{7,6},{8,9},{9,8},{10,11... | collective-permute-start | bytes 3145736 | tf_op jit(solution)/shard_map/ppermute | solution.py:240
  15.3 8.5 %collective-permute-start.5 = (bf16[1024,128]{1,0:T(8,128)(2,1)}, bf16[1024,128]{1,0:T(8,128)(2,1)S(1)}, u32[]{:S(2)}, u32[]{:S(2)}) collective-permute-start(bf16[1024,128]{1,0:T(8,128)(2,1)} %wk.1), channel_id=1, source_target_pairs={{0,448},{1,65},{2,450},{3,67},{4,452},{5,69},{6,454},{7,71},{8,456... | collective-permute-start | bytes 786440 | tf_op jit(solution)/shard_map/ppermute | solution.py:31
  17.3 9.4 %collective-permute-start.6 = (bf16[1024,128]{1,0:T(8,128)(2,1)}, bf16[1024,128]{1,0:T(8,128)(2,1)S(1)}, u32[]{:S(2)}, u32[]{:S(2)}) collective-permute-start(bf16[1024,128]{1,0:T(8,128)(2,1)} %wv.1), channel_id=1, source_target_pairs={{0,448},{1,65},{2,450},{3,67},{4,452},{5,69},{6,454},{7,71},{8,456... | collective-permute-start | bytes 786440 | tf_op jit(solution)/shard_map/ppermute | solution.py:31
  23.9 9.1 %collective-permute-start.7 = (bf16[1024,128]{1,0:T(8,128)(2,1)S(1)}, bf16[1024,128]{1,0:T(8,128)(2,1)S(1)}, u32[]{:S(2)}, u32[]{:S(2)}) collective-permute-start(bf16[1024,128]{1,0:T(8,128)(2,1)S(1)} %collective-permute-done.5.wk), channel_id=1, source_target_pairs={{0,448},{1,65},{2,450},{3,67},{4,452},{5,69},{6,454},{7,71},{8,456... | collective-permute-start | bytes 786440 | tf_op jit(solution)/shard_map/ppermute | solution.py:31
  26.7 8.3 %collective-permute-start.8 = (bf16[1024,128]{1,0:T(8,128)(2,1)S(1)}, bf16[1024,128]{1,0:T(8,128)(2,1)S(1)}, u32[]{:S(2)}, u32[]{:S(2)}) collective-permute-start(bf16[1024,128]{1,0:T(8,128)(2,1)S(1)} %collective-permute-done.6.wv), channel_id=1, source_target_pairs={{0,448},{1,65},{2,450},{3,67},{4,452},{5,69},{6,454},{7,71},{8,456... | collective-permute-start | bytes 786440 | tf_op jit(solution)/shard_map/ppermute | solution.py:31
  29.8 40.8 %copy-start.2 = (bf16[512,1024]{1,0:T(8,128)(2,1)}, bf16[512,1024]{1,0:T(8,128)(2,1)S(1)}, u32[]{:S(2)}) copy-start(bf16[512,1024]{1,0:T(8,128)(2,1)S(1)} %collective-permute-done.other) | copy-start | bytes 3145732
  32.9 37.7 %copy-start.3 = (f32[2,128,128]{2,1,0:T(8,128)}, f32[2,128,128]{2,1,0:T(8,128)S(1)}, u32[]{:S(2)}) copy-start(f32[2,128,128]{2,1,0:T(8,128)S(1)} %get-tuple-element.36.s0) | copy-start | bytes 393220
  35.0 35.6 %copy-start.6 = (bf16[1024,128]{1,0:T(8,128)(2,1)S(1)}, bf16[1024,128]{1,0:T(8,128)(2,1)}, u32[]{:S(2)}) copy-start(bf16[1024,128]{1,0:T(8,128)(2,1)} %wk.1) | copy-start | bytes 786436
  35.0 35.6 %copy-start.7 = (bf16[1024,128]{1,0:T(8,128)(2,1)S(1)}, bf16[1024,128]{1,0:T(8,128)(2,1)}, u32[]{:S(2)}) copy-start(bf16[1024,128]{1,0:T(8,128)(2,1)} %wv.1) | copy-start | bytes 786436
  35.0 8.5 %collective-permute-start.1 = (bf16[1024,128]{1,0:T(8,128)(2,1)S(1)}, bf16[1024,128]{1,0:T(8,128)(2,1)S(1)}, u32[]{:S(2)}, u32[]{:S(2)}) collective-permute-start(bf16[1024,128]{1,0:T(8,128)(2,1)S(1)} %copy-done.15), channel_id=1, source_target_pairs={{0,448},{1,65},{2,450},{3,67},{4,452},{5,69},{6,454},{7,71},{8,456... | collective-permute-start | bytes 786440 | tf_op jit(solution)/shard_map/ppermute | solution.py:31
  37.1 11.4 %collective-permute-start.9 = (bf16[1024,128]{1,0:T(8,128)(2,1)S(1)}, bf16[1024,128]{1,0:T(8,128)(2,1)S(1)}, u32[]{:S(2)}, u32[]{:S(2)}) collective-permute-start(bf16[1024,128]{1,0:T(8,128)(2,1)S(1)} %collective-permute-done.7.wk), channel_id=1, source_target_pairs={{0,448},{1,65},{2,450},{3,67},{4,452},{5,69},{6,454},{7,71},{8,456... | collective-permute-start | bytes 786440 | tf_op jit(solution)/shard_map/ppermute | solution.py:31
  39.0 10.1 %collective-permute-start.10 = (bf16[1024,128]{1,0:T(8,128)(2,1)S(1)}, bf16[1024,128]{1,0:T(8,128)(2,1)S(1)}, u32[]{:S(2)}, u32[]{:S(2)}) collective-permute-start(bf16[1024,128]{1,0:T(8,128)(2,1)S(1)} %collective-permute-done.8.wv), channel_id=1, source_target_pairs={{0,448},{1,65},{2,450},{3,67},{4,452},{5,69},{6,454},{7,71},{8,456... | collective-permute-start | bytes 786440 | tf_op jit(solution)/shard_map/ppermute | solution.py:31
  43.5 10.4 %collective-permute-start.2 = (bf16[1024,128]{1,0:T(8,128)(2,1)S(1)}, bf16[1024,128]{1,0:T(8,128)(2,1)S(1)}, u32[]{:S(2)}, u32[]{:S(2)}) collective-permute-start(bf16[1024,128]{1,0:T(8,128)(2,1)S(1)} %collective-permute-done.1.q0), channel_id=1, source_target_pairs={{0,448},{1,65},{2,450},{3,67},{4,452},{5,69},{6,454},{7,71},{8,456... | collective-permute-start | bytes 786440 | tf_op jit(solution)/shard_map/ppermute | solution.py:31
  48.5 25.7 %copy-start.4 = (f32[2,128,128]{2,1,0:T(8,128)}, f32[2,128,128]{2,1,0:T(8,128)S(1)}, u32[]{:S(2)}) copy-start(f32[2,128,128]{2,1,0:T(8,128)S(1)} %get-tuple-element.37.s1) | copy-start | bytes 393220
  49.1 13.5 %collective-permute-start.11 = (bf16[1024,128]{1,0:T(8,128)(2,1)S(1)}, bf16[1024,128]{1,0:T(8,128)(2,1)S(1)}, u32[]{:S(2)}, u32[]{:S(2)}) collective-permute-start(bf16[1024,128]{1,0:T(8,128)(2,1)S(1)} %collective-permute-done.9.wk), channel_id=1, source_target_pairs={{0,448},{1,65},{2,450},{3,67},{4,452},{5,69},{6,454},{7,71},{8,456... | collective-permute-start | bytes 786440 | tf_op jit(solution)/shard_map/ppermute | solution.py:31
  51.0 19.6 %collective-permute-start.12 = (bf16[1024,128]{1,0:T(8,128)(2,1)S(1)}, bf16[1024,128]{1,0:T(8,128)(2,1)S(1)}, u32[]{:S(2)}, u32[]{:S(2)}) collective-permute-start(bf16[1024,128]{1,0:T(8,128)(2,1)S(1)} %collective-permute-done.10.wv), channel_id=1, source_target_pairs={{0,448},{1,65},{2,450},{3,67},{4,452},{5,69},{6,454},{7,71},{8,456... | collective-permute-start | bytes 786440 | tf_op jit(solution)/shard_map/ppermute | solution.py:31
  53.9 20.3 %copy-start.17 = (bf16[1024,128]{1,0:T(8,128)(2,1)}, bf16[1024,128]{1,0:T(8,128)(2,1)S(1)}, u32[]{:S(2)}) copy-start(bf16[1024,128]{1,0:T(8,128)(2,1)S(1)} %collective-permute-done.2.q1) | copy-start | bytes 786436
  53.9 33.5 %collective-permute-start.3 = (bf16[1024,128]{1,0:T(8,128)(2,1)S(1)}, bf16[1024,128]{1,0:T(8,128)(2,1)S(1)}, u32[]{:S(2)}, u32[]{:S(2)}) collective-permute-start(bf16[1024,128]{1,0:T(8,128)(2,1)S(1)} %collective-permute-done.2.q1), channel_id=1, source_target_pairs={{0,448},{1,65},{2,450},{3,67},{4,452},{5,69},{6,454},{7,71},{8,456... | collective-permute-start | bytes 786440 | tf_op jit(solution)/shard_map/ppermute | solution.py:31
  59.3 38.2 %copy-start.5 = (f32[2,128,128]{2,1,0:T(8,128)}, f32[2,128,128]{2,1,0:T(8,128)S(1)}, u32[]{:S(2)}) copy-start(f32[2,128,128]{2,1,0:T(8,128)S(1)} %get-tuple-element.38.s2) | copy-start | bytes 393220
  75.7 21.1 %all-to-all-start = ((bf16[32,16,128]{2,1,0:T(8,128)(2,1)}), bf16[32,16,128]{2,1,0:T(8,128)(2,1)S(1)}, u32[]{:S(2)}, u32[]{:S(2)}) async-start(bf16[32,16,128]{2,1,0:T(8,128)(2,1)} %bitcast.1), calls=%async_computation | async-start | bytes 262144 | tf_op jit(solution)/shard_map/all_to_all | solution.py:275
  87.5 14.0 %collective-permute-start.4 = (bf16[1024,128]{1,0:T(8,128)(2,1)S(1)}, bf16[1024,128]{1,0:T(8,128)(2,1)S(1)}, u32[]{:S(2)}, u32[]{:S(2)}) collective-permute-start(bf16[1024,128]{1,0:T(8,128)(2,1)S(1)} %collective-permute-done.3.q2), channel_id=1, source_target_pairs={{0,448},{1,65},{2,450},{3,67},{4,452},{5,69},{6,454},{7,71},{8,456... | collective-permute-start | bytes 786440 | tf_op jit(solution)/shard_map/ppermute | solution.py:31
  97.5 13.9 %all-to-all-start.1 = ((bf16[32,16,128]{2,1,0:T(8,128)(2,1)}), bf16[32,16,128]{2,1,0:T(8,128)(2,1)S(1)}, u32[]{:S(2)}, u32[]{:S(2)}) async-start(bf16[32,16,128]{2,1,0:T(8,128)(2,1)} %shard_map.69), calls=%async_computation.1 | async-start | bytes 262144 | tf_op jit(solution)/shard_map/all_to_all | solution.py:277
  115.8 13.2 %collective-permute-start.13 = (bf16[512,512]{1,0:T(8,128)(2,1)}, bf16[512,512]{1,0:T(8,128)(2,1)S(1)}, u32[]{:S(2)}, u32[]{:S(2)}) collective-permute-start(bf16[512,512]{1,0:T(8,128)(2,1)} %get-tuple-element.45), channel_id=1, source_target_pairs={{0,1},{1,0},{2,3},{3,2},{4,5},{5,4},{6,7},{7,6},{8,9},{9,8},{10,11... | collective-permute-start | bytes 1572872 | tf_op jit(solution)/shard_map/ppermute | solution.py:315
  (13 other events, 73.5 us)
Sparse Core Ops, SparseCore 0:
  35.1 45.2 all-gather.1

commit v4 on v3

--- a/solution.py
+++ b/solution.py
@@ -1,3 +1,5 @@
+import functools
+
 import jax
 import jax.numpy as jnp
 from jax import lax
@@ -178,58 +180,53 @@
         total = total + chunk_ref[chip].astype(F32)
 
 
-def norm_kernel(
-    query_ref, within_ref, prior_ref, s0, s1, s2, s3, gain_ref, own_ref, other_ref,
-    query, within, prior, state, gain, own, other, sems,
+def out_kernel(
+    block, query_ref, within_ref, prior_ref, s0, s1, s2, s3, gain_ref, o0, o1, o2, o_own, o_far, out_ref,
+    query, within, prior, state, gain, weight, normed, out, sems, out_sems,
 ):
     core = lax.axis_index("core")
     y = lax.axis_index("dp")
     first = [begin(prior_ref, prior, sems.at[0]), begin(gain_ref, gain, sems.at[1])]
-    loads = []
+    loads, weights = [], []
     for slot, ref in enumerate((s0, s1, s2, s3)):
         loads.append(
             [
-                begin(ref, state.at[slot], sems.at[2 + 3 * slot]),
-                begin(query_ref.at[slot], query.at[slot], sems.at[3 + 3 * slot]),
-                begin(within_ref.at[slot], within.at[slot], sems.at[4 + 3 * slot]),
+                begin(ref.at[1 - block], state.at[slot], sems.at[2 + 3 * slot]),
+                begin(query_ref.at[slot, block], query.at[slot], sems.at[3 + 3 * slot]),
+                begin(within_ref.at[slot, block], within.at[slot], sems.at[4 + 3 * slot]),
             ]
         )
+    for slot, ref in enumerate((o0, o1, o2)):
+        weights.append(begin(ref, weight.at[pl.ds(slot * DH, DH), :], sems.at[14 + slot]))
+    final = weight.at[pl.ds(3 * DH, DH), :]
+
+    @pl.when(core == 0)
+    def _():
+        begin(o_own, final, sems.at[17])
+
+    @pl.when(core != 0)
+    def _():
+        begin(o_far, final, sems.at[17])
+
+    weights.append(pltpu.make_async_copy(o_own, final, sems.at[17]))
     for load in first:
         load.wait()
-    shares = (core.astype(F32), 1.0 - core.astype(F32))
+    share = (core if block == 0 else 1 - core).astype(F32)
     for slot in range(SLOTS):
         for load in loads[slot]:
             load.wait()
         g = gain[pl.ds(head_of(y, core, slot), 1), :]
-        for block, out in enumerate((own, other)):
-            before = (prior[slot].astype(F32) + shares[block] * state[slot, 1 - block]).astype(BF16)
-            mixed = within[slot, block] + mm(query[slot, block], before)
-            scale = lax.rsqrt(jnp.mean(mixed * mixed, axis=-1, keepdims=True) + 1e-05)
-            out[:, slot * DH : (slot + 1) * DH] = (mixed * scale * g).astype(BF16)
-    copies = [begin(own, own_ref, sems.at[14]), begin(other, other_ref, sems.at[15])]
-    for copy in copies:
-        copy.wait()
-
-
-def out_kernel(own_ref, got_ref, weight_ref, out_ref, normed, weight, out, sems, out_sems):
-    core = lax.axis_index("core")
-    y = lax.axis_index("dp")
-    loads = [
-        begin(own_ref, normed.at[:, pl.ds(0, HALF)], sems.at[0]),
-        begin(got_ref, normed.at[:, pl.ds(HALF, HALF)], sems.at[1]),
-    ]
-    for place in range(2):
-        for slot in range(SLOTS):
-            rows = pl.ds(pl.multiple_of(head_of(y, core if place == 0 else 1 - core, slot) * DH, DH), DH)
-            index = place * SLOTS + slot
-            loads.append(begin(weight_ref.at[rows, :], weight.at[pl.ds(index * DH, DH), :], sems.at[2 + index]))
-    for load in loads:
+        before = (prior[slot].astype(F32) + share * state[slot]).astype(BF16)
+        mixed = within[slot] + mm(query[slot], before)
+        scale = lax.rsqrt(jnp.mean(mixed * mixed, axis=-1, keepdims=True) + 1e-05)
+        normed[:, slot * DH : (slot + 1) * DH] = (mixed * scale * g).astype(BF16)
+    for load in weights:
         load.wait()
     copies = []
     for c in range(4):
         cols = pl.ds(c * 2 * DH, 2 * DH)
-        out[:, cols] = mm(normed[...], weight[:, cols]).astype(BF16)
-        copies.append(begin(out.at[:, cols], out_ref.at[0, :, cols], out_sems.at[c]))
+        out[:, cols] = mm(normed[...], weight[:, cols]).astype(out.dtype)
+        copies.append(begin(out.at[:, cols], out_ref.at[:, cols], out_sems.at[c]))
     for copy in copies:
         copy.wait()
 
@@ -263,12 +260,15 @@
     key_2, value_2, query_2 = hop(key_1), hop(value_1), hop(query_1)
     key_2, value_2, s0 = lax.optimization_barrier((key_2, value_2, s0))
     kv1, s1 = one(own, other, key_2, value_2)
-    w_out, key_2 = lax.optimization_barrier((w_out, key_2))
-    full_out = lax.all_gather(w_out, "dp", axis=0, tiled=True)
     key_3, value_3, query_3 = hop(key_2), hop(value_2), hop(query_2)
     key_3, value_3, s1 = lax.optimization_barrier((key_3, value_3, s1))
     kv2, s2 = one(own, other, key_3, value_3)
     key_4, value_4, query_4 = hop(key_3), hop(value_3), hop(query_3)
+    w_out, s2 = lax.optimization_barrier((w_out, s2))
+    out_1 = hop(w_out)
+    out_2 = hop(out_1)
+    out_3 = hop(out_2)
+    out_4 = hop(out_3)
     kv3, s3, total = last(own, other, w_key, w_value, key_4, value_4, s0, s1, s2)
 
     chunks = total.reshape(CHIPS, SLOTS * DH // CHIPS, DH)
@@ -294,39 +294,34 @@
         8 << 20,
     )(own, other, query_1, query_2, query_3, w_query, query_4, kv0, kv1, kv2, kv3)
 
-    normed = (TOK, SLOTS * DH)
-    normed_own, normed_other = call(
-        norm_kernel,
-        8,
-        (shape(normed, BF16), shape(normed, BF16)),
-        [
-            pltpu.VMEM(queries, BF16),
-            pltpu.VMEM(withins, F32),
-            pltpu.VMEM((SLOTS, DH, DH), BF16),
-            pltpu.VMEM((SLOTS, 2, DH, DH), F32),
-            pltpu.VMEM((DP, DH), F32),
-            pltpu.VMEM(normed, BF16),
-            pltpu.VMEM(normed, BF16),
-            DMA((16,)),
-        ],
-        1 << 28,
-        4 << 20,
-    )(query, within, prior, s0, s1, s2, s3, norm_gain.reshape(DP, DH))
-    got = lax.ppermute(normed_other, "core", SWAP)
-    return call(
-        out_kernel,
-        3,
-        shape((1, TOK, D), BF16),
-        [
-            pltpu.VMEM((TOK, D), BF16),
-            pltpu.VMEM((D, D), BF16),
-            pltpu.VMEM((TOK, D), BF16),
-            DMA((10,)),
-            DMA((4,)),
-        ],
-        1 << 30,
-        5 << 20,
-    )(normed_own, got, full_out)
+    operands = (query, within, prior, s0, s1, s2, s3, norm_gain.reshape(DP, DH), out_1, out_2, out_3, w_out, out_4)
+    partial = []
+    for block, kind in ((1, BF16), (0, F32)):
+        partial.append(
+            call(
+                functools.partial(out_kernel, block),
+                13,
+                shape((TOK, D), kind),
+                [
+                    pltpu.VMEM((SLOTS, TOK, DH), BF16),
+                    pltpu.VMEM((SLOTS, TOK, DH), F32),
+                    pltpu.VMEM((SLOTS, DH, DH), BF16),
+                    pltpu.VMEM((SLOTS, DH, DH), F32),
+                    pltpu.VMEM((DP, DH), F32),
+                    pltpu.VMEM((SLOTS * DH, D), BF16),
+                    pltpu.VMEM((TOK, SLOTS * DH), BF16),
+                    pltpu.VMEM((TOK, D), kind),
+                    DMA((18,)),
+                    DMA((4,)),
+                ],
+                5 << 28,
+                5 << 20,
+                HBM,
+                16,
+            )(*operands)
+        )
+    got = lax.ppermute(partial[0], "core", SWAP)
+    return (partial[1] + got.astype(F32)).astype(BF16)[None]
 
 
 def solution(mesh):

time: 141 us -> 128 us (0.908)
  between operations: 13.8 us -> 0.44 us
  waiting for transfers between devices: 29.9 us -> 20.3 us
  starting transfers between devices: 62.7 us -> 68.6 us
  Pallas kernels: 27.9 us -> 29.6 us
    ppermute x12 -> x16, starting transfers between devices: 26.7 us -> 35.4 us  [hop(): return lax.ppermute(weight, ('dp', 'z', 'x', 'core'), pairs)]
    ppermute x12 -> x16, waiting for transfers between devices: 22.2 us -> 16.4 us  [hop(): return lax.ppermute(weight, ('dp', 'z', 'x', 'core'), pairs)]
    all_to_all x1, starting transfers between devices: 11.8 us -> 9.62 us  [body(): chunks = lax.all_to_all(chunks, ('z', 'x'), 0, 0, tiled=True)]
    ppermute x1, starting transfers between devices: 11.5 us -> 9.43 us  [body(): got = lax.ppermute(partial[0], 'core', SWAP)]
    all_to_all x1, waiting for transfers between devices: 5.94 us -> 3.9 us  [body(): chunks = lax.all_to_all(chunks, ('z', 'x'), 0, 0, tiled=True)]
    pallas_call x2, Pallas kernels: 7.86 us -> 9.64 us  [body(): call(functools.partial(out_kernel, block), 13, shape((TOK, D), kind), [pl...]
    ppermute x1, waiting for transfers between devices: 1.73 us -> 0.01 us  [body(): got = lax.ppermute(partial[0], 'core', SWAP)]
    unnamed x40 -> x34, local copies, waits for them, and re-layouts: 6.45 us -> 6.37 us
  transfers between devices with their start and end apart: 17 -> 20, of which waited for: 9 -> 8; matrix products, arithmetic and copies ran while one was open for 0% -> 0% of each run, Pallas kernels for 17% -> 20%
where the time goes in v4:
time: 128 us; the launch traced here: 127 us
  starting transfers between devices  68.6 us (54%)
  Pallas kernels  29.6 us (23%)
  waiting for transfers between devices  20.3 us (16%)
  local copies, waits for them, and re-layouts  6.37 us (5%)
  other arithmetic  1.37 us (1%)
    ppermute x16, starting transfers between devices, hop(): return lax.ppermute(weight, ('dp', 'z', 'x', 'core'), pairs)  35.4 us
    ppermute x16, waiting for transfers between devices, hop(): return lax.ppermute(weight, ('dp', 'z', 'x', 'core'), pairs)  16.4 us
    pallas_call x2, Pallas kernels, body(): call(functools.partial(out_kernel, block), 13, shape((TOK, D), kind), [pl...  9.64 us
    all_to_all x1, starting transfers between devices, body(): chunks = lax.all_to_all(chunks, ('z', 'x'), 0, 0, tiled=True)  9.62 us
    ppermute x1, starting transfers between devices, body(): got = lax.ppermute(partial[0], 'core', SWAP)  9.43 us
    pallas_call x1, Pallas kernels, body(): call(within_kernel, 11, (shape(queries, BF16), shape(withins, F32)), [plt...  9.07 us
    ppermute x1, starting transfers between devices, body(): other = lax.ppermute(own, 'core', SWAP)  8.78 us
    unnamed x34, local copies, waits for them, and re-layouts  6.37 us
  transfers between devices with their start and end apart: 20, of which 8 were waited for; matrix products, arithmetic and copies ran while one was open for 0% of the time, Pallas kernels for 20%

profile of v4, /device:TPU:1, one launch (start us, length us, event | category | flops | bytes accessed | tf_op | source)
XLA Modules:
  0.0 126.7 jit_solution(7112463900727103785)
XLA Ops:
  0.0 8.8 %collective-permute-start = (bf16[512,1024]{1,0:T(8,128)(2,1)}, bf16[512,1024]{1,0:T(8,128)(2,1)S(1)}, u32[]{:S(2)}, u32[]{:S(2)}) collective-permute-start(bf16[512,1024]{1,0:T(8,128)(2,1)} %bitcast.6), channel_id=1, source_target_pairs={{0,1},{1,0},{2,3},{3,2},{4,5},{5,4},{6,7},{7,6},{8,9},{9,8},{10,11... | collective-permute-start | bytes 3145736 | tf_op jit(solution)/shard_map/ppermute | solution.py:237
  8.8 1.9 %collective-permute-start.5 = (bf16[1024,128]{1,0:T(8,128)(2,1)}, bf16[1024,128]{1,0:T(8,128)(2,1)S(1)}, u32[]{:S(2)}, u32[]{:S(2)}) collective-permute-start(bf16[1024,128]{1,0:T(8,128)(2,1)} %wk.1), channel_id=1, source_target_pairs={{0,448},{1,65},{2,450},{3,67},{4,452},{5,69},{6,454},{7,71},{8,456... | collective-permute-start | bytes 786440 | tf_op jit(solution)/shard_map/ppermute | solution.py:33
  10.7 1.9 %collective-permute-start.6 = (bf16[1024,128]{1,0:T(8,128)(2,1)}, bf16[1024,128]{1,0:T(8,128)(2,1)S(1)}, u32[]{:S(2)}, u32[]{:S(2)}) collective-permute-start(bf16[1024,128]{1,0:T(8,128)(2,1)} %wv.1), channel_id=1, source_target_pairs={{0,448},{1,65},{2,450},{3,67},{4,452},{5,69},{6,454},{7,71},{8,456... | collective-permute-start | bytes 786440 | tf_op jit(solution)/shard_map/ppermute | solution.py:33
  12.6 4.7 %collective-permute-done.5.wk = bf16[1024,128]{1,0:T(8,128)(2,1)S(1)} collective-permute-done((bf16[1024,128]{1,0:T(8,128)(2,1)}, bf16[1024,128]{1,0:T(8,128)(2,1)S(1)}, u32[]{:S(2)}, u32[]{:S(2)}) %collective-permute-start.5) | collective-permute-done | bytes 262176 | tf_op jit(solution)/shard_map/ppermute | solution.py:33
  23.3 2.3 %shard_map.64 = (bf16[2,512,256]{2,1,0:T(8,128)(2,1)S(1)}, f32[2,128,128]{2,1,0:T(8,128)S(1)}) custom-call(bf16[512,1024]{1,0:T(8,128)(2,1)S(1)} %bitcast.8, bf16[512,1024]{1,0:T(8,128)(2,1)S(1)} %collective-permute-done.other, bf16[1024,128]{1,0:T(8,128)(2,1)S(1)} %collective-permute-done.5.wk, bf16[1024,128]{1,0:T(8,128)(2,1)S(1)} %collective-permute-done.6.wv), custom_call_target="tpu_custom_call" | custom-call | flops 536870912 | bytes 3145728 | tf_op jit(solution)/shard_map/pallas_call | solution.py:259
  26.4 2.1 %collective-permute-done.8.wv = bf16[1024,128]{1,0:T(8,128)(2,1)S(1)} collective-permute-done((bf16[1024,128]{1,0:T(8,128)(2,1)S(1)}, bf16[1024,128]{1,0:T(8,128)(2,1)S(1)}, u32[]{:S(2)}, u32[]{:S(2)}) %collective-permute-start.8) | collective-permute-done | bytes 262176 | tf_op jit(solution)/shard_map/ppermute | solution.py:33
  28.5 2.0 %collective-permute-start.9 = (bf16[1024,128]{1,0:T(8,128)(2,1)S(1)}, bf16[1024,128]{1,0:T(8,128)(2,1)S(1)}, u32[]{:S(2)}, u32[]{:S(2)}) collective-permute-start(bf16[1024,128]{1,0:T(8,128)(2,1)S(1)} %collective-permute-done.7.wk), channel_id=1, source_target_pairs={{0,448},{1,65},{2,450},{3,67},{4,452},{5,69},{6,454},{7,71},{8,456... | collective-permute-start | bytes 786440 | tf_op jit(solution)/shard_map/ppermute | solution.py:33
  30.5 1.9 %collective-permute-start.10 = (bf16[1024,128]{1,0:T(8,128)(2,1)S(1)}, bf16[1024,128]{1,0:T(8,128)(2,1)S(1)}, u32[]{:S(2)}, u32[]{:S(2)}) collective-permute-start(bf16[1024,128]{1,0:T(8,128)(2,1)S(1)} %collective-permute-done.8.wv), channel_id=1, source_target_pairs={{0,448},{1,65},{2,450},{3,67},{4,452},{5,69},{6,454},{7,71},{8,456... | collective-permute-start | bytes 786440 | tf_op jit(solution)/shard_map/ppermute | solution.py:33
  34.4 2.3 %shard_map.65 = (bf16[2,512,256]{2,1,0:T(8,128)(2,1)S(1)}, f32[2,128,128]{2,1,0:T(8,128)S(1)}) custom-call(bf16[512,1024]{1,0:T(8,128)(2,1)S(1)} %bitcast.9, bf16[512,1024]{1,0:T(8,128)(2,1)S(1)} %collective-permute-done.other, bf16[1024,128]{1,0:T(8,128)(2,1)S(1)} %collective-permute-done.7.wk, bf16[1024,128]{1,0:T(8,128)(2,1)S(1)} %collective-permute-done.8.wv), custom_call_target="tpu_custom_call" | custom-call | flops 536870912 | bytes 3145728 | tf_op jit(solution)/shard_map/pallas_call | solution.py:262
  36.9 2.8 %collective-permute-done.10.wv = bf16[1024,128]{1,0:T(8,128)(2,1)S(1)} collective-permute-done((bf16[1024,128]{1,0:T(8,128)(2,1)S(1)}, bf16[1024,128]{1,0:T(8,128)(2,1)S(1)}, u32[]{:S(2)}, u32[]{:S(2)}) %collective-permute-start.10) | collective-permute-done | bytes 262176 | tf_op jit(solution)/shard_map/ppermute | solution.py:33
  39.7 2.3 %shard_map.66 = (bf16[2,512,256]{2,1,0:T(8,128)(2,1)S(1)}, f32[2,128,128]{2,1,0:T(8,128)S(1)}) custom-call(bf16[512,1024]{1,0:T(8,128)(2,1)S(1)} %bitcast.10, bf16[512,1024]{1,0:T(8,128)(2,1)S(1)} %collective-permute-done.other, bf16[1024,128]{1,0:T(8,128)(2,1)S(1)} %collective-permute-done.9.wk, bf16[1024,128]{1,0:T(8,128)(2,1)S(1)} %collective-permute-done.10.wv), custom_call_target="tpu_custom_call" | custom-call | flops 536870912 | bytes 3145728 | tf_op jit(solution)/shard_map/pallas_call | solution.py:265
  45.9 4.4 %collective-permute-done.13.o0 = bf16[128,1024]{1,0:T(8,128)(2,1)S(1)} collective-permute-done((bf16[128,1024]{1,0:T(8,128)(2,1)S(1)}, bf16[128,1024]{1,0:T(8,128)(2,1)S(1)}, u32[]{:S(2)}, u32[]{:S(2)}) %collective-permute-start.13) | collective-permute-done | bytes 262176 | tf_op jit(solution)/shard_map/ppermute | solution.py:33
  56.1 4.1 %collective-permute-start.3 = (bf16[1024,128]{1,0:T(8,128)(2,1)S(1)}, bf16[1024,128]{1,0:T(8,128)(2,1)S(1)}, u32[]{:S(2)}, u32[]{:S(2)}) collective-permute-start(bf16[1024,128]{1,0:T(8,128)(2,1)S(1)} %collective-permute-done.2.q1), channel_id=1, source_target_pairs={{0,448},{1,65},{2,450},{3,67},{4,452},{5,69},{6,454},{7,71},{8,456... | collective-permute-start | bytes 786440 | tf_op jit(solution)/shard_map/ppermute | solution.py:33
  60.2 2.8 %collective-permute-start.15 = (bf16[128,1024]{1,0:T(8,128)(2,1)S(1)}, bf16[128,1024]{1,0:T(8,128)(2,1)S(1)}, u32[]{:S(2)}, u32[]{:S(2)}) collective-permute-start(bf16[128,1024]{1,0:T(8,128)(2,1)S(1)} %collective-permute-done.14.o1), channel_id=1, source_target_pairs={{0,448},{1,65},{2,450},{3,67},{4,452},{5,69},{6,454},{7,71},{8,456... | collective-permute-start | bytes 786440 | tf_op jit(solution)/shard_map/ppermute | solution.py:33
  64.3 3.5 %shard_map.67 = (bf16[2,512,256]{2,1,0:T(8,128)(2,1)S(1)}, f32[2,128,128]{2,1,0:T(8,128)S(1)}, bf16[4,128,128]{2,1,0:T(8,128)(2,1)}) custom-call(bf16[512,1024]{1,0:T(8,128)(2,1)S(1)} %bitcast.11, bf16[512,1024]{1,0:T(8,128)(2,1)S(1)} %collective-permute-done.other, bf16[1024,128]{1,0:T(8,128)(2,1)S(1)} %copy-done.5, bf16[1024,128]{1,0:T(8,128)(2,1)S(1)} %copy-done.6, ...), custom_call_target="tpu_custom_call" | custom-call | flops 536870912 | bytes 3145728 | tf_op jit(solution)/shard_map/pallas_call | solution.py:272
  68.6 9.6 %all-to-all-start = ((bf16[32,16,128]{2,1,0:T(8,128)(2,1)}), bf16[32,16,128]{2,1,0:T(8,128)(2,1)S(1)}, u32[]{:S(2)}, u32[]{:S(2)}) async-start(bf16[32,16,128]{2,1,0:T(8,128)(2,1)} %bitcast.1), calls=%async_computation | async-start | bytes 262144 | tf_op jit(solution)/shard_map/all_to_all | solution.py:275
  78.3 1.9 %collective-permute-start.4 = (bf16[1024,128]{1,0:T(8,128)(2,1)S(1)}, bf16[1024,128]{1,0:T(8,128)(2,1)S(1)}, u32[]{:S(2)}, u32[]{:S(2)}) collective-permute-start(bf16[1024,128]{1,0:T(8,128)(2,1)S(1)} %collective-permute-done.3.q2), channel_id=1, source_target_pairs={{0,448},{1,65},{2,450},{3,67},{4,452},{5,69},{6,454},{7,71},{8,456... | collective-permute-start | bytes 786440 | tf_op jit(solution)/shard_map/ppermute | solution.py:33
  80.2 3.5 %collective-permute-start.16 = (bf16[128,1024]{1,0:T(8,128)(2,1)S(1)}, bf16[128,1024]{1,0:T(8,128)(2,1)S(1)}, u32[]{:S(2)}, u32[]{:S(2)}) collective-permute-start(bf16[128,1024]{1,0:T(8,128)(2,1)S(1)} %collective-permute-done.15.o2), channel_id=1, source_target_pairs={{0,448},{1,65},{2,450},{3,67},{4,452},{5,69},{6,454},{7,71},{8,456... | collective-permute-start | bytes 786440 | tf_op jit(solution)/shard_map/ppermute | solution.py:33
  83.7 3.9 %all-to-all-done.chunk_ref = bf16[32,16,128]{2,1,0:T(8,128)(2,1)S(1)} async-done(((bf16[32,16,128]{2,1,0:T(8,128)(2,1)}), bf16[32,16,128]{2,1,0:T(8,128)(2,1)S(1)}, u32[]{:S(2)}, u32[]{:S(2)}) %all-to-all-start) | async-done | bytes 131104 | tf_op jit(solution)/shard_map/all_to_all | solution.py:275
  88.3 5.3 %all-to-all-start.1 = ((bf16[32,16,128]{2,1,0:T(8,128)(2,1)}), bf16[32,16,128]{2,1,0:T(8,128)(2,1)S(1)}, u32[]{:S(2)}, u32[]{:S(2)}) async-start(bf16[32,16,128]{2,1,0:T(8,128)(2,1)} %shard_map.69), calls=%async_computation.1 | async-start | bytes 262144 | tf_op jit(solution)/shard_map/all_to_all | solution.py:277
  94.3 9.1 %shard_map.68 = (bf16[4,2,512,128]{3,2,1,0:T(8,128)(2,1)}, f32[4,2,512,128]{3,2,1,0:T(8,128)}) custom-call(bf16[512,1024]{1,0:T(8,128)(2,1)} %bitcast.7, bf16[512,1024]{1,0:T(8,128)(2,1)} %copy-done.1, bf16[1024,128]{1,0:T(8,128)(2,1)} %copy-done.13, bf16[1024,128]{1,0:T(8,128)(2,1)} %copy-done.14, bf16[1024,128]{1,0:T(8,128)(2,1)} %copy-done.15, ...), custom_call_target="tpu_custom_call" | custom-call | flops 1610612736 | bytes 8388608 | tf_op jit(solution)/shard_map/pallas_call | solution.py:280
  106.2 4.7 %shard_map.71 = bf16[512,1024]{1,0:T(8,128)(2,1)S(1)} custom-call(bf16[4,2,512,128]{3,2,1,0:T(8,128)(2,1)S(1)} %copy-done.3, f32[4,2,512,128]{3,2,1,0:T(8,128)S(1)} %copy-done.2, bf16[4,128,128]{2,1,0:T(8,128)(2,1)S(1)} %bitcast.12, f32[2,128,128]{2,1,0:T(8,128)S(1)} %get-tuple-element.33.s0, f32[2,128,128]{2,1,0:T(8,128)S(1)} %get-tuple-element.34.s1, ...), custom_call_target="tpu_custom_call" | custom-call | flops 1342177280 | bytes 5242880 | tf_op jit(solution)/shard_map/pallas_call | solution.py:301
  111.0 9.4 %collective-permute-start.17 = (bf16[512,1024]{1,0:T(8,128)(2,1)S(1)}, bf16[512,1024]{1,0:T(8,128)(2,1)S(1)}, u32[]{:S(2)}, u32[]{:S(2)}) collective-permute-start(bf16[512,1024]{1,0:T(8,128)(2,1)S(1)} %shard_map.71), channel_id=1, source_target_pairs={{0,1},{1,0},{2,3},{3,2},{4,5},{5,4},{6,7},{7,6},{8,9},{9,8},{10,11... | collective-permute-start | bytes 3145736 | tf_op jit(solution)/shard_map/ppermute | solution.py:323
  120.4 4.9 %shard_map.70 = f32[512,1024]{1,0:T(8,128)S(1)} custom-call(bf16[4,2,512,128]{3,2,1,0:T(8,128)(2,1)S(1)} %copy-done.3, f32[4,2,512,128]{3,2,1,0:T(8,128)S(1)} %copy-done.2, bf16[4,128,128]{2,1,0:T(8,128)(2,1)S(1)} %bitcast.13, f32[2,128,128]{2,1,0:T(8,128)S(1)} %get-tuple-element.33.s0, f32[2,128,128]{2,1,0:T(8,128)S(1)} %get-tuple-element.34.s1, ...), custom_call_target="tpu_custom_call" | custom-call | flops 1342177280 | bytes 5242880 | tf_op jit(solution)/shard_map/pallas_call | solution.py:301
  (59 shorter events, 26.2 us)
Async XLA Ops:
  0.0 22.1 %collective-permute-start = (bf16[512,1024]{1,0:T(8,128)(2,1)}, bf16[512,1024]{1,0:T(8,128)(2,1)S(1)}, u32[]{:S(2)}, u32[]{:S(2)}) collective-permute-start(bf16[512,1024]{1,0:T(8,128)(2,1)} %bitcast.6), channel_id=1, source_target_pairs={{0,1},{1,0},{2,3},{3,2},{4,5},{5,4},{6,7},{7,6},{8,9},{9,8},{10,11... | collective-permute-start | bytes 3145736 | tf_op jit(solution)/shard_map/ppermute | solution.py:237
  8.8 8.5 %collective-permute-start.5 = (bf16[1024,128]{1,0:T(8,128)(2,1)}, bf16[1024,128]{1,0:T(8,128)(2,1)S(1)}, u32[]{:S(2)}, u32[]{:S(2)}) collective-permute-start(bf16[1024,128]{1,0:T(8,128)(2,1)} %wk.1), channel_id=1, source_target_pairs={{0,448},{1,65},{2,450},{3,67},{4,452},{5,69},{6,454},{7,71},{8,456... | collective-permute-start | bytes 786440 | tf_op jit(solution)/shard_map/ppermute | solution.py:33
  10.7 9.4 %collective-permute-start.6 = (bf16[1024,128]{1,0:T(8,128)(2,1)}, bf16[1024,128]{1,0:T(8,128)(2,1)S(1)}, u32[]{:S(2)}, u32[]{:S(2)}) collective-permute-start(bf16[1024,128]{1,0:T(8,128)(2,1)} %wv.1), channel_id=1, source_target_pairs={{0,448},{1,65},{2,450},{3,67},{4,452},{5,69},{6,454},{7,71},{8,456... | collective-permute-start | bytes 786440 | tf_op jit(solution)/shard_map/ppermute | solution.py:33
  17.3 9.0 %collective-permute-start.7 = (bf16[1024,128]{1,0:T(8,128)(2,1)S(1)}, bf16[1024,128]{1,0:T(8,128)(2,1)S(1)}, u32[]{:S(2)}, u32[]{:S(2)}) collective-permute-start(bf16[1024,128]{1,0:T(8,128)(2,1)S(1)} %collective-permute-done.5.wk), channel_id=1, source_target_pairs={{0,448},{1,65},{2,450},{3,67},{4,452},{5,69},{6,454},{7,71},{8,456... | collective-permute-start | bytes 786440 | tf_op jit(solution)/shard_map/ppermute | solution.py:33
  20.1 8.3 %collective-permute-start.8 = (bf16[1024,128]{1,0:T(8,128)(2,1)S(1)}, bf16[1024,128]{1,0:T(8,128)(2,1)S(1)}, u32[]{:S(2)}, u32[]{:S(2)}) collective-permute-start(bf16[1024,128]{1,0:T(8,128)(2,1)S(1)} %collective-permute-done.6.wv), channel_id=1, source_target_pairs={{0,448},{1,65},{2,450},{3,67},{4,452},{5,69},{6,454},{7,71},{8,456... | collective-permute-start | bytes 786440 | tf_op jit(solution)/shard_map/ppermute | solution.py:33
  23.3 41.0 %copy-start.1 = (bf16[512,1024]{1,0:T(8,128)(2,1)}, bf16[512,1024]{1,0:T(8,128)(2,1)S(1)}, u32[]{:S(2)}) copy-start(bf16[512,1024]{1,0:T(8,128)(2,1)S(1)} %collective-permute-done.other) | copy-start | bytes 3145732
  28.5 35.8 %copy-start.5 = (bf16[1024,128]{1,0:T(8,128)(2,1)S(1)}, bf16[1024,128]{1,0:T(8,128)(2,1)}, u32[]{:S(2)}) copy-start(bf16[1024,128]{1,0:T(8,128)(2,1)} %wk.1) | copy-start | bytes 786436
  28.5 35.8 %copy-start.6 = (bf16[1024,128]{1,0:T(8,128)(2,1)S(1)}, bf16[1024,128]{1,0:T(8,128)(2,1)}, u32[]{:S(2)}) copy-start(bf16[1024,128]{1,0:T(8,128)(2,1)} %wv.1) | copy-start | bytes 786436
  28.5 8.4 %collective-permute-start.9 = (bf16[1024,128]{1,0:T(8,128)(2,1)S(1)}, bf16[1024,128]{1,0:T(8,128)(2,1)S(1)}, u32[]{:S(2)}, u32[]{:S(2)}) collective-permute-start(bf16[1024,128]{1,0:T(8,128)(2,1)S(1)} %collective-permute-done.7.wk), channel_id=1, source_target_pairs={{0,448},{1,65},{2,450},{3,67},{4,452},{5,69},{6,454},{7,71},{8,456... | collective-permute-start | bytes 786440 | tf_op jit(solution)/shard_map/ppermute | solution.py:33
  30.5 9.2 %collective-permute-start.10 = (bf16[1024,128]{1,0:T(8,128)(2,1)S(1)}, bf16[1024,128]{1,0:T(8,128)(2,1)S(1)}, u32[]{:S(2)}, u32[]{:S(2)}) collective-permute-start(bf16[1024,128]{1,0:T(8,128)(2,1)S(1)} %collective-permute-done.8.wv), channel_id=1, source_target_pairs={{0,448},{1,65},{2,450},{3,67},{4,452},{5,69},{6,454},{7,71},{8,456... | collective-permute-start | bytes 786440 | tf_op jit(solution)/shard_map/ppermute | solution.py:33
  32.4 11.5 %collective-permute-start.1 = (bf16[1024,128]{1,0:T(8,128)(2,1)S(1)}, bf16[1024,128]{1,0:T(8,128)(2,1)S(1)}, u32[]{:S(2)}, u32[]{:S(2)}) collective-permute-start(bf16[1024,128]{1,0:T(8,128)(2,1)S(1)} %copy-done.12), channel_id=1, source_target_pairs={{0,448},{1,65},{2,450},{3,67},{4,452},{5,69},{6,454},{7,71},{8,456... | collective-permute-start | bytes 786440 | tf_op jit(solution)/shard_map/ppermute | solution.py:33
  42.0 8.3 %collective-permute-start.13 = (bf16[128,1024]{1,0:T(8,128)(2,1)S(1)}, bf16[128,1024]{1,0:T(8,128)(2,1)S(1)}, u32[]{:S(2)}, u32[]{:S(2)}) collective-permute-start(bf16[128,1024]{1,0:T(8,128)(2,1)S(1)} %copy-done.4), channel_id=1, source_target_pairs={{0,448},{1,65},{2,450},{3,67},{4,452},{5,69},{6,454},{7,71},{8,456... | collective-permute-start | bytes 786440 | tf_op jit(solution)/shard_map/ppermute | solution.py:33
  43.9 44.3 %copy-start.13 = (bf16[1024,128]{1,0:T(8,128)(2,1)}, bf16[1024,128]{1,0:T(8,128)(2,1)S(1)}, u32[]{:S(2)}) copy-start(bf16[1024,128]{1,0:T(8,128)(2,1)S(1)} %collective-permute-done.1.q0) | copy-start | bytes 786436
  43.9 12.2 %collective-permute-start.2 = (bf16[1024,128]{1,0:T(8,128)(2,1)S(1)}, bf16[1024,128]{1,0:T(8,128)(2,1)S(1)}, u32[]{:S(2)}, u32[]{:S(2)}) collective-permute-start(bf16[1024,128]{1,0:T(8,128)(2,1)S(1)} %collective-permute-done.1.q0), channel_id=1, source_target_pairs={{0,448},{1,65},{2,450},{3,67},{4,452},{5,69},{6,454},{7,71},{8,456... | collective-permute-start | bytes 786440 | tf_op jit(solution)/shard_map/ppermute | solution.py:33
  50.3 9.9 %collective-permute-start.14 = (bf16[128,1024]{1,0:T(8,128)(2,1)S(1)}, bf16[128,1024]{1,0:T(8,128)(2,1)S(1)}, u32[]{:S(2)}, u32[]{:S(2)}) collective-permute-start(bf16[128,1024]{1,0:T(8,128)(2,1)S(1)} %collective-permute-done.13.o0), channel_id=1, source_target_pairs={{0,448},{1,65},{2,450},{3,67},{4,452},{5,69},{6,454},{7,71},{8,456... | collective-permute-start | bytes 786440 | tf_op jit(solution)/shard_map/ppermute | solution.py:33
  52.2 10.8 %collective-permute-start.11 = (bf16[1024,128]{1,0:T(8,128)(2,1)S(1)}, bf16[1024,128]{1,0:T(8,128)(2,1)S(1)}, u32[]{:S(2)}, u32[]{:S(2)}) collective-permute-start(bf16[1024,128]{1,0:T(8,128)(2,1)S(1)} %collective-permute-done.9.wk), channel_id=1, source_target_pairs={{0,448},{1,65},{2,450},{3,67},{4,452},{5,69},{6,454},{7,71},{8,456... | collective-permute-start | bytes 786440 | tf_op jit(solution)/shard_map/ppermute | solution.py:33
  54.2 10.1 %collective-permute-start.12 = (bf16[1024,128]{1,0:T(8,128)(2,1)S(1)}, bf16[1024,128]{1,0:T(8,128)(2,1)S(1)}, u32[]{:S(2)}, u32[]{:S(2)}) collective-permute-start(bf16[1024,128]{1,0:T(8,128)(2,1)S(1)} %collective-permute-done.10.wv), channel_id=1, source_target_pairs={{0,448},{1,65},{2,450},{3,67},{4,452},{5,69},{6,454},{7,71},{8,456... | collective-permute-start | bytes 786440 | tf_op jit(solution)/shard_map/ppermute | solution.py:33
  56.1 22.1 %collective-permute-start.3 = (bf16[1024,128]{1,0:T(8,128)(2,1)S(1)}, bf16[1024,128]{1,0:T(8,128)(2,1)S(1)}, u32[]{:S(2)}, u32[]{:S(2)}) collective-permute-start(bf16[1024,128]{1,0:T(8,128)(2,1)S(1)} %collective-permute-done.2.q1), channel_id=1, source_target_pairs={{0,448},{1,65},{2,450},{3,67},{4,452},{5,69},{6,454},{7,71},{8,456... | collective-permute-start | bytes 786440 | tf_op jit(solution)/shard_map/ppermute | solution.py:33
  60.2 20.0 %collective-permute-start.15 = (bf16[128,1024]{1,0:T(8,128)(2,1)S(1)}, bf16[128,1024]{1,0:T(8,128)(2,1)S(1)}, u32[]{:S(2)}, u32[]{:S(2)}) collective-permute-start(bf16[128,1024]{1,0:T(8,128)(2,1)S(1)} %collective-permute-done.14.o1), channel_id=1, source_target_pairs={{0,448},{1,65},{2,450},{3,67},{4,452},{5,69},{6,454},{7,71},{8,456... | collective-permute-start | bytes 786440 | tf_op jit(solution)/shard_map/ppermute | solution.py:33
  68.6 19.0 %all-to-all-start = ((bf16[32,16,128]{2,1,0:T(8,128)(2,1)}), bf16[32,16,128]{2,1,0:T(8,128)(2,1)S(1)}, u32[]{:S(2)}, u32[]{:S(2)}) async-start(bf16[32,16,128]{2,1,0:T(8,128)(2,1)} %bitcast.1), calls=%async_computation | async-start | bytes 262144 | tf_op jit(solution)/shard_map/all_to_all | solution.py:275
  78.3 15.3 %collective-permute-start.4 = (bf16[1024,128]{1,0:T(8,128)(2,1)S(1)}, bf16[1024,128]{1,0:T(8,128)(2,1)S(1)}, u32[]{:S(2)}, u32[]{:S(2)}) collective-permute-start(bf16[1024,128]{1,0:T(8,128)(2,1)S(1)} %collective-permute-done.3.q2), channel_id=1, source_target_pairs={{0,448},{1,65},{2,450},{3,67},{4,452},{5,69},{6,454},{7,71},{8,456... | collective-permute-start | bytes 786440 | tf_op jit(solution)/shard_map/ppermute | solution.py:33
  80.2 23.2 %collective-permute-start.16 = (bf16[128,1024]{1,0:T(8,128)(2,1)S(1)}, bf16[128,1024]{1,0:T(8,128)(2,1)S(1)}, u32[]{:S(2)}, u32[]{:S(2)}) collective-permute-start(bf16[128,1024]{1,0:T(8,128)(2,1)S(1)} %collective-permute-done.15.o2), channel_id=1, source_target_pairs={{0,448},{1,65},{2,450},{3,67},{4,452},{5,69},{6,454},{7,71},{8,456... | collective-permute-start | bytes 786440 | tf_op jit(solution)/shard_map/ppermute | solution.py:33
  88.3 15.1 %all-to-all-start.1 = ((bf16[32,16,128]{2,1,0:T(8,128)(2,1)}), bf16[32,16,128]{2,1,0:T(8,128)(2,1)S(1)}, u32[]{:S(2)}, u32[]{:S(2)}) async-start(bf16[32,16,128]{2,1,0:T(8,128)(2,1)} %shard_map.69), calls=%async_computation.1 | async-start | bytes 262144 | tf_op jit(solution)/shard_map/all_to_all | solution.py:277
  111.0 14.4 %collective-permute-start.17 = (bf16[512,1024]{1,0:T(8,128)(2,1)S(1)}, bf16[512,1024]{1,0:T(8,128)(2,1)S(1)}, u32[]{:S(2)}, u32[]{:S(2)}) collective-permute-start(bf16[512,1024]{1,0:T(8,128)(2,1)S(1)} %shard_map.71), channel_id=1, source_target_pairs={{0,1},{1,0},{2,3},{3,2},{4,5},{5,4},{6,7},{7,6},{8,9},{9,8},{10,11... | collective-permute-start | bytes 3145736 | tf_op jit(solution)/shard_map/ppermute | solution.py:323
  (13 other events, 125.2 us)

commit v5 on v4

--- a/solution.py
+++ b/solution.py
@@ -256,23 +256,28 @@
         HBM,
         16,
     )
+    barrier = lax.optimization_barrier
     kv0, s0 = one(own, other, key_1, value_1)
     key_2, value_2, query_2 = hop(key_1), hop(value_1), hop(query_1)
-    key_2, value_2, s0 = lax.optimization_barrier((key_2, value_2, s0))
+    key_2, value_2, query_1, s0 = barrier((key_2, value_2, query_1, s0))
     kv1, s1 = one(own, other, key_2, value_2)
     key_3, value_3, query_3 = hop(key_2), hop(value_2), hop(query_2)
-    key_3, value_3, s1 = lax.optimization_barrier((key_3, value_3, s1))
+    key_3, value_3, query_2, s1 = barrier((key_3, value_3, query_2, s1))
     kv2, s2 = one(own, other, key_3, value_3)
-    key_4, value_4, query_4 = hop(key_3), hop(value_3), hop(query_3)
-    w_out, s2 = lax.optimization_barrier((w_out, s2))
+    key_4, value_4 = hop(key_3), hop(value_3)
+    key_4, value_4, query_3, w_out, s2 = barrier((key_4, value_4, query_3, w_out, s2))
+    query_4 = hop(query_3)
     out_1 = hop(w_out)
+    kv3, s3, total = last(own, other, w_key, w_value, key_4, value_4, s0, s1, s2)
+    out_1, total = barrier((out_1, total))
     out_2 = hop(out_1)
-    out_3 = hop(out_2)
-    out_4 = hop(out_3)
-    kv3, s3, total = last(own, other, w_key, w_value, key_4, value_4, s0, s1, s2)
 
     chunks = total.reshape(CHIPS, SLOTS * DH // CHIPS, DH)
     chunks = lax.all_to_all(chunks, ("z", "x"), 0, 0, tiled=True)
+    out_2, chunks = barrier((out_2, chunks))
+    out_3 = hop(out_2)
+    out_3, query_4 = barrier((out_3, query_4))
+    out_4 = hop(out_3)
     priors = call(prefix_kernel, 1, shape(chunks.shape, BF16), [], 1 << 16, 1 << 18, VMEM, 4)(chunks)
     prior = lax.all_to_all(priors, ("z", "x"), 0, 0, tiled=True).reshape(SLOTS, DH, DH)
 

time: 128 us -> 133 us (1.039)
  starting transfers between devices: 68.6 us -> 72.5 us
  waiting for transfers between devices: 20.3 us -> 22 us
    all_to_all x1, waiting for transfers between devices: 3.9 us -> 7.42 us  [body(): chunks = lax.all_to_all(chunks, ('z', 'x'), 0, 0, tiled=True)]
    ppermute x1, starting transfers between devices: 9.43 us -> 11.6 us  [body(): got = lax.ppermute(partial[0], 'core', SWAP)]
    ppermute x16, waiting for transfers between devices: 16.4 us -> 14.3 us  [hop(): return lax.ppermute(weight, ('dp', 'z', 'x', 'core'), pairs)]
    all_to_all x1, starting transfers between devices: 9.62 us -> 11.3 us  [body(): chunks = lax.all_to_all(chunks, ('z', 'x'), 0, 0, tiled=True)]
    ppermute x16, starting transfers between devices: 35.4 us -> 37 us  [hop(): return lax.ppermute(weight, ('dp', 'z', 'x', 'core'), pairs)]
    all_to_all x1, starting transfers between devices: 5.33 us -> 3.85 us  [body(): lax.all_to_all(priors, ('z', 'x'), 0, 0, tiled=True).reshape(SLOTS, DH, DH)]
    unnamed x34 -> x32, local copies, waits for them, and re-layouts: 6.37 us -> 6.49 us
  transfers between devices with their start and end apart: 20 -> 20, of which waited for: 8 -> 8; matrix products, arithmetic and copies ran while one was open for 0% -> 0% of each run, Pallas kernels for 20% -> 19%
where the time goes in v5:
time: 133 us; the launch traced here: 132 us
  starting transfers between devices  72.5 us (55%)
  Pallas kernels  29.7 us (22%)
  waiting for transfers between devices  22 us (17%)
  local copies, waits for them, and re-layouts  6.49 us (5%)
  other arithmetic  1.37 us (1%)
    ppermute x16, starting transfers between devices, hop(): return lax.ppermute(weight, ('dp', 'z', 'x', 'core'), pairs)  37 us
    ppermute x16, waiting for transfers between devices, hop(): return lax.ppermute(weight, ('dp', 'z', 'x', 'core'), pairs)  14.3 us
    ppermute x1, starting transfers between devices, body(): got = lax.ppermute(partial[0], 'core', SWAP)  11.6 us
    all_to_all x1, starting transfers between devices, body(): chunks = lax.all_to_all(chunks, ('z', 'x'), 0, 0, tiled=True)  11.3 us
    pallas_call x2, Pallas kernels, body(): call(functools.partial(out_kernel, block), 13, shape((TOK, D), kind), [pl...  9.65 us
    pallas_call x1, Pallas kernels, body(): call(within_kernel, 11, (shape(queries, BF16), shape(withins, F32)), [plt...  9.08 us
    ppermute x1, starting transfers between devices, body(): other = lax.ppermute(own, 'core', SWAP)  8.78 us
    all_to_all x1, waiting for transfers between devices, body(): chunks = lax.all_to_all(chunks, ('z', 'x'), 0, 0, tiled=True)  7.42 us
  transfers between devices with their start and end apart: 20, of which 8 were waited for; matrix products, arithmetic and copies ran while one was open for 0% of the time, Pallas kernels for 19%

profile of v5, /device:TPU:1, one launch (start us, length us, event | category | flops | bytes accessed | tf_op | source)
XLA Modules:
  0.0 132.5 jit_solution(7584289308214380429)
XLA Ops:
  0.0 8.8 %collective-permute-start = (bf16[512,1024]{1,0:T(8,128)(2,1)}, bf16[512,1024]{1,0:T(8,128)(2,1)S(1)}, u32[]{:S(2)}, u32[]{:S(2)}) collective-permute-start(bf16[512,1024]{1,0:T(8,128)(2,1)} %bitcast.6), channel_id=1, source_target_pairs={{0,1},{1,0},{2,3},{3,2},{4,5},{5,4},{6,7},{7,6},{8,9},{9,8},{10,11... | collective-permute-start | bytes 3145736 | tf_op jit(solution)/shard_map/ppermute | solution.py:237
  8.8 1.9 %collective-permute-start.1 = (bf16[1024,128]{1,0:T(8,128)(2,1)}, bf16[1024,128]{1,0:T(8,128)(2,1)S(1)}, u32[]{:S(2)}, u32[]{:S(2)}) collective-permute-start(bf16[1024,128]{1,0:T(8,128)(2,1)} %wk.1), channel_id=1, source_target_pairs={{0,448},{1,65},{2,450},{3,67},{4,452},{5,69},{6,454},{7,71},{8,456... | collective-permute-start | bytes 786440 | tf_op jit(solution)/shard_map/ppermute | solution.py:33
  10.7 1.9 %collective-permute-start.3 = (bf16[1024,128]{1,0:T(8,128)(2,1)}, bf16[1024,128]{1,0:T(8,128)(2,1)S(1)}, u32[]{:S(2)}, u32[]{:S(2)}) collective-permute-start(bf16[1024,128]{1,0:T(8,128)(2,1)} %wv.1), channel_id=1, source_target_pairs={{0,448},{1,65},{2,450},{3,67},{4,452},{5,69},{6,454},{7,71},{8,456... | collective-permute-start | bytes 786440 | tf_op jit(solution)/shard_map/ppermute | solution.py:33
  12.6 1.9 %collective-permute-start.5 = (bf16[1024,128]{1,0:T(8,128)(2,1)}, bf16[1024,128]{1,0:T(8,128)(2,1)S(1)}, u32[]{:S(2)}, u32[]{:S(2)}) collective-permute-start(bf16[1024,128]{1,0:T(8,128)(2,1)} %q_own.1), channel_id=1, source_target_pairs={{0,448},{1,65},{2,450},{3,67},{4,452},{5,69},{6,454},{7,71},{8,456... | collective-permute-start | bytes 786440 | tf_op jit(solution)/shard_map/ppermute | solution.py:33
  14.6 2.7 %collective-permute-done.1.wk = bf16[1024,128]{1,0:T(8,128)(2,1)S(1)} collective-permute-done((bf16[1024,128]{1,0:T(8,128)(2,1)}, bf16[1024,128]{1,0:T(8,128)(2,1)S(1)}, u32[]{:S(2)}, u32[]{:S(2)}) %collective-permute-start.1) | collective-permute-done | bytes 262176 | tf_op jit(solution)/shard_map/ppermute | solution.py:33
  26.1 2.3 %shard_map.64 = (bf16[2,512,256]{2,1,0:T(8,128)(2,1)S(1)}, f32[2,128,128]{2,1,0:T(8,128)S(1)}) custom-call(bf16[512,1024]{1,0:T(8,128)(2,1)S(1)} %bitcast.8, bf16[512,1024]{1,0:T(8,128)(2,1)S(1)} %collective-permute-done.other, bf16[1024,128]{1,0:T(8,128)(2,1)S(1)} %collective-permute-done.1.wk, bf16[1024,128]{1,0:T(8,128)(2,1)S(1)} %collective-permute-done.3.wv), custom_call_target="tpu_custom_call" | custom-call | flops 536870912 | bytes 3145728 | tf_op jit(solution)/shard_map/pallas_call | solution.py:260
  29.2 2.1 %collective-permute-start.6 = (bf16[1024,128]{1,0:T(8,128)(2,1)S(1)}, bf16[1024,128]{1,0:T(8,128)(2,1)S(1)}, u32[]{:S(2)}, u32[]{:S(2)}) collective-permute-start(bf16[1024,128]{1,0:T(8,128)(2,1)S(1)} %collective-permute-done.2.wk), channel_id=1, source_target_pairs={{0,448},{1,65},{2,450},{3,67},{4,452},{5,69},{6,454},{7,71},{8,456... | collective-permute-start | bytes 786440 | tf_op jit(solution)/shard_map/ppermute | solution.py:33
  31.2 4.4 %collective-permute-start.7 = (bf16[1024,128]{1,0:T(8,128)(2,1)S(1)}, bf16[1024,128]{1,0:T(8,128)(2,1)S(1)}, u32[]{:S(2)}, u32[]{:S(2)}) collective-permute-start(bf16[1024,128]{1,0:T(8,128)(2,1)S(1)} %collective-permute-done.4.wv), channel_id=1, source_target_pairs={{0,448},{1,65},{2,450},{3,67},{4,452},{5,69},{6,454},{7,71},{8,456... | collective-permute-start | bytes 786440 | tf_op jit(solution)/shard_map/ppermute | solution.py:33
  35.7 1.9 %collective-permute-start.11 = (bf16[1024,128]{1,0:T(8,128)(2,1)S(1)}, bf16[1024,128]{1,0:T(8,128)(2,1)S(1)}, u32[]{:S(2)}, u32[]{:S(2)}) collective-permute-start(bf16[1024,128]{1,0:T(8,128)(2,1)S(1)} %collective-permute-done.8.q1), channel_id=1, source_target_pairs={{0,448},{1,65},{2,450},{3,67},{4,452},{5,69},{6,454},{7,71},{8,456... | collective-permute-start | bytes 786440 | tf_op jit(solution)/shard_map/ppermute | solution.py:33
  37.6 2.3 %shard_map.65 = (bf16[2,512,256]{2,1,0:T(8,128)(2,1)S(1)}, f32[2,128,128]{2,1,0:T(8,128)S(1)}) custom-call(bf16[512,1024]{1,0:T(8,128)(2,1)S(1)} %bitcast.9, bf16[512,1024]{1,0:T(8,128)(2,1)S(1)} %collective-permute-done.other, bf16[1024,128]{1,0:T(8,128)(2,1)S(1)} %collective-permute-done.2.wk, bf16[1024,128]{1,0:T(8,128)(2,1)S(1)} %collective-permute-done.4.wv), custom_call_target="tpu_custom_call" | custom-call | flops 536870912 | bytes 3145728 | tf_op jit(solution)/shard_map/pallas_call | solution.py:263
  40.7 2.4 %collective-permute-start.9 = (bf16[1024,128]{1,0:T(8,128)(2,1)S(1)}, bf16[1024,128]{1,0:T(8,128)(2,1)S(1)}, u32[]{:S(2)}, u32[]{:S(2)}) collective-permute-start(bf16[1024,128]{1,0:T(8,128)(2,1)S(1)} %collective-permute-done.6.wk), channel_id=1, source_target_pairs={{0,448},{1,65},{2,450},{3,67},{4,452},{5,69},{6,454},{7,71},{8,456... | collective-permute-start | bytes 786440 | tf_op jit(solution)/shard_map/ppermute | solution.py:33
  43.1 4.2 %collective-permute-start.10 = (bf16[1024,128]{1,0:T(8,128)(2,1)S(1)}, bf16[1024,128]{1,0:T(8,128)(2,1)S(1)}, u32[]{:S(2)}, u32[]{:S(2)}) collective-permute-start(bf16[1024,128]{1,0:T(8,128)(2,1)S(1)} %collective-permute-done.7.wv), channel_id=1, source_target_pairs={{0,448},{1,65},{2,450},{3,67},{4,452},{5,69},{6,454},{7,71},{8,456... | collective-permute-start | bytes 786440 | tf_op jit(solution)/shard_map/ppermute | solution.py:33
  47.3 2.3 %shard_map.66 = (bf16[2,512,256]{2,1,0:T(8,128)(2,1)S(1)}, f32[2,128,128]{2,1,0:T(8,128)S(1)}) custom-call(bf16[512,1024]{1,0:T(8,128)(2,1)S(1)} %bitcast.10, bf16[512,1024]{1,0:T(8,128)(2,1)S(1)} %collective-permute-done.other, bf16[1024,128]{1,0:T(8,128)(2,1)S(1)} %collective-permute-done.6.wk, bf16[1024,128]{1,0:T(8,128)(2,1)S(1)} %collective-permute-done.7.wv), custom_call_target="tpu_custom_call" | custom-call | flops 536870912 | bytes 3145728 | tf_op jit(solution)/shard_map/pallas_call | solution.py:266
  49.6 2.2 %collective-permute-done.10.wv_far = bf16[1024,128]{1,0:T(8,128)(2,1)S(1)} collective-permute-done((bf16[1024,128]{1,0:T(8,128)(2,1)S(1)}, bf16[1024,128]{1,0:T(8,128)(2,1)S(1)}, u32[]{:S(2)}, u32[]{:S(2)}) %collective-permute-start.10) | collective-permute-done | bytes 262176 | tf_op jit(solution)/shard_map/ppermute | solution.py:33
  51.9 2.8 %collective-permute-start.12 = (bf16[128,1024]{1,0:T(8,128)(2,1)S(1)}, bf16[128,1024]{1,0:T(8,128)(2,1)S(1)}, u32[]{:S(2)}, u32[]{:S(2)}) collective-permute-start(bf16[128,1024]{1,0:T(8,128)(2,1)S(1)} %copy-done.4), channel_id=1, source_target_pairs={{0,448},{1,65},{2,450},{3,67},{4,452},{5,69},{6,454},{7,71},{8,456... | collective-permute-start | bytes 786440 | tf_op jit(solution)/shard_map/ppermute | solution.py:33
  54.7 3.5 %shard_map.67 = (bf16[2,512,256]{2,1,0:T(8,128)(2,1)S(1)}, f32[2,128,128]{2,1,0:T(8,128)S(1)}, bf16[4,128,128]{2,1,0:T(8,128)(2,1)}) custom-call(bf16[512,1024]{1,0:T(8,128)(2,1)S(1)} %bitcast.11, bf16[512,1024]{1,0:T(8,128)(2,1)S(1)} %collective-permute-done.other, bf16[1024,128]{1,0:T(8,128)(2,1)S(1)} %copy-done.5, bf16[1024,128]{1,0:T(8,128)(2,1)S(1)} %copy-done.6, ...), custom_call_target="tpu_custom_call" | custom-call | flops 536870912 | bytes 3145728 | tf_op jit(solution)/shard_map/pallas_call | solution.py:271
  62.1 11.3 %all-to-all-start = ((bf16[32,16,128]{2,1,0:T(8,128)(2,1)}), bf16[32,16,128]{2,1,0:T(8,128)(2,1)S(1)}, u32[]{:S(2)}, u32[]{:S(2)}) async-start(bf16[32,16,128]{2,1,0:T(8,128)(2,1)} %bitcast.1), calls=%async_computation | async-start | bytes 262144 | tf_op jit(solution)/shard_map/all_to_all | solution.py:276
  75.4 7.4 %all-to-all-done.chunk_ref = bf16[32,16,128]{2,1,0:T(8,128)(2,1)S(1)} async-done(((bf16[32,16,128]{2,1,0:T(8,128)(2,1)}), bf16[32,16,128]{2,1,0:T(8,128)(2,1)S(1)}, u32[]{:S(2)}, u32[]{:S(2)}) %all-to-all-start) | async-done | bytes 131104 | tf_op jit(solution)/shard_map/all_to_all | solution.py:276
  84.7 6.4 %collective-permute-done.14.o2 = bf16[128,1024]{1,0:T(8,128)(2,1)S(1)} collective-permute-done((bf16[128,1024]{1,0:T(8,128)(2,1)S(1)}, bf16[128,1024]{1,0:T(8,128)(2,1)S(1)}, u32[]{:S(2)}, u32[]{:S(2)}) %collective-permute-start.14) | collective-permute-done | bytes 262176 | tf_op jit(solution)/shard_map/ppermute | solution.py:33
  93.7 3.8 %all-to-all-start.1 = ((bf16[32,16,128]{2,1,0:T(8,128)(2,1)}), bf16[32,16,128]{2,1,0:T(8,128)(2,1)S(1)}, u32[]{:S(2)}, u32[]{:S(2)}) async-start(bf16[32,16,128]{2,1,0:T(8,128)(2,1)} %shard_map.69), calls=%async_computation.1 | async-start | bytes 262144 | tf_op jit(solution)/shard_map/all_to_all | solution.py:282
  97.6 9.1 %shard_map.68 = (bf16[4,2,512,128]{3,2,1,0:T(8,128)(2,1)}, f32[4,2,512,128]{3,2,1,0:T(8,128)}) custom-call(bf16[512,1024]{1,0:T(8,128)(2,1)} %bitcast.7, bf16[512,1024]{1,0:T(8,128)(2,1)} %copy-done.1, bf16[1024,128]{1,0:T(8,128)(2,1)} %copy-done.12, bf16[1024,128]{1,0:T(8,128)(2,1)} %copy-done.13, bf16[1024,128]{1,0:T(8,128)(2,1)} %copy-done.14, ...), custom_call_target="tpu_custom_call" | custom-call | flops 1610612736 | bytes 8388608 | tf_op jit(solution)/shard_map/pallas_call | solution.py:285
  109.8 4.7 %shard_map.71 = bf16[512,1024]{1,0:T(8,128)(2,1)S(1)} custom-call(bf16[4,2,512,128]{3,2,1,0:T(8,128)(2,1)S(1)} %copy-done.3, f32[4,2,512,128]{3,2,1,0:T(8,128)S(1)} %copy-done.2, bf16[4,128,128]{2,1,0:T(8,128)(2,1)S(1)} %bitcast.12, f32[2,128,128]{2,1,0:T(8,128)S(1)} %get-tuple-element.48.s0, f32[2,128,128]{2,1,0:T(8,128)S(1)} %get-tuple-element.49.s1, ...), custom_call_target="tpu_custom_call" | custom-call | flops 1342177280 | bytes 5242880 | tf_op jit(solution)/shard_map/pallas_call | solution.py:306
  114.5 11.6 %collective-permute-start.17 = (bf16[512,1024]{1,0:T(8,128)(2,1)S(1)}, bf16[512,1024]{1,0:T(8,128)(2,1)S(1)}, u32[]{:S(2)}, u32[]{:S(2)}) collective-permute-start(bf16[512,1024]{1,0:T(8,128)(2,1)S(1)} %shard_map.71), channel_id=1, source_target_pairs={{0,1},{1,0},{2,3},{3,2},{4,5},{5,4},{6,7},{7,6},{8,9},{9,8},{10,11... | collective-permute-start | bytes 3145736 | tf_op jit(solution)/shard_map/ppermute | solution.py:328
  126.1 4.9 %shard_map.70 = f32[512,1024]{1,0:T(8,128)S(1)} custom-call(bf16[4,2,512,128]{3,2,1,0:T(8,128)(2,1)S(1)} %copy-done.3, f32[4,2,512,128]{3,2,1,0:T(8,128)S(1)} %copy-done.2, bf16[4,128,128]{2,1,0:T(8,128)(2,1)S(1)} %bitcast.13, f32[2,128,128]{2,1,0:T(8,128)S(1)} %get-tuple-element.48.s0, f32[2,128,128]{2,1,0:T(8,128)S(1)} %get-tuple-element.49.s1, ...), custom_call_target="tpu_custom_call" | custom-call | flops 1342177280 | bytes 5242880 | tf_op jit(solution)/shard_map/pallas_call | solution.py:306
  (57 shorter events, 25.1 us)
Async XLA Ops:
  0.0 24.9 %collective-permute-start = (bf16[512,1024]{1,0:T(8,128)(2,1)}, bf16[512,1024]{1,0:T(8,128)(2,1)S(1)}, u32[]{:S(2)}, u32[]{:S(2)}) collective-permute-start(bf16[512,1024]{1,0:T(8,128)(2,1)} %bitcast.6), channel_id=1, source_target_pairs={{0,1},{1,0},{2,3},{3,2},{4,5},{5,4},{6,7},{7,6},{8,9},{9,8},{10,11... | collective-permute-start | bytes 3145736 | tf_op jit(solution)/shard_map/ppermute | solution.py:237
  8.8 8.5 %collective-permute-start.1 = (bf16[1024,128]{1,0:T(8,128)(2,1)}, bf16[1024,128]{1,0:T(8,128)(2,1)S(1)}, u32[]{:S(2)}, u32[]{:S(2)}) collective-permute-start(bf16[1024,128]{1,0:T(8,128)(2,1)} %wk.1), channel_id=1, source_target_pairs={{0,448},{1,65},{2,450},{3,67},{4,452},{5,69},{6,454},{7,71},{8,456... | collective-permute-start | bytes 786440 | tf_op jit(solution)/shard_map/ppermute | solution.py:33
  10.7 9.4 %collective-permute-start.3 = (bf16[1024,128]{1,0:T(8,128)(2,1)}, bf16[1024,128]{1,0:T(8,128)(2,1)S(1)}, u32[]{:S(2)}, u32[]{:S(2)}) collective-permute-start(bf16[1024,128]{1,0:T(8,128)(2,1)} %wv.1), channel_id=1, source_target_pairs={{0,448},{1,65},{2,450},{3,67},{4,452},{5,69},{6,454},{7,71},{8,456... | collective-permute-start | bytes 786440 | tf_op jit(solution)/shard_map/ppermute | solution.py:33
  12.6 10.3 %collective-permute-start.5 = (bf16[1024,128]{1,0:T(8,128)(2,1)}, bf16[1024,128]{1,0:T(8,128)(2,1)S(1)}, u32[]{:S(2)}, u32[]{:S(2)}) collective-permute-start(bf16[1024,128]{1,0:T(8,128)(2,1)} %q_own.1), channel_id=1, source_target_pairs={{0,448},{1,65},{2,450},{3,67},{4,452},{5,69},{6,454},{7,71},{8,456... | collective-permute-start | bytes 786440 | tf_op jit(solution)/shard_map/ppermute | solution.py:33
  17.3 11.8 %collective-permute-start.2 = (bf16[1024,128]{1,0:T(8,128)(2,1)S(1)}, bf16[1024,128]{1,0:T(8,128)(2,1)S(1)}, u32[]{:S(2)}, u32[]{:S(2)}) collective-permute-start(bf16[1024,128]{1,0:T(8,128)(2,1)S(1)} %collective-permute-done.1.wk), channel_id=1, source_target_pairs={{0,448},{1,65},{2,450},{3,67},{4,452},{5,69},{6,454},{7,71},{8,456... | collective-permute-start | bytes 786440 | tf_op jit(solution)/shard_map/ppermute | solution.py:33
  20.1 9.0 %collective-permute-start.4 = (bf16[1024,128]{1,0:T(8,128)(2,1)S(1)}, bf16[1024,128]{1,0:T(8,128)(2,1)S(1)}, u32[]{:S(2)}, u32[]{:S(2)}) collective-permute-start(bf16[1024,128]{1,0:T(8,128)(2,1)S(1)} %collective-permute-done.3.wv), channel_id=1, source_target_pairs={{0,448},{1,65},{2,450},{3,67},{4,452},{5,69},{6,454},{7,71},{8,456... | collective-permute-start | bytes 786440 | tf_op jit(solution)/shard_map/ppermute | solution.py:33
  22.9 12.8 %collective-permute-start.8 = (bf16[1024,128]{1,0:T(8,128)(2,1)S(1)}, bf16[1024,128]{1,0:T(8,128)(2,1)S(1)}, u32[]{:S(2)}, u32[]{:S(2)}) collective-permute-start(bf16[1024,128]{1,0:T(8,128)(2,1)S(1)} %collective-permute-done.5.q0), channel_id=1, source_target_pairs={{0,448},{1,65},{2,450},{3,67},{4,452},{5,69},{6,454},{7,71},{8,456... | collective-permute-start | bytes 786440 | tf_op jit(solution)/shard_map/ppermute | solution.py:33
  26.1 28.6 %copy-start.1 = (bf16[512,1024]{1,0:T(8,128)(2,1)}, bf16[512,1024]{1,0:T(8,128)(2,1)S(1)}, u32[]{:S(2)}) copy-start(bf16[512,1024]{1,0:T(8,128)(2,1)S(1)} %collective-permute-done.other) | copy-start | bytes 3145732
  29.2 25.6 %copy-start.5 = (bf16[1024,128]{1,0:T(8,128)(2,1)S(1)}, bf16[1024,128]{1,0:T(8,128)(2,1)}, u32[]{:S(2)}) copy-start(bf16[1024,128]{1,0:T(8,128)(2,1)} %wk.1) | copy-start | bytes 786436
  29.2 25.6 %copy-start.6 = (bf16[1024,128]{1,0:T(8,128)(2,1)S(1)}, bf16[1024,128]{1,0:T(8,128)(2,1)}, u32[]{:S(2)}) copy-start(bf16[1024,128]{1,0:T(8,128)(2,1)} %wv.1) | copy-start | bytes 786436
  29.2 11.5 %collective-permute-start.6 = (bf16[1024,128]{1,0:T(8,128)(2,1)S(1)}, bf16[1024,128]{1,0:T(8,128)(2,1)S(1)}, u32[]{:S(2)}, u32[]{:S(2)}) collective-permute-start(bf16[1024,128]{1,0:T(8,128)(2,1)S(1)} %collective-permute-done.2.wk), channel_id=1, source_target_pairs={{0,448},{1,65},{2,450},{3,67},{4,452},{5,69},{6,454},{7,71},{8,456... | collective-permute-start | bytes 786440 | tf_op jit(solution)/shard_map/ppermute | solution.py:33
  31.2 9.5 %collective-permute-start.7 = (bf16[1024,128]{1,0:T(8,128)(2,1)S(1)}, bf16[1024,128]{1,0:T(8,128)(2,1)S(1)}, u32[]{:S(2)}, u32[]{:S(2)}) collective-permute-start(bf16[1024,128]{1,0:T(8,128)(2,1)S(1)} %collective-permute-done.4.wv), channel_id=1, source_target_pairs={{0,448},{1,65},{2,450},{3,67},{4,452},{5,69},{6,454},{7,71},{8,456... | collective-permute-start | bytes 786440 | tf_op jit(solution)/shard_map/ppermute | solution.py:33
  35.7 13.9 %collective-permute-start.11 = (bf16[1024,128]{1,0:T(8,128)(2,1)S(1)}, bf16[1024,128]{1,0:T(8,128)(2,1)S(1)}, u32[]{:S(2)}, u32[]{:S(2)}) collective-permute-start(bf16[1024,128]{1,0:T(8,128)(2,1)S(1)} %collective-permute-done.8.q1), channel_id=1, source_target_pairs={{0,448},{1,65},{2,450},{3,67},{4,452},{5,69},{6,454},{7,71},{8,456... | collective-permute-start | bytes 786440 | tf_op jit(solution)/shard_map/ppermute | solution.py:33
  40.7 8.9 %collective-permute-start.9 = (bf16[1024,128]{1,0:T(8,128)(2,1)S(1)}, bf16[1024,128]{1,0:T(8,128)(2,1)S(1)}, u32[]{:S(2)}, u32[]{:S(2)}) collective-permute-start(bf16[1024,128]{1,0:T(8,128)(2,1)S(1)} %collective-permute-done.6.wk), channel_id=1, source_target_pairs={{0,448},{1,65},{2,450},{3,67},{4,452},{5,69},{6,454},{7,71},{8,456... | collective-permute-start | bytes 786440 | tf_op jit(solution)/shard_map/ppermute | solution.py:33
  43.1 8.8 %collective-permute-start.10 = (bf16[1024,128]{1,0:T(8,128)(2,1)S(1)}, bf16[1024,128]{1,0:T(8,128)(2,1)S(1)}, u32[]{:S(2)}, u32[]{:S(2)}) collective-permute-start(bf16[1024,128]{1,0:T(8,128)(2,1)S(1)} %collective-permute-done.7.wv), channel_id=1, source_target_pairs={{0,448},{1,65},{2,450},{3,67},{4,452},{5,69},{6,454},{7,71},{8,456... | collective-permute-start | bytes 786440 | tf_op jit(solution)/shard_map/ppermute | solution.py:33
  49.6 44.1 %copy-start.14 = (bf16[1024,128]{1,0:T(8,128)(2,1)}, bf16[1024,128]{1,0:T(8,128)(2,1)S(1)}, u32[]{:S(2)}) copy-start(bf16[1024,128]{1,0:T(8,128)(2,1)S(1)} %collective-permute-done.11.q2) | copy-start | bytes 786436
  51.9 8.3 %collective-permute-start.12 = (bf16[128,1024]{1,0:T(8,128)(2,1)S(1)}, bf16[128,1024]{1,0:T(8,128)(2,1)S(1)}, u32[]{:S(2)}, u32[]{:S(2)}) collective-permute-start(bf16[128,1024]{1,0:T(8,128)(2,1)S(1)} %copy-done.4), channel_id=1, source_target_pairs={{0,448},{1,65},{2,450},{3,67},{4,452},{5,69},{6,454},{7,71},{8,456... | collective-permute-start | bytes 786440 | tf_op jit(solution)/shard_map/ppermute | solution.py:33
  60.2 22.6 %collective-permute-start.13 = (bf16[128,1024]{1,0:T(8,128)(2,1)S(1)}, bf16[128,1024]{1,0:T(8,128)(2,1)S(1)}, u32[]{:S(2)}, u32[]{:S(2)}) collective-permute-start(bf16[128,1024]{1,0:T(8,128)(2,1)S(1)} %collective-permute-done.12.o0), channel_id=1, source_target_pairs={{0,448},{1,65},{2,450},{3,67},{4,452},{5,69},{6,454},{7,71},{8,456... | collective-permute-start | bytes 786440 | tf_op jit(solution)/shard_map/ppermute | solution.py:33
  62.1 20.7 %all-to-all-start = ((bf16[32,16,128]{2,1,0:T(8,128)(2,1)}), bf16[32,16,128]{2,1,0:T(8,128)(2,1)S(1)}, u32[]{:S(2)}, u32[]{:S(2)}) async-start(bf16[32,16,128]{2,1,0:T(8,128)(2,1)} %bitcast.1), calls=%async_computation | async-start | bytes 262144 | tf_op jit(solution)/shard_map/all_to_all | solution.py:276
  73.5 11.3 %collective-permute-start.15 = (bf16[1024,128]{1,0:T(8,128)(2,1)S(1)}, bf16[1024,128]{1,0:T(8,128)(2,1)S(1)}, u32[]{:S(2)}, u32[]{:S(2)}) collective-permute-start(bf16[1024,128]{1,0:T(8,128)(2,1)S(1)} %collective-permute-done.11.q2), channel_id=1, source_target_pairs={{0,448},{1,65},{2,450},{3,67},{4,452},{5,69},{6,454},{7,71},{8,456... | collective-permute-start | bytes 786440 | tf_op jit(solution)/shard_map/ppermute | solution.py:33
  82.8 8.3 %collective-permute-start.14 = (bf16[128,1024]{1,0:T(8,128)(2,1)S(1)}, bf16[128,1024]{1,0:T(8,128)(2,1)S(1)}, u32[]{:S(2)}, u32[]{:S(2)}) collective-permute-start(bf16[128,1024]{1,0:T(8,128)(2,1)S(1)} %collective-permute-done.13.o1), channel_id=1, source_target_pairs={{0,448},{1,65},{2,450},{3,67},{4,452},{5,69},{6,454},{7,71},{8,456... | collective-permute-start | bytes 786440 | tf_op jit(solution)/shard_map/ppermute | solution.py:33
  91.1 15.9 %collective-permute-start.16 = (bf16[128,1024]{1,0:T(8,128)(2,1)S(1)}, bf16[128,1024]{1,0:T(8,128)(2,1)S(1)}, u32[]{:S(2)}, u32[]{:S(2)}) collective-permute-start(bf16[128,1024]{1,0:T(8,128)(2,1)S(1)} %collective-permute-done.14.o2), channel_id=1, source_target_pairs={{0,448},{1,65},{2,450},{3,67},{4,452},{5,69},{6,454},{7,71},{8,456... | collective-permute-start | bytes 786440 | tf_op jit(solution)/shard_map/ppermute | solution.py:33
  93.7 13.3 %all-to-all-start.1 = ((bf16[32,16,128]{2,1,0:T(8,128)(2,1)}), bf16[32,16,128]{2,1,0:T(8,128)(2,1)S(1)}, u32[]{:S(2)}, u32[]{:S(2)}) async-start(bf16[32,16,128]{2,1,0:T(8,128)(2,1)} %shard_map.69), calls=%async_computation.1 | async-start | bytes 262144 | tf_op jit(solution)/shard_map/all_to_all | solution.py:282
  114.5 16.6 %collective-permute-start.17 = (bf16[512,1024]{1,0:T(8,128)(2,1)S(1)}, bf16[512,1024]{1,0:T(8,128)(2,1)S(1)}, u32[]{:S(2)}, u32[]{:S(2)}) collective-permute-start(bf16[512,1024]{1,0:T(8,128)(2,1)S(1)} %shard_map.71), channel_id=1, source_target_pairs={{0,1},{1,0},{2,3},{3,2},{4,5},{5,4},{6,7},{7,6},{8,9},{9,8},{10,11... | collective-permute-start | bytes 3145736 | tf_op jit(solution)/shard_map/ppermute | solution.py:328
  (12 other events, 92.9 us)

commit v6 on v5

--- a/solution.py
+++ b/solution.py
@@ -24,11 +24,11 @@
 DMA = pltpu.SemaphoreType.DMA
 
 
-def hop(weight):
+def hop(weight, distance=1):
     pairs = []
     for y in range(DP):
         for place in range(2 * CHIPS):
-            step = -1 if place % 2 == 0 else 1
+            step = -distance if place % 2 == 0 else distance
             pairs.append((y * 2 * CHIPS + place, (y + step) % DP * 2 * CHIPS + place))
     return lax.ppermute(weight, ("dp", "z", "x", "core"), pairs)
 
@@ -258,26 +258,25 @@
     )
     barrier = lax.optimization_barrier
     kv0, s0 = one(own, other, key_1, value_1)
-    key_2, value_2, query_2 = hop(key_1), hop(value_1), hop(query_1)
-    key_2, value_2, query_1, s0 = barrier((key_2, value_2, query_1, s0))
+    key_1, value_1, w_query = barrier((key_1, value_1, w_query))
+    key_2, value_2 = hop(key_1), hop(value_1)
+    query_2 = hop(w_query, 2)
+    key_2, value_2, query_1, w_out, s0 = barrier((key_2, value_2, query_1, w_out, s0))
     kv1, s1 = one(own, other, key_2, value_2)
-    key_3, value_3, query_3 = hop(key_2), hop(value_2), hop(query_2)
+    key_3, value_3 = hop(key_2), hop(value_2)
+    out_1 = hop(w_out)
     key_3, value_3, query_2, s1 = barrier((key_3, value_3, query_2, s1))
     kv2, s2 = one(own, other, key_3, value_3)
     key_4, value_4 = hop(key_3), hop(value_3)
-    key_4, value_4, query_3, w_out, s2 = barrier((key_4, value_4, query_3, w_out, s2))
-    query_4 = hop(query_3)
-    out_1 = hop(w_out)
+    key_4, value_4, out_1, s2 = barrier((key_4, value_4, out_1, s2))
     kv3, s3, total = last(own, other, w_key, w_value, key_4, value_4, s0, s1, s2)
-    out_1, total = barrier((out_1, total))
-    out_2 = hop(out_1)
+    w_out, s2 = barrier((w_out, s2))
+    out_2 = hop(w_out, 2)
+    query_3, query_4 = hop(query_2), hop(query_2, 2)
+    out_3, out_4 = hop(out_2), hop(out_2, 2)
 
     chunks = total.reshape(CHIPS, SLOTS * DH // CHIPS, DH)
     chunks = lax.all_to_all(chunks, ("z", "x"), 0, 0, tiled=True)
-    out_2, chunks = barrier((out_2, chunks))
-    out_3 = hop(out_2)
-    out_3, query_4 = barrier((out_3, query_4))
-    out_4 = hop(out_3)
     priors = call(prefix_kernel, 1, shape(chunks.shape, BF16), [], 1 << 16, 1 << 18, VMEM, 4)(chunks)
     prior = lax.all_to_all(priors, ("z", "x"), 0, 0, tiled=True).reshape(SLOTS, DH, DH)
 
@@ -322,7 +321,7 @@
                 5 << 28,
                 5 << 20,
                 HBM,
-                16,
+                56,
             )(*operands)
         )
     got = lax.ppermute(partial[0], "core", SWAP)

time: 133 us -> 127 us (0.955)
  waiting for transfers between devices: 22 us -> 10.1 us
  starting transfers between devices: 72.5 us -> 78.7 us
  other arithmetic: 1.37 us -> 2.91 us
    all_to_all x1, waiting for transfers between devices: 7.42 us -> 0.01 us  [body(): chunks = lax.all_to_all(chunks, ('z', 'x'), 0, 0, tiled=True)]
    ppermute x16, starting transfers between devices: 37 us -> 43.3 us  [hop(): return lax.ppermute(weight, ('dp', 'z', 'x', 'core'), pairs)]
    all_to_all x1, starting transfers between devices: 3.85 us -> 9.4 us  [body(): lax.all_to_all(priors, ('z', 'x'), 0, 0, tiled=True).reshape(SLOTS, DH, DH)]
    ppermute x1, starting transfers between devices: 11.6 us -> 7.19 us  [body(): got = lax.ppermute(partial[0], 'core', SWAP)]
    ppermute x16, waiting for transfers between devices: 14.3 us -> 10.1 us  [hop(): return lax.ppermute(weight, ('dp', 'z', 'x', 'core'), pairs)]
    broadcast_in_dim x1, other arithmetic: 1.37 us -> 2.91 us  [body(): return (partial[1] + got.astype(F32)).astype(BF16)[None]]
    all_to_all x1, starting transfers between devices: 11.3 us -> 10 us  [body(): chunks = lax.all_to_all(chunks, ('z', 'x'), 0, 0, tiled=True)]
    unnamed x32 -> x44, local copies, waits for them, and re-layouts: 6.49 us -> 5.91 us
  transfers between devices with their start and end apart: 20 -> 20, of which waited for: 8 -> 5; matrix products, arithmetic and copies ran while one was open for 0% -> 0% of each run, Pallas kernels for 19% -> 19%
where the time goes in v6:
time: 127 us; the launch traced here: 126 us
  starting transfers between devices  78.7 us (62%)
  Pallas kernels  28.4 us (22%)
  waiting for transfers between devices  10.1 us (8%)
  local copies, waits for them, and re-layouts  5.91 us (5%)
  other arithmetic  2.91 us (2%)
    ppermute x16, starting transfers between devices, hop(): return lax.ppermute(weight, ('dp', 'z', 'x', 'core'), pairs)  43.3 us
    ppermute x16, waiting for transfers between devices, hop(): return lax.ppermute(weight, ('dp', 'z', 'x', 'core'), pairs)  10.1 us
    all_to_all x1, starting transfers between devices, body(): chunks = lax.all_to_all(chunks, ('z', 'x'), 0, 0, tiled=True)  10 us
    all_to_all x1, starting transfers between devices, body(): lax.all_to_all(priors, ('z', 'x'), 0, 0, tiled=True).reshape(SLOTS, DH, DH)  9.4 us
    pallas_call x1, Pallas kernels, body(): call(within_kernel, 11, (shape(queries, BF16), shape(withins, F32)), [plt...  9.08 us
    ppermute x1, starting transfers between devices, body(): other = lax.ppermute(own, 'core', SWAP)  8.78 us
    pallas_call x2, Pallas kernels, body(): call(functools.partial(out_kernel, block), 13, shape((TOK, D), kind), [pl...  8.33 us
    ppermute x1, starting transfers between devices, body(): got = lax.ppermute(partial[0], 'core', SWAP)  7.19 us
  transfers between devices with their start and end apart: 20, of which 5 were waited for; matrix products, arithmetic and copies ran while one was open for 0% of the time, Pallas kernels for 19%

profile of v6, /device:TPU:1, one launch (start us, length us, event | category | flops | bytes accessed | tf_op | source)
XLA Modules:
  0.0 126.5 jit_solution(5022552004494571007)
XLA Ops:
  0.0 8.8 %collective-permute-start = (bf16[512,1024]{1,0:T(8,128)(2,1)}, bf16[512,1024]{1,0:T(8,128)(2,1)S(1)}, u32[]{:S(2)}, u32[]{:S(2)}) collective-permute-start(bf16[512,1024]{1,0:T(8,128)(2,1)} %bitcast.6), channel_id=1, source_target_pairs={{0,1},{1,0},{2,3},{3,2},{4,5},{5,4},{6,7},{7,6},{8,9},{9,8},{10,11... | collective-permute-start | bytes 3145736 | tf_op jit(solution)/shard_map/ppermute | solution.py:237
  8.8 1.9 %collective-permute-start.1 = (bf16[1024,128]{1,0:T(8,128)(2,1)}, bf16[1024,128]{1,0:T(8,128)(2,1)S(1)}, u32[]{:S(2)}, u32[]{:S(2)}) collective-permute-start(bf16[1024,128]{1,0:T(8,128)(2,1)} %wk.1), channel_id=1, source_target_pairs={{0,448},{1,65},{2,450},{3,67},{4,452},{5,69},{6,454},{7,71},{8,456... | collective-permute-start | bytes 786440 | tf_op jit(solution)/shard_map/ppermute | solution.py:33
  14.6 2.7 %collective-permute-done.1.wk = bf16[1024,128]{1,0:T(8,128)(2,1)S(1)} collective-permute-done((bf16[1024,128]{1,0:T(8,128)(2,1)}, bf16[1024,128]{1,0:T(8,128)(2,1)S(1)}, u32[]{:S(2)}, u32[]{:S(2)}) %collective-permute-start.1) | collective-permute-done | bytes 262176 | tf_op jit(solution)/shard_map/ppermute | solution.py:33
  17.3 2.8 %collective-permute-done.2.wv = bf16[1024,128]{1,0:T(8,128)(2,1)S(1)} collective-permute-done((bf16[1024,128]{1,0:T(8,128)(2,1)}, bf16[1024,128]{1,0:T(8,128)(2,1)S(1)}, u32[]{:S(2)}, u32[]{:S(2)}) %collective-permute-start.2) | collective-permute-done | bytes 262176 | tf_op jit(solution)/shard_map/ppermute | solution.py:33
  24.0 2.6 %collective-permute-start.8 = (bf16[1024,128]{1,0:T(8,128)(2,1)}, bf16[1024,128]{1,0:T(8,128)(2,1)S(1)}, u32[]{:S(2)}, u32[]{:S(2)}) collective-permute-start(bf16[1024,128]{1,0:T(8,128)(2,1)} %q_own), channel_id=1, source_target_pairs={{0,384},{1,129},{2,386},{3,131},{4,388},{5,133},{6,390},{7,135},{8... | collective-permute-start | bytes 786440 | tf_op jit(solution)/shard_map/ppermute | solution.py:33
  27.9 2.3 %shard_map.64 = (bf16[2,512,256]{2,1,0:T(8,128)(2,1)S(1)}, f32[2,128,128]{2,1,0:T(8,128)S(1)}) custom-call(bf16[512,1024]{1,0:T(8,128)(2,1)S(1)} %bitcast.8, bf16[512,1024]{1,0:T(8,128)(2,1)S(1)} %collective-permute-done.other, bf16[1024,128]{1,0:T(8,128)(2,1)S(1)} %collective-permute-done.1.wk, bf16[1024,128]{1,0:T(8,128)(2,1)S(1)} %collective-permute-done.2.wv), custom_call_target="tpu_custom_call" | custom-call | flops 536870912 | bytes 3145728 | tf_op jit(solution)/shard_map/pallas_call | solution.py:260
  31.4 2.1 %collective-permute-start.6 = (bf16[1024,128]{1,0:T(8,128)(2,1)S(1)}, bf16[1024,128]{1,0:T(8,128)(2,1)S(1)}, u32[]{:S(2)}, u32[]{:S(2)}) collective-permute-start(bf16[1024,128]{1,0:T(8,128)(2,1)S(1)} %collective-permute-done.3.wk), channel_id=1, source_target_pairs={{0,448},{1,65},{2,450},{3,67},{4,452},{5,69},{6,454},{7,71},{8,456... | collective-permute-start | bytes 786440 | tf_op jit(solution)/shard_map/ppermute | solution.py:33
  33.5 3.6 %collective-permute-start.7 = (bf16[1024,128]{1,0:T(8,128)(2,1)S(1)}, bf16[1024,128]{1,0:T(8,128)(2,1)S(1)}, u32[]{:S(2)}, u32[]{:S(2)}) collective-permute-start(bf16[1024,128]{1,0:T(8,128)(2,1)S(1)} %collective-permute-done.4.wv), channel_id=1, source_target_pairs={{0,448},{1,65},{2,450},{3,67},{4,452},{5,69},{6,454},{7,71},{8,456... | collective-permute-start | bytes 786440 | tf_op jit(solution)/shard_map/ppermute | solution.py:33
  37.1 4.0 %collective-permute-start.13 = (bf16[128,1024]{1,0:T(8,128)(2,1)S(1)}, bf16[128,1024]{1,0:T(8,128)(2,1)S(1)}, u32[]{:S(2)}, u32[]{:S(2)}) collective-permute-start(bf16[128,1024]{1,0:T(8,128)(2,1)S(1)} %copy-done.13), channel_id=1, source_target_pairs={{0,448},{1,65},{2,450},{3,67},{4,452},{5,69},{6,454},{7,71},{8,456... | collective-permute-start | bytes 786440 | tf_op jit(solution)/shard_map/ppermute | solution.py:33
  41.1 2.3 %shard_map.65 = (bf16[2,512,256]{2,1,0:T(8,128)(2,1)S(1)}, f32[2,128,128]{2,1,0:T(8,128)S(1)}) custom-call(bf16[512,1024]{1,0:T(8,128)(2,1)S(1)} %bitcast.9, bf16[512,1024]{1,0:T(8,128)(2,1)S(1)} %collective-permute-done.other, bf16[1024,128]{1,0:T(8,128)(2,1)S(1)} %collective-permute-done.3.wk, bf16[1024,128]{1,0:T(8,128)(2,1)S(1)} %collective-permute-done.4.wv), custom_call_target="tpu_custom_call" | custom-call | flops 536870912 | bytes 3145728 | tf_op jit(solution)/shard_map/pallas_call | solution.py:265
  44.2 3.7 %collective-permute-start.11 = (bf16[1024,128]{1,0:T(8,128)(2,1)S(1)}, bf16[1024,128]{1,0:T(8,128)(2,1)S(1)}, u32[]{:S(2)}, u32[]{:S(2)}) collective-permute-start(bf16[1024,128]{1,0:T(8,128)(2,1)S(1)} %collective-permute-done.6.wk), channel_id=1, source_target_pairs={{0,448},{1,65},{2,450},{3,67},{4,452},{5,69},{6,454},{7,71},{8,456... | collective-permute-start | bytes 786440 | tf_op jit(solution)/shard_map/ppermute | solution.py:33
  49.9 2.3 %shard_map.66 = (bf16[2,512,256]{2,1,0:T(8,128)(2,1)S(1)}, f32[2,128,128]{2,1,0:T(8,128)S(1)}) custom-call(bf16[512,1024]{1,0:T(8,128)(2,1)S(1)} %bitcast.10, bf16[512,1024]{1,0:T(8,128)(2,1)S(1)} %collective-permute-done.other, bf16[1024,128]{1,0:T(8,128)(2,1)S(1)} %collective-permute-done.6.wk, bf16[1024,128]{1,0:T(8,128)(2,1)S(1)} %collective-permute-done.7.wv), custom_call_target="tpu_custom_call" | custom-call | flops 536870912 | bytes 3145728 | tf_op jit(solution)/shard_map/pallas_call | solution.py:269
  52.5 3.7 %collective-permute-done.12.wv_far = bf16[1024,128]{1,0:T(8,128)(2,1)S(1)} collective-permute-done((bf16[1024,128]{1,0:T(8,128)(2,1)S(1)}, bf16[1024,128]{1,0:T(8,128)(2,1)S(1)}, u32[]{:S(2)}, u32[]{:S(2)}) %collective-permute-start.12) | collective-permute-done | bytes 262176 | tf_op jit(solution)/shard_map/ppermute | solution.py:33
  58.2 3.5 %shard_map.67 = (bf16[2,512,256]{2,1,0:T(8,128)(2,1)S(1)}, f32[2,128,128]{2,1,0:T(8,128)S(1)}, bf16[4,128,128]{2,1,0:T(8,128)(2,1)}) custom-call(bf16[512,1024]{1,0:T(8,128)(2,1)S(1)} %bitcast.11, bf16[512,1024]{1,0:T(8,128)(2,1)S(1)} %collective-permute-done.other, bf16[1024,128]{1,0:T(8,128)(2,1)S(1)} %copy-done.6, bf16[1024,128]{1,0:T(8,128)(2,1)S(1)} %copy-done.7, ...), custom_call_target="tpu_custom_call" | custom-call | flops 536870912 | bytes 3145728 | tf_op jit(solution)/shard_map/pallas_call | solution.py:272
  63.2 10.0 %all-to-all-start = ((bf16[32,16,128]{2,1,0:T(8,128)(2,1)}), bf16[32,16,128]{2,1,0:T(8,128)(2,1)S(1)}, u32[]{:S(2)}, u32[]{:S(2)}) async-start(bf16[32,16,128]{2,1,0:T(8,128)(2,1)} %bitcast.1), calls=%async_computation | async-start | bytes 262144 | tf_op jit(solution)/shard_map/all_to_all | solution.py:279
  73.2 5.2 %collective-permute-start.10 = (bf16[1024,128]{1,0:T(8,128)(2,1)S(1)}, bf16[1024,128]{1,0:T(8,128)(2,1)S(1)}, u32[]{:S(2)}, u32[]{:S(2)}) collective-permute-start(bf16[1024,128]{1,0:T(8,128)(2,1)S(1)} %collective-permute-done.8.q1), channel_id=1, source_target_pairs={{0,384},{1,129},{2,386},{3,131},{4,388},{5,133},{6,390},{7,135},{8... | collective-permute-start | bytes 786440 | tf_op jit(solution)/shard_map/ppermute | solution.py:33
  80.4 3.0 %collective-permute-start.16 = (bf16[128,1024]{1,0:T(8,128)(2,1)S(1)}, bf16[128,1024]{1,0:T(8,128)(2,1)S(1)}, u32[]{:S(2)}, u32[]{:S(2)}) collective-permute-start(bf16[128,1024]{1,0:T(8,128)(2,1)S(1)} %collective-permute-done.14.o1), channel_id=1, source_target_pairs={{0,384},{1,129},{2,386},{3,131},{4,388},{5,133},{6,390},{7,135},{8... | collective-permute-start | bytes 786440 | tf_op jit(solution)/shard_map/ppermute | solution.py:33
  83.4 3.7 %collective-permute-start.15 = (bf16[128,1024]{1,0:T(8,128)(2,1)S(1)}, bf16[128,1024]{1,0:T(8,128)(2,1)S(1)}, u32[]{:S(2)}, u32[]{:S(2)}) collective-permute-start(bf16[128,1024]{1,0:T(8,128)(2,1)S(1)} %collective-permute-done.14.o1), channel_id=1, source_target_pairs={{0,448},{1,65},{2,450},{3,67},{4,452},{5,69},{6,454},{7,71},{8,456... | collective-permute-start | bytes 786440 | tf_op jit(solution)/shard_map/ppermute | solution.py:33
  87.8 9.4 %all-to-all-start.1 = ((bf16[32,16,128]{2,1,0:T(8,128)(2,1)}), bf16[32,16,128]{2,1,0:T(8,128)(2,1)S(1)}, u32[]{:S(2)}, u32[]{:S(2)}) async-start(bf16[32,16,128]{2,1,0:T(8,128)(2,1)} %shard_map.69), calls=%async_computation.1 | async-start | bytes 262144 | tf_op jit(solution)/shard_map/all_to_all | solution.py:281
  98.0 9.1 %shard_map.68 = (bf16[4,2,512,128]{3,2,1,0:T(8,128)(2,1)}, f32[4,2,512,128]{3,2,1,0:T(8,128)}) custom-call(bf16[512,1024]{1,0:T(8,128)(2,1)} %bitcast.7, bf16[512,1024]{1,0:T(8,128)(2,1)} %copy-done.1, bf16[1024,128]{1,0:T(8,128)(2,1)} %copy-done.18, bf16[1024,128]{1,0:T(8,128)(2,1)} %copy-done.19, bf16[1024,128]{1,0:T(8,128)(2,1)} %copy-done.21, ...), custom_call_target="tpu_custom_call" | custom-call | flops 1610612736 | bytes 8388608 | tf_op jit(solution)/shard_map/pallas_call | solution.py:284
  108.0 4.1 %shard_map.71 = bf16[512,1024]{1,0:T(8,128)(2,1)} custom-call(bf16[4,2,512,128]{3,2,1,0:T(8,128)(2,1)} %get-tuple-element.56.query_ref, f32[4,2,512,128]{3,2,1,0:T(8,128)} %get-tuple-element.57.within_ref, bf16[4,128,128]{2,1,0:T(8,128)(2,1)} %bitcast.12, f32[2,128,128]{2,1,0:T(8,128)} %copy-done.2, f32[2,128,128]{2,1,0:T(8,128)} %copy-done.3, ...), custom_call_target="tpu_custom_call" | custom-call | flops 1342177280 | bytes 5242880 | tf_op jit(solution)/shard_map/pallas_call | solution.py:305
  112.1 7.2 %collective-permute-start.17 = (bf16[512,1024]{1,0:T(8,128)(2,1)}, bf16[512,1024]{1,0:T(8,128)(2,1)S(1)}, u32[]{:S(2)}, u32[]{:S(2)}) collective-permute-start(bf16[512,1024]{1,0:T(8,128)(2,1)} %shard_map.71), channel_id=1, source_target_pairs={{0,1},{1,0},{2,3},{3,2},{4,5},{5,4},{6,7},{7,6},{8,9},{9,8},{10,11... | collective-permute-start | bytes 3145736 | tf_op jit(solution)/shard_map/ppermute | solution.py:327
  119.3 4.3 %shard_map.70 = f32[512,1024]{1,0:T(8,128)} custom-call(bf16[4,2,512,128]{3,2,1,0:T(8,128)(2,1)} %get-tuple-element.56.query_ref, f32[4,2,512,128]{3,2,1,0:T(8,128)} %get-tuple-element.57.within_ref, bf16[4,128,128]{2,1,0:T(8,128)(2,1)} %bitcast.13, f32[2,128,128]{2,1,0:T(8,128)} %copy-done.2, f32[2,128,128]{2,1,0:T(8,128)} %copy-done.3, ...), custom_call_target="tpu_custom_call" | custom-call | flops 1342177280 | bytes 5242880 | tf_op jit(solution)/shard_map/pallas_call | solution.py:305
  123.6 2.9 %fusion = bf16[1,512,1024]{2,1,0:T(8,128)(2,1)} fusion(f32[512,1024]{1,0:T(8,128)} %shard_map.70, bf16[512,1024]{1,0:T(8,128)(2,1)S(1)} %collective-permute-done.17), kind=kLoop, calls=%fused_computation.1 | loop fusion | flops 1572864 | bytes 4194304 | tf_op jit(solution)/shard_map/broadcast_in_dim | solution.py:328
  (69 shorter events, 20.9 us)
Async XLA Ops:
  0.0 26.6 %collective-permute-start = (bf16[512,1024]{1,0:T(8,128)(2,1)}, bf16[512,1024]{1,0:T(8,128)(2,1)S(1)}, u32[]{:S(2)}, u32[]{:S(2)}) collective-permute-start(bf16[512,1024]{1,0:T(8,128)(2,1)} %bitcast.6), channel_id=1, source_target_pairs={{0,1},{1,0},{2,3},{3,2},{4,5},{5,4},{6,7},{7,6},{8,9},{9,8},{10,11... | collective-permute-start | bytes 3145736 | tf_op jit(solution)/shard_map/ppermute | solution.py:237
  8.8 8.5 %collective-permute-start.1 = (bf16[1024,128]{1,0:T(8,128)(2,1)}, bf16[1024,128]{1,0:T(8,128)(2,1)S(1)}, u32[]{:S(2)}, u32[]{:S(2)}) collective-permute-start(bf16[1024,128]{1,0:T(8,128)(2,1)} %wk.1), channel_id=1, source_target_pairs={{0,448},{1,65},{2,450},{3,67},{4,452},{5,69},{6,454},{7,71},{8,456... | collective-permute-start | bytes 786440 | tf_op jit(solution)/shard_map/ppermute | solution.py:33
  10.7 9.4 %collective-permute-start.2 = (bf16[1024,128]{1,0:T(8,128)(2,1)}, bf16[1024,128]{1,0:T(8,128)(2,1)S(1)}, u32[]{:S(2)}, u32[]{:S(2)}) collective-permute-start(bf16[1024,128]{1,0:T(8,128)(2,1)} %wv.1), channel_id=1, source_target_pairs={{0,448},{1,65},{2,450},{3,67},{4,452},{5,69},{6,454},{7,71},{8,456... | collective-permute-start | bytes 786440 | tf_op jit(solution)/shard_map/ppermute | solution.py:33
  12.6 18.3 %collective-permute-start.5 = (bf16[1024,128]{1,0:T(8,128)(2,1)}, bf16[1024,128]{1,0:T(8,128)(2,1)S(1)}, u32[]{:S(2)}, u32[]{:S(2)}) collective-permute-start(bf16[1024,128]{1,0:T(8,128)(2,1)} %q_own), channel_id=1, source_target_pairs={{0,448},{1,65},{2,450},{3,67},{4,452},{5,69},{6,454},{7,71},{8,456... | collective-permute-start | bytes 786440 | tf_op jit(solution)/shard_map/ppermute | solution.py:33
  20.1 10.8 %collective-permute-start.3 = (bf16[1024,128]{1,0:T(8,128)(2,1)S(1)}, bf16[1024,128]{1,0:T(8,128)(2,1)S(1)}, u32[]{:S(2)}, u32[]{:S(2)}) collective-permute-start(bf16[1024,128]{1,0:T(8,128)(2,1)S(1)} %collective-permute-done.1.wk), channel_id=1, source_target_pairs={{0,448},{1,65},{2,450},{3,67},{4,452},{5,69},{6,454},{7,71},{8,456... | collective-permute-start | bytes 786440 | tf_op jit(solution)/shard_map/ppermute | solution.py:33
  22.1 9.3 %collective-permute-start.4 = (bf16[1024,128]{1,0:T(8,128)(2,1)S(1)}, bf16[1024,128]{1,0:T(8,128)(2,1)S(1)}, u32[]{:S(2)}, u32[]{:S(2)}) collective-permute-start(bf16[1024,128]{1,0:T(8,128)(2,1)S(1)} %collective-permute-done.2.wv), channel_id=1, source_target_pairs={{0,448},{1,65},{2,450},{3,67},{4,452},{5,69},{6,454},{7,71},{8,456... | collective-permute-start | bytes 786440 | tf_op jit(solution)/shard_map/ppermute | solution.py:33
  24.0 20.2 %collective-permute-start.8 = (bf16[1024,128]{1,0:T(8,128)(2,1)}, bf16[1024,128]{1,0:T(8,128)(2,1)S(1)}, u32[]{:S(2)}, u32[]{:S(2)}) collective-permute-start(bf16[1024,128]{1,0:T(8,128)(2,1)} %q_own), channel_id=1, source_target_pairs={{0,384},{1,129},{2,386},{3,131},{4,388},{5,133},{6,390},{7,135},{8... | collective-permute-start | bytes 786440 | tf_op jit(solution)/shard_map/ppermute | solution.py:33
  27.9 30.3 %copy-start.1 = (bf16[512,1024]{1,0:T(8,128)(2,1)}, bf16[512,1024]{1,0:T(8,128)(2,1)S(1)}, u32[]{:S(2)}) copy-start(bf16[512,1024]{1,0:T(8,128)(2,1)S(1)} %collective-permute-done.other) | copy-start | bytes 3145732
  31.4 12.8 %collective-permute-start.6 = (bf16[1024,128]{1,0:T(8,128)(2,1)S(1)}, bf16[1024,128]{1,0:T(8,128)(2,1)S(1)}, u32[]{:S(2)}, u32[]{:S(2)}) collective-permute-start(bf16[1024,128]{1,0:T(8,128)(2,1)S(1)} %collective-permute-done.3.wk), channel_id=1, source_target_pairs={{0,448},{1,65},{2,450},{3,67},{4,452},{5,69},{6,454},{7,71},{8,456... | collective-permute-start | bytes 786440 | tf_op jit(solution)/shard_map/ppermute | solution.py:33
  33.5 10.7 %collective-permute-start.7 = (bf16[1024,128]{1,0:T(8,128)(2,1)S(1)}, bf16[1024,128]{1,0:T(8,128)(2,1)S(1)}, u32[]{:S(2)}, u32[]{:S(2)}) collective-permute-start(bf16[1024,128]{1,0:T(8,128)(2,1)S(1)} %collective-permute-done.4.wv), channel_id=1, source_target_pairs={{0,448},{1,65},{2,450},{3,67},{4,452},{5,69},{6,454},{7,71},{8,456... | collective-permute-start | bytes 786440 | tf_op jit(solution)/shard_map/ppermute | solution.py:33
  37.1 15.1 %collective-permute-start.13 = (bf16[128,1024]{1,0:T(8,128)(2,1)S(1)}, bf16[128,1024]{1,0:T(8,128)(2,1)S(1)}, u32[]{:S(2)}, u32[]{:S(2)}) collective-permute-start(bf16[128,1024]{1,0:T(8,128)(2,1)S(1)} %copy-done.13), channel_id=1, source_target_pairs={{0,448},{1,65},{2,450},{3,67},{4,452},{5,69},{6,454},{7,71},{8,456... | collective-permute-start | bytes 786440 | tf_op jit(solution)/shard_map/ppermute | solution.py:33
  44.2 34.3 %copy-start.19 = (bf16[1024,128]{1,0:T(8,128)(2,1)}, bf16[1024,128]{1,0:T(8,128)(2,1)S(1)}, u32[]{:S(2)}) copy-start(bf16[1024,128]{1,0:T(8,128)(2,1)S(1)} %collective-permute-done.8.q1) | copy-start | bytes 786436
  44.2 8.3 %collective-permute-start.11 = (bf16[1024,128]{1,0:T(8,128)(2,1)S(1)}, bf16[1024,128]{1,0:T(8,128)(2,1)S(1)}, u32[]{:S(2)}, u32[]{:S(2)}) collective-permute-start(bf16[1024,128]{1,0:T(8,128)(2,1)S(1)} %collective-permute-done.6.wk), channel_id=1, source_target_pairs={{0,448},{1,65},{2,450},{3,67},{4,452},{5,69},{6,454},{7,71},{8,456... | collective-permute-start | bytes 786440 | tf_op jit(solution)/shard_map/ppermute | solution.py:33
  47.9 8.3 %collective-permute-start.12 = (bf16[1024,128]{1,0:T(8,128)(2,1)S(1)}, bf16[1024,128]{1,0:T(8,128)(2,1)S(1)}, u32[]{:S(2)}, u32[]{:S(2)}) collective-permute-start(bf16[1024,128]{1,0:T(8,128)(2,1)S(1)} %collective-permute-done.7.wv), channel_id=1, source_target_pairs={{0,448},{1,65},{2,450},{3,67},{4,452},{5,69},{6,454},{7,71},{8,456... | collective-permute-start | bytes 786440 | tf_op jit(solution)/shard_map/ppermute | solution.py:33
  52.1 35.7 %copy-start.4 = (f32[2,128,128]{2,1,0:T(8,128)}, f32[2,128,128]{2,1,0:T(8,128)S(1)}, u32[]{:S(2)}) copy-start(f32[2,128,128]{2,1,0:T(8,128)S(1)} %get-tuple-element.59.s2) | copy-start | bytes 393220
  52.2 35.7 %copy-start.14 = (bf16[128,1024]{1,0:T(8,128)(2,1)}, bf16[128,1024]{1,0:T(8,128)(2,1)S(1)}, u32[]{:S(2)}) copy-start(bf16[128,1024]{1,0:T(8,128)(2,1)S(1)} %collective-permute-done.13.o0) | copy-start | bytes 786436
  56.3 24.1 %collective-permute-start.14 = (bf16[128,1024]{1,0:T(8,128)(2,1)S(1)}, bf16[128,1024]{1,0:T(8,128)(2,1)S(1)}, u32[]{:S(2)}, u32[]{:S(2)}) collective-permute-start(bf16[128,1024]{1,0:T(8,128)(2,1)S(1)} %copy-done.13), channel_id=1, source_target_pairs={{0,384},{1,129},{2,386},{3,131},{4,388},{5,133},{6,390},{7,135},{8... | collective-permute-start | bytes 786440 | tf_op jit(solution)/shard_map/ppermute | solution.py:33
  63.2 23.9 %all-to-all-start = ((bf16[32,16,128]{2,1,0:T(8,128)(2,1)}), bf16[32,16,128]{2,1,0:T(8,128)(2,1)S(1)}, u32[]{:S(2)}, u32[]{:S(2)}) async-start(bf16[32,16,128]{2,1,0:T(8,128)(2,1)} %bitcast.1), calls=%async_computation | async-start | bytes 262144 | tf_op jit(solution)/shard_map/all_to_all | solution.py:279
  73.2 24.0 %collective-permute-start.10 = (bf16[1024,128]{1,0:T(8,128)(2,1)S(1)}, bf16[1024,128]{1,0:T(8,128)(2,1)S(1)}, u32[]{:S(2)}, u32[]{:S(2)}) collective-permute-start(bf16[1024,128]{1,0:T(8,128)(2,1)S(1)} %collective-permute-done.8.q1), channel_id=1, source_target_pairs={{0,384},{1,129},{2,386},{3,131},{4,388},{5,133},{6,390},{7,135},{8... | collective-permute-start | bytes 786440 | tf_op jit(solution)/shard_map/ppermute | solution.py:33
  78.5 18.8 %collective-permute-start.9 = (bf16[1024,128]{1,0:T(8,128)(2,1)S(1)}, bf16[1024,128]{1,0:T(8,128)(2,1)S(1)}, u32[]{:S(2)}, u32[]{:S(2)}) collective-permute-start(bf16[1024,128]{1,0:T(8,128)(2,1)S(1)} %collective-permute-done.8.q1), channel_id=1, source_target_pairs={{0,448},{1,65},{2,450},{3,67},{4,452},{5,69},{6,454},{7,71},{8,456... | collective-permute-start | bytes 786440 | tf_op jit(solution)/shard_map/ppermute | solution.py:33
  80.4 26.7 %collective-permute-start.16 = (bf16[128,1024]{1,0:T(8,128)(2,1)S(1)}, bf16[128,1024]{1,0:T(8,128)(2,1)S(1)}, u32[]{:S(2)}, u32[]{:S(2)}) collective-permute-start(bf16[128,1024]{1,0:T(8,128)(2,1)S(1)} %collective-permute-done.14.o1), channel_id=1, source_target_pairs={{0,384},{1,129},{2,386},{3,131},{4,388},{5,133},{6,390},{7,135},{8... | collective-permute-start | bytes 786440 | tf_op jit(solution)/shard_map/ppermute | solution.py:33
  83.4 23.8 %collective-permute-start.15 = (bf16[128,1024]{1,0:T(8,128)(2,1)S(1)}, bf16[128,1024]{1,0:T(8,128)(2,1)S(1)}, u32[]{:S(2)}, u32[]{:S(2)}) collective-permute-start(bf16[128,1024]{1,0:T(8,128)(2,1)S(1)} %collective-permute-done.14.o1), channel_id=1, source_target_pairs={{0,448},{1,65},{2,450},{3,67},{4,452},{5,69},{6,454},{7,71},{8,456... | collective-permute-start | bytes 786440 | tf_op jit(solution)/shard_map/ppermute | solution.py:33
  87.8 19.3 %all-to-all-start.1 = ((bf16[32,16,128]{2,1,0:T(8,128)(2,1)}), bf16[32,16,128]{2,1,0:T(8,128)(2,1)S(1)}, u32[]{:S(2)}, u32[]{:S(2)}) async-start(bf16[32,16,128]{2,1,0:T(8,128)(2,1)} %shard_map.69), calls=%async_computation.1 | async-start | bytes 262144 | tf_op jit(solution)/shard_map/all_to_all | solution.py:281
  112.1 11.5 %collective-permute-start.17 = (bf16[512,1024]{1,0:T(8,128)(2,1)}, bf16[512,1024]{1,0:T(8,128)(2,1)S(1)}, u32[]{:S(2)}, u32[]{:S(2)}) collective-permute-start(bf16[512,1024]{1,0:T(8,128)(2,1)} %shard_map.71), channel_id=1, source_target_pairs={{0,1},{1,0},{2,3},{3,2},{4,5},{5,4},{6,7},{7,6},{8,9},{9,8},{10,11... | collective-permute-start | bytes 3145736 | tf_op jit(solution)/shard_map/ppermute | solution.py:327
  (18 other events, 174.7 us)

commit v7 on v6

--- a/solution.py
+++ b/solution.py
@@ -22,6 +22,7 @@
 VMEM = pl.BlockSpec(memory_space=pltpu.VMEM)
 HBM = pl.BlockSpec(memory_space=pl.ANY)
 DMA = pltpu.SemaphoreType.DMA
+TOP, LOW = pl.ds(0, D), pl.ds(D, D)
 
 
 def hop(weight, distance=1):
@@ -130,18 +131,18 @@
     loads = [begin(ref, tokens.at[block], sems.at[block]) for block, ref in enumerate((own, other))]
     weights, pairs = [], []
     for slot, ref in enumerate((q0, q1, q2)):
-        weights.append(begin(ref, weight.at[:, pl.ds(slot * DH, DH)], sems.at[2 + slot]))
+        weights.append(begin(ref.at[TOP, :], weight.at[:, pl.ds(slot * DH, DH)], sems.at[2 + slot]))
     final = weight.at[:, pl.ds(3 * DH, DH)]
 
     @pl.when(core == 0)
     def _():
-        begin(q_own, final, sems.at[5])
+        begin(q_own.at[TOP, :], final, sems.at[5])
 
     @pl.when(core != 0)
     def _():
-        begin(q_far, final, sems.at[5])
-
-    weights.append(pltpu.make_async_copy(q_own, final, sems.at[5]))
+        begin(q_far.at[TOP, :], final, sems.at[5])
+
+    weights.append(pltpu.make_async_copy(q_own.at[TOP, :], final, sems.at[5]))
     for slot, ref in enumerate((kv0, kv1, kv2, kv3)):
         pairs.append(begin(ref, kv.at[slot], sems.at[10 + slot]))
     half = TOK // 2
@@ -197,18 +198,18 @@
             ]
         )
     for slot, ref in enumerate((o0, o1, o2)):
-        weights.append(begin(ref, weight.at[pl.ds(slot * DH, DH), :], sems.at[14 + slot]))
-    final = weight.at[pl.ds(3 * DH, DH), :]
+        weights.append(begin(ref.at[LOW, :], weight.at[slot], sems.at[14 + slot]))
+    final = weight.at[3]
 
     @pl.when(core == 0)
     def _():
-        begin(o_own, final, sems.at[17])
+        begin(o_own.at[LOW, :], final, sems.at[17])
 
     @pl.when(core != 0)
     def _():
-        begin(o_far, final, sems.at[17])
-
-    weights.append(pltpu.make_async_copy(o_own, final, sems.at[17]))
+        begin(o_far.at[LOW, :], final, sems.at[17])
+
+    weights.append(pltpu.make_async_copy(o_own.at[LOW, :], final, sems.at[17]))
     for load in first:
         load.wait()
     share = (core if block == 0 else 1 - core).astype(F32)
@@ -225,7 +226,11 @@
     copies = []
     for c in range(4):
         cols = pl.ds(c * 2 * DH, 2 * DH)
-        out[:, cols] = mm(normed[...], weight[:, cols]).astype(out.dtype)
+        tiles = [
+            jnp.concatenate([weight[slot, k * DH : (k + 1) * DH, :] for slot in range(SLOTS)], axis=0)
+            for k in (2 * c, 2 * c + 1)
+        ]
+        out[:, cols] = mm(normed[...], jnp.concatenate(tiles, axis=1)).astype(out.dtype)
         copies.append(begin(out.at[:, cols], out_ref.at[:, cols], out_sems.at[c]))
     for copy in copies:
         copy.wait()
@@ -233,7 +238,7 @@
 
 def body(tokens, w_query, w_key, w_value, w_out, norm_gain):
     own = tokens[0]
-    key_1, value_1, query_1 = hop(w_key), hop(w_value), hop(w_query)
+    key_1, value_1 = hop(w_key), hop(w_value)
     other = lax.ppermute(own, "core", SWAP)
 
     pair = shape((2, TOK, 2 * DH), BF16)
@@ -257,26 +262,27 @@
         16,
     )
     barrier = lax.optimization_barrier
+    blocks = w_out.reshape(DH, DP, DH).transpose(1, 0, 2).reshape(D, DH)
+    pack = jnp.concatenate([w_query, blocks], axis=0)
     kv0, s0 = one(own, other, key_1, value_1)
-    key_1, value_1, w_query = barrier((key_1, value_1, w_query))
     key_2, value_2 = hop(key_1), hop(value_1)
-    query_2 = hop(w_query, 2)
-    key_2, value_2, query_1, w_out, s0 = barrier((key_2, value_2, query_1, w_out, s0))
+    pack_1 = hop(pack)
+    key_2, value_2, s0 = barrier((key_2, value_2, s0))
     kv1, s1 = one(own, other, key_2, value_2)
     key_3, value_3 = hop(key_2), hop(value_2)
-    out_1 = hop(w_out)
-    key_3, value_3, query_2, s1 = barrier((key_3, value_3, query_2, s1))
+    pack_1, key_3 = barrier((pack_1, key_3))
+    pack_2 = hop(pack_1)
+    key_3, value_3, s1 = barrier((key_3, value_3, s1))
     kv2, s2 = one(own, other, key_3, value_3)
     key_4, value_4 = hop(key_3), hop(value_3)
-    key_4, value_4, out_1, s2 = barrier((key_4, value_4, out_1, s2))
+    pack_2, key_4, value_4, s2 = barrier((pack_2, key_4, value_4, s2))
+    pack_3 = hop(pack_2)
     kv3, s3, total = last(own, other, w_key, w_value, key_4, value_4, s0, s1, s2)
-    w_out, s2 = barrier((w_out, s2))
-    out_2 = hop(w_out, 2)
-    query_3, query_4 = hop(query_2), hop(query_2, 2)
-    out_3, out_4 = hop(out_2), hop(out_2, 2)
 
     chunks = total.reshape(CHIPS, SLOTS * DH // CHIPS, DH)
     chunks = lax.all_to_all(chunks, ("z", "x"), 0, 0, tiled=True)
+    pack_3, chunks = barrier((pack_3, chunks))
+    pack_4 = hop(pack_3)
     priors = call(prefix_kernel, 1, shape(chunks.shape, BF16), [], 1 << 16, 1 << 18, VMEM, 4)(chunks)
     prior = lax.all_to_all(priors, ("z", "x"), 0, 0, tiled=True).reshape(SLOTS, DH, DH)
 
@@ -296,11 +302,11 @@
         ],
         3 * 2 * TOK * D * SLOTS * DH,
         8 << 20,
-    )(own, other, query_1, query_2, query_3, w_query, query_4, kv0, kv1, kv2, kv3)
-
-    operands = (query, within, prior, s0, s1, s2, s3, norm_gain.reshape(DP, DH), out_1, out_2, out_3, w_out, out_4)
+    )(own, other, pack_1, pack_2, pack_3, pack, pack_4, kv0, kv1, kv2, kv3)
+
+    operands = (query, within, prior, s0, s1, s2, s3, norm_gain.reshape(DP, DH), pack_1, pack_2, pack_3, pack, pack_4)
     partial = []
-    for block, kind in ((1, BF16), (0, F32)):
+    for block, kind, limit in ((1, BF16, 56), (0, F32, 56)):
         partial.append(
             call(
                 functools.partial(out_kernel, block),
@@ -312,7 +318,7 @@
                     pltpu.VMEM((SLOTS, DH, DH), BF16),
                     pltpu.VMEM((SLOTS, DH, DH), F32),
                     pltpu.VMEM((DP, DH), F32),
-                    pltpu.VMEM((SLOTS * DH, D), BF16),
+                    pltpu.VMEM((SLOTS, D, DH), BF16),
                     pltpu.VMEM((TOK, SLOTS * DH), BF16),
                     pltpu.VMEM((TOK, D), kind),
                     DMA((18,)),
@@ -321,7 +327,7 @@
                 5 << 28,
                 5 << 20,
                 HBM,
-                56,
+                limit,
             )(*operands)
         )
     got = lax.ppermute(partial[0], "core", SWAP)

time: 127 us -> 122 us (0.961)
  starting transfers between devices: 78.7 us -> 47.3 us
  blocking collectives: 0 us -> 18.9 us
  waiting for transfers between devices: 10.1 us -> 20.2 us
  local copies, waits for them, and re-layouts: 5.91 us -> 3.03 us
    all_to_all x0 -> x1, blocking collectives: none -> 18.9 us  [body(): chunks = lax.all_to_all(chunks, ('z', 'x'), 0, 0, tiled=True)]
    ppermute x16 -> x12, starting transfers between devices: 43.3 us -> 25 us  [hop(): return lax.ppermute(weight, ('dp', 'z', 'x', 'core'), pairs)]
    ppermute x16 -> x12, waiting for transfers between devices: 10.1 us -> 20.2 us  [hop(): return lax.ppermute(weight, ('dp', 'z', 'x', 'core'), pairs)]
    all_to_all x1 -> x0, starting transfers between devices: 10 us -> none  [body(): chunks = lax.all_to_all(chunks, ('z', 'x'), 0, 0, tiled=True)]
    all_to_all x1, starting transfers between devices: 9.4 us -> 4.03 us  [body(): lax.all_to_all(priors, ('z', 'x'), 0, 0, tiled=True).reshape(SLOTS, DH, DH)]
    unnamed x44 -> x38, local copies, waits for them, and re-layouts: 5.91 us -> 2.99 us
    ppermute x1, starting transfers between devices: 7.19 us -> 9.41 us  [body(): got = lax.ppermute(partial[0], 'core', SWAP)]
  transfers between devices with their start and end apart: 20 -> 15, of which waited for: 5 -> 8; matrix products, arithmetic and copies ran while one was open for 0% -> 1% of each run, Pallas kernels for 19% -> 20%
where the time goes in v7:
time: 122 us
  starting transfers between devices  47.3 us (39%)
  Pallas kernels  27.9 us (23%)
  waiting for transfers between devices  20.2 us (17%)
  blocking collectives  18.9 us (15%)
  other arithmetic  3.9 us (3%)
  local copies, waits for them, and re-layouts  3.03 us (2%)
    ppermute x12, starting transfers between devices, hop(): return lax.ppermute(weight, ('dp', 'z', 'x', 'core'), pairs)  25 us
    ppermute x12, waiting for transfers between devices, hop(): return lax.ppermute(weight, ('dp', 'z', 'x', 'core'), pairs)  20.2 us
    all_to_all x1, blocking collectives, body(): chunks = lax.all_to_all(chunks, ('z', 'x'), 0, 0, tiled=True)  18.9 us
    ppermute x1, starting transfers between devices, body(): got = lax.ppermute(partial[0], 'core', SWAP)  9.41 us
    pallas_call x1, Pallas kernels, body(): call(within_kernel, 11, (shape(queries, BF16), shape(withins, F32)), [plt...  9.07 us
    ppermute x1, starting transfers between devices, body(): other = lax.ppermute(own, 'core', SWAP)  8.91 us
    pallas_call x2, Pallas kernels, body(): call(functools.partial(out_kernel, block), 13, shape((TOK, D), kind), [pl...  8.33 us
    all_to_all x1, starting transfers between devices, body(): lax.all_to_all(priors, ('z', 'x'), 0, 0, tiled=True).reshape(SLOTS, DH, DH)  4.03 us
  transfers between devices with their start and end apart: 15, of which 8 were waited for; matrix products, arithmetic and copies ran while one was open for 1% of the time, Pallas kernels for 20%

profile of v7, /device:TPU:1, one launch (start us, length us, event | category | flops | bytes accessed | tf_op | source)
XLA Modules:
  0.0 121.7 jit_solution(17882550142567263766)
XLA Ops:
  0.0 8.9 %collective-permute-start = (bf16[512,1024]{1,0:T(8,128)(2,1)}, bf16[512,1024]{1,0:T(8,128)(2,1)S(1)}, u32[]{:S(2)}, u32[]{:S(2)}) collective-permute-start(bf16[512,1024]{1,0:T(8,128)(2,1)} %bitcast.14), channel_id=1, source_target_pairs={{0,1},{1,0},{2,3},{3,2},{4,5},{5,4},{6,7},{7,6},{8,9},{9,8},{10,11... | collective-permute-start | bytes 3145736 | tf_op jit(solution)/shard_map/ppermute | solution.py:242
  8.9 1.9 %collective-permute-start.2 = (bf16[1024,128]{1,0:T(8,128)(2,1)}, bf16[1024,128]{1,0:T(8,128)(2,1)S(1)}, u32[]{:S(2)}, u32[]{:S(2)}) collective-permute-start(bf16[1024,128]{1,0:T(8,128)(2,1)} %wk.1), channel_id=1, source_target_pairs={{0,448},{1,65},{2,450},{3,67},{4,452},{5,69},{6,454},{7,71},{8,456... | collective-permute-start | bytes 786440 | tf_op jit(solution)/shard_map/ppermute | solution.py:34
  10.9 1.9 %collective-permute-start.4 = (bf16[1024,128]{1,0:T(8,128)(2,1)}, bf16[1024,128]{1,0:T(8,128)(2,1)S(1)}, u32[]{:S(2)}, u32[]{:S(2)}) collective-permute-start(bf16[1024,128]{1,0:T(8,128)(2,1)} %wv.1), channel_id=1, source_target_pairs={{0,448},{1,65},{2,450},{3,67},{4,452},{5,69},{6,454},{7,71},{8,456... | collective-permute-start | bytes 786440 | tf_op jit(solution)/shard_map/ppermute | solution.py:34
  12.8 4.6 %collective-permute-done.2.wk = bf16[1024,128]{1,0:T(8,128)(2,1)S(1)} collective-permute-done((bf16[1024,128]{1,0:T(8,128)(2,1)}, bf16[1024,128]{1,0:T(8,128)(2,1)S(1)}, u32[]{:S(2)}, u32[]{:S(2)}) %collective-permute-start.2) | collective-permute-done | bytes 262176 | tf_op jit(solution)/shard_map/ppermute | solution.py:34
  23.2 1.9 %collective-permute-start.1 = (bf16[2048,128]{1,0:T(8,128)(2,1)S(1)}, bf16[2048,128]{1,0:T(8,128)(2,1)S(1)}, u32[]{:S(2)}, u32[]{:S(2)}) collective-permute-start(bf16[2048,128]{1,0:T(8,128)(2,1)S(1)} %pad_maximum_fusion.q_own.o_own), channel_id=1, source_target_pairs={{0,448},{1,65},{2,450},{3,67},{4,452},{5,69},{6,454},{7,71},{8,456... | collective-permute-start | bytes 1572872 | tf_op jit(solution)/shard_map/ppermute | solution.py:34
  25.1 2.3 %shard_map.64 = (bf16[2,512,256]{2,1,0:T(8,128)(2,1)S(1)}, f32[2,128,128]{2,1,0:T(8,128)S(1)}) custom-call(bf16[512,1024]{1,0:T(8,128)(2,1)S(1)} %bitcast.16, bf16[512,1024]{1,0:T(8,128)(2,1)S(1)} %collective-permute-done.other, bf16[1024,128]{1,0:T(8,128)(2,1)S(1)} %collective-permute-done.2.wk, bf16[1024,128]{1,0:T(8,128)(2,1)S(1)} %collective-permute-done.4.wv), custom_call_target="tpu_custom_call" | custom-call | flops 536870912 | bytes 3145728 | tf_op jit(solution)/shard_map/pallas_call | solution.py:267
  28.6 2.0 %collective-permute-start.6 = (bf16[1024,128]{1,0:T(8,128)(2,1)S(1)}, bf16[1024,128]{1,0:T(8,128)(2,1)S(1)}, u32[]{:S(2)}, u32[]{:S(2)}) collective-permute-start(bf16[1024,128]{1,0:T(8,128)(2,1)S(1)} %collective-permute-done.3.wk), channel_id=1, source_target_pairs={{0,448},{1,65},{2,450},{3,67},{4,452},{5,69},{6,454},{7,71},{8,456... | collective-permute-start | bytes 786440 | tf_op jit(solution)/shard_map/ppermute | solution.py:34
  30.6 1.9 %collective-permute-start.8 = (bf16[1024,128]{1,0:T(8,128)(2,1)S(1)}, bf16[1024,128]{1,0:T(8,128)(2,1)S(1)}, u32[]{:S(2)}, u32[]{:S(2)}) collective-permute-start(bf16[1024,128]{1,0:T(8,128)(2,1)S(1)} %collective-permute-done.5.wv), channel_id=1, source_target_pairs={{0,448},{1,65},{2,450},{3,67},{4,452},{5,69},{6,454},{7,71},{8,456... | collective-permute-start | bytes 786440 | tf_op jit(solution)/shard_map/ppermute | solution.py:34
  34.3 2.8 %collective-permute-done.6.wk = bf16[1024,128]{1,0:T(8,128)(2,1)S(1)} collective-permute-done((bf16[1024,128]{1,0:T(8,128)(2,1)S(1)}, bf16[1024,128]{1,0:T(8,128)(2,1)S(1)}, u32[]{:S(2)}, u32[]{:S(2)}) %collective-permute-start.6) | collective-permute-done | bytes 262176 | tf_op jit(solution)/shard_map/ppermute | solution.py:34
  39.0 2.3 %shard_map.65 = (bf16[2,512,256]{2,1,0:T(8,128)(2,1)S(1)}, f32[2,128,128]{2,1,0:T(8,128)S(1)}) custom-call(bf16[512,1024]{1,0:T(8,128)(2,1)S(1)} %bitcast.17, bf16[512,1024]{1,0:T(8,128)(2,1)S(1)} %collective-permute-done.other, bf16[1024,128]{1,0:T(8,128)(2,1)S(1)} %collective-permute-done.3.wk, bf16[1024,128]{1,0:T(8,128)(2,1)S(1)} %collective-permute-done.5.wv), custom_call_target="tpu_custom_call" | custom-call | flops 536870912 | bytes 3145728 | tf_op jit(solution)/shard_map/pallas_call | solution.py:271
  43.3 2.4 %collective-permute-start.10 = (bf16[1024,128]{1,0:T(8,128)(2,1)S(1)}, bf16[1024,128]{1,0:T(8,128)(2,1)S(1)}, u32[]{:S(2)}, u32[]{:S(2)}) collective-permute-start(bf16[1024,128]{1,0:T(8,128)(2,1)S(1)} %collective-permute-done.8.wv), channel_id=1, source_target_pairs={{0,448},{1,65},{2,450},{3,67},{4,452},{5,69},{6,454},{7,71},{8,456... | collective-permute-start | bytes 786440 | tf_op jit(solution)/shard_map/ppermute | solution.py:34
  45.7 2.3 %shard_map.66 = (bf16[2,512,256]{2,1,0:T(8,128)(2,1)S(1)}, f32[2,128,128]{2,1,0:T(8,128)S(1)}) custom-call(bf16[512,1024]{1,0:T(8,128)(2,1)S(1)} %bitcast.18, bf16[512,1024]{1,0:T(8,128)(2,1)S(1)} %collective-permute-done.other, bf16[1024,128]{1,0:T(8,128)(2,1)S(1)} %collective-permute-done.6.wk, bf16[1024,128]{1,0:T(8,128)(2,1)S(1)} %collective-permute-done.8.wv), custom_call_target="tpu_custom_call" | custom-call | flops 536870912 | bytes 3145728 | tf_op jit(solution)/shard_map/pallas_call | solution.py:276
  48.0 3.1 %collective-permute-done.9.wk_far = bf16[1024,128]{1,0:T(8,128)(2,1)S(1)} collective-permute-done((bf16[1024,128]{1,0:T(8,128)(2,1)S(1)}, bf16[1024,128]{1,0:T(8,128)(2,1)S(1)}, u32[]{:S(2)}, u32[]{:S(2)}) %collective-permute-start.9) | collective-permute-done | bytes 262176 | tf_op jit(solution)/shard_map/ppermute | solution.py:34
  51.1 2.8 %collective-permute-done.10.wv_far = bf16[1024,128]{1,0:T(8,128)(2,1)S(1)} collective-permute-done((bf16[1024,128]{1,0:T(8,128)(2,1)S(1)}, bf16[1024,128]{1,0:T(8,128)(2,1)S(1)}, u32[]{:S(2)}, u32[]{:S(2)}) %collective-permute-start.10) | collective-permute-done | bytes 262176 | tf_op jit(solution)/shard_map/ppermute | solution.py:34
  55.8 3.0 %shard_map.67 = (bf16[2,512,256]{2,1,0:T(8,128)(2,1)S(1)}, f32[2,128,128]{2,1,0:T(8,128)S(1)}, bf16[4,128,128]{2,1,0:T(8,128)(2,1)S(1)}) custom-call(bf16[512,1024]{1,0:T(8,128)(2,1)S(1)} %bitcast.19, bf16[512,1024]{1,0:T(8,128)(2,1)S(1)} %collective-permute-done.other, bf16[1024,128]{1,0:T(8,128)(2,1)S(1)} %copy-done.11, bf16[1024,128]{1,0:T(8,128)(2,1)S(1)} %copy-done.12, ...), custom_call_target="tpu_custom_call" | custom-call | flops 536870912 | bytes 3145728 | tf_op jit(solution)/shard_map/pallas_call | solution.py:280
  60.3 18.9 %all_to_all.10.chunk_ref = bf16[32,16,128]{2,1,0:T(8,128)(2,1)S(1)} all-to-all(bf16[32,16,128]{2,1,0:T(8,128)(2,1)S(1)} %bitcast.20), channel_id=1, replica_groups=mesh['dp'=8,'z'=8,'x'=4,'core'=2] {'z','x'}, dimensions={0} | all-to-all | bytes 262144 | tf_op jit(solution)/shard_map/all_to_all | solution.py:283
  79.3 3.3 %collective-permute-start.12 = (bf16[2048,128]{1,0:T(8,128)(2,1)S(1)}, bf16[2048,128]{1,0:T(8,128)(2,1)S(1)}, u32[]{:S(2)}, u32[]{:S(2)}) collective-permute-start(bf16[2048,128]{1,0:T(8,128)(2,1)S(1)} %collective-permute-done.11.q2.o2), channel_id=1, source_target_pairs={{0,448},{1,65},{2,450},{3,67},{4,452},{5,69},{6,454},{7,71},{8,456... | collective-permute-start | bytes 1572872 | tf_op jit(solution)/shard_map/ppermute | solution.py:34
  83.3 4.0 %all-to-all-start.1 = ((bf16[32,16,128]{2,1,0:T(8,128)(2,1)}), bf16[32,16,128]{2,1,0:T(8,128)(2,1)S(1)}, u32[]{:S(2)}, u32[]{:S(2)}) async-start(bf16[32,16,128]{2,1,0:T(8,128)(2,1)} %shard_map.69), calls=%async_computation.1 | async-start | bytes 262144 | tf_op jit(solution)/shard_map/all_to_all | solution.py:287
  87.3 3.1 %collective-permute-done.12.q_far.o_far = bf16[2048,128]{1,0:T(8,128)(2,1)S(1)} collective-permute-done((bf16[2048,128]{1,0:T(8,128)(2,1)S(1)}, bf16[2048,128]{1,0:T(8,128)(2,1)S(1)}, u32[]{:S(2)}, u32[]{:S(2)}) %collective-permute-start.12) | collective-permute-done | bytes 524320 | tf_op jit(solution)/shard_map/ppermute | solution.py:34
  91.3 9.1 %shard_map.68 = (bf16[4,2,512,128]{3,2,1,0:T(8,128)(2,1)}, f32[4,2,512,128]{3,2,1,0:T(8,128)}) custom-call(bf16[512,1024]{1,0:T(8,128)(2,1)} %bitcast.15, bf16[512,1024]{1,0:T(8,128)(2,1)} %copy-done.2, bf16[2048,128]{1,0:T(8,128)(2,1)} %copy-done.14, bf16[2048,128]{1,0:T(8,128)(2,1)} %copy-done.15, bf16[2048,128]{1,0:T(8,128)(2,1)} %copy-done.16, ...), custom_call_target="tpu_custom_call" | custom-call | flops 1610612736 | bytes 8388608 | tf_op jit(solution)/shard_map/pallas_call | solution.py:290
  101.0 4.1 %shard_map.71 = bf16[512,1024]{1,0:T(8,128)(2,1)} custom-call(bf16[4,2,512,128]{3,2,1,0:T(8,128)(2,1)} %get-tuple-element.51.query_ref, f32[4,2,512,128]{3,2,1,0:T(8,128)} %get-tuple-element.52.within_ref, bf16[4,128,128]{2,1,0:T(8,128)(2,1)} %bitcast.21, f32[2,128,128]{2,1,0:T(8,128)} %copy-done.3, f32[2,128,128]{2,1,0:T(8,128)} %copy-done.4, ...), custom_call_target="tpu_custom_call" | custom-call | flops 1342177280 | bytes 5242880 | tf_op jit(solution)/shard_map/pallas_call | solution.py:311
  105.1 9.4 %collective-permute-start.13 = (bf16[512,1024]{1,0:T(8,128)(2,1)}, bf16[512,1024]{1,0:T(8,128)(2,1)S(1)}, u32[]{:S(2)}, u32[]{:S(2)}) collective-permute-start(bf16[512,1024]{1,0:T(8,128)(2,1)} %shard_map.71), channel_id=1, source_target_pairs={{0,1},{1,0},{2,3},{3,2},{4,5},{5,4},{6,7},{7,6},{8,9},{9,8},{10,11... | collective-permute-start | bytes 3145736 | tf_op jit(solution)/shard_map/ppermute | solution.py:333
  114.5 4.3 %shard_map.70 = f32[512,1024]{1,0:T(8,128)} custom-call(bf16[4,2,512,128]{3,2,1,0:T(8,128)(2,1)} %get-tuple-element.51.query_ref, f32[4,2,512,128]{3,2,1,0:T(8,128)} %get-tuple-element.52.within_ref, bf16[4,128,128]{2,1,0:T(8,128)(2,1)} %bitcast.22, f32[2,128,128]{2,1,0:T(8,128)} %copy-done.3, f32[2,128,128]{2,1,0:T(8,128)} %copy-done.4, ...), custom_call_target="tpu_custom_call" | custom-call | flops 1342177280 | bytes 5242880 | tf_op jit(solution)/shard_map/pallas_call | solution.py:311
  118.8 2.9 %fusion = bf16[1,512,1024]{2,1,0:T(8,128)(2,1)} fusion(f32[512,1024]{1,0:T(8,128)} %shard_map.70, bf16[512,1024]{1,0:T(8,128)(2,1)S(1)} %collective-permute-done.13), kind=kLoop, calls=%fused_computation.1 | loop fusion | flops 1572864 | bytes 4194304 | tf_op jit(solution)/shard_map/broadcast_in_dim | solution.py:334
  (56 shorter events, 18.1 us)
Async XLA Ops:
  0.0 25.1 %copy-start.1 = (bf16[1,512,1024]{2,1,0:T(8,128)(2,1)S(1)}, bf16[1,512,1024]{2,1,0:T(8,128)(2,1)}, u32[]{:S(2)}) copy-start(bf16[1,512,1024]{2,1,0:T(8,128)(2,1)} %param.6) | copy-start | bytes 3145732
  0.0 25.1 %collective-permute-start = (bf16[512,1024]{1,0:T(8,128)(2,1)}, bf16[512,1024]{1,0:T(8,128)(2,1)S(1)}, u32[]{:S(2)}, u32[]{:S(2)}) collective-permute-start(bf16[512,1024]{1,0:T(8,128)(2,1)} %bitcast.14), channel_id=1, source_target_pairs={{0,1},{1,0},{2,3},{3,2},{4,5},{5,4},{6,7},{7,6},{8,9},{9,8},{10,11... | collective-permute-start | bytes 3145736 | tf_op jit(solution)/shard_map/ppermute | solution.py:242
  8.9 8.5 %collective-permute-start.2 = (bf16[1024,128]{1,0:T(8,128)(2,1)}, bf16[1024,128]{1,0:T(8,128)(2,1)S(1)}, u32[]{:S(2)}, u32[]{:S(2)}) collective-permute-start(bf16[1024,128]{1,0:T(8,128)(2,1)} %wk.1), channel_id=1, source_target_pairs={{0,448},{1,65},{2,450},{3,67},{4,452},{5,69},{6,454},{7,71},{8,456... | collective-permute-start | bytes 786440 | tf_op jit(solution)/shard_map/ppermute | solution.py:34
  10.9 9.4 %collective-permute-start.4 = (bf16[1024,128]{1,0:T(8,128)(2,1)}, bf16[1024,128]{1,0:T(8,128)(2,1)S(1)}, u32[]{:S(2)}, u32[]{:S(2)}) collective-permute-start(bf16[1024,128]{1,0:T(8,128)(2,1)} %wv.1), channel_id=1, source_target_pairs={{0,448},{1,65},{2,450},{3,67},{4,452},{5,69},{6,454},{7,71},{8,456... | collective-permute-start | bytes 786440 | tf_op jit(solution)/shard_map/ppermute | solution.py:34
  17.5 10.0 %collective-permute-start.3 = (bf16[1024,128]{1,0:T(8,128)(2,1)S(1)}, bf16[1024,128]{1,0:T(8,128)(2,1)S(1)}, u32[]{:S(2)}, u32[]{:S(2)}) collective-permute-start(bf16[1024,128]{1,0:T(8,128)(2,1)S(1)} %collective-permute-done.2.wk), channel_id=1, source_target_pairs={{0,448},{1,65},{2,450},{3,67},{4,452},{5,69},{6,454},{7,71},{8,456... | collective-permute-start | bytes 786440 | tf_op jit(solution)/shard_map/ppermute | solution.py:34
  20.3 8.3 %collective-permute-start.5 = (bf16[1024,128]{1,0:T(8,128)(2,1)S(1)}, bf16[1024,128]{1,0:T(8,128)(2,1)S(1)}, u32[]{:S(2)}, u32[]{:S(2)}) collective-permute-start(bf16[1024,128]{1,0:T(8,128)(2,1)S(1)} %collective-permute-done.4.wv), channel_id=1, source_target_pairs={{0,448},{1,65},{2,450},{3,67},{4,452},{5,69},{6,454},{7,71},{8,456... | collective-permute-start | bytes 786440 | tf_op jit(solution)/shard_map/ppermute | solution.py:34
  23.2 18.1 %copy-start.13 = (bf16[2048,128]{1,0:T(8,128)(2,1)}, bf16[2048,128]{1,0:T(8,128)(2,1)S(1)}, u32[]{:S(2)}) copy-start(bf16[2048,128]{1,0:T(8,128)(2,1)S(1)} %pad_maximum_fusion.q_own.o_own) | copy-start | bytes 1572868
  23.2 11.1 %collective-permute-start.1 = (bf16[2048,128]{1,0:T(8,128)(2,1)S(1)}, bf16[2048,128]{1,0:T(8,128)(2,1)S(1)}, u32[]{:S(2)}, u32[]{:S(2)}) collective-permute-start(bf16[2048,128]{1,0:T(8,128)(2,1)S(1)} %pad_maximum_fusion.q_own.o_own), channel_id=1, source_target_pairs={{0,448},{1,65},{2,450},{3,67},{4,452},{5,69},{6,454},{7,71},{8,456... | collective-permute-start | bytes 1572872 | tf_op jit(solution)/shard_map/ppermute | solution.py:34
  25.1 30.7 %copy-start.2 = (bf16[512,1024]{1,0:T(8,128)(2,1)}, bf16[512,1024]{1,0:T(8,128)(2,1)S(1)}, u32[]{:S(2)}) copy-start(bf16[512,1024]{1,0:T(8,128)(2,1)S(1)} %collective-permute-done.other) | copy-start | bytes 3145732
  27.4 20.6 %copy-start.7 = (bf16[2,512,256]{2,1,0:T(8,128)(2,1)}, bf16[2,512,256]{2,1,0:T(8,128)(2,1)S(1)}, u32[]{:S(2)}) copy-start(bf16[2,512,256]{2,1,0:T(8,128)(2,1)S(1)} %get-tuple-element.47.kv0) | copy-start | bytes 1572868
  27.4 28.4 %copy-start.3 = (f32[2,128,128]{2,1,0:T(8,128)}, f32[2,128,128]{2,1,0:T(8,128)S(1)}, u32[]{:S(2)}) copy-start(f32[2,128,128]{2,1,0:T(8,128)S(1)} %get-tuple-element.42.s0) | copy-start | bytes 393220
  28.6 27.2 %copy-start.11 = (bf16[1024,128]{1,0:T(8,128)(2,1)S(1)}, bf16[1024,128]{1,0:T(8,128)(2,1)}, u32[]{:S(2)}) copy-start(bf16[1024,128]{1,0:T(8,128)(2,1)} %wk.1) | copy-start | bytes 786436
  28.6 27.2 %copy-start.12 = (bf16[1024,128]{1,0:T(8,128)(2,1)S(1)}, bf16[1024,128]{1,0:T(8,128)(2,1)}, u32[]{:S(2)}) copy-start(bf16[1024,128]{1,0:T(8,128)(2,1)} %wv.1) | copy-start | bytes 786436
  28.6 8.5 %collective-permute-start.6 = (bf16[1024,128]{1,0:T(8,128)(2,1)S(1)}, bf16[1024,128]{1,0:T(8,128)(2,1)S(1)}, u32[]{:S(2)}, u32[]{:S(2)}) collective-permute-start(bf16[1024,128]{1,0:T(8,128)(2,1)S(1)} %collective-permute-done.3.wk), channel_id=1, source_target_pairs={{0,448},{1,65},{2,450},{3,67},{4,452},{5,69},{6,454},{7,71},{8,456... | collective-permute-start | bytes 786440 | tf_op jit(solution)/shard_map/ppermute | solution.py:34
  30.6 10.7 %collective-permute-start.8 = (bf16[1024,128]{1,0:T(8,128)(2,1)S(1)}, bf16[1024,128]{1,0:T(8,128)(2,1)S(1)}, u32[]{:S(2)}, u32[]{:S(2)}) collective-permute-start(bf16[1024,128]{1,0:T(8,128)(2,1)S(1)} %collective-permute-done.5.wv), channel_id=1, source_target_pairs={{0,448},{1,65},{2,450},{3,67},{4,452},{5,69},{6,454},{7,71},{8,456... | collective-permute-start | bytes 786440 | tf_op jit(solution)/shard_map/ppermute | solution.py:34
  37.1 16.7 %collective-permute-start.7 = (bf16[2048,128]{1,0:T(8,128)(2,1)S(1)}, bf16[2048,128]{1,0:T(8,128)(2,1)S(1)}, u32[]{:S(2)}, u32[]{:S(2)}) collective-permute-start(bf16[2048,128]{1,0:T(8,128)(2,1)S(1)} %collective-permute-done.1.q0.o0), channel_id=1, source_target_pairs={{0,448},{1,65},{2,450},{3,67},{4,452},{5,69},{6,454},{7,71},{8,456... | collective-permute-start | bytes 1572872 | tf_op jit(solution)/shard_map/ppermute | solution.py:34
  41.4 9.7 %collective-permute-start.9 = (bf16[1024,128]{1,0:T(8,128)(2,1)S(1)}, bf16[1024,128]{1,0:T(8,128)(2,1)S(1)}, u32[]{:S(2)}, u32[]{:S(2)}) collective-permute-start(bf16[1024,128]{1,0:T(8,128)(2,1)S(1)} %collective-permute-done.6.wk), channel_id=1, source_target_pairs={{0,448},{1,65},{2,450},{3,67},{4,452},{5,69},{6,454},{7,71},{8,456... | collective-permute-start | bytes 786440 | tf_op jit(solution)/shard_map/ppermute | solution.py:34
  43.3 10.6 %collective-permute-start.10 = (bf16[1024,128]{1,0:T(8,128)(2,1)S(1)}, bf16[1024,128]{1,0:T(8,128)(2,1)S(1)}, u32[]{:S(2)}, u32[]{:S(2)}) collective-permute-start(bf16[1024,128]{1,0:T(8,128)(2,1)S(1)} %collective-permute-done.8.wv), channel_id=1, source_target_pairs={{0,448},{1,65},{2,450},{3,67},{4,452},{5,69},{6,454},{7,71},{8,456... | collective-permute-start | bytes 786440 | tf_op jit(solution)/shard_map/ppermute | solution.py:34
  48.0 35.3 %copy-start.5 = (f32[2,128,128]{2,1,0:T(8,128)}, f32[2,128,128]{2,1,0:T(8,128)S(1)}, u32[]{:S(2)}) copy-start(f32[2,128,128]{2,1,0:T(8,128)S(1)} %get-tuple-element.44.s2) | copy-start | bytes 393220
  53.9 25.4 %copy-start.15 = (bf16[2048,128]{1,0:T(8,128)(2,1)}, bf16[2048,128]{1,0:T(8,128)(2,1)S(1)}, u32[]{:S(2)}) copy-start(bf16[2048,128]{1,0:T(8,128)(2,1)S(1)} %collective-permute-done.7.q1.o1) | copy-start | bytes 1572868
  53.9 25.4 %collective-permute-start.11 = (bf16[2048,128]{1,0:T(8,128)(2,1)S(1)}, bf16[2048,128]{1,0:T(8,128)(2,1)S(1)}, u32[]{:S(2)}, u32[]{:S(2)}) collective-permute-start(bf16[2048,128]{1,0:T(8,128)(2,1)S(1)} %collective-permute-done.7.q1.o1), channel_id=1, source_target_pairs={{0,448},{1,65},{2,450},{3,67},{4,452},{5,69},{6,454},{7,71},{8,456... | collective-permute-start | bytes 1572872 | tf_op jit(solution)/shard_map/ppermute | solution.py:34
  79.3 11.1 %collective-permute-start.12 = (bf16[2048,128]{1,0:T(8,128)(2,1)S(1)}, bf16[2048,128]{1,0:T(8,128)(2,1)S(1)}, u32[]{:S(2)}, u32[]{:S(2)}) collective-permute-start(bf16[2048,128]{1,0:T(8,128)(2,1)S(1)} %collective-permute-done.11.q2.o2), channel_id=1, source_target_pairs={{0,448},{1,65},{2,450},{3,67},{4,452},{5,69},{6,454},{7,71},{8,456... | collective-permute-start | bytes 1572872 | tf_op jit(solution)/shard_map/ppermute | solution.py:34
  83.3 17.1 %all-to-all-start.1 = ((bf16[32,16,128]{2,1,0:T(8,128)(2,1)}), bf16[32,16,128]{2,1,0:T(8,128)(2,1)S(1)}, u32[]{:S(2)}, u32[]{:S(2)}) async-start(bf16[32,16,128]{2,1,0:T(8,128)(2,1)} %shard_map.69), calls=%async_computation.1 | async-start | bytes 262144 | tf_op jit(solution)/shard_map/all_to_all | solution.py:287
  105.1 13.7 %collective-permute-start.13 = (bf16[512,1024]{1,0:T(8,128)(2,1)}, bf16[512,1024]{1,0:T(8,128)(2,1)S(1)}, u32[]{:S(2)}, u32[]{:S(2)}) collective-permute-start(bf16[512,1024]{1,0:T(8,128)(2,1)} %shard_map.71), channel_id=1, source_target_pairs={{0,1},{1,0},{2,3},{3,2},{4,5},{5,4},{6,7},{7,6},{8,9},{9,8},{10,11... | collective-permute-start | bytes 3145736 | tf_op jit(solution)/shard_map/ppermute | solution.py:333
  (10 other events, 88.0 us)

commit v8 on v7

--- a/solution.py
+++ b/solution.py
@@ -123,53 +123,53 @@
         copy.wait()
 
 
-def within_kernel(
-    own, other, q0, q1, q2, q_own, q_far, kv0, kv1, kv2, kv3, query_ref, within_ref,
-    tokens, weight, kv, query, within, sems, out_sems,
-):
+def within_kernel(final, *refs):
+    count = 7 if final else 6
+    own, other, *packs = refs[: count - 2]
+    kvs = refs[count - 2 : count]
+    query_ref, within_ref, tokens, weight, kv, query, within, sems, out_sems = refs[count:]
     core = lax.axis_index("core")
     loads = [begin(ref, tokens.at[block], sems.at[block]) for block, ref in enumerate((own, other))]
-    weights, pairs = [], []
-    for slot, ref in enumerate((q0, q1, q2)):
-        weights.append(begin(ref.at[TOP, :], weight.at[:, pl.ds(slot * DH, DH)], sems.at[2 + slot]))
-    final = weight.at[:, pl.ds(3 * DH, DH)]
-
-    @pl.when(core == 0)
-    def _():
-        begin(q_own.at[TOP, :], final, sems.at[5])
-
-    @pl.when(core != 0)
-    def _():
-        begin(q_far.at[TOP, :], final, sems.at[5])
-
-    weights.append(pltpu.make_async_copy(q_own.at[TOP, :], final, sems.at[5]))
-    for slot, ref in enumerate((kv0, kv1, kv2, kv3)):
-        pairs.append(begin(ref, kv.at[slot], sems.at[10 + slot]))
+    left, right = weight.at[:, pl.ds(0, DH)], weight.at[:, pl.ds(DH, DH)]
+    loads.append(begin(packs[0].at[TOP, :], left, sems.at[2]))
+    if final:
+
+        @pl.when(core == 0)
+        def _():
+            begin(packs[1].at[TOP, :], right, sems.at[3])
+
+        @pl.when(core != 0)
+        def _():
+            begin(packs[2].at[TOP, :], right, sems.at[3])
+
+        loads.append(pltpu.make_async_copy(packs[1].at[TOP, :], right, sems.at[3]))
+    else:
+        loads.append(begin(packs[1].at[TOP, :], right, sems.at[3]))
+    pairs = [begin(ref, kv.at[side], sems.at[4 + side]) for side, ref in enumerate(kvs)]
     half = TOK // 2
     rows = lax.broadcasted_iota(jnp.int32, (half, half), 0)
     cols = lax.broadcasted_iota(jnp.int32, (half, half), 1)
     keep = cols <= rows
-    for load in loads:
-        load.wait()
+    for index in (0, 2, 3):
+        loads[index].wait()
     copies = []
-    for pair in range(2):
-        for slot in (2 * pair, 2 * pair + 1):
-            weights[slot].wait()
-            pairs[slot].wait()
-        for block in range(2):
-            both = mm(tokens[block], weight[:, 2 * pair * DH : 2 * (pair + 1) * DH]).astype(BF16)
-            for side in range(2):
-                slot = 2 * pair + side
-                q = both[:, side * DH : (side + 1) * DH]
-                query[slot, block] = q
-                copies.append(begin(query.at[slot, block], query_ref.at[slot, block], out_sems.at[0, slot, block]))
-                key, value = kv[slot, block, :, :DH], kv[slot, block, :, DH:]
-                top = jnp.where(keep, mm_t(q[:half], key[:half]), 0.0).astype(BF16)
-                within[slot, block, :half] = mm(top, value[:half])
-                left = mm_t(q[half:], key[:half]).astype(BF16)
-                right = jnp.where(keep, mm_t(q[half:], key[half:]), 0.0).astype(BF16)
-                within[slot, block, half:] = mm(left, value[:half]) + mm(right, value[half:])
-                copies.append(begin(within.at[slot, block], within_ref.at[slot, block], out_sems.at[1, slot, block]))
+    for block in range(2):
+        if block == 1:
+            loads[1].wait()
+        both = mm(tokens[block], weight[...]).astype(BF16)
+        for side in range(2):
+            if block == 0:
+                pairs[side].wait()
+            q = both[:, side * DH : (side + 1) * DH]
+            query[side, block] = q
+            copies.append(begin(query.at[side, block], query_ref.at[side, block], out_sems.at[0, side, block]))
+            key, value = kv[side, block, :, :DH], kv[side, block, :, DH:]
+            top = jnp.where(keep, mm_t(q[:half], key[:half]), 0.0).astype(BF16)
+            within[side, block, :half] = mm(top, value[:half])
+            low = mm_t(q[half:], key[:half]).astype(BF16)
+            corner = jnp.where(keep, mm_t(q[half:], key[half:]), 0.0).astype(BF16)
+            within[side, block, half:] = mm(low, value[:half]) + mm(corner, value[half:])
+            copies.append(begin(within.at[side, block], within_ref.at[side, block], out_sems.at[1, side, block]))
     for copy in copies:
         copy.wait()
 
@@ -182,7 +182,7 @@
 
 
 def out_kernel(
-    block, query_ref, within_ref, prior_ref, s0, s1, s2, s3, gain_ref, o0, o1, o2, o_own, o_far, out_ref,
+    block, query_a, query_b, within_a, within_b, prior_ref, s0, s1, s2, s3, gain_ref, o0, o1, o2, o_own, o_far, out_ref,
     query, within, prior, state, gain, weight, normed, out, sems, out_sems,
 ):
     core = lax.axis_index("core")
@@ -193,8 +193,8 @@
         loads.append(
             [
                 begin(ref.at[1 - block], state.at[slot], sems.at[2 + 3 * slot]),
-                begin(query_ref.at[slot, block], query.at[slot], sems.at[3 + 3 * slot]),
-                begin(within_ref.at[slot, block], within.at[slot], sems.at[4 + 3 * slot]),
+                begin((query_a, query_b)[slot // 2].at[slot % 2, block], query.at[slot], sems.at[3 + 3 * slot]),
+                begin((within_a, within_b)[slot // 2].at[slot % 2, block], within.at[slot], sems.at[4 + 3 * slot]),
             ]
         )
     for slot, ref in enumerate((o0, o1, o2)):
@@ -275,42 +275,47 @@
     key_3, value_3, s1 = barrier((key_3, value_3, s1))
     kv2, s2 = one(own, other, key_3, value_3)
     key_4, value_4 = hop(key_3), hop(value_3)
-    pack_2, key_4, value_4, s2 = barrier((pack_2, key_4, value_4, s2))
-    pack_3 = hop(pack_2)
+    key_4, value_4, s2 = barrier((key_4, value_4, s2))
     kv3, s3, total = last(own, other, w_key, w_value, key_4, value_4, s0, s1, s2)
+    pack_3, pack_4 = hop(pack_2), hop(pack_2, 2)
+
+    half = (2, 2, TOK, DH)
+
+    def attend(final, *arrays):
+        return call(
+            functools.partial(within_kernel, final),
+            len(arrays),
+            (shape(half, BF16), shape(half, F32)),
+            [
+                pltpu.VMEM((2, TOK, D), BF16),
+                pltpu.VMEM((D, 2 * DH), BF16),
+                pltpu.VMEM((2, 2, TOK, 2 * DH), BF16),
+                pltpu.VMEM(half, BF16),
+                pltpu.VMEM(half, F32),
+                DMA((6,)),
+                DMA((2, 2, 2)),
+            ],
+            3 * TOK * D * SLOTS * DH,
+            5 << 20,
+        )(*arrays)
+
+    query_a, within_a = attend(False, own, other, pack_1, pack_2, kv0, kv1)
 
     chunks = total.reshape(CHIPS, SLOTS * DH // CHIPS, DH)
     chunks = lax.all_to_all(chunks, ("z", "x"), 0, 0, tiled=True)
-    pack_3, chunks = barrier((pack_3, chunks))
-    pack_4 = hop(pack_3)
+    chunks, query_a = barrier((chunks, query_a))
     priors = call(prefix_kernel, 1, shape(chunks.shape, BF16), [], 1 << 16, 1 << 18, VMEM, 4)(chunks)
     prior = lax.all_to_all(priors, ("z", "x"), 0, 0, tiled=True).reshape(SLOTS, DH, DH)
 
-    queries, withins = (SLOTS, 2, TOK, DH), (SLOTS, 2, TOK, DH)
-    query, within = call(
-        within_kernel,
-        11,
-        (shape(queries, BF16), shape(withins, F32)),
-        [
-            pltpu.VMEM((2, TOK, D), BF16),
-            pltpu.VMEM((D, SLOTS * DH), BF16),
-            pltpu.VMEM((SLOTS, 2, TOK, 2 * DH), BF16),
-            pltpu.VMEM(queries, BF16),
-            pltpu.VMEM(withins, F32),
-            DMA((14,)),
-            DMA((2, SLOTS, 2)),
-        ],
-        3 * 2 * TOK * D * SLOTS * DH,
-        8 << 20,
-    )(own, other, pack_1, pack_2, pack_3, pack, pack_4, kv0, kv1, kv2, kv3)
-
-    operands = (query, within, prior, s0, s1, s2, s3, norm_gain.reshape(DP, DH), pack_1, pack_2, pack_3, pack, pack_4)
+    query_b, within_b = attend(True, own, other, pack_3, pack, pack_4, kv2, kv3)
+
+    operands = (query_a, query_b, within_a, within_b, prior, s0, s1, s2, s3, norm_gain.reshape(DP, DH), pack_1, pack_2, pack_3, pack, pack_4)
     partial = []
-    for block, kind, limit in ((1, BF16, 56), (0, F32, 56)):
+    for block, kind, limit in ((1, BF16, 56), (0, BF16, 56)):
         partial.append(
             call(
                 functools.partial(out_kernel, block),
-                13,
+                15,
                 shape((TOK, D), kind),
                 [
                     pltpu.VMEM((SLOTS, TOK, DH), BF16),
@@ -331,7 +336,7 @@
             )(*operands)
         )
     got = lax.ppermute(partial[0], "core", SWAP)
-    return (partial[1] + got.astype(F32)).astype(BF16)[None]
+    return (partial[1].astype(F32) + got.astype(F32)).astype(BF16)[None]
 
 
 def solution(mesh):

time: 122 us -> 127 us (1.041)
  blocking collectives: 18.9 us -> 0 us
  starting transfers between devices: 47.3 us -> 61.2 us
  waiting for transfers between devices: 20.2 us -> 26.9 us
  Pallas kernels: 27.9 us -> 31 us
    all_to_all x1 -> x0, blocking collectives: 18.9 us -> none  [body(): chunks = lax.all_to_all(chunks, ('z', 'x'), 0, 0, tiled=True)]
    all_to_all x0 -> x1, starting transfers between devices: none -> 11.2 us  [body(): chunks = lax.all_to_all(chunks, ('z', 'x'), 0, 0, tiled=True)]
    all_to_all x0 -> x1, waiting for transfers between devices: none -> 3.39 us  [body(): chunks = lax.all_to_all(chunks, ('z', 'x'), 0, 0, tiled=True)]
    pallas_call x3 -> x4, Pallas kernels: 17.4 us -> 20 us  [the longest x2 11.9 us: attend(): call(functools.partial(within_kernel, final), len(arrays), (shape(half, B...]
    all_to_all x1, waiting for transfers between devices: 0.01 us -> 2.4 us  [body(): lax.all_to_all(priors, ('z', 'x'), 0, 0, tiled=True).reshape(SLOTS, DH, DH)]
    all_to_all x1, starting transfers between devices: 4.03 us -> 6.02 us  [body(): lax.all_to_all(priors, ('z', 'x'), 0, 0, tiled=True).reshape(SLOTS, DH, DH)]
    unnamed x38 -> x34, local copies, waits for them, and re-layouts: 2.99 us -> 2.94 us
  transfers between devices with their start and end apart: 15 -> 16, of which waited for: 8 -> 8; matrix products, arithmetic and copies ran while one was open for 1% -> 1% of each run, Pallas kernels for 20% -> 21%
where the time goes in v8:
time: 127 us; the launch traced here: 126 us
  starting transfers between devices  61.2 us (48%)
  Pallas kernels  31 us (24%)
  waiting for transfers between devices  26.9 us (21%)
  other arithmetic  3.58 us (3%)
  local copies, waits for them, and re-layouts  2.99 us (2%)
    ppermute x12, starting transfers between devices, hop(): return lax.ppermute(weight, ('dp', 'z', 'x', 'core'), pairs)  25.5 us
    ppermute x12, waiting for transfers between devices, hop(): return lax.ppermute(weight, ('dp', 'z', 'x', 'core'), pairs)  21.1 us
    pallas_call x2, Pallas kernels, attend(): call(functools.partial(within_kernel, final), len(arrays), (shape(half, B...  11.9 us
    all_to_all x1, starting transfers between devices, body(): chunks = lax.all_to_all(chunks, ('z', 'x'), 0, 0, tiled=True)  11.2 us
    ppermute x1, starting transfers between devices, body(): got = lax.ppermute(partial[0], 'core', SWAP)  9.55 us
    ppermute x1, starting transfers between devices, body(): other = lax.ppermute(own, 'core', SWAP)  8.91 us
    pallas_call x2, Pallas kernels, body(): call(functools.partial(out_kernel, block), 15, shape((TOK, D), kind), [pl...  8.15 us
    all_to_all x1, starting transfers between devices, body(): lax.all_to_all(priors, ('z', 'x'), 0, 0, tiled=True).reshape(SLOTS, DH, DH)  6.02 us
  transfers between devices with their start and end apart: 16, of which 8 were waited for; matrix products, arithmetic and copies ran while one was open for 1% of the time, Pallas kernels for 21%

profile of v8, /device:TPU:1, one launch (start us, length us, event | category | flops | bytes accessed | tf_op | source)
XLA Modules:
  0.0 126.1 jit_solution(1918892434744692052)
XLA Ops:
  0.0 8.9 %collective-permute-start = (bf16[512,1024]{1,0:T(8,128)(2,1)}, bf16[512,1024]{1,0:T(8,128)(2,1)S(1)}, u32[]{:S(2)}, u32[]{:S(2)}) collective-permute-start(bf16[512,1024]{1,0:T(8,128)(2,1)} %bitcast.14), channel_id=1, source_target_pairs={{0,1},{1,0},{2,3},{3,2},{4,5},{5,4},{6,7},{7,6},{8,9},{9,8},{10,11... | collective-permute-start | bytes 3145736 | tf_op jit(solution)/shard_map/ppermute | solution.py:242
  8.9 1.9 %collective-permute-start.2 = (bf16[1024,128]{1,0:T(8,128)(2,1)}, bf16[1024,128]{1,0:T(8,128)(2,1)S(1)}, u32[]{:S(2)}, u32[]{:S(2)}) collective-permute-start(bf16[1024,128]{1,0:T(8,128)(2,1)} %wk.1), channel_id=1, source_target_pairs={{0,448},{1,65},{2,450},{3,67},{4,452},{5,69},{6,454},{7,71},{8,456... | collective-permute-start | bytes 786440 | tf_op jit(solution)/shard_map/ppermute | solution.py:34
  10.9 1.9 %collective-permute-start.4 = (bf16[1024,128]{1,0:T(8,128)(2,1)}, bf16[1024,128]{1,0:T(8,128)(2,1)S(1)}, u32[]{:S(2)}, u32[]{:S(2)}) collective-permute-start(bf16[1024,128]{1,0:T(8,128)(2,1)} %wv.1), channel_id=1, source_target_pairs={{0,448},{1,65},{2,450},{3,67},{4,452},{5,69},{6,454},{7,71},{8,456... | collective-permute-start | bytes 786440 | tf_op jit(solution)/shard_map/ppermute | solution.py:34
  12.8 4.6 %collective-permute-done.2.wk = bf16[1024,128]{1,0:T(8,128)(2,1)S(1)} collective-permute-done((bf16[1024,128]{1,0:T(8,128)(2,1)}, bf16[1024,128]{1,0:T(8,128)(2,1)S(1)}, u32[]{:S(2)}, u32[]{:S(2)}) %collective-permute-start.2) | collective-permute-done | bytes 262176 | tf_op jit(solution)/shard_map/ppermute | solution.py:34
  25.1 2.3 %shard_map.64 = (bf16[2,512,256]{2,1,0:T(8,128)(2,1)S(1)}, f32[2,128,128]{2,1,0:T(8,128)S(1)}) custom-call(bf16[512,1024]{1,0:T(8,128)(2,1)S(1)} %bitcast.17, bf16[512,1024]{1,0:T(8,128)(2,1)S(1)} %collective-permute-done.other.refs_1_, bf16[1024,128]{1,0:T(8,128)(2,1)S(1)} %collective-permute-done.2.wk, bf16[1024,128]{1,0:T(8,128)(2,1)S(1)} %collective-permute-done.4.wv), custom_call_target="tpu_custom_call" | custom-call | flops 536870912 | bytes 3145728 | tf_op jit(solution)/shard_map/pallas_call | solution.py:267
  30.5 3.8 %collective-permute-done.1.refs_2_.o0 = bf16[2048,128]{1,0:T(8,128)(2,1)S(1)} collective-permute-done((bf16[2048,128]{1,0:T(8,128)(2,1)S(1)}, bf16[2048,128]{1,0:T(8,128)(2,1)S(1)}, u32[]{:S(2)}, u32[]{:S(2)}) %collective-permute-start.1) | collective-permute-done | bytes 524320 | tf_op jit(solution)/shard_map/ppermute | solution.py:34
  34.3 2.8 %collective-permute-done.6.wk = bf16[1024,128]{1,0:T(8,128)(2,1)S(1)} collective-permute-done((bf16[1024,128]{1,0:T(8,128)(2,1)S(1)}, bf16[1024,128]{1,0:T(8,128)(2,1)S(1)}, u32[]{:S(2)}, u32[]{:S(2)}) %collective-permute-start.6) | collective-permute-done | bytes 262176 | tf_op jit(solution)/shard_map/ppermute | solution.py:34
  41.0 2.3 %shard_map.65 = (bf16[2,512,256]{2,1,0:T(8,128)(2,1)S(1)}, f32[2,128,128]{2,1,0:T(8,128)S(1)}) custom-call(bf16[512,1024]{1,0:T(8,128)(2,1)S(1)} %bitcast.18, bf16[512,1024]{1,0:T(8,128)(2,1)S(1)} %collective-permute-done.other.refs_1_, bf16[1024,128]{1,0:T(8,128)(2,1)S(1)} %collective-permute-done.3.wk, bf16[1024,128]{1,0:T(8,128)(2,1)S(1)} %collective-permute-done.5.wv), custom_call_target="tpu_custom_call" | custom-call | flops 536870912 | bytes 3145728 | tf_op jit(solution)/shard_map/pallas_call | solution.py:271
  43.3 7.8 %collective-permute-done.7.wv = bf16[1024,128]{1,0:T(8,128)(2,1)S(1)} collective-permute-done((bf16[1024,128]{1,0:T(8,128)(2,1)S(1)}, bf16[1024,128]{1,0:T(8,128)(2,1)S(1)}, u32[]{:S(2)}, u32[]{:S(2)}) %collective-permute-start.7) | collective-permute-done | bytes 262176 | tf_op jit(solution)/shard_map/ppermute | solution.py:34
  51.1 2.0 %collective-permute-start.8 = (bf16[1024,128]{1,0:T(8,128)(2,1)S(1)}, bf16[1024,128]{1,0:T(8,128)(2,1)S(1)}, u32[]{:S(2)}, u32[]{:S(2)}) collective-permute-start(bf16[1024,128]{1,0:T(8,128)(2,1)S(1)} %collective-permute-done.6.wk), channel_id=1, source_target_pairs={{0,448},{1,65},{2,450},{3,67},{4,452},{5,69},{6,454},{7,71},{8,456... | collective-permute-start | bytes 786440 | tf_op jit(solution)/shard_map/ppermute | solution.py:34
  55.1 3.4 %collective-permute-start.12 = (bf16[2048,128]{1,0:T(8,128)(2,1)}, bf16[2048,128]{1,0:T(8,128)(2,1)S(1)}, u32[]{:S(2)}, u32[]{:S(2)}) collective-permute-start(bf16[2048,128]{1,0:T(8,128)(2,1)} %collective-permute-done.10.refs_3_.o1), channel_id=1, source_target_pairs={{0,384},{1,129},{2,386},{3,131},{4,388},{5,133},{6,390},{7,135},{8... | collective-permute-start | bytes 1572872 | tf_op jit(solution)/shard_map/ppermute | solution.py:34
  58.5 2.8 %collective-permute-start.11 = (bf16[2048,128]{1,0:T(8,128)(2,1)}, bf16[2048,128]{1,0:T(8,128)(2,1)}, u32[]{:S(2)}, u32[]{:S(2)}) collective-permute-start(bf16[2048,128]{1,0:T(8,128)(2,1)} %collective-permute-done.10.refs_3_.o1), channel_id=1, source_target_pairs={{0,448},{1,65},{2,450},{3,67},{4,452},{5,69},{6,454},{7,71},{8,456... | collective-permute-start | bytes 1572872 | tf_op jit(solution)/shard_map/ppermute | solution.py:34
  61.3 2.3 %shard_map.66 = (bf16[2,512,256]{2,1,0:T(8,128)(2,1)S(1)}, f32[2,128,128]{2,1,0:T(8,128)S(1)}) custom-call(bf16[512,1024]{1,0:T(8,128)(2,1)S(1)} %bitcast.19, bf16[512,1024]{1,0:T(8,128)(2,1)S(1)} %collective-permute-done.other.refs_1_, bf16[1024,128]{1,0:T(8,128)(2,1)S(1)} %collective-permute-done.6.wk, bf16[1024,128]{1,0:T(8,128)(2,1)S(1)} %collective-permute-done.7.wv), custom_call_target="tpu_custom_call" | custom-call | flops 536870912 | bytes 3145728 | tf_op jit(solution)/shard_map/pallas_call | solution.py:276
  63.7 3.5 %shard_map.67 = (bf16[2,512,256]{2,1,0:T(8,128)(2,1)S(1)}, f32[2,128,128]{2,1,0:T(8,128)S(1)}, bf16[4,128,128]{2,1,0:T(8,128)(2,1)}) custom-call(bf16[512,1024]{1,0:T(8,128)(2,1)S(1)} %bitcast.20, bf16[512,1024]{1,0:T(8,128)(2,1)S(1)} %collective-permute-done.other.refs_1_, bf16[1024,128]{1,0:T(8,128)(2,1)S(1)} %copy-done.11, ...), custom_call_target="tpu_custom_call" | custom-call | flops 536870912 | bytes 3145728 | tf_op jit(solution)/shard_map/pallas_call | solution.py:279
  68.6 11.2 %all-to-all-start = ((bf16[32,16,128]{2,1,0:T(8,128)(2,1)}), bf16[32,16,128]{2,1,0:T(8,128)(2,1)S(1)}, u32[]{:S(2)}, u32[]{:S(2)}) async-start(bf16[32,16,128]{2,1,0:T(8,128)(2,1)} %bitcast.3), calls=%async_computation | async-start | bytes 262144 | tf_op jit(solution)/shard_map/all_to_all | solution.py:305
  79.9 5.9 %shard_map.68 = (bf16[2,2,512,128]{3,2,1,0:T(8,128)(2,1)}, f32[2,2,512,128]{3,2,1,0:T(8,128)}) custom-call(bf16[512,1024]{1,0:T(8,128)(2,1)} %bitcast.15, bf16[512,1024]{1,0:T(8,128)(2,1)} %copy-done.2, bf16[2048,128]{1,0:T(8,128)(2,1)} %copy-done.15, bf16[2048,128]{1,0:T(8,128)(2,1)} %collective-permute-done.10.refs_3_.o1, bf16[2,512,256]{2,1,0:T(8,128)(2,1)} %copy-done.9, ...), custom_call_target="tpu_custom_call" | custom-call | flops 805306368 | bytes 5242880 | tf_op jit(solution)/shard_map/pallas_call | solution.py:285
  85.8 3.4 %all-to-all-done.chunk_ref = bf16[32,16,128]{2,1,0:T(8,128)(2,1)S(1)} async-done(((bf16[32,16,128]{2,1,0:T(8,128)(2,1)}), bf16[32,16,128]{2,1,0:T(8,128)(2,1)S(1)}, u32[]{:S(2)}, u32[]{:S(2)}) %all-to-all-start) | async-done | bytes 131104 | tf_op jit(solution)/shard_map/all_to_all | solution.py:305
  89.9 6.0 %all-to-all-start.1 = ((bf16[32,16,128]{2,1,0:T(8,128)(2,1)}), bf16[32,16,128]{2,1,0:T(8,128)(2,1)S(1)}, u32[]{:S(2)}, u32[]{:S(2)}) async-start(bf16[32,16,128]{2,1,0:T(8,128)(2,1)} %shard_map.70), calls=%async_computation.1 | async-start | bytes 262144 | tf_op jit(solution)/shard_map/all_to_all | solution.py:308
  96.8 5.9 %shard_map.69 = (bf16[2,2,512,128]{3,2,1,0:T(8,128)(2,1)}, f32[2,2,512,128]{3,2,1,0:T(8,128)}) custom-call(bf16[512,1024]{1,0:T(8,128)(2,1)} %bitcast.16, bf16[512,1024]{1,0:T(8,128)(2,1)} %copy-done.2, bf16[2048,128]{1,0:T(8,128)(2,1)} %collective-permute-done.11.refs_2_.o2, bf16[2048,128]{1,0:T(8,128)(2,1)} %copy-done.13, bf16[2048,128]{1,0:T(8,128)(2,1)} %copy-done.14, ...), custom_call_target="tpu_custom_call" | custom-call | flops 805306368 | bytes 5242880 | tf_op jit(solution)/shard_map/pallas_call | solution.py:285
  102.7 2.4 %all-to-all-done.1 = bf16[32,16,128]{2,1,0:T(8,128)(2,1)S(1)} async-done(((bf16[32,16,128]{2,1,0:T(8,128)(2,1)}), bf16[32,16,128]{2,1,0:T(8,128)(2,1)S(1)}, u32[]{:S(2)}, u32[]{:S(2)}) %all-to-all-start.1) | async-done | bytes 131104 | tf_op jit(solution)/shard_map/all_to_all | solution.py:308
  105.8 4.1 %shard_map.72 = bf16[512,1024]{1,0:T(8,128)(2,1)} custom-call(bf16[2,2,512,128]{3,2,1,0:T(8,128)(2,1)} %get-tuple-element.49.query_a, bf16[2,2,512,128]{3,2,1,0:T(8,128)(2,1)} %get-tuple-element.52.query_b, f32[2,2,512,128]{3,2,1,0:T(8,128)} %get-tuple-element.53.within_a, f32[2,2,512,128]{3,2,1,0:T(8,128)} %get-tuple-element.54.within_b, ...), custom_call_target="tpu_custom_call" | custom-call | flops 1342177280 | bytes 5242880 | tf_op jit(solution)/shard_map/pallas_call | solution.py:316
  109.8 9.6 %collective-permute-start.13 = (bf16[512,1024]{1,0:T(8,128)(2,1)}, bf16[512,1024]{1,0:T(8,128)(2,1)S(1)}, u32[]{:S(2)}, u32[]{:S(2)}) collective-permute-start(bf16[512,1024]{1,0:T(8,128)(2,1)} %shard_map.72), channel_id=1, source_target_pairs={{0,1},{1,0},{2,3},{3,2},{4,5},{5,4},{6,7},{7,6},{8,9},{9,8},{10,11... | collective-permute-start | bytes 3145736 | tf_op jit(solution)/shard_map/ppermute | solution.py:338
  119.4 4.1 %shard_map.71 = bf16[512,1024]{1,0:T(8,128)(2,1)} custom-call(bf16[2,2,512,128]{3,2,1,0:T(8,128)(2,1)} %get-tuple-element.49.query_a, bf16[2,2,512,128]{3,2,1,0:T(8,128)(2,1)} %get-tuple-element.52.query_b, f32[2,2,512,128]{3,2,1,0:T(8,128)} %get-tuple-element.53.within_a, f32[2,2,512,128]{3,2,1,0:T(8,128)} %get-tuple-element.54.within_b, ...), custom_call_target="tpu_custom_call" | custom-call | flops 1342177280 | bytes 5242880 | tf_op jit(solution)/shard_map/pallas_call | solution.py:316
  123.5 2.6 %fusion = bf16[1,512,1024]{2,1,0:T(8,128)(2,1)} fusion(bf16[512,1024]{1,0:T(8,128)(2,1)S(1)} %collective-permute-done.13, bf16[512,1024]{1,0:T(8,128)(2,1)} %shard_map.71), kind=kLoop, calls=%fused_computation.1 | loop fusion | flops 2097152 | bytes 3145728 | tf_op jit(solution)/shard_map/broadcast_in_dim | solution.py:339
  (54 shorter events, 20.1 us)
Async XLA Ops:
  0.0 12.8 %copy-start = (bf16[128,1024]{1,0:T(8,128)(2,1)S(1)}, bf16[128,1024]{1,0:T(8,128)(2,1)}, u32[]{:S(2)}) copy-start(bf16[128,1024]{1,0:T(8,128)(2,1)} %param.10) | copy-start | bytes 786436
  0.0 25.1 %copy-start.1 = (bf16[1,512,1024]{2,1,0:T(8,128)(2,1)S(1)}, bf16[1,512,1024]{2,1,0:T(8,128)(2,1)}, u32[]{:S(2)}) copy-start(bf16[1,512,1024]{2,1,0:T(8,128)(2,1)} %param.6) | copy-start | bytes 3145732
  0.0 25.1 %collective-permute-start = (bf16[512,1024]{1,0:T(8,128)(2,1)}, bf16[512,1024]{1,0:T(8,128)(2,1)S(1)}, u32[]{:S(2)}, u32[]{:S(2)}) collective-permute-start(bf16[512,1024]{1,0:T(8,128)(2,1)} %bitcast.14), channel_id=1, source_target_pairs={{0,1},{1,0},{2,3},{3,2},{4,5},{5,4},{6,7},{7,6},{8,9},{9,8},{10,11... | collective-permute-start | bytes 3145736 | tf_op jit(solution)/shard_map/ppermute | solution.py:242
  8.9 8.5 %collective-permute-start.2 = (bf16[1024,128]{1,0:T(8,128)(2,1)}, bf16[1024,128]{1,0:T(8,128)(2,1)S(1)}, u32[]{:S(2)}, u32[]{:S(2)}) collective-permute-start(bf16[1024,128]{1,0:T(8,128)(2,1)} %wk.1), channel_id=1, source_target_pairs={{0,448},{1,65},{2,450},{3,67},{4,452},{5,69},{6,454},{7,71},{8,456... | collective-permute-start | bytes 786440 | tf_op jit(solution)/shard_map/ppermute | solution.py:34
  10.9 9.4 %collective-permute-start.4 = (bf16[1024,128]{1,0:T(8,128)(2,1)}, bf16[1024,128]{1,0:T(8,128)(2,1)S(1)}, u32[]{:S(2)}, u32[]{:S(2)}) collective-permute-start(bf16[1024,128]{1,0:T(8,128)(2,1)} %wv.1), channel_id=1, source_target_pairs={{0,448},{1,65},{2,450},{3,67},{4,452},{5,69},{6,454},{7,71},{8,456... | collective-permute-start | bytes 786440 | tf_op jit(solution)/shard_map/ppermute | solution.py:34
  17.5 10.0 %collective-permute-start.3 = (bf16[1024,128]{1,0:T(8,128)(2,1)S(1)}, bf16[1024,128]{1,0:T(8,128)(2,1)S(1)}, u32[]{:S(2)}, u32[]{:S(2)}) collective-permute-start(bf16[1024,128]{1,0:T(8,128)(2,1)S(1)} %collective-permute-done.2.wk), channel_id=1, source_target_pairs={{0,448},{1,65},{2,450},{3,67},{4,452},{5,69},{6,454},{7,71},{8,456... | collective-permute-start | bytes 786440 | tf_op jit(solution)/shard_map/ppermute | solution.py:34
  20.3 8.3 %collective-permute-start.5 = (bf16[1024,128]{1,0:T(8,128)(2,1)S(1)}, bf16[1024,128]{1,0:T(8,128)(2,1)S(1)}, u32[]{:S(2)}, u32[]{:S(2)}) collective-permute-start(bf16[1024,128]{1,0:T(8,128)(2,1)S(1)} %collective-permute-done.4.wv), channel_id=1, source_target_pairs={{0,448},{1,65},{2,450},{3,67},{4,452},{5,69},{6,454},{7,71},{8,456... | collective-permute-start | bytes 786440 | tf_op jit(solution)/shard_map/ppermute | solution.py:34
  23.2 11.1 %collective-permute-start.1 = (bf16[2048,128]{1,0:T(8,128)(2,1)S(1)}, bf16[2048,128]{1,0:T(8,128)(2,1)S(1)}, u32[]{:S(2)}, u32[]{:S(2)}) collective-permute-start(bf16[2048,128]{1,0:T(8,128)(2,1)S(1)} %pad_maximum_fusion.refs_3_.o_own), channel_id=1, source_target_pairs={{0,448},{1,65},{2,450},{3,67},{4,452},{5,69},{6,454},{7,71},{8,456... | collective-permute-start | bytes 1572872 | tf_op jit(solution)/shard_map/ppermute | solution.py:34
  25.1 38.5 %copy-start.2 = (bf16[512,1024]{1,0:T(8,128)(2,1)}, bf16[512,1024]{1,0:T(8,128)(2,1)S(1)}, u32[]{:S(2)}) copy-start(bf16[512,1024]{1,0:T(8,128)(2,1)S(1)} %collective-permute-done.other.refs_1_) | copy-start | bytes 3145732
  27.4 15.8 %copy-start.9 = (bf16[2,512,256]{2,1,0:T(8,128)(2,1)}, bf16[2,512,256]{2,1,0:T(8,128)(2,1)S(1)}, u32[]{:S(2)}) copy-start(bf16[2,512,256]{2,1,0:T(8,128)(2,1)S(1)} %get-tuple-element.46.refs_4_) | copy-start | bytes 1572868
  27.4 36.2 %copy-start.3 = (f32[2,128,128]{2,1,0:T(8,128)}, f32[2,128,128]{2,1,0:T(8,128)S(1)}, u32[]{:S(2)}) copy-start(f32[2,128,128]{2,1,0:T(8,128)S(1)} %get-tuple-element.41.s0) | copy-start | bytes 393220
  28.6 8.5 %collective-permute-start.6 = (bf16[1024,128]{1,0:T(8,128)(2,1)S(1)}, bf16[1024,128]{1,0:T(8,128)(2,1)S(1)}, u32[]{:S(2)}, u32[]{:S(2)}) collective-permute-start(bf16[1024,128]{1,0:T(8,128)(2,1)S(1)} %collective-permute-done.3.wk), channel_id=1, source_target_pairs={{0,448},{1,65},{2,450},{3,67},{4,452},{5,69},{6,454},{7,71},{8,456... | collective-permute-start | bytes 786440 | tf_op jit(solution)/shard_map/ppermute | solution.py:34
  37.1 17.9 %collective-permute-start.10 = (bf16[2048,128]{1,0:T(8,128)(2,1)S(1)}, bf16[2048,128]{1,0:T(8,128)(2,1)}, u32[]{:S(2)}, u32[]{:S(2)}) collective-permute-start(bf16[2048,128]{1,0:T(8,128)(2,1)S(1)} %collective-permute-done.1.refs_2_.o0), channel_id=1, source_target_pairs={{0,448},{1,65},{2,450},{3,67},{4,452},{5,69},{6,454},{7,71},{8,456... | collective-permute-start | bytes 1572872 | tf_op jit(solution)/shard_map/ppermute | solution.py:34
  39.1 12.0 %collective-permute-start.7 = (bf16[1024,128]{1,0:T(8,128)(2,1)S(1)}, bf16[1024,128]{1,0:T(8,128)(2,1)S(1)}, u32[]{:S(2)}, u32[]{:S(2)}) collective-permute-start(bf16[1024,128]{1,0:T(8,128)(2,1)S(1)} %collective-permute-done.5.wv), channel_id=1, source_target_pairs={{0,448},{1,65},{2,450},{3,67},{4,452},{5,69},{6,454},{7,71},{8,456... | collective-permute-start | bytes 786440 | tf_op jit(solution)/shard_map/ppermute | solution.py:34
  43.3 20.3 %copy-start.10 = (bf16[2,512,256]{2,1,0:T(8,128)(2,1)}, bf16[2,512,256]{2,1,0:T(8,128)(2,1)S(1)}, u32[]{:S(2)}) copy-start(bf16[2,512,256]{2,1,0:T(8,128)(2,1)S(1)} %get-tuple-element.47.refs_5_) | copy-start | bytes 1572868
  43.3 20.4 %copy-start.4 = (f32[2,128,128]{2,1,0:T(8,128)}, f32[2,128,128]{2,1,0:T(8,128)S(1)}, u32[]{:S(2)}) copy-start(f32[2,128,128]{2,1,0:T(8,128)S(1)} %get-tuple-element.42.s1) | copy-start | bytes 393220
  51.1 12.6 %copy-start.12 = (bf16[1024,128]{1,0:T(8,128)(2,1)S(1)}, bf16[1024,128]{1,0:T(8,128)(2,1)}, u32[]{:S(2)}) copy-start(bf16[1024,128]{1,0:T(8,128)(2,1)} %wv.1) | copy-start | bytes 786436
  51.1 12.5 %collective-permute-start.8 = (bf16[1024,128]{1,0:T(8,128)(2,1)S(1)}, bf16[1024,128]{1,0:T(8,128)(2,1)S(1)}, u32[]{:S(2)}, u32[]{:S(2)}) collective-permute-start(bf16[1024,128]{1,0:T(8,128)(2,1)S(1)} %collective-permute-done.6.wk), channel_id=1, source_target_pairs={{0,448},{1,65},{2,450},{3,67},{4,452},{5,69},{6,454},{7,71},{8,456... | collective-permute-start | bytes 786440 | tf_op jit(solution)/shard_map/ppermute | solution.py:34
  53.1 10.5 %collective-permute-start.9 = (bf16[1024,128]{1,0:T(8,128)(2,1)S(1)}, bf16[1024,128]{1,0:T(8,128)(2,1)S(1)}, u32[]{:S(2)}, u32[]{:S(2)}) collective-permute-start(bf16[1024,128]{1,0:T(8,128)(2,1)S(1)} %collective-permute-done.7.wv), channel_id=1, source_target_pairs={{0,448},{1,65},{2,450},{3,67},{4,452},{5,69},{6,454},{7,71},{8,456... | collective-permute-start | bytes 786440 | tf_op jit(solution)/shard_map/ppermute | solution.py:34
  55.1 40.9 %collective-permute-start.12 = (bf16[2048,128]{1,0:T(8,128)(2,1)}, bf16[2048,128]{1,0:T(8,128)(2,1)S(1)}, u32[]{:S(2)}, u32[]{:S(2)}) collective-permute-start(bf16[2048,128]{1,0:T(8,128)(2,1)} %collective-permute-done.10.refs_3_.o1), channel_id=1, source_target_pairs={{0,384},{1,129},{2,386},{3,131},{4,388},{5,133},{6,390},{7,135},{8... | collective-permute-start | bytes 1572872 | tf_op jit(solution)/shard_map/ppermute | solution.py:34
  58.5 37.5 %collective-permute-start.11 = (bf16[2048,128]{1,0:T(8,128)(2,1)}, bf16[2048,128]{1,0:T(8,128)(2,1)}, u32[]{:S(2)}, u32[]{:S(2)}) collective-permute-start(bf16[2048,128]{1,0:T(8,128)(2,1)} %collective-permute-done.10.refs_3_.o1), channel_id=1, source_target_pairs={{0,448},{1,65},{2,450},{3,67},{4,452},{5,69},{6,454},{7,71},{8,456... | collective-permute-start | bytes 1572872 | tf_op jit(solution)/shard_map/ppermute | solution.py:34
  68.6 20.6 %all-to-all-start = ((bf16[32,16,128]{2,1,0:T(8,128)(2,1)}), bf16[32,16,128]{2,1,0:T(8,128)(2,1)S(1)}, u32[]{:S(2)}, u32[]{:S(2)}) async-start(bf16[32,16,128]{2,1,0:T(8,128)(2,1)} %bitcast.3), calls=%async_computation | async-start | bytes 262144 | tf_op jit(solution)/shard_map/all_to_all | solution.py:305
  89.9 15.2 %all-to-all-start.1 = ((bf16[32,16,128]{2,1,0:T(8,128)(2,1)}), bf16[32,16,128]{2,1,0:T(8,128)(2,1)S(1)}, u32[]{:S(2)}, u32[]{:S(2)}) async-start(bf16[32,16,128]{2,1,0:T(8,128)(2,1)} %shard_map.70), calls=%async_computation.1 | async-start | bytes 262144 | tf_op jit(solution)/shard_map/all_to_all | solution.py:308
  109.8 13.7 %collective-permute-start.13 = (bf16[512,1024]{1,0:T(8,128)(2,1)}, bf16[512,1024]{1,0:T(8,128)(2,1)S(1)}, u32[]{:S(2)}, u32[]{:S(2)}) collective-permute-start(bf16[512,1024]{1,0:T(8,128)(2,1)} %shard_map.72), channel_id=1, source_target_pairs={{0,1},{1,0},{2,3},{3,2},{4,5},{5,4},{6,7},{7,6},{8,9},{9,8},{10,11... | collective-permute-start | bytes 3145736 | tf_op jit(solution)/shard_map/ppermute | solution.py:338
  (9 other events, 35.9 us)

commit v9 on v8

--- a/solution.py
+++ b/solution.py
@@ -275,8 +275,9 @@
     key_3, value_3, s1 = barrier((key_3, value_3, s1))
     kv2, s2 = one(own, other, key_3, value_3)
     key_4, value_4 = hop(key_3), hop(value_3)
-    key_4, value_4, s2 = barrier((key_4, value_4, s2))
+    pack_2, key_4, value_4, s2 = barrier((pack_2, key_4, value_4, s2))
     kv3, s3, total = last(own, other, w_key, w_value, key_4, value_4, s0, s1, s2)
+    pack_2, total = barrier((pack_2, total))
     pack_3, pack_4 = hop(pack_2), hop(pack_2, 2)
 
     half = (2, 2, TOK, DH)

time: 127 us -> 120 us (0.945)
  waiting for transfers between devices: 26.9 us -> 22.8 us
  starting transfers between devices: 61.2 us -> 58.2 us
    ppermute x12, waiting for transfers between devices: 21.1 us -> 17.2 us  [hop(): return lax.ppermute(weight, ('dp', 'z', 'x', 'core'), pairs)]
    ppermute x12, starting transfers between devices: 25.5 us -> 23.7 us  [hop(): return lax.ppermute(weight, ('dp', 'z', 'x', 'core'), pairs)]
    ppermute x1, starting transfers between devices: 9.55 us -> 8.04 us  [body(): got = lax.ppermute(partial[0], 'core', SWAP)]
    unnamed x34 -> x38, local copies, waits for them, and re-layouts: 2.94 us -> 3.15 us
  transfers between devices with their start and end apart: 16 -> 16, of which waited for: 8 -> 9; matrix products, arithmetic and copies ran while one was open for 1% -> 1% of each run, Pallas kernels for 21% -> 20%
where the time goes in v9:
time: 120 us; the launch traced here: 119 us
  starting transfers between devices  58.2 us (48%)
  Pallas kernels  31 us (26%)
  waiting for transfers between devices  22.8 us (19%)
  other arithmetic  3.58 us (3%)
  local copies, waits for them, and re-layouts  3.2 us (3%)
    ppermute x12, starting transfers between devices, hop(): return lax.ppermute(weight, ('dp', 'z', 'x', 'core'), pairs)  23.7 us
    ppermute x12, waiting for transfers between devices, hop(): return lax.ppermute(weight, ('dp', 'z', 'x', 'core'), pairs)  17.2 us
    pallas_call x2, Pallas kernels, attend(): call(functools.partial(within_kernel, final), len(arrays), (shape(half, B...  11.9 us
    all_to_all x1, starting transfers between devices, body(): chunks = lax.all_to_all(chunks, ('z', 'x'), 0, 0, tiled=True)  11.5 us
    ppermute x1, starting transfers between devices, body(): other = lax.ppermute(own, 'core', SWAP)  8.91 us
    pallas_call x2, Pallas kernels, body(): call(functools.partial(out_kernel, block), 15, shape((TOK, D), kind), [pl...  8.11 us
    ppermute x1, starting transfers between devices, body(): got = lax.ppermute(partial[0], 'core', SWAP)  8.04 us
    all_to_all x1, starting transfers between devices, body(): lax.all_to_all(priors, ('z', 'x'), 0, 0, tiled=True).reshape(SLOTS, DH, DH)  6.02 us
  transfers between devices with their start and end apart: 16, of which 9 were waited for; matrix products, arithmetic and copies ran while one was open for 1% of the time, Pallas kernels for 20%

profile of v9, /device:TPU:1, one launch (start us, length us, event | category | flops | bytes accessed | tf_op | source)
XLA Modules:
  0.0 119.2 jit_solution(3741732178558588346)
XLA Ops:
  0.0 8.9 %collective-permute-start.5 = (bf16[512,1024]{1,0:T(8,128)(2,1)}, bf16[512,1024]{1,0:T(8,128)(2,1)S(1)}, u32[]{:S(2)}, u32[]{:S(2)}) collective-permute-start(bf16[512,1024]{1,0:T(8,128)(2,1)} %bitcast.14), channel_id=1, source_target_pairs={{0,1},{1,0},{2,3},{3,2},{4,5},{5,4},{6,7},{7,6},{8,9},{9,8},{10,11... | collective-permute-start | bytes 3145736 | tf_op jit(solution)/shard_map/ppermute | solution.py:242
  8.9 1.9 %collective-permute-start.1 = (bf16[1024,128]{1,0:T(8,128)(2,1)}, bf16[1024,128]{1,0:T(8,128)(2,1)S(1)}, u32[]{:S(2)}, u32[]{:S(2)}) collective-permute-start(bf16[1024,128]{1,0:T(8,128)(2,1)} %wk.1), channel_id=1, source_target_pairs={{0,448},{1,65},{2,450},{3,67},{4,452},{5,69},{6,454},{7,71},{8,456... | collective-permute-start | bytes 786440 | tf_op jit(solution)/shard_map/ppermute | solution.py:34
  10.9 1.9 %collective-permute-start.3 = (bf16[1024,128]{1,0:T(8,128)(2,1)}, bf16[1024,128]{1,0:T(8,128)(2,1)S(1)}, u32[]{:S(2)}, u32[]{:S(2)}) collective-permute-start(bf16[1024,128]{1,0:T(8,128)(2,1)} %wv.1), channel_id=1, source_target_pairs={{0,448},{1,65},{2,450},{3,67},{4,452},{5,69},{6,454},{7,71},{8,456... | collective-permute-start | bytes 786440 | tf_op jit(solution)/shard_map/ppermute | solution.py:34
  12.8 4.6 %collective-permute-done.1.wk = bf16[1024,128]{1,0:T(8,128)(2,1)S(1)} collective-permute-done((bf16[1024,128]{1,0:T(8,128)(2,1)}, bf16[1024,128]{1,0:T(8,128)(2,1)S(1)}, u32[]{:S(2)}, u32[]{:S(2)}) %collective-permute-start.1) | collective-permute-done | bytes 262176 | tf_op jit(solution)/shard_map/ppermute | solution.py:34
  25.1 2.3 %shard_map.64 = (bf16[2,512,256]{2,1,0:T(8,128)(2,1)S(1)}, f32[2,128,128]{2,1,0:T(8,128)S(1)}) custom-call(bf16[512,1024]{1,0:T(8,128)(2,1)S(1)} %bitcast.17, bf16[512,1024]{1,0:T(8,128)(2,1)S(1)} %collective-permute-done.5.other.refs_1_, bf16[1024,128]{1,0:T(8,128)(2,1)S(1)} %collective-permute-done.1.wk, bf16[1024,128]{1,0:T(8,128)(2,1)S(1)} %collective-permute-done.3.wv), custom_call_target="tpu_custom_call" | custom-call | flops 536870912 | bytes 3145728 | tf_op jit(solution)/shard_map/pallas_call | solution.py:267
  34.3 2.8 %collective-permute-done.6.wk = bf16[1024,128]{1,0:T(8,128)(2,1)S(1)} collective-permute-done((bf16[1024,128]{1,0:T(8,128)(2,1)S(1)}, bf16[1024,128]{1,0:T(8,128)(2,1)S(1)}, u32[]{:S(2)}, u32[]{:S(2)}) %collective-permute-start.6) | collective-permute-done | bytes 262176 | tf_op jit(solution)/shard_map/ppermute | solution.py:34
  39.0 2.3 %shard_map.65 = (bf16[2,512,256]{2,1,0:T(8,128)(2,1)S(1)}, f32[2,128,128]{2,1,0:T(8,128)S(1)}) custom-call(bf16[512,1024]{1,0:T(8,128)(2,1)S(1)} %bitcast.18, bf16[512,1024]{1,0:T(8,128)(2,1)S(1)} %collective-permute-done.5.other.refs_1_, bf16[1024,128]{1,0:T(8,128)(2,1)S(1)} %collective-permute-done.2.wk, bf16[1024,128]{1,0:T(8,128)(2,1)S(1)} %collective-permute-done.4.wv), custom_call_target="tpu_custom_call" | custom-call | flops 536870912 | bytes 3145728 | tf_op jit(solution)/shard_map/pallas_call | solution.py:271
  41.4 2.1 %collective-permute-start.9 = (bf16[1024,128]{1,0:T(8,128)(2,1)S(1)}, bf16[1024,128]{1,0:T(8,128)(2,1)S(1)}, u32[]{:S(2)}, u32[]{:S(2)}) collective-permute-start(bf16[1024,128]{1,0:T(8,128)(2,1)S(1)} %collective-permute-done.6.wk), channel_id=1, source_target_pairs={{0,448},{1,65},{2,450},{3,67},{4,452},{5,69},{6,454},{7,71},{8,456... | collective-permute-start | bytes 786440 | tf_op jit(solution)/shard_map/ppermute | solution.py:34
  43.5 2.3 %collective-permute-start.10 = (bf16[1024,128]{1,0:T(8,128)(2,1)S(1)}, bf16[1024,128]{1,0:T(8,128)(2,1)S(1)}, u32[]{:S(2)}, u32[]{:S(2)}) collective-permute-start(bf16[1024,128]{1,0:T(8,128)(2,1)S(1)} %collective-permute-done.8.wv), channel_id=1, source_target_pairs={{0,448},{1,65},{2,450},{3,67},{4,452},{5,69},{6,454},{7,71},{8,456... | collective-permute-start | bytes 786440 | tf_op jit(solution)/shard_map/ppermute | solution.py:34
  45.7 2.3 %shard_map.66 = (bf16[2,512,256]{2,1,0:T(8,128)(2,1)S(1)}, f32[2,128,128]{2,1,0:T(8,128)S(1)}) custom-call(bf16[512,1024]{1,0:T(8,128)(2,1)S(1)} %bitcast.19, bf16[512,1024]{1,0:T(8,128)(2,1)S(1)} %collective-permute-done.5.other.refs_1_, bf16[1024,128]{1,0:T(8,128)(2,1)S(1)} %collective-permute-done.6.wk, bf16[1024,128]{1,0:T(8,128)(2,1)S(1)} %collective-permute-done.8.wv), custom_call_target="tpu_custom_call" | custom-call | flops 536870912 | bytes 3145728 | tf_op jit(solution)/shard_map/pallas_call | solution.py:276
  48.0 3.0 %collective-permute-done.9.wk_far = bf16[1024,128]{1,0:T(8,128)(2,1)S(1)} collective-permute-done((bf16[1024,128]{1,0:T(8,128)(2,1)S(1)}, bf16[1024,128]{1,0:T(8,128)(2,1)S(1)}, u32[]{:S(2)}, u32[]{:S(2)}) %collective-permute-start.9) | collective-permute-done | bytes 262176 | tf_op jit(solution)/shard_map/ppermute | solution.py:34
  51.1 2.8 %collective-permute-done.10.wv_far = bf16[1024,128]{1,0:T(8,128)(2,1)S(1)} collective-permute-done((bf16[1024,128]{1,0:T(8,128)(2,1)S(1)}, bf16[1024,128]{1,0:T(8,128)(2,1)S(1)}, u32[]{:S(2)}, u32[]{:S(2)}) %collective-permute-start.10) | collective-permute-done | bytes 262176 | tf_op jit(solution)/shard_map/ppermute | solution.py:34
  53.9 3.5 %shard_map.67 = (bf16[2,512,256]{2,1,0:T(8,128)(2,1)S(1)}, f32[2,128,128]{2,1,0:T(8,128)S(1)}, bf16[4,128,128]{2,1,0:T(8,128)(2,1)}) custom-call(bf16[512,1024]{1,0:T(8,128)(2,1)S(1)} %bitcast.20, bf16[512,1024]{1,0:T(8,128)(2,1)S(1)} %collective-permute-done.5.other.refs_1_, bf16[1024,128]{1,0:T(8,128)(2,1)S(1)} %copy-done.11, ...), custom_call_target="tpu_custom_call" | custom-call | flops 536870912 | bytes 3145728 | tf_op jit(solution)/shard_map/pallas_call | solution.py:279
  60.8 2.2 %collective-permute-start.11 = (bf16[2048,128]{1,0:T(8,128)(2,1)S(1)}, bf16[2048,128]{1,0:T(8,128)(2,1)S(1)}, u32[]{:S(2)}, u32[]{:S(2)}) collective-permute-start(bf16[2048,128]{1,0:T(8,128)(2,1)S(1)} %collective-permute-done.7.refs_3_.o1), channel_id=1, source_target_pairs={{0,448},{1,65},{2,450},{3,67},{4,452},{5,69},{6,454},{7,71},{8,456... | collective-permute-start | bytes 1572872 | tf_op jit(solution)/shard_map/ppermute | solution.py:34
  63.0 11.5 %all-to-all-start = ((bf16[32,16,128]{2,1,0:T(8,128)(2,1)}), bf16[32,16,128]{2,1,0:T(8,128)(2,1)S(1)}, u32[]{:S(2)}, u32[]{:S(2)}) async-start(bf16[32,16,128]{2,1,0:T(8,128)(2,1)} %bitcast.3), calls=%async_computation | async-start | bytes 262144 | tf_op jit(solution)/shard_map/all_to_all | solution.py:306
  74.5 5.9 %shard_map.68 = (bf16[2,2,512,128]{3,2,1,0:T(8,128)(2,1)}, f32[2,2,512,128]{3,2,1,0:T(8,128)}) custom-call(bf16[512,1024]{1,0:T(8,128)(2,1)} %bitcast.15, bf16[512,1024]{1,0:T(8,128)(2,1)} %copy-done.2, bf16[2048,128]{1,0:T(8,128)(2,1)} %copy-done.16, bf16[2048,128]{1,0:T(8,128)(2,1)} %copy-done.17, bf16[2,512,256]{2,1,0:T(8,128)(2,1)} %copy-done.9, ...), custom_call_target="tpu_custom_call" | custom-call | flops 805306368 | bytes 5242880 | tf_op jit(solution)/shard_map/pallas_call | solution.py:286
  80.5 3.4 %all-to-all-done.chunk_ref = bf16[32,16,128]{2,1,0:T(8,128)(2,1)S(1)} async-done(((bf16[32,16,128]{2,1,0:T(8,128)(2,1)}), bf16[32,16,128]{2,1,0:T(8,128)(2,1)S(1)}, u32[]{:S(2)}, u32[]{:S(2)}) %all-to-all-start) | async-done | bytes 131104 | tf_op jit(solution)/shard_map/all_to_all | solution.py:306
  84.6 6.0 %all-to-all-start.1 = ((bf16[32,16,128]{2,1,0:T(8,128)(2,1)}), bf16[32,16,128]{2,1,0:T(8,128)(2,1)S(1)}, u32[]{:S(2)}, u32[]{:S(2)}) async-start(bf16[32,16,128]{2,1,0:T(8,128)(2,1)} %shard_map.70), calls=%async_computation.1 | async-start | bytes 262144 | tf_op jit(solution)/shard_map/all_to_all | solution.py:309
  91.6 5.9 %shard_map.69 = (bf16[2,2,512,128]{3,2,1,0:T(8,128)(2,1)}, f32[2,2,512,128]{3,2,1,0:T(8,128)}) custom-call(bf16[512,1024]{1,0:T(8,128)(2,1)} %bitcast.16, bf16[512,1024]{1,0:T(8,128)(2,1)} %copy-done.2, bf16[2048,128]{1,0:T(8,128)(2,1)} %copy-done.15, bf16[2048,128]{1,0:T(8,128)(2,1)} %copy-done.13, bf16[2048,128]{1,0:T(8,128)(2,1)} %copy-done.14, ...), custom_call_target="tpu_custom_call" | custom-call | flops 805306368 | bytes 5242880 | tf_op jit(solution)/shard_map/pallas_call | solution.py:286
  97.6 2.2 %all-to-all-done.1 = bf16[32,16,128]{2,1,0:T(8,128)(2,1)S(1)} async-done(((bf16[32,16,128]{2,1,0:T(8,128)(2,1)}), bf16[32,16,128]{2,1,0:T(8,128)(2,1)S(1)}, u32[]{:S(2)}, u32[]{:S(2)}) %all-to-all-start.1) | async-done | bytes 131104 | tf_op jit(solution)/shard_map/all_to_all | solution.py:309
  100.5 4.0 %shard_map.72 = bf16[512,1024]{1,0:T(8,128)(2,1)} custom-call(bf16[2,2,512,128]{3,2,1,0:T(8,128)(2,1)} %get-tuple-element.55.query_a, bf16[2,2,512,128]{3,2,1,0:T(8,128)(2,1)} %get-tuple-element.58.query_b, f32[2,2,512,128]{3,2,1,0:T(8,128)} %get-tuple-element.59.within_a, f32[2,2,512,128]{3,2,1,0:T(8,128)} %get-tuple-element.60.within_b, ...), custom_call_target="tpu_custom_call" | custom-call | flops 1342177280 | bytes 5242880 | tf_op jit(solution)/shard_map/pallas_call | solution.py:317
  104.5 8.0 %collective-permute-start.13 = (bf16[512,1024]{1,0:T(8,128)(2,1)}, bf16[512,1024]{1,0:T(8,128)(2,1)S(1)}, u32[]{:S(2)}, u32[]{:S(2)}) collective-permute-start(bf16[512,1024]{1,0:T(8,128)(2,1)} %shard_map.72), channel_id=1, source_target_pairs={{0,1},{1,0},{2,3},{3,2},{4,5},{5,4},{6,7},{7,6},{8,9},{9,8},{10,11... | collective-permute-start | bytes 3145736 | tf_op jit(solution)/shard_map/ppermute | solution.py:339
  112.6 4.1 %shard_map.71 = bf16[512,1024]{1,0:T(8,128)(2,1)} custom-call(bf16[2,2,512,128]{3,2,1,0:T(8,128)(2,1)} %get-tuple-element.55.query_a, bf16[2,2,512,128]{3,2,1,0:T(8,128)(2,1)} %get-tuple-element.58.query_b, f32[2,2,512,128]{3,2,1,0:T(8,128)} %get-tuple-element.59.within_a, f32[2,2,512,128]{3,2,1,0:T(8,128)} %get-tuple-element.60.within_b, ...), custom_call_target="tpu_custom_call" | custom-call | flops 1342177280 | bytes 5242880 | tf_op jit(solution)/shard_map/pallas_call | solution.py:317
  116.6 2.6 %fusion = bf16[1,512,1024]{2,1,0:T(8,128)(2,1)} fusion(bf16[512,1024]{1,0:T(8,128)(2,1)S(1)} %collective-permute-done.13, bf16[512,1024]{1,0:T(8,128)(2,1)} %shard_map.71), kind=kLoop, calls=%fused_computation.1 | loop fusion | flops 2097152 | bytes 3145728 | tf_op jit(solution)/shard_map/broadcast_in_dim | solution.py:340
  (58 shorter events, 22.2 us)
Async XLA Ops:
  0.0 12.8 %copy-start = (bf16[128,1024]{1,0:T(8,128)(2,1)S(1)}, bf16[128,1024]{1,0:T(8,128)(2,1)}, u32[]{:S(2)}) copy-start(bf16[128,1024]{1,0:T(8,128)(2,1)} %param.10) | copy-start | bytes 786436
  0.0 25.1 %copy-start.1 = (bf16[1,512,1024]{2,1,0:T(8,128)(2,1)S(1)}, bf16[1,512,1024]{2,1,0:T(8,128)(2,1)}, u32[]{:S(2)}) copy-start(bf16[1,512,1024]{2,1,0:T(8,128)(2,1)} %param.6) | copy-start | bytes 3145732
  0.0 25.1 %collective-permute-start.5 = (bf16[512,1024]{1,0:T(8,128)(2,1)}, bf16[512,1024]{1,0:T(8,128)(2,1)S(1)}, u32[]{:S(2)}, u32[]{:S(2)}) collective-permute-start(bf16[512,1024]{1,0:T(8,128)(2,1)} %bitcast.14), channel_id=1, source_target_pairs={{0,1},{1,0},{2,3},{3,2},{4,5},{5,4},{6,7},{7,6},{8,9},{9,8},{10,11... | collective-permute-start | bytes 3145736 | tf_op jit(solution)/shard_map/ppermute | solution.py:242
  8.9 8.5 %collective-permute-start.1 = (bf16[1024,128]{1,0:T(8,128)(2,1)}, bf16[1024,128]{1,0:T(8,128)(2,1)S(1)}, u32[]{:S(2)}, u32[]{:S(2)}) collective-permute-start(bf16[1024,128]{1,0:T(8,128)(2,1)} %wk.1), channel_id=1, source_target_pairs={{0,448},{1,65},{2,450},{3,67},{4,452},{5,69},{6,454},{7,71},{8,456... | collective-permute-start | bytes 786440 | tf_op jit(solution)/shard_map/ppermute | solution.py:34
  10.9 9.4 %collective-permute-start.3 = (bf16[1024,128]{1,0:T(8,128)(2,1)}, bf16[1024,128]{1,0:T(8,128)(2,1)S(1)}, u32[]{:S(2)}, u32[]{:S(2)}) collective-permute-start(bf16[1024,128]{1,0:T(8,128)(2,1)} %wv.1), channel_id=1, source_target_pairs={{0,448},{1,65},{2,450},{3,67},{4,452},{5,69},{6,454},{7,71},{8,456... | collective-permute-start | bytes 786440 | tf_op jit(solution)/shard_map/ppermute | solution.py:34
  17.5 10.0 %collective-permute-start.2 = (bf16[1024,128]{1,0:T(8,128)(2,1)S(1)}, bf16[1024,128]{1,0:T(8,128)(2,1)S(1)}, u32[]{:S(2)}, u32[]{:S(2)}) collective-permute-start(bf16[1024,128]{1,0:T(8,128)(2,1)S(1)} %collective-permute-done.1.wk), channel_id=1, source_target_pairs={{0,448},{1,65},{2,450},{3,67},{4,452},{5,69},{6,454},{7,71},{8,456... | collective-permute-start | bytes 786440 | tf_op jit(solution)/shard_map/ppermute | solution.py:34
  20.3 8.3 %collective-permute-start.4 = (bf16[1024,128]{1,0:T(8,128)(2,1)S(1)}, bf16[1024,128]{1,0:T(8,128)(2,1)S(1)}, u32[]{:S(2)}, u32[]{:S(2)}) collective-permute-start(bf16[1024,128]{1,0:T(8,128)(2,1)S(1)} %collective-permute-done.3.wv), channel_id=1, source_target_pairs={{0,448},{1,65},{2,450},{3,67},{4,452},{5,69},{6,454},{7,71},{8,456... | collective-permute-start | bytes 786440 | tf_op jit(solution)/shard_map/ppermute | solution.py:34
  23.2 11.1 %collective-permute-start = (bf16[2048,128]{1,0:T(8,128)(2,1)S(1)}, bf16[2048,128]{1,0:T(8,128)(2,1)S(1)}, u32[]{:S(2)}, u32[]{:S(2)}) collective-permute-start(bf16[2048,128]{1,0:T(8,128)(2,1)S(1)} %pad_maximum_fusion.refs_3_.o_own), channel_id=1, source_target_pairs={{0,448},{1,65},{2,450},{3,67},{4,452},{5,69},{6,454},{7,71},{8,456... | collective-permute-start | bytes 1572872 | tf_op jit(solution)/shard_map/ppermute | solution.py:34
  25.1 28.7 %copy-start.2 = (bf16[512,1024]{1,0:T(8,128)(2,1)}, bf16[512,1024]{1,0:T(8,128)(2,1)S(1)}, u32[]{:S(2)}) copy-start(bf16[512,1024]{1,0:T(8,128)(2,1)S(1)} %collective-permute-done.5.other.refs_1_) | copy-start | bytes 3145732
  27.4 13.9 %copy-start.9 = (bf16[2,512,256]{2,1,0:T(8,128)(2,1)}, bf16[2,512,256]{2,1,0:T(8,128)(2,1)S(1)}, u32[]{:S(2)}) copy-start(bf16[2,512,256]{2,1,0:T(8,128)(2,1)S(1)} %get-tuple-element.52.refs_4_) | copy-start | bytes 1572868
  27.4 26.5 %copy-start.3 = (f32[2,128,128]{2,1,0:T(8,128)}, f32[2,128,128]{2,1,0:T(8,128)S(1)}, u32[]{:S(2)}) copy-start(f32[2,128,128]{2,1,0:T(8,128)S(1)} %get-tuple-element.46.s0) | copy-start | bytes 393220
  28.6 8.5 %collective-permute-start.6 = (bf16[1024,128]{1,0:T(8,128)(2,1)S(1)}, bf16[1024,128]{1,0:T(8,128)(2,1)S(1)}, u32[]{:S(2)}, u32[]{:S(2)}) collective-permute-start(bf16[1024,128]{1,0:T(8,128)(2,1)S(1)} %collective-permute-done.2.wk), channel_id=1, source_target_pairs={{0,448},{1,65},{2,450},{3,67},{4,452},{5,69},{6,454},{7,71},{8,456... | collective-permute-start | bytes 786440 | tf_op jit(solution)/shard_map/ppermute | solution.py:34
  30.5 10.9 %collective-permute-start.8 = (bf16[1024,128]{1,0:T(8,128)(2,1)S(1)}, bf16[1024,128]{1,0:T(8,128)(2,1)S(1)}, u32[]{:S(2)}, u32[]{:S(2)}) collective-permute-start(bf16[1024,128]{1,0:T(8,128)(2,1)S(1)} %collective-permute-done.4.wv), channel_id=1, source_target_pairs={{0,448},{1,65},{2,450},{3,67},{4,452},{5,69},{6,454},{7,71},{8,456... | collective-permute-start | bytes 786440 | tf_op jit(solution)/shard_map/ppermute | solution.py:34
  37.1 16.7 %collective-permute-start.7 = (bf16[2048,128]{1,0:T(8,128)(2,1)S(1)}, bf16[2048,128]{1,0:T(8,128)(2,1)S(1)}, u32[]{:S(2)}, u32[]{:S(2)}) collective-permute-start(bf16[2048,128]{1,0:T(8,128)(2,1)S(1)} %collective-permute-done.refs_2_.o0), channel_id=1, source_target_pairs={{0,448},{1,65},{2,450},{3,67},{4,452},{5,69},{6,454},{7,71},{8,456... | collective-permute-start | bytes 1572872 | tf_op jit(solution)/shard_map/ppermute | solution.py:34
  41.3 12.5 %copy-start.4 = (f32[2,128,128]{2,1,0:T(8,128)}, f32[2,128,128]{2,1,0:T(8,128)S(1)}, u32[]{:S(2)}) copy-start(f32[2,128,128]{2,1,0:T(8,128)S(1)} %get-tuple-element.47.s1) | copy-start | bytes 393220
  41.4 12.5 %copy-start.11 = (bf16[1024,128]{1,0:T(8,128)(2,1)S(1)}, bf16[1024,128]{1,0:T(8,128)(2,1)}, u32[]{:S(2)}) copy-start(bf16[1024,128]{1,0:T(8,128)(2,1)} %wk.1) | copy-start | bytes 786436
  41.4 12.5 %copy-start.12 = (bf16[1024,128]{1,0:T(8,128)(2,1)S(1)}, bf16[1024,128]{1,0:T(8,128)(2,1)}, u32[]{:S(2)}) copy-start(bf16[1024,128]{1,0:T(8,128)(2,1)} %wv.1) | copy-start | bytes 786436
  41.4 9.7 %collective-permute-start.9 = (bf16[1024,128]{1,0:T(8,128)(2,1)S(1)}, bf16[1024,128]{1,0:T(8,128)(2,1)S(1)}, u32[]{:S(2)}, u32[]{:S(2)}) collective-permute-start(bf16[1024,128]{1,0:T(8,128)(2,1)S(1)} %collective-permute-done.6.wk), channel_id=1, source_target_pairs={{0,448},{1,65},{2,450},{3,67},{4,452},{5,69},{6,454},{7,71},{8,456... | collective-permute-start | bytes 786440 | tf_op jit(solution)/shard_map/ppermute | solution.py:34
  43.5 10.4 %collective-permute-start.10 = (bf16[1024,128]{1,0:T(8,128)(2,1)S(1)}, bf16[1024,128]{1,0:T(8,128)(2,1)S(1)}, u32[]{:S(2)}, u32[]{:S(2)}) collective-permute-start(bf16[1024,128]{1,0:T(8,128)(2,1)S(1)} %collective-permute-done.8.wv), channel_id=1, source_target_pairs={{0,448},{1,65},{2,450},{3,67},{4,452},{5,69},{6,454},{7,71},{8,456... | collective-permute-start | bytes 786440 | tf_op jit(solution)/shard_map/ppermute | solution.py:34
  58.9 31.7 %collective-permute-start.12 = (bf16[2048,128]{1,0:T(8,128)(2,1)S(1)}, bf16[2048,128]{1,0:T(8,128)(2,1)S(1)}, u32[]{:S(2)}, u32[]{:S(2)}) collective-permute-start(bf16[2048,128]{1,0:T(8,128)(2,1)S(1)} %collective-permute-done.7.refs_3_.o1), channel_id=1, source_target_pairs={{0,384},{1,129},{2,386},{3,131},{4,388},{5,133},{6,390},{7,135},{8... | collective-permute-start | bytes 1572872 | tf_op jit(solution)/shard_map/ppermute | solution.py:34
  60.8 29.8 %collective-permute-start.11 = (bf16[2048,128]{1,0:T(8,128)(2,1)S(1)}, bf16[2048,128]{1,0:T(8,128)(2,1)S(1)}, u32[]{:S(2)}, u32[]{:S(2)}) collective-permute-start(bf16[2048,128]{1,0:T(8,128)(2,1)S(1)} %collective-permute-done.7.refs_3_.o1), channel_id=1, source_target_pairs={{0,448},{1,65},{2,450},{3,67},{4,452},{5,69},{6,454},{7,71},{8,456... | collective-permute-start | bytes 1572872 | tf_op jit(solution)/shard_map/ppermute | solution.py:34
  63.0 20.8 %all-to-all-start = ((bf16[32,16,128]{2,1,0:T(8,128)(2,1)}), bf16[32,16,128]{2,1,0:T(8,128)(2,1)S(1)}, u32[]{:S(2)}, u32[]{:S(2)}) async-start(bf16[32,16,128]{2,1,0:T(8,128)(2,1)} %bitcast.3), calls=%async_computation | async-start | bytes 262144 | tf_op jit(solution)/shard_map/all_to_all | solution.py:306
  84.6 15.2 %all-to-all-start.1 = ((bf16[32,16,128]{2,1,0:T(8,128)(2,1)}), bf16[32,16,128]{2,1,0:T(8,128)(2,1)S(1)}, u32[]{:S(2)}, u32[]{:S(2)}) async-start(bf16[32,16,128]{2,1,0:T(8,128)(2,1)} %shard_map.70), calls=%async_computation.1 | async-start | bytes 262144 | tf_op jit(solution)/shard_map/all_to_all | solution.py:309
  104.5 12.1 %collective-permute-start.13 = (bf16[512,1024]{1,0:T(8,128)(2,1)}, bf16[512,1024]{1,0:T(8,128)(2,1)S(1)}, u32[]{:S(2)}, u32[]{:S(2)}) collective-permute-start(bf16[512,1024]{1,0:T(8,128)(2,1)} %shard_map.72), channel_id=1, source_target_pairs={{0,1},{1,0},{2,3},{3,2},{4,5},{5,4},{6,7},{7,6},{8,9},{9,8},{10,11... | collective-permute-start | bytes 3145736 | tf_op jit(solution)/shard_map/ppermute | solution.py:339
  (11 other events, 47.6 us)

commit v10 on v9

--- a/solution.py
+++ b/solution.py
@@ -74,53 +74,23 @@
     return lax.rem(y + DP + (slot + 1) * (1 - 2 * core), DP)
 
 
-def project(own, other, loads, kv, state, tokens, weight, kv_out, state_out, sems):
-    copies = [begin(ref, tokens.at[block], sems.at[2 + block]) for block, ref in enumerate((own, other))]
-    for load in loads:
-        load.wait()
-    for block in range(2):
-        copies[block].wait()
-        both = mm(tokens[block], weight[...]).astype(BF16)
-        kv_out[block] = both
-        state_out[block] = t_mm(both[:, :DH], both[:, DH:])
-    return [begin(kv_out, kv, sems.at[4]), begin(state_out, state, sems.at[5])]
-
-
-def key_value_kernel(own, other, wk, wv, kv, state, tokens, weight, kv_out, state_out, sems):
-    loads = [
-        begin(wk, weight.at[:, pl.ds(0, DH)], sems.at[0]),
-        begin(wv, weight.at[:, pl.ds(DH, DH)], sems.at[1]),
-    ]
-    for copy in project(own, other, loads, kv, state, tokens, weight, kv_out, state_out, sems):
-        copy.wait()
-
-
-def last_key_value_kernel(
-    own, other, wk, wv, wk_far, wv_far, s0, s1, s2, kv, state, total, tokens, weight, kv_out, state_out, sums, total_out, sems
-):
-    core = lax.axis_index("core")
-    left, right = weight.at[:, pl.ds(0, DH)], weight.at[:, pl.ds(DH, DH)]
-
-    @pl.when(core == 0)
-    def _():
-        begin(wk, left, sems.at[0])
-        begin(wv, right, sems.at[1])
-
-    @pl.when(core != 0)
-    def _():
-        begin(wk_far, left, sems.at[0])
-        begin(wv_far, right, sems.at[1])
-
-    loads = [pltpu.make_async_copy(wk, left, sems.at[0]), pltpu.make_async_copy(wv, right, sems.at[1])]
-    early = [begin(ref, sums.at[slot], sems.at[6 + slot]) for slot, ref in enumerate((s0, s1, s2))]
-    copies = project(own, other, loads, kv, state, tokens, weight, kv_out, state_out, sems)
-    for slot in range(3):
-        early[slot].wait()
-        total_out[slot] = (sums[slot, 0] + sums[slot, 1]).astype(BF16)
-    total_out[3] = (state_out[0] + state_out[1]).astype(BF16)
-    copies.append(begin(total_out, total, sems.at[9]))
-    for copy in copies:
-        copy.wait()
+def project(tokens, weight, kv, state):
+    for block, ref in enumerate(tokens):
+        both = mm(ref[...], weight).astype(BF16)
+        kv[block] = both
+        state[block] = t_mm(both[:, :DH], both[:, DH:])
+
+
+def key_value_kernel(own, other, wk, wv, kv, state):
+    project((own, other), jnp.concatenate([wk[...], wv[...]], axis=1), kv, state)
+
+
+def last_key_value_kernel(own, other, wk, wv, wk_far, wv_far, s0, s1, s2, kv, state, total):
+    first = lax.axis_index("core") == 0
+    weight = [jnp.where(first, wk[...], wk_far[...]), jnp.where(first, wv[...], wv_far[...])]
+    project((own, other), jnp.concatenate(weight, axis=1), kv, state)
+    for slot, ref in enumerate((s0, s1, s2, state)):
+        total[slot] = (ref[0] + ref[1]).astype(BF16)
 
 
 def within_kernel(final, *refs):
@@ -244,23 +214,10 @@
     pair = shape((2, TOK, 2 * DH), BF16)
     state = shape((2, DH, DH), F32)
     flops = 2 * 2 * TOK * D * 2 * DH
-    room = [
-        pltpu.VMEM((2, TOK, D), BF16),
-        pltpu.VMEM((D, 2 * DH), BF16),
-        pltpu.VMEM((2, TOK, 2 * DH), BF16),
-        pltpu.VMEM((2, DH, DH), F32),
-    ]
-    one = call(key_value_kernel, 4, (pair, state), [*room, DMA((6,))], flops, 3 << 20, HBM, 16)
-    last = call(
-        last_key_value_kernel,
-        9,
-        (pair, state, shape((SLOTS, DH, DH), BF16)),
-        [*room, pltpu.VMEM((3, 2, DH, DH), F32), pltpu.VMEM((SLOTS, DH, DH), BF16), DMA((10,))],
-        flops,
-        3 << 20,
-        HBM,
-        16,
-    )
+    one = call(key_value_kernel, 4, (pair, state), [], flops, 3 << 20, VMEM, 16)
+    outs = (pair, state, shape((SLOTS, DH, DH), BF16))
+    last = call(last_key_value_kernel, 9, outs, [], flops, 3 << 20, VMEM, 16)
+
     barrier = lax.optimization_barrier
     blocks = w_out.reshape(DH, DP, DH).transpose(1, 0, 2).reshape(D, DH)
     pack = jnp.concatenate([w_query, blocks], axis=0)

time: 120 us -> 119 us (level)
  Pallas kernels: 31 us -> 27.8 us
  waiting for transfers between devices: 22.8 us -> 25.1 us
    ppermute x12, waiting for transfers between devices: 17.2 us -> 19.5 us  [hop(): return lax.ppermute(weight, ('dp', 'z', 'x', 'core'), pairs)]
    pallas_call x1, Pallas kernels: 3.49 us -> 2.28 us  [body(): last(own, other, w_key, w_value, key_4, value_4, s0, s1, s2)]
  transfers between devices with their start and end apart: 16 -> 16, of which waited for: 9 -> 9; matrix products, arithmetic and copies ran while one was open for 1% -> 1% of each run, Pallas kernels for 20% -> 18%
where the time goes in v10:
time: 119 us; the launch traced here: 118 us
  starting transfers between devices  57.8 us (49%)
  Pallas kernels  27.8 us (23%)
  waiting for transfers between devices  25.1 us (21%)
  other arithmetic  3.58 us (3%)
  local copies, waits for them, and re-layouts  3.21 us (3%)
    ppermute x12, starting transfers between devices, hop(): return lax.ppermute(weight, ('dp', 'z', 'x', 'core'), pairs)  23.1 us
    ppermute x12, waiting for transfers between devices, hop(): return lax.ppermute(weight, ('dp', 'z', 'x', 'core'), pairs)  19.5 us
    pallas_call x2, Pallas kernels, attend(): call(functools.partial(within_kernel, final), len(arrays), (shape(half, B...  11.9 us
    all_to_all x1, starting transfers between devices, body(): chunks = lax.all_to_all(chunks, ('z', 'x'), 0, 0, tiled=True)  11.8 us
    ppermute x1, starting transfers between devices, body(): other = lax.ppermute(own, 'core', SWAP)  8.91 us
    pallas_call x2, Pallas kernels, body(): call(functools.partial(out_kernel, block), 15, shape((TOK, D), kind), [pl...  8.12 us
    ppermute x1, starting transfers between devices, body(): got = lax.ppermute(partial[0], 'core', SWAP)  7.95 us
    all_to_all x1, starting transfers between devices, body(): lax.all_to_all(priors, ('z', 'x'), 0, 0, tiled=True).reshape(SLOTS, DH, DH)  6.01 us
  transfers between devices with their start and end apart: 16, of which 9 were waited for; matrix products, arithmetic and copies ran while one was open for 1% of the time, Pallas kernels for 18%

profile of v10, /device:TPU:1, one launch (start us, length us, event | category | flops | bytes accessed | tf_op | source)
XLA Modules:
  0.0 117.9 jit_solution(5779273981894765667)
XLA Ops:
  0.0 8.9 %collective-permute-start.5 = (bf16[512,1024]{1,0:T(8,128)(2,1)}, bf16[512,1024]{1,0:T(8,128)(2,1)S(1)}, u32[]{:S(2)}, u32[]{:S(2)}) collective-permute-start(bf16[512,1024]{1,0:T(8,128)(2,1)} %bitcast.14), channel_id=1, source_target_pairs={{0,1},{1,0},{2,3},{3,2},{4,5},{5,4},{6,7},{7,6},{8,9},{9,8},{10,11... | collective-permute-start | bytes 3145736 | tf_op jit(solution)/shard_map/ppermute | solution.py:212
  8.9 1.9 %collective-permute-start.1 = (bf16[1024,128]{1,0:T(8,128)(2,1)}, bf16[1024,128]{1,0:T(8,128)(2,1)S(1)}, u32[]{:S(2)}, u32[]{:S(2)}) collective-permute-start(bf16[1024,128]{1,0:T(8,128)(2,1)} %wk.1), channel_id=1, source_target_pairs={{0,448},{1,65},{2,450},{3,67},{4,452},{5,69},{6,454},{7,71},{8,456... | collective-permute-start | bytes 786440 | tf_op jit(solution)/shard_map/ppermute | solution.py:34
  10.9 1.9 %collective-permute-start.3 = (bf16[1024,128]{1,0:T(8,128)(2,1)}, bf16[1024,128]{1,0:T(8,128)(2,1)S(1)}, u32[]{:S(2)}, u32[]{:S(2)}) collective-permute-start(bf16[1024,128]{1,0:T(8,128)(2,1)} %wv.1), channel_id=1, source_target_pairs={{0,448},{1,65},{2,450},{3,67},{4,452},{5,69},{6,454},{7,71},{8,456... | collective-permute-start | bytes 786440 | tf_op jit(solution)/shard_map/ppermute | solution.py:34
  12.8 4.6 %collective-permute-done.1.wk = bf16[1024,128]{1,0:T(8,128)(2,1)S(1)} collective-permute-done((bf16[1024,128]{1,0:T(8,128)(2,1)}, bf16[1024,128]{1,0:T(8,128)(2,1)S(1)}, u32[]{:S(2)}, u32[]{:S(2)}) %collective-permute-start.1) | collective-permute-done | bytes 262176 | tf_op jit(solution)/shard_map/ppermute | solution.py:34
  20.3 1.9 %collective-permute-start.4 = (bf16[1024,128]{1,0:T(8,128)(2,1)S(1)}, bf16[1024,128]{1,0:T(8,128)(2,1)S(1)}, u32[]{:S(2)}, u32[]{:S(2)}) collective-permute-start(bf16[1024,128]{1,0:T(8,128)(2,1)S(1)} %collective-permute-done.3.wv), channel_id=1, source_target_pairs={{0,448},{1,65},{2,450},{3,67},{4,452},{5,69},{6,454},{7,71},{8,456... | collective-permute-start | bytes 786440 | tf_op jit(solution)/shard_map/ppermute | solution.py:34
  23.2 1.9 %collective-permute-start = (bf16[2048,128]{1,0:T(8,128)(2,1)S(1)}, bf16[2048,128]{1,0:T(8,128)(2,1)S(1)}, u32[]{:S(2)}, u32[]{:S(2)}) collective-permute-start(bf16[2048,128]{1,0:T(8,128)(2,1)S(1)} %pad_maximum_fusion.refs_3_.o_own), channel_id=1, source_target_pairs={{0,448},{1,65},{2,450},{3,67},{4,452},{5,69},{6,454},{7,71},{8,456... | collective-permute-start | bytes 1572872 | tf_op jit(solution)/shard_map/ppermute | solution.py:34
  30.5 1.9 %collective-permute-start.8 = (bf16[1024,128]{1,0:T(8,128)(2,1)S(1)}, bf16[1024,128]{1,0:T(8,128)(2,1)S(1)}, u32[]{:S(2)}, u32[]{:S(2)}) collective-permute-start(bf16[1024,128]{1,0:T(8,128)(2,1)S(1)} %collective-permute-done.4.wv), channel_id=1, source_target_pairs={{0,448},{1,65},{2,450},{3,67},{4,452},{5,69},{6,454},{7,71},{8,456... | collective-permute-start | bytes 786440 | tf_op jit(solution)/shard_map/ppermute | solution.py:34
  34.3 2.8 %collective-permute-done.6.wk = bf16[1024,128]{1,0:T(8,128)(2,1)S(1)} collective-permute-done((bf16[1024,128]{1,0:T(8,128)(2,1)S(1)}, bf16[1024,128]{1,0:T(8,128)(2,1)S(1)}, u32[]{:S(2)}, u32[]{:S(2)}) %collective-permute-start.6) | collective-permute-done | bytes 262176 | tf_op jit(solution)/shard_map/ppermute | solution.py:34
  40.7 2.1 %collective-permute-start.9 = (bf16[1024,128]{1,0:T(8,128)(2,1)S(1)}, bf16[1024,128]{1,0:T(8,128)(2,1)S(1)}, u32[]{:S(2)}, u32[]{:S(2)}) collective-permute-start(bf16[1024,128]{1,0:T(8,128)(2,1)S(1)} %collective-permute-done.6.wk), channel_id=1, source_target_pairs={{0,448},{1,65},{2,450},{3,67},{4,452},{5,69},{6,454},{7,71},{8,456... | collective-permute-start | bytes 786440 | tf_op jit(solution)/shard_map/ppermute | solution.py:34
  42.8 1.9 %collective-permute-start.10 = (bf16[1024,128]{1,0:T(8,128)(2,1)S(1)}, bf16[1024,128]{1,0:T(8,128)(2,1)S(1)}, u32[]{:S(2)}, u32[]{:S(2)}) collective-permute-start(bf16[1024,128]{1,0:T(8,128)(2,1)S(1)} %collective-permute-done.8.wv), channel_id=1, source_target_pairs={{0,448},{1,65},{2,450},{3,67},{4,452},{5,69},{6,454},{7,71},{8,456... | collective-permute-start | bytes 786440 | tf_op jit(solution)/shard_map/ppermute | solution.py:34
  46.4 4.7 %collective-permute-done.9.wk_far = bf16[1024,128]{1,0:T(8,128)(2,1)S(1)} collective-permute-done((bf16[1024,128]{1,0:T(8,128)(2,1)S(1)}, bf16[1024,128]{1,0:T(8,128)(2,1)S(1)}, u32[]{:S(2)}, u32[]{:S(2)}) %collective-permute-start.9) | collective-permute-done | bytes 262176 | tf_op jit(solution)/shard_map/ppermute | solution.py:34
  51.1 2.8 %collective-permute-done.10.wv_far = bf16[1024,128]{1,0:T(8,128)(2,1)S(1)} collective-permute-done((bf16[1024,128]{1,0:T(8,128)(2,1)S(1)}, bf16[1024,128]{1,0:T(8,128)(2,1)S(1)}, u32[]{:S(2)}, u32[]{:S(2)}) %collective-permute-start.10) | collective-permute-done | bytes 262176 | tf_op jit(solution)/shard_map/ppermute | solution.py:34
  53.9 2.3 %shard_map.67 = (bf16[2,512,256]{2,1,0:T(8,128)(2,1)S(1)}, f32[2,128,128]{2,1,0:T(8,128)S(1)}, bf16[4,128,128]{2,1,0:T(8,128)(2,1)}) custom-call(bf16[512,1024]{1,0:T(8,128)(2,1)S(1)} %bitcast.20, bf16[512,1024]{1,0:T(8,128)(2,1)S(1)} %collective-permute-done.5.other.refs_1_, bf16[1024,128]{1,0:T(8,128)(2,1)S(1)} %copy-done.11, ...), custom_call_target="tpu_custom_call" | custom-call | flops 536870912 | bytes 3145728 | tf_op jit(solution)/shard_map/pallas_call | solution.py:236
  59.6 1.9 %collective-permute-start.11 = (bf16[2048,128]{1,0:T(8,128)(2,1)S(1)}, bf16[2048,128]{1,0:T(8,128)(2,1)S(1)}, u32[]{:S(2)}, u32[]{:S(2)}) collective-permute-start(bf16[2048,128]{1,0:T(8,128)(2,1)S(1)} %collective-permute-done.7.refs_3_.o1), channel_id=1, source_target_pairs={{0,448},{1,65},{2,450},{3,67},{4,452},{5,69},{6,454},{7,71},{8,456... | collective-permute-start | bytes 1572872 | tf_op jit(solution)/shard_map/ppermute | solution.py:34
  61.5 11.8 %all-to-all-start = ((bf16[32,16,128]{2,1,0:T(8,128)(2,1)}), bf16[32,16,128]{2,1,0:T(8,128)(2,1)S(1)}, u32[]{:S(2)}, u32[]{:S(2)}) async-start(bf16[32,16,128]{2,1,0:T(8,128)(2,1)} %bitcast.3), calls=%async_computation | async-start | bytes 262144 | tf_op jit(solution)/shard_map/all_to_all | solution.py:263
  73.3 5.9 %shard_map.68 = (bf16[2,2,512,128]{3,2,1,0:T(8,128)(2,1)}, f32[2,2,512,128]{3,2,1,0:T(8,128)}) custom-call(bf16[512,1024]{1,0:T(8,128)(2,1)} %bitcast.15, bf16[512,1024]{1,0:T(8,128)(2,1)} %copy-done.2, bf16[2048,128]{1,0:T(8,128)(2,1)} %copy-done.16, bf16[2048,128]{1,0:T(8,128)(2,1)} %copy-done.17, bf16[2,512,256]{2,1,0:T(8,128)(2,1)} %copy-done.9, ...), custom_call_target="tpu_custom_call" | custom-call | flops 805306368 | bytes 5242880 | tf_op jit(solution)/shard_map/pallas_call | solution.py:243
  79.3 3.4 %all-to-all-done.chunk_ref = bf16[32,16,128]{2,1,0:T(8,128)(2,1)S(1)} async-done(((bf16[32,16,128]{2,1,0:T(8,128)(2,1)}), bf16[32,16,128]{2,1,0:T(8,128)(2,1)S(1)}, u32[]{:S(2)}, u32[]{:S(2)}) %all-to-all-start) | async-done | bytes 131104 | tf_op jit(solution)/shard_map/all_to_all | solution.py:263
  83.3 6.0 %all-to-all-start.1 = ((bf16[32,16,128]{2,1,0:T(8,128)(2,1)}), bf16[32,16,128]{2,1,0:T(8,128)(2,1)S(1)}, u32[]{:S(2)}, u32[]{:S(2)}) async-start(bf16[32,16,128]{2,1,0:T(8,128)(2,1)} %shard_map.70), calls=%async_computation.1 | async-start | bytes 262144 | tf_op jit(solution)/shard_map/all_to_all | solution.py:266
  90.4 5.9 %shard_map.69 = (bf16[2,2,512,128]{3,2,1,0:T(8,128)(2,1)}, f32[2,2,512,128]{3,2,1,0:T(8,128)}) custom-call(bf16[512,1024]{1,0:T(8,128)(2,1)} %bitcast.16, bf16[512,1024]{1,0:T(8,128)(2,1)} %copy-done.2, bf16[2048,128]{1,0:T(8,128)(2,1)} %copy-done.15, bf16[2048,128]{1,0:T(8,128)(2,1)} %copy-done.13, bf16[2048,128]{1,0:T(8,128)(2,1)} %copy-done.14, ...), custom_call_target="tpu_custom_call" | custom-call | flops 805306368 | bytes 5242880 | tf_op jit(solution)/shard_map/pallas_call | solution.py:243
  96.3 2.2 %all-to-all-done.1 = bf16[32,16,128]{2,1,0:T(8,128)(2,1)S(1)} async-done(((bf16[32,16,128]{2,1,0:T(8,128)(2,1)}), bf16[32,16,128]{2,1,0:T(8,128)(2,1)S(1)}, u32[]{:S(2)}, u32[]{:S(2)}) %all-to-all-start.1) | async-done | bytes 131104 | tf_op jit(solution)/shard_map/all_to_all | solution.py:266
  99.2 4.1 %shard_map.72 = bf16[512,1024]{1,0:T(8,128)(2,1)} custom-call(bf16[2,2,512,128]{3,2,1,0:T(8,128)(2,1)} %get-tuple-element.55.query_a, bf16[2,2,512,128]{3,2,1,0:T(8,128)(2,1)} %get-tuple-element.58.query_b, f32[2,2,512,128]{3,2,1,0:T(8,128)} %get-tuple-element.59.within_a, f32[2,2,512,128]{3,2,1,0:T(8,128)} %get-tuple-element.60.within_b, ...), custom_call_target="tpu_custom_call" | custom-call | flops 1342177280 | bytes 5242880 | tf_op jit(solution)/shard_map/pallas_call | solution.py:274
  103.2 7.9 %collective-permute-start.13 = (bf16[512,1024]{1,0:T(8,128)(2,1)}, bf16[512,1024]{1,0:T(8,128)(2,1)S(1)}, u32[]{:S(2)}, u32[]{:S(2)}) collective-permute-start(bf16[512,1024]{1,0:T(8,128)(2,1)} %shard_map.72), channel_id=1, source_target_pairs={{0,1},{1,0},{2,3},{3,2},{4,5},{5,4},{6,7},{7,6},{8,9},{9,8},{10,11... | collective-permute-start | bytes 3145736 | tf_op jit(solution)/shard_map/ppermute | solution.py:296
  111.2 4.1 %shard_map.71 = bf16[512,1024]{1,0:T(8,128)(2,1)} custom-call(bf16[2,2,512,128]{3,2,1,0:T(8,128)(2,1)} %get-tuple-element.55.query_a, bf16[2,2,512,128]{3,2,1,0:T(8,128)(2,1)} %get-tuple-element.58.query_b, f32[2,2,512,128]{3,2,1,0:T(8,128)} %get-tuple-element.59.within_a, f32[2,2,512,128]{3,2,1,0:T(8,128)} %get-tuple-element.60.within_b, ...), custom_call_target="tpu_custom_call" | custom-call | flops 1342177280 | bytes 5242880 | tf_op jit(solution)/shard_map/pallas_call | solution.py:274
  115.3 2.6 %fusion = bf16[1,512,1024]{2,1,0:T(8,128)(2,1)} fusion(bf16[512,1024]{1,0:T(8,128)(2,1)S(1)} %collective-permute-done.13, bf16[512,1024]{1,0:T(8,128)(2,1)} %shard_map.71), kind=kLoop, calls=%fused_computation.1 | loop fusion | flops 2097152 | bytes 3145728 | tf_op jit(solution)/shard_map/broadcast_in_dim | solution.py:297
  (58 shorter events, 21.9 us)
Async XLA Ops:
  0.0 12.8 %copy-start = (bf16[128,1024]{1,0:T(8,128)(2,1)S(1)}, bf16[128,1024]{1,0:T(8,128)(2,1)}, u32[]{:S(2)}) copy-start(bf16[128,1024]{1,0:T(8,128)(2,1)} %param.10) | copy-start | bytes 786436
  0.0 25.1 %copy-start.1 = (bf16[1,512,1024]{2,1,0:T(8,128)(2,1)S(1)}, bf16[1,512,1024]{2,1,0:T(8,128)(2,1)}, u32[]{:S(2)}) copy-start(bf16[1,512,1024]{2,1,0:T(8,128)(2,1)} %param.6) | copy-start | bytes 3145732
  0.0 25.1 %collective-permute-start.5 = (bf16[512,1024]{1,0:T(8,128)(2,1)}, bf16[512,1024]{1,0:T(8,128)(2,1)S(1)}, u32[]{:S(2)}, u32[]{:S(2)}) collective-permute-start(bf16[512,1024]{1,0:T(8,128)(2,1)} %bitcast.14), channel_id=1, source_target_pairs={{0,1},{1,0},{2,3},{3,2},{4,5},{5,4},{6,7},{7,6},{8,9},{9,8},{10,11... | collective-permute-start | bytes 3145736 | tf_op jit(solution)/shard_map/ppermute | solution.py:212
  8.9 8.5 %collective-permute-start.1 = (bf16[1024,128]{1,0:T(8,128)(2,1)}, bf16[1024,128]{1,0:T(8,128)(2,1)S(1)}, u32[]{:S(2)}, u32[]{:S(2)}) collective-permute-start(bf16[1024,128]{1,0:T(8,128)(2,1)} %wk.1), channel_id=1, source_target_pairs={{0,448},{1,65},{2,450},{3,67},{4,452},{5,69},{6,454},{7,71},{8,456... | collective-permute-start | bytes 786440 | tf_op jit(solution)/shard_map/ppermute | solution.py:34
  10.9 9.4 %collective-permute-start.3 = (bf16[1024,128]{1,0:T(8,128)(2,1)}, bf16[1024,128]{1,0:T(8,128)(2,1)S(1)}, u32[]{:S(2)}, u32[]{:S(2)}) collective-permute-start(bf16[1024,128]{1,0:T(8,128)(2,1)} %wv.1), channel_id=1, source_target_pairs={{0,448},{1,65},{2,450},{3,67},{4,452},{5,69},{6,454},{7,71},{8,456... | collective-permute-start | bytes 786440 | tf_op jit(solution)/shard_map/ppermute | solution.py:34
  17.5 9.3 %collective-permute-start.2 = (bf16[1024,128]{1,0:T(8,128)(2,1)S(1)}, bf16[1024,128]{1,0:T(8,128)(2,1)S(1)}, u32[]{:S(2)}, u32[]{:S(2)}) collective-permute-start(bf16[1024,128]{1,0:T(8,128)(2,1)S(1)} %collective-permute-done.1.wk), channel_id=1, source_target_pairs={{0,448},{1,65},{2,450},{3,67},{4,452},{5,69},{6,454},{7,71},{8,456... | collective-permute-start | bytes 786440 | tf_op jit(solution)/shard_map/ppermute | solution.py:34
  20.3 8.3 %collective-permute-start.4 = (bf16[1024,128]{1,0:T(8,128)(2,1)S(1)}, bf16[1024,128]{1,0:T(8,128)(2,1)S(1)}, u32[]{:S(2)}, u32[]{:S(2)}) collective-permute-start(bf16[1024,128]{1,0:T(8,128)(2,1)S(1)} %collective-permute-done.3.wv), channel_id=1, source_target_pairs={{0,448},{1,65},{2,450},{3,67},{4,452},{5,69},{6,454},{7,71},{8,456... | collective-permute-start | bytes 786440 | tf_op jit(solution)/shard_map/ppermute | solution.py:34
  23.2 11.1 %collective-permute-start = (bf16[2048,128]{1,0:T(8,128)(2,1)S(1)}, bf16[2048,128]{1,0:T(8,128)(2,1)S(1)}, u32[]{:S(2)}, u32[]{:S(2)}) collective-permute-start(bf16[2048,128]{1,0:T(8,128)(2,1)S(1)} %pad_maximum_fusion.refs_3_.o_own), channel_id=1, source_target_pairs={{0,448},{1,65},{2,450},{3,67},{4,452},{5,69},{6,454},{7,71},{8,456... | collective-permute-start | bytes 1572872 | tf_op jit(solution)/shard_map/ppermute | solution.py:34
  25.1 28.7 %copy-start.2 = (bf16[512,1024]{1,0:T(8,128)(2,1)}, bf16[512,1024]{1,0:T(8,128)(2,1)S(1)}, u32[]{:S(2)}) copy-start(bf16[512,1024]{1,0:T(8,128)(2,1)S(1)} %collective-permute-done.5.other.refs_1_) | copy-start | bytes 3145732
  26.8 13.9 %copy-start.9 = (bf16[2,512,256]{2,1,0:T(8,128)(2,1)}, bf16[2,512,256]{2,1,0:T(8,128)(2,1)S(1)}, u32[]{:S(2)}) copy-start(bf16[2,512,256]{2,1,0:T(8,128)(2,1)S(1)} %get-tuple-element.52.refs_4_) | copy-start | bytes 1572868
  26.8 27.1 %copy-start.3 = (f32[2,128,128]{2,1,0:T(8,128)}, f32[2,128,128]{2,1,0:T(8,128)S(1)}, u32[]{:S(2)}) copy-start(f32[2,128,128]{2,1,0:T(8,128)S(1)} %get-tuple-element.46.s0) | copy-start | bytes 393220
  28.6 8.5 %collective-permute-start.6 = (bf16[1024,128]{1,0:T(8,128)(2,1)S(1)}, bf16[1024,128]{1,0:T(8,128)(2,1)S(1)}, u32[]{:S(2)}, u32[]{:S(2)}) collective-permute-start(bf16[1024,128]{1,0:T(8,128)(2,1)S(1)} %collective-permute-done.2.wk), channel_id=1, source_target_pairs={{0,448},{1,65},{2,450},{3,67},{4,452},{5,69},{6,454},{7,71},{8,456... | collective-permute-start | bytes 786440 | tf_op jit(solution)/shard_map/ppermute | solution.py:34
  30.5 10.2 %collective-permute-start.8 = (bf16[1024,128]{1,0:T(8,128)(2,1)S(1)}, bf16[1024,128]{1,0:T(8,128)(2,1)S(1)}, u32[]{:S(2)}, u32[]{:S(2)}) collective-permute-start(bf16[1024,128]{1,0:T(8,128)(2,1)S(1)} %collective-permute-done.4.wv), channel_id=1, source_target_pairs={{0,448},{1,65},{2,450},{3,67},{4,452},{5,69},{6,454},{7,71},{8,456... | collective-permute-start | bytes 786440 | tf_op jit(solution)/shard_map/ppermute | solution.py:34
  37.1 16.7 %collective-permute-start.7 = (bf16[2048,128]{1,0:T(8,128)(2,1)S(1)}, bf16[2048,128]{1,0:T(8,128)(2,1)S(1)}, u32[]{:S(2)}, u32[]{:S(2)}) collective-permute-start(bf16[2048,128]{1,0:T(8,128)(2,1)S(1)} %collective-permute-done.refs_2_.o0), channel_id=1, source_target_pairs={{0,448},{1,65},{2,450},{3,67},{4,452},{5,69},{6,454},{7,71},{8,456... | collective-permute-start | bytes 1572872 | tf_op jit(solution)/shard_map/ppermute | solution.py:34
  40.7 13.2 %copy-start.4 = (f32[2,128,128]{2,1,0:T(8,128)}, f32[2,128,128]{2,1,0:T(8,128)S(1)}, u32[]{:S(2)}) copy-start(f32[2,128,128]{2,1,0:T(8,128)S(1)} %get-tuple-element.47.s1) | copy-start | bytes 393220
  40.7 13.2 %copy-start.11 = (bf16[1024,128]{1,0:T(8,128)(2,1)S(1)}, bf16[1024,128]{1,0:T(8,128)(2,1)}, u32[]{:S(2)}) copy-start(bf16[1024,128]{1,0:T(8,128)(2,1)} %wk.1) | copy-start | bytes 786436
  40.7 13.2 %copy-start.12 = (bf16[1024,128]{1,0:T(8,128)(2,1)S(1)}, bf16[1024,128]{1,0:T(8,128)(2,1)}, u32[]{:S(2)}) copy-start(bf16[1024,128]{1,0:T(8,128)(2,1)} %wv.1) | copy-start | bytes 786436
  40.7 10.3 %collective-permute-start.9 = (bf16[1024,128]{1,0:T(8,128)(2,1)S(1)}, bf16[1024,128]{1,0:T(8,128)(2,1)S(1)}, u32[]{:S(2)}, u32[]{:S(2)}) collective-permute-start(bf16[1024,128]{1,0:T(8,128)(2,1)S(1)} %collective-permute-done.6.wk), channel_id=1, source_target_pairs={{0,448},{1,65},{2,450},{3,67},{4,452},{5,69},{6,454},{7,71},{8,456... | collective-permute-start | bytes 786440 | tf_op jit(solution)/shard_map/ppermute | solution.py:34
  42.8 11.1 %collective-permute-start.10 = (bf16[1024,128]{1,0:T(8,128)(2,1)S(1)}, bf16[1024,128]{1,0:T(8,128)(2,1)S(1)}, u32[]{:S(2)}, u32[]{:S(2)}) collective-permute-start(bf16[1024,128]{1,0:T(8,128)(2,1)S(1)} %collective-permute-done.8.wv), channel_id=1, source_target_pairs={{0,448},{1,65},{2,450},{3,67},{4,452},{5,69},{6,454},{7,71},{8,456... | collective-permute-start | bytes 786440 | tf_op jit(solution)/shard_map/ppermute | solution.py:34
  57.7 31.7 %collective-permute-start.12 = (bf16[2048,128]{1,0:T(8,128)(2,1)S(1)}, bf16[2048,128]{1,0:T(8,128)(2,1)S(1)}, u32[]{:S(2)}, u32[]{:S(2)}) collective-permute-start(bf16[2048,128]{1,0:T(8,128)(2,1)S(1)} %collective-permute-done.7.refs_3_.o1), channel_id=1, source_target_pairs={{0,384},{1,129},{2,386},{3,131},{4,388},{5,133},{6,390},{7,135},{8... | collective-permute-start | bytes 1572872 | tf_op jit(solution)/shard_map/ppermute | solution.py:34
  59.6 29.8 %collective-permute-start.11 = (bf16[2048,128]{1,0:T(8,128)(2,1)S(1)}, bf16[2048,128]{1,0:T(8,128)(2,1)S(1)}, u32[]{:S(2)}, u32[]{:S(2)}) collective-permute-start(bf16[2048,128]{1,0:T(8,128)(2,1)S(1)} %collective-permute-done.7.refs_3_.o1), channel_id=1, source_target_pairs={{0,448},{1,65},{2,450},{3,67},{4,452},{5,69},{6,454},{7,71},{8,456... | collective-permute-start | bytes 1572872 | tf_op jit(solution)/shard_map/ppermute | solution.py:34
  61.5 21.1 %all-to-all-start = ((bf16[32,16,128]{2,1,0:T(8,128)(2,1)}), bf16[32,16,128]{2,1,0:T(8,128)(2,1)S(1)}, u32[]{:S(2)}, u32[]{:S(2)}) async-start(bf16[32,16,128]{2,1,0:T(8,128)(2,1)} %bitcast.3), calls=%async_computation | async-start | bytes 262144 | tf_op jit(solution)/shard_map/all_to_all | solution.py:263
  83.3 15.2 %all-to-all-start.1 = ((bf16[32,16,128]{2,1,0:T(8,128)(2,1)}), bf16[32,16,128]{2,1,0:T(8,128)(2,1)S(1)}, u32[]{:S(2)}, u32[]{:S(2)}) async-start(bf16[32,16,128]{2,1,0:T(8,128)(2,1)} %shard_map.70), calls=%async_computation.1 | async-start | bytes 262144 | tf_op jit(solution)/shard_map/all_to_all | solution.py:266
  103.2 12.0 %collective-permute-start.13 = (bf16[512,1024]{1,0:T(8,128)(2,1)}, bf16[512,1024]{1,0:T(8,128)(2,1)S(1)}, u32[]{:S(2)}, u32[]{:S(2)}) collective-permute-start(bf16[512,1024]{1,0:T(8,128)(2,1)} %shard_map.72), channel_id=1, source_target_pairs={{0,1},{1,0},{2,3},{3,2},{4,5},{5,4},{6,7},{7,6},{8,9},{9,8},{10,11... | collective-permute-start | bytes 3145736 | tf_op jit(solution)/shard_map/ppermute | solution.py:296
  (11 other events, 44.9 us)

commit v11 on v10

--- a/solution.py
+++ b/solution.py
@@ -227,15 +227,15 @@
     key_2, value_2, s0 = barrier((key_2, value_2, s0))
     kv1, s1 = one(own, other, key_2, value_2)
     key_3, value_3 = hop(key_2), hop(value_2)
-    pack_1, key_3 = barrier((pack_1, key_3))
+    pack_1, key_3, value_3 = barrier((pack_1, key_3, value_3))
     pack_2 = hop(pack_1)
     key_3, value_3, s1 = barrier((key_3, value_3, s1))
     kv2, s2 = one(own, other, key_3, value_3)
     key_4, value_4 = hop(key_3), hop(value_3)
+    pack_2, s2 = barrier((pack_2, s2))
+    pack_3, pack_4 = hop(pack_2), hop(pack_2, 2)
     pack_2, key_4, value_4, s2 = barrier((pack_2, key_4, value_4, s2))
     kv3, s3, total = last(own, other, w_key, w_value, key_4, value_4, s0, s1, s2)
-    pack_2, total = barrier((pack_2, total))
-    pack_3, pack_4 = hop(pack_2), hop(pack_2, 2)
 
     half = (2, 2, TOK, DH)
 

time: 119 us -> 117 us (0.983)
  waiting for transfers between devices: 25.1 us -> 22.6 us
    ppermute x12, waiting for transfers between devices: 19.5 us -> 16.7 us  [hop(): return lax.ppermute(weight, ('dp', 'z', 'x', 'core'), pairs)]
    ppermute x12, starting transfers between devices: 23.1 us -> 25.9 us  [hop(): return lax.ppermute(weight, ('dp', 'z', 'x', 'core'), pairs)]
    all_to_all x1, starting transfers between devices: 11.8 us -> 9.24 us  [body(): chunks = lax.all_to_all(chunks, ('z', 'x'), 0, 0, tiled=True)]
    unnamed x38 -> x34, local copies, waits for them, and re-layouts: 3.16 us -> 2.96 us
  transfers between devices with their start and end apart: 16 -> 16, of which waited for: 9 -> 9; matrix products, arithmetic and copies ran while one was open for 1% -> 1% of each run, Pallas kernels for 18% -> 21%
where the time goes in v11:
time: 117 us; the launch traced here: 116 us
  starting transfers between devices  58.2 us (50%)
  Pallas kernels  27.8 us (24%)
  waiting for transfers between devices  22.6 us (19%)
  other arithmetic  3.58 us (3%)
  local copies, waits for them, and re-layouts  3 us (3%)
    ppermute x12, starting transfers between devices, hop(): return lax.ppermute(weight, ('dp', 'z', 'x', 'core'), pairs)  25.9 us
    ppermute x12, waiting for transfers between devices, hop(): return lax.ppermute(weight, ('dp', 'z', 'x', 'core'), pairs)  16.7 us
    pallas_call x2, Pallas kernels, attend(): call(functools.partial(within_kernel, final), len(arrays), (shape(half, B...  11.9 us
    all_to_all x1, starting transfers between devices, body(): chunks = lax.all_to_all(chunks, ('z', 'x'), 0, 0, tiled=True)  9.24 us
    ppermute x1, starting transfers between devices, body(): other = lax.ppermute(own, 'core', SWAP)  8.91 us
    ppermute x1, starting transfers between devices, body(): got = lax.ppermute(partial[0], 'core', SWAP)  8.36 us
    pallas_call x2, Pallas kernels, body(): call(functools.partial(out_kernel, block), 15, shape((TOK, D), kind), [pl...  8.14 us
    all_to_all x1, starting transfers between devices, body(): lax.all_to_all(priors, ('z', 'x'), 0, 0, tiled=True).reshape(SLOTS, DH, DH)  5.83 us
  transfers between devices with their start and end apart: 16, of which 9 were waited for; matrix products, arithmetic and copies ran while one was open for 1% of the time, Pallas kernels for 21%

profile of v11, /device:TPU:1, one launch (start us, length us, event | category | flops | bytes accessed | tf_op | source)
XLA Modules:
  0.0 115.8 jit_solution(9243888830356227278)
XLA Ops:
  0.0 8.9 %collective-permute-start = (bf16[512,1024]{1,0:T(8,128)(2,1)}, bf16[512,1024]{1,0:T(8,128)(2,1)S(1)}, u32[]{:S(2)}, u32[]{:S(2)}) collective-permute-start(bf16[512,1024]{1,0:T(8,128)(2,1)} %bitcast.14), channel_id=1, source_target_pairs={{0,1},{1,0},{2,3},{3,2},{4,5},{5,4},{6,7},{7,6},{8,9},{9,8},{10,11... | collective-permute-start | bytes 3145736 | tf_op jit(solution)/shard_map/ppermute | solution.py:212
  8.9 1.9 %collective-permute-start.2 = (bf16[1024,128]{1,0:T(8,128)(2,1)}, bf16[1024,128]{1,0:T(8,128)(2,1)S(1)}, u32[]{:S(2)}, u32[]{:S(2)}) collective-permute-start(bf16[1024,128]{1,0:T(8,128)(2,1)} %wk.1), channel_id=1, source_target_pairs={{0,448},{1,65},{2,450},{3,67},{4,452},{5,69},{6,454},{7,71},{8,456... | collective-permute-start | bytes 786440 | tf_op jit(solution)/shard_map/ppermute | solution.py:34
  10.9 1.9 %collective-permute-start.4 = (bf16[1024,128]{1,0:T(8,128)(2,1)}, bf16[1024,128]{1,0:T(8,128)(2,1)S(1)}, u32[]{:S(2)}, u32[]{:S(2)}) collective-permute-start(bf16[1024,128]{1,0:T(8,128)(2,1)} %wv.1), channel_id=1, source_target_pairs={{0,448},{1,65},{2,450},{3,67},{4,452},{5,69},{6,454},{7,71},{8,456... | collective-permute-start | bytes 786440 | tf_op jit(solution)/shard_map/ppermute | solution.py:34
  12.8 4.6 %collective-permute-done.2.wk = bf16[1024,128]{1,0:T(8,128)(2,1)S(1)} collective-permute-done((bf16[1024,128]{1,0:T(8,128)(2,1)}, bf16[1024,128]{1,0:T(8,128)(2,1)S(1)}, u32[]{:S(2)}, u32[]{:S(2)}) %collective-permute-start.2) | collective-permute-done | bytes 262176 | tf_op jit(solution)/shard_map/ppermute | solution.py:34
  23.2 1.9 %collective-permute-start.1 = (bf16[2048,128]{1,0:T(8,128)(2,1)S(1)}, bf16[2048,128]{1,0:T(8,128)(2,1)S(1)}, u32[]{:S(2)}, u32[]{:S(2)}) collective-permute-start(bf16[2048,128]{1,0:T(8,128)(2,1)S(1)} %pad_maximum_fusion.refs_3_.o_own), channel_id=1, source_target_pairs={{0,448},{1,65},{2,450},{3,67},{4,452},{5,69},{6,454},{7,71},{8,456... | collective-permute-start | bytes 1572872 | tf_op jit(solution)/shard_map/ppermute | solution.py:34
  30.5 1.9 %collective-permute-start.7 = (bf16[1024,128]{1,0:T(8,128)(2,1)S(1)}, bf16[1024,128]{1,0:T(8,128)(2,1)S(1)}, u32[]{:S(2)}, u32[]{:S(2)}) collective-permute-start(bf16[1024,128]{1,0:T(8,128)(2,1)S(1)} %collective-permute-done.5.wv), channel_id=1, source_target_pairs={{0,448},{1,65},{2,450},{3,67},{4,452},{5,69},{6,454},{7,71},{8,456... | collective-permute-start | bytes 786440 | tf_op jit(solution)/shard_map/ppermute | solution.py:34
  34.3 2.8 %collective-permute-done.6.wk = bf16[1024,128]{1,0:T(8,128)(2,1)S(1)} collective-permute-done((bf16[1024,128]{1,0:T(8,128)(2,1)S(1)}, bf16[1024,128]{1,0:T(8,128)(2,1)S(1)}, u32[]{:S(2)}, u32[]{:S(2)}) %collective-permute-start.6) | collective-permute-done | bytes 262176 | tf_op jit(solution)/shard_map/ppermute | solution.py:34
  37.1 2.8 %collective-permute-done.7.wv = bf16[1024,128]{1,0:T(8,128)(2,1)S(1)} collective-permute-done((bf16[1024,128]{1,0:T(8,128)(2,1)S(1)}, bf16[1024,128]{1,0:T(8,128)(2,1)S(1)}, u32[]{:S(2)}, u32[]{:S(2)}) %collective-permute-start.7) | collective-permute-done | bytes 262176 | tf_op jit(solution)/shard_map/ppermute | solution.py:34
  39.9 1.9 %collective-permute-start.8 = (bf16[2048,128]{1,0:T(8,128)(2,1)S(1)}, bf16[2048,128]{1,0:T(8,128)(2,1)}, u32[]{:S(2)}, u32[]{:S(2)}) collective-permute-start(bf16[2048,128]{1,0:T(8,128)(2,1)S(1)} %collective-permute-done.1.refs_2_.o0), channel_id=1, source_target_pairs={{0,448},{1,65},{2,450},{3,67},{4,452},{5,69},{6,454},{7,71},{8,456... | collective-permute-start | bytes 1572872 | tf_op jit(solution)/shard_map/ppermute | solution.py:34
  43.5 2.1 %collective-permute-start.9 = (bf16[1024,128]{1,0:T(8,128)(2,1)S(1)}, bf16[1024,128]{1,0:T(8,128)(2,1)S(1)}, u32[]{:S(2)}, u32[]{:S(2)}) collective-permute-start(bf16[1024,128]{1,0:T(8,128)(2,1)S(1)} %collective-permute-done.6.wk), channel_id=1, source_target_pairs={{0,448},{1,65},{2,450},{3,67},{4,452},{5,69},{6,454},{7,71},{8,456... | collective-permute-start | bytes 786440 | tf_op jit(solution)/shard_map/ppermute | solution.py:34
  45.6 2.1 %collective-permute-start.10 = (bf16[1024,128]{1,0:T(8,128)(2,1)S(1)}, bf16[1024,128]{1,0:T(8,128)(2,1)S(1)}, u32[]{:S(2)}, u32[]{:S(2)}) collective-permute-start(bf16[1024,128]{1,0:T(8,128)(2,1)S(1)} %collective-permute-done.7.wv), channel_id=1, source_target_pairs={{0,448},{1,65},{2,450},{3,67},{4,452},{5,69},{6,454},{7,71},{8,456... | collective-permute-start | bytes 786440 | tf_op jit(solution)/shard_map/ppermute | solution.py:34
  51.2 2.9 %collective-permute-start.12 = (bf16[2048,128]{1,0:T(8,128)(2,1)}, bf16[2048,128]{1,0:T(8,128)(2,1)S(1)}, u32[]{:S(2)}, u32[]{:S(2)}) collective-permute-start(bf16[2048,128]{1,0:T(8,128)(2,1)} %collective-permute-done.8.refs_3_.o1), channel_id=1, source_target_pairs={{0,384},{1,129},{2,386},{3,131},{4,388},{5,133},{6,390},{7,135},{8... | collective-permute-start | bytes 1572872 | tf_op jit(solution)/shard_map/ppermute | solution.py:34
  54.1 3.6 %collective-permute-start.11 = (bf16[2048,128]{1,0:T(8,128)(2,1)}, bf16[2048,128]{1,0:T(8,128)(2,1)}, u32[]{:S(2)}, u32[]{:S(2)}) collective-permute-start(bf16[2048,128]{1,0:T(8,128)(2,1)} %collective-permute-done.8.refs_3_.o1), channel_id=1, source_target_pairs={{0,448},{1,65},{2,450},{3,67},{4,452},{5,69},{6,454},{7,71},{8,456... | collective-permute-start | bytes 1572872 | tf_op jit(solution)/shard_map/ppermute | solution.py:34
  57.7 2.3 %shard_map.67 = (bf16[2,512,256]{2,1,0:T(8,128)(2,1)S(1)}, f32[2,128,128]{2,1,0:T(8,128)S(1)}, bf16[4,128,128]{2,1,0:T(8,128)(2,1)}) custom-call(bf16[512,1024]{1,0:T(8,128)(2,1)S(1)} %bitcast.20, bf16[512,1024]{1,0:T(8,128)(2,1)S(1)} %collective-permute-done.other.refs_1_, bf16[1024,128]{1,0:T(8,128)(2,1)S(1)} %copy-done.11, ...), custom_call_target="tpu_custom_call" | custom-call | flops 536870912 | bytes 3145728 | tf_op jit(solution)/shard_map/pallas_call | solution.py:238
  61.5 9.2 %all-to-all-start = ((bf16[32,16,128]{2,1,0:T(8,128)(2,1)}), bf16[32,16,128]{2,1,0:T(8,128)(2,1)S(1)}, u32[]{:S(2)}, u32[]{:S(2)}) async-start(bf16[32,16,128]{2,1,0:T(8,128)(2,1)} %bitcast.3), calls=%async_computation | async-start | bytes 262144 | tf_op jit(solution)/shard_map/all_to_all | solution.py:263
  70.7 5.9 %shard_map.68 = (bf16[2,2,512,128]{3,2,1,0:T(8,128)(2,1)}, f32[2,2,512,128]{3,2,1,0:T(8,128)}) custom-call(bf16[512,1024]{1,0:T(8,128)(2,1)} %bitcast.15, bf16[512,1024]{1,0:T(8,128)(2,1)} %copy-done.2, bf16[2048,128]{1,0:T(8,128)(2,1)} %copy-done.15, bf16[2048,128]{1,0:T(8,128)(2,1)} %collective-permute-done.8.refs_3_.o1, bf16[2,512,256]{2,1,0:T(8,128)(2,1)} %copy-done.9, ...), custom_call_target="tpu_custom_call" | custom-call | flops 805306368 | bytes 5242880 | tf_op jit(solution)/shard_map/pallas_call | solution.py:243
  76.7 3.4 %all-to-all-done.chunk_ref = bf16[32,16,128]{2,1,0:T(8,128)(2,1)S(1)} async-done(((bf16[32,16,128]{2,1,0:T(8,128)(2,1)}), bf16[32,16,128]{2,1,0:T(8,128)(2,1)S(1)}, u32[]{:S(2)}, u32[]{:S(2)}) %all-to-all-start) | async-done | bytes 131104 | tf_op jit(solution)/shard_map/all_to_all | solution.py:263
  80.8 5.8 %all-to-all-start.1 = ((bf16[32,16,128]{2,1,0:T(8,128)(2,1)}), bf16[32,16,128]{2,1,0:T(8,128)(2,1)S(1)}, u32[]{:S(2)}, u32[]{:S(2)}) async-start(bf16[32,16,128]{2,1,0:T(8,128)(2,1)} %shard_map.70), calls=%async_computation.1 | async-start | bytes 262144 | tf_op jit(solution)/shard_map/all_to_all | solution.py:266
  87.4 5.9 %shard_map.69 = (bf16[2,2,512,128]{3,2,1,0:T(8,128)(2,1)}, f32[2,2,512,128]{3,2,1,0:T(8,128)}) custom-call(bf16[512,1024]{1,0:T(8,128)(2,1)} %bitcast.16, bf16[512,1024]{1,0:T(8,128)(2,1)} %copy-done.2, bf16[2048,128]{1,0:T(8,128)(2,1)} %collective-permute-done.11.refs_2_.o2, bf16[2048,128]{1,0:T(8,128)(2,1)} %copy-done.13, bf16[2048,128]{1,0:T(8,128)(2,1)} %copy-done.14, ...), custom_call_target="tpu_custom_call" | custom-call | flops 805306368 | bytes 5242880 | tf_op jit(solution)/shard_map/pallas_call | solution.py:243
  93.4 2.6 %all-to-all-done.1 = bf16[32,16,128]{2,1,0:T(8,128)(2,1)S(1)} async-done(((bf16[32,16,128]{2,1,0:T(8,128)(2,1)}), bf16[32,16,128]{2,1,0:T(8,128)(2,1)S(1)}, u32[]{:S(2)}, u32[]{:S(2)}) %all-to-all-start.1) | async-done | bytes 131104 | tf_op jit(solution)/shard_map/all_to_all | solution.py:266
  96.6 4.0 %shard_map.72 = bf16[512,1024]{1,0:T(8,128)(2,1)} custom-call(bf16[2,2,512,128]{3,2,1,0:T(8,128)(2,1)} %get-tuple-element.57.query_a, bf16[2,2,512,128]{3,2,1,0:T(8,128)(2,1)} %get-tuple-element.60.query_b, f32[2,2,512,128]{3,2,1,0:T(8,128)} %get-tuple-element.61.within_a, f32[2,2,512,128]{3,2,1,0:T(8,128)} %get-tuple-element.62.within_b, ...), custom_call_target="tpu_custom_call" | custom-call | flops 1342177280 | bytes 5242880 | tf_op jit(solution)/shard_map/pallas_call | solution.py:274
  100.7 8.4 %collective-permute-start.13 = (bf16[512,1024]{1,0:T(8,128)(2,1)}, bf16[512,1024]{1,0:T(8,128)(2,1)S(1)}, u32[]{:S(2)}, u32[]{:S(2)}) collective-permute-start(bf16[512,1024]{1,0:T(8,128)(2,1)} %shard_map.72), channel_id=1, source_target_pairs={{0,1},{1,0},{2,3},{3,2},{4,5},{5,4},{6,7},{7,6},{8,9},{9,8},{10,11... | collective-permute-start | bytes 3145736 | tf_op jit(solution)/shard_map/ppermute | solution.py:296
  109.0 4.1 %shard_map.71 = bf16[512,1024]{1,0:T(8,128)(2,1)} custom-call(bf16[2,2,512,128]{3,2,1,0:T(8,128)(2,1)} %get-tuple-element.57.query_a, bf16[2,2,512,128]{3,2,1,0:T(8,128)(2,1)} %get-tuple-element.60.query_b, f32[2,2,512,128]{3,2,1,0:T(8,128)} %get-tuple-element.61.within_a, f32[2,2,512,128]{3,2,1,0:T(8,128)} %get-tuple-element.62.within_b, ...), custom_call_target="tpu_custom_call" | custom-call | flops 1342177280 | bytes 5242880 | tf_op jit(solution)/shard_map/pallas_call | solution.py:274
  113.2 2.6 %fusion = bf16[1,512,1024]{2,1,0:T(8,128)(2,1)} fusion(bf16[512,1024]{1,0:T(8,128)(2,1)S(1)} %collective-permute-done.13, bf16[512,1024]{1,0:T(8,128)(2,1)} %shard_map.71), kind=kLoop, calls=%fused_computation.1 | loop fusion | flops 2097152 | bytes 3145728 | tf_op jit(solution)/shard_map/broadcast_in_dim | solution.py:297
  (54 shorter events, 21.7 us)
Async XLA Ops:
  0.0 12.8 %copy-start = (bf16[128,1024]{1,0:T(8,128)(2,1)S(1)}, bf16[128,1024]{1,0:T(8,128)(2,1)}, u32[]{:S(2)}) copy-start(bf16[128,1024]{1,0:T(8,128)(2,1)} %param.10) | copy-start | bytes 786436
  0.0 25.1 %copy-start.1 = (bf16[1,512,1024]{2,1,0:T(8,128)(2,1)S(1)}, bf16[1,512,1024]{2,1,0:T(8,128)(2,1)}, u32[]{:S(2)}) copy-start(bf16[1,512,1024]{2,1,0:T(8,128)(2,1)} %param.6) | copy-start | bytes 3145732
  0.0 25.1 %collective-permute-start = (bf16[512,1024]{1,0:T(8,128)(2,1)}, bf16[512,1024]{1,0:T(8,128)(2,1)S(1)}, u32[]{:S(2)}, u32[]{:S(2)}) collective-permute-start(bf16[512,1024]{1,0:T(8,128)(2,1)} %bitcast.14), channel_id=1, source_target_pairs={{0,1},{1,0},{2,3},{3,2},{4,5},{5,4},{6,7},{7,6},{8,9},{9,8},{10,11... | collective-permute-start | bytes 3145736 | tf_op jit(solution)/shard_map/ppermute | solution.py:212
  8.9 8.5 %collective-permute-start.2 = (bf16[1024,128]{1,0:T(8,128)(2,1)}, bf16[1024,128]{1,0:T(8,128)(2,1)S(1)}, u32[]{:S(2)}, u32[]{:S(2)}) collective-permute-start(bf16[1024,128]{1,0:T(8,128)(2,1)} %wk.1), channel_id=1, source_target_pairs={{0,448},{1,65},{2,450},{3,67},{4,452},{5,69},{6,454},{7,71},{8,456... | collective-permute-start | bytes 786440 | tf_op jit(solution)/shard_map/ppermute | solution.py:34
  10.9 9.4 %collective-permute-start.4 = (bf16[1024,128]{1,0:T(8,128)(2,1)}, bf16[1024,128]{1,0:T(8,128)(2,1)S(1)}, u32[]{:S(2)}, u32[]{:S(2)}) collective-permute-start(bf16[1024,128]{1,0:T(8,128)(2,1)} %wv.1), channel_id=1, source_target_pairs={{0,448},{1,65},{2,450},{3,67},{4,452},{5,69},{6,454},{7,71},{8,456... | collective-permute-start | bytes 786440 | tf_op jit(solution)/shard_map/ppermute | solution.py:34
  17.5 9.3 %collective-permute-start.3 = (bf16[1024,128]{1,0:T(8,128)(2,1)S(1)}, bf16[1024,128]{1,0:T(8,128)(2,1)S(1)}, u32[]{:S(2)}, u32[]{:S(2)}) collective-permute-start(bf16[1024,128]{1,0:T(8,128)(2,1)S(1)} %collective-permute-done.2.wk), channel_id=1, source_target_pairs={{0,448},{1,65},{2,450},{3,67},{4,452},{5,69},{6,454},{7,71},{8,456... | collective-permute-start | bytes 786440 | tf_op jit(solution)/shard_map/ppermute | solution.py:34
  20.3 8.3 %collective-permute-start.5 = (bf16[1024,128]{1,0:T(8,128)(2,1)S(1)}, bf16[1024,128]{1,0:T(8,128)(2,1)S(1)}, u32[]{:S(2)}, u32[]{:S(2)}) collective-permute-start(bf16[1024,128]{1,0:T(8,128)(2,1)S(1)} %collective-permute-done.4.wv), channel_id=1, source_target_pairs={{0,448},{1,65},{2,450},{3,67},{4,452},{5,69},{6,454},{7,71},{8,456... | collective-permute-start | bytes 786440 | tf_op jit(solution)/shard_map/ppermute | solution.py:34
  23.2 11.1 %collective-permute-start.1 = (bf16[2048,128]{1,0:T(8,128)(2,1)S(1)}, bf16[2048,128]{1,0:T(8,128)(2,1)S(1)}, u32[]{:S(2)}, u32[]{:S(2)}) collective-permute-start(bf16[2048,128]{1,0:T(8,128)(2,1)S(1)} %pad_maximum_fusion.refs_3_.o_own), channel_id=1, source_target_pairs={{0,448},{1,65},{2,450},{3,67},{4,452},{5,69},{6,454},{7,71},{8,456... | collective-permute-start | bytes 1572872 | tf_op jit(solution)/shard_map/ppermute | solution.py:34
  25.1 32.6 %copy-start.2 = (bf16[512,1024]{1,0:T(8,128)(2,1)}, bf16[512,1024]{1,0:T(8,128)(2,1)S(1)}, u32[]{:S(2)}) copy-start(bf16[512,1024]{1,0:T(8,128)(2,1)S(1)} %collective-permute-done.other.refs_1_) | copy-start | bytes 3145732
  26.8 16.7 %copy-start.9 = (bf16[2,512,256]{2,1,0:T(8,128)(2,1)}, bf16[2,512,256]{2,1,0:T(8,128)(2,1)S(1)}, u32[]{:S(2)}) copy-start(bf16[2,512,256]{2,1,0:T(8,128)(2,1)S(1)} %get-tuple-element.54.refs_4_) | copy-start | bytes 1572868
  26.8 30.9 %copy-start.3 = (f32[2,128,128]{2,1,0:T(8,128)}, f32[2,128,128]{2,1,0:T(8,128)S(1)}, u32[]{:S(2)}) copy-start(f32[2,128,128]{2,1,0:T(8,128)S(1)} %get-tuple-element.49.s0) | copy-start | bytes 393220
  28.6 8.5 %collective-permute-start.6 = (bf16[1024,128]{1,0:T(8,128)(2,1)S(1)}, bf16[1024,128]{1,0:T(8,128)(2,1)S(1)}, u32[]{:S(2)}, u32[]{:S(2)}) collective-permute-start(bf16[1024,128]{1,0:T(8,128)(2,1)S(1)} %collective-permute-done.3.wk), channel_id=1, source_target_pairs={{0,448},{1,65},{2,450},{3,67},{4,452},{5,69},{6,454},{7,71},{8,456... | collective-permute-start | bytes 786440 | tf_op jit(solution)/shard_map/ppermute | solution.py:34
  30.5 9.4 %collective-permute-start.7 = (bf16[1024,128]{1,0:T(8,128)(2,1)S(1)}, bf16[1024,128]{1,0:T(8,128)(2,1)S(1)}, u32[]{:S(2)}, u32[]{:S(2)}) collective-permute-start(bf16[1024,128]{1,0:T(8,128)(2,1)S(1)} %collective-permute-done.5.wv), channel_id=1, source_target_pairs={{0,448},{1,65},{2,450},{3,67},{4,452},{5,69},{6,454},{7,71},{8,456... | collective-permute-start | bytes 786440 | tf_op jit(solution)/shard_map/ppermute | solution.py:34
  39.9 11.2 %collective-permute-start.8 = (bf16[2048,128]{1,0:T(8,128)(2,1)S(1)}, bf16[2048,128]{1,0:T(8,128)(2,1)}, u32[]{:S(2)}, u32[]{:S(2)}) collective-permute-start(bf16[2048,128]{1,0:T(8,128)(2,1)S(1)} %collective-permute-done.1.refs_2_.o0), channel_id=1, source_target_pairs={{0,448},{1,65},{2,450},{3,67},{4,452},{5,69},{6,454},{7,71},{8,456... | collective-permute-start | bytes 1572872 | tf_op jit(solution)/shard_map/ppermute | solution.py:34
  43.5 14.2 %copy-start.4 = (f32[2,128,128]{2,1,0:T(8,128)}, f32[2,128,128]{2,1,0:T(8,128)S(1)}, u32[]{:S(2)}) copy-start(f32[2,128,128]{2,1,0:T(8,128)S(1)} %get-tuple-element.50.s1) | copy-start | bytes 393220
  43.5 14.2 %copy-start.11 = (bf16[1024,128]{1,0:T(8,128)(2,1)S(1)}, bf16[1024,128]{1,0:T(8,128)(2,1)}, u32[]{:S(2)}) copy-start(bf16[1024,128]{1,0:T(8,128)(2,1)} %wk.1) | copy-start | bytes 786436
  43.5 14.2 %copy-start.12 = (bf16[1024,128]{1,0:T(8,128)(2,1)S(1)}, bf16[1024,128]{1,0:T(8,128)(2,1)}, u32[]{:S(2)}) copy-start(bf16[1024,128]{1,0:T(8,128)(2,1)} %wv.1) | copy-start | bytes 786436
  43.5 14.1 %collective-permute-start.9 = (bf16[1024,128]{1,0:T(8,128)(2,1)S(1)}, bf16[1024,128]{1,0:T(8,128)(2,1)S(1)}, u32[]{:S(2)}, u32[]{:S(2)}) collective-permute-start(bf16[1024,128]{1,0:T(8,128)(2,1)S(1)} %collective-permute-done.6.wk), channel_id=1, source_target_pairs={{0,448},{1,65},{2,450},{3,67},{4,452},{5,69},{6,454},{7,71},{8,456... | collective-permute-start | bytes 786440 | tf_op jit(solution)/shard_map/ppermute | solution.py:34
  45.6 12.1 %collective-permute-start.10 = (bf16[1024,128]{1,0:T(8,128)(2,1)S(1)}, bf16[1024,128]{1,0:T(8,128)(2,1)S(1)}, u32[]{:S(2)}, u32[]{:S(2)}) collective-permute-start(bf16[1024,128]{1,0:T(8,128)(2,1)S(1)} %collective-permute-done.7.wv), channel_id=1, source_target_pairs={{0,448},{1,65},{2,450},{3,67},{4,452},{5,69},{6,454},{7,71},{8,456... | collective-permute-start | bytes 786440 | tf_op jit(solution)/shard_map/ppermute | solution.py:34
  51.2 35.4 %collective-permute-start.12 = (bf16[2048,128]{1,0:T(8,128)(2,1)}, bf16[2048,128]{1,0:T(8,128)(2,1)S(1)}, u32[]{:S(2)}, u32[]{:S(2)}) collective-permute-start(bf16[2048,128]{1,0:T(8,128)(2,1)} %collective-permute-done.8.refs_3_.o1), channel_id=1, source_target_pairs={{0,384},{1,129},{2,386},{3,131},{4,388},{5,133},{6,390},{7,135},{8... | collective-permute-start | bytes 1572872 | tf_op jit(solution)/shard_map/ppermute | solution.py:34
  54.1 32.6 %collective-permute-start.11 = (bf16[2048,128]{1,0:T(8,128)(2,1)}, bf16[2048,128]{1,0:T(8,128)(2,1)}, u32[]{:S(2)}, u32[]{:S(2)}) collective-permute-start(bf16[2048,128]{1,0:T(8,128)(2,1)} %collective-permute-done.8.refs_3_.o1), channel_id=1, source_target_pairs={{0,448},{1,65},{2,450},{3,67},{4,452},{5,69},{6,454},{7,71},{8,456... | collective-permute-start | bytes 1572872 | tf_op jit(solution)/shard_map/ppermute | solution.py:34
  61.5 18.6 %all-to-all-start = ((bf16[32,16,128]{2,1,0:T(8,128)(2,1)}), bf16[32,16,128]{2,1,0:T(8,128)(2,1)S(1)}, u32[]{:S(2)}, u32[]{:S(2)}) async-start(bf16[32,16,128]{2,1,0:T(8,128)(2,1)} %bitcast.3), calls=%async_computation | async-start | bytes 262144 | tf_op jit(solution)/shard_map/all_to_all | solution.py:263
  80.8 15.2 %all-to-all-start.1 = ((bf16[32,16,128]{2,1,0:T(8,128)(2,1)}), bf16[32,16,128]{2,1,0:T(8,128)(2,1)S(1)}, u32[]{:S(2)}, u32[]{:S(2)}) async-start(bf16[32,16,128]{2,1,0:T(8,128)(2,1)} %shard_map.70), calls=%async_computation.1 | async-start | bytes 262144 | tf_op jit(solution)/shard_map/all_to_all | solution.py:266
  100.7 12.5 %collective-permute-start.13 = (bf16[512,1024]{1,0:T(8,128)(2,1)}, bf16[512,1024]{1,0:T(8,128)(2,1)S(1)}, u32[]{:S(2)}, u32[]{:S(2)}) collective-permute-start(bf16[512,1024]{1,0:T(8,128)(2,1)} %shard_map.72), channel_id=1, source_target_pairs={{0,1},{1,0},{2,3},{3,2},{4,5},{5,4},{6,7},{7,6},{8,9},{9,8},{10,11... | collective-permute-start | bytes 3145736 | tf_op jit(solution)/shard_map/ppermute | solution.py:296
  (9 other events, 42.9 us)

commit v12 on v11

--- a/solution.py
+++ b/solution.py
@@ -227,7 +227,7 @@
     key_2, value_2, s0 = barrier((key_2, value_2, s0))
     kv1, s1 = one(own, other, key_2, value_2)
     key_3, value_3 = hop(key_2), hop(value_2)
-    pack_1, key_3, value_3 = barrier((pack_1, key_3, value_3))
+    pack_1, key_3, value_3, s1 = barrier((pack_1, key_3, value_3, s1))
     pack_2 = hop(pack_1)
     key_3, value_3, s1 = barrier((key_3, value_3, s1))
     kv2, s2 = one(own, other, key_3, value_3)

time: 117 us -> 116 us (level)
  starting transfers between devices: 58.2 us -> 56.9 us
    ppermute x12, starting transfers between devices: 25.9 us -> 24.1 us  [hop(): return lax.ppermute(weight, ('dp', 'z', 'x', 'core'), pairs)]
  transfers between devices with their start and end apart: 16 -> 16, of which waited for: 9 -> 10; matrix products, arithmetic and copies ran while one was open for 1% -> 1% of each run, Pallas kernels for 21% -> 21%
where the time goes in v12:
time: 116 us; the launch traced here: 115 us
  starting transfers between devices  56.9 us (49%)
  Pallas kernels  27.9 us (24%)
  waiting for transfers between devices  23.6 us (20%)
  other arithmetic  3.58 us (3%)
  local copies, waits for them, and re-layouts  3 us (3%)
    ppermute x12, starting transfers between devices, hop(): return lax.ppermute(weight, ('dp', 'z', 'x', 'core'), pairs)  24.1 us
    ppermute x12, waiting for transfers between devices, hop(): return lax.ppermute(weight, ('dp', 'z', 'x', 'core'), pairs)  17.6 us
    pallas_call x2, Pallas kernels, attend(): call(functools.partial(within_kernel, final), len(arrays), (shape(half, B...  11.9 us
    all_to_all x1, starting transfers between devices, body(): chunks = lax.all_to_all(chunks, ('z', 'x'), 0, 0, tiled=True)  10.1 us
    ppermute x1, starting transfers between devices, body(): other = lax.ppermute(own, 'core', SWAP)  8.91 us
    pallas_call x2, Pallas kernels, body(): call(functools.partial(out_kernel, block), 15, shape((TOK, D), kind), [pl...  8.15 us
    ppermute x1, starting transfers between devices, body(): got = lax.ppermute(partial[0], 'core', SWAP)  7.95 us
    all_to_all x1, starting transfers between devices, body(): lax.all_to_all(priors, ('z', 'x'), 0, 0, tiled=True).reshape(SLOTS, DH, DH)  5.83 us
  transfers between devices with their start and end apart: 16, of which 10 were waited for; matrix products, arithmetic and copies ran while one was open for 1% of the time, Pallas kernels for 21%

profile of v12, /device:TPU:1, one launch (start us, length us, event | category | flops | bytes accessed | tf_op | source)
XLA Modules:
  0.0 115.3 jit_solution(6275538210294374556)
XLA Ops:
  0.0 8.9 %collective-permute-start = (bf16[512,1024]{1,0:T(8,128)(2,1)}, bf16[512,1024]{1,0:T(8,128)(2,1)S(1)}, u32[]{:S(2)}, u32[]{:S(2)}) collective-permute-start(bf16[512,1024]{1,0:T(8,128)(2,1)} %bitcast.14), channel_id=1, source_target_pairs={{0,1},{1,0},{2,3},{3,2},{4,5},{5,4},{6,7},{7,6},{8,9},{9,8},{10,11... | collective-permute-start | bytes 3145736 | tf_op jit(solution)/shard_map/ppermute | solution.py:212
  8.9 1.9 %collective-permute-start.2 = (bf16[1024,128]{1,0:T(8,128)(2,1)}, bf16[1024,128]{1,0:T(8,128)(2,1)S(1)}, u32[]{:S(2)}, u32[]{:S(2)}) collective-permute-start(bf16[1024,128]{1,0:T(8,128)(2,1)} %wk.1), channel_id=1, source_target_pairs={{0,448},{1,65},{2,450},{3,67},{4,452},{5,69},{6,454},{7,71},{8,456... | collective-permute-start | bytes 786440 | tf_op jit(solution)/shard_map/ppermute | solution.py:34
  10.9 1.9 %collective-permute-start.4 = (bf16[1024,128]{1,0:T(8,128)(2,1)}, bf16[1024,128]{1,0:T(8,128)(2,1)S(1)}, u32[]{:S(2)}, u32[]{:S(2)}) collective-permute-start(bf16[1024,128]{1,0:T(8,128)(2,1)} %wv.1), channel_id=1, source_target_pairs={{0,448},{1,65},{2,450},{3,67},{4,452},{5,69},{6,454},{7,71},{8,456... | collective-permute-start | bytes 786440 | tf_op jit(solution)/shard_map/ppermute | solution.py:34
  12.8 4.6 %collective-permute-done.2.wk = bf16[1024,128]{1,0:T(8,128)(2,1)S(1)} collective-permute-done((bf16[1024,128]{1,0:T(8,128)(2,1)}, bf16[1024,128]{1,0:T(8,128)(2,1)S(1)}, u32[]{:S(2)}, u32[]{:S(2)}) %collective-permute-start.2) | collective-permute-done | bytes 262176 | tf_op jit(solution)/shard_map/ppermute | solution.py:34
  23.2 1.9 %collective-permute-start.1 = (bf16[2048,128]{1,0:T(8,128)(2,1)S(1)}, bf16[2048,128]{1,0:T(8,128)(2,1)S(1)}, u32[]{:S(2)}, u32[]{:S(2)}) collective-permute-start(bf16[2048,128]{1,0:T(8,128)(2,1)S(1)} %pad_maximum_fusion.refs_3_.o_own), channel_id=1, source_target_pairs={{0,448},{1,65},{2,450},{3,67},{4,452},{5,69},{6,454},{7,71},{8,456... | collective-permute-start | bytes 1572872 | tf_op jit(solution)/shard_map/ppermute | solution.py:34
  30.5 1.9 %collective-permute-start.7 = (bf16[1024,128]{1,0:T(8,128)(2,1)S(1)}, bf16[1024,128]{1,0:T(8,128)(2,1)S(1)}, u32[]{:S(2)}, u32[]{:S(2)}) collective-permute-start(bf16[1024,128]{1,0:T(8,128)(2,1)S(1)} %collective-permute-done.5.wv), channel_id=1, source_target_pairs={{0,448},{1,65},{2,450},{3,67},{4,452},{5,69},{6,454},{7,71},{8,456... | collective-permute-start | bytes 786440 | tf_op jit(solution)/shard_map/ppermute | solution.py:34
  34.3 2.8 %collective-permute-done.6.wk = bf16[1024,128]{1,0:T(8,128)(2,1)S(1)} collective-permute-done((bf16[1024,128]{1,0:T(8,128)(2,1)S(1)}, bf16[1024,128]{1,0:T(8,128)(2,1)S(1)}, u32[]{:S(2)}, u32[]{:S(2)}) %collective-permute-start.6) | collective-permute-done | bytes 262176 | tf_op jit(solution)/shard_map/ppermute | solution.py:34
  37.1 2.8 %collective-permute-done.7.wv = bf16[1024,128]{1,0:T(8,128)(2,1)S(1)} collective-permute-done((bf16[1024,128]{1,0:T(8,128)(2,1)S(1)}, bf16[1024,128]{1,0:T(8,128)(2,1)S(1)}, u32[]{:S(2)}, u32[]{:S(2)}) %collective-permute-start.7) | collective-permute-done | bytes 262176 | tf_op jit(solution)/shard_map/ppermute | solution.py:34
  39.9 2.0 %collective-permute-start.8 = (bf16[2048,128]{1,0:T(8,128)(2,1)S(1)}, bf16[2048,128]{1,0:T(8,128)(2,1)}, u32[]{:S(2)}, u32[]{:S(2)}) collective-permute-start(bf16[2048,128]{1,0:T(8,128)(2,1)S(1)} %collective-permute-done.1.refs_2_.o0), channel_id=1, source_target_pairs={{0,448},{1,65},{2,450},{3,67},{4,452},{5,69},{6,454},{7,71},{8,456... | collective-permute-start | bytes 1572872 | tf_op jit(solution)/shard_map/ppermute | solution.py:34
  42.0 1.9 %collective-permute-start.9 = (bf16[1024,128]{1,0:T(8,128)(2,1)S(1)}, bf16[1024,128]{1,0:T(8,128)(2,1)S(1)}, u32[]{:S(2)}, u32[]{:S(2)}) collective-permute-start(bf16[1024,128]{1,0:T(8,128)(2,1)S(1)} %collective-permute-done.6.wk), channel_id=1, source_target_pairs={{0,448},{1,65},{2,450},{3,67},{4,452},{5,69},{6,454},{7,71},{8,456... | collective-permute-start | bytes 786440 | tf_op jit(solution)/shard_map/ppermute | solution.py:34
  43.9 2.1 %collective-permute-start.10 = (bf16[1024,128]{1,0:T(8,128)(2,1)S(1)}, bf16[1024,128]{1,0:T(8,128)(2,1)S(1)}, u32[]{:S(2)}, u32[]{:S(2)}) collective-permute-start(bf16[1024,128]{1,0:T(8,128)(2,1)S(1)} %collective-permute-done.7.wv), channel_id=1, source_target_pairs={{0,448},{1,65},{2,450},{3,67},{4,452},{5,69},{6,454},{7,71},{8,456... | collective-permute-start | bytes 786440 | tf_op jit(solution)/shard_map/ppermute | solution.py:34
  47.6 3.7 %collective-permute-done.8.refs_3_.o1 = bf16[2048,128]{1,0:T(8,128)(2,1)} collective-permute-done((bf16[2048,128]{1,0:T(8,128)(2,1)S(1)}, bf16[2048,128]{1,0:T(8,128)(2,1)}, u32[]{:S(2)}, u32[]{:S(2)}) %collective-permute-start.8) | collective-permute-done | bytes 524320 | tf_op jit(solution)/shard_map/ppermute | solution.py:34
  53.2 2.8 %collective-permute-start.11 = (bf16[2048,128]{1,0:T(8,128)(2,1)}, bf16[2048,128]{1,0:T(8,128)(2,1)}, u32[]{:S(2)}, u32[]{:S(2)}) collective-permute-start(bf16[2048,128]{1,0:T(8,128)(2,1)} %collective-permute-done.8.refs_3_.o1), channel_id=1, source_target_pairs={{0,448},{1,65},{2,450},{3,67},{4,452},{5,69},{6,454},{7,71},{8,456... | collective-permute-start | bytes 1572872 | tf_op jit(solution)/shard_map/ppermute | solution.py:34
  56.9 2.3 %shard_map.67 = (bf16[2,512,256]{2,1,0:T(8,128)(2,1)S(1)}, f32[2,128,128]{2,1,0:T(8,128)S(1)}, bf16[4,128,128]{2,1,0:T(8,128)(2,1)}) custom-call(bf16[512,1024]{1,0:T(8,128)(2,1)S(1)} %bitcast.20, bf16[512,1024]{1,0:T(8,128)(2,1)S(1)} %collective-permute-done.other.refs_1_, bf16[1024,128]{1,0:T(8,128)(2,1)S(1)} %copy-done.11, ...), custom_call_target="tpu_custom_call" | custom-call | flops 536870912 | bytes 3145728 | tf_op jit(solution)/shard_map/pallas_call | solution.py:238
  60.6 10.1 %all-to-all-start = ((bf16[32,16,128]{2,1,0:T(8,128)(2,1)}), bf16[32,16,128]{2,1,0:T(8,128)(2,1)S(1)}, u32[]{:S(2)}, u32[]{:S(2)}) async-start(bf16[32,16,128]{2,1,0:T(8,128)(2,1)} %bitcast.3), calls=%async_computation | async-start | bytes 262144 | tf_op jit(solution)/shard_map/all_to_all | solution.py:263
  70.7 5.9 %shard_map.68 = (bf16[2,2,512,128]{3,2,1,0:T(8,128)(2,1)}, f32[2,2,512,128]{3,2,1,0:T(8,128)}) custom-call(bf16[512,1024]{1,0:T(8,128)(2,1)} %bitcast.15, bf16[512,1024]{1,0:T(8,128)(2,1)} %copy-done.2, bf16[2048,128]{1,0:T(8,128)(2,1)} %copy-done.15, bf16[2048,128]{1,0:T(8,128)(2,1)} %collective-permute-done.8.refs_3_.o1, bf16[2,512,256]{2,1,0:T(8,128)(2,1)} %copy-done.9, ...), custom_call_target="tpu_custom_call" | custom-call | flops 805306368 | bytes 5242880 | tf_op jit(solution)/shard_map/pallas_call | solution.py:243
  76.7 3.4 %all-to-all-done.chunk_ref = bf16[32,16,128]{2,1,0:T(8,128)(2,1)S(1)} async-done(((bf16[32,16,128]{2,1,0:T(8,128)(2,1)}), bf16[32,16,128]{2,1,0:T(8,128)(2,1)S(1)}, u32[]{:S(2)}, u32[]{:S(2)}) %all-to-all-start) | async-done | bytes 131104 | tf_op jit(solution)/shard_map/all_to_all | solution.py:263
  80.8 5.8 %all-to-all-start.1 = ((bf16[32,16,128]{2,1,0:T(8,128)(2,1)}), bf16[32,16,128]{2,1,0:T(8,128)(2,1)S(1)}, u32[]{:S(2)}, u32[]{:S(2)}) async-start(bf16[32,16,128]{2,1,0:T(8,128)(2,1)} %shard_map.70), calls=%async_computation.1 | async-start | bytes 262144 | tf_op jit(solution)/shard_map/all_to_all | solution.py:266
  87.4 5.9 %shard_map.69 = (bf16[2,2,512,128]{3,2,1,0:T(8,128)(2,1)}, f32[2,2,512,128]{3,2,1,0:T(8,128)}) custom-call(bf16[512,1024]{1,0:T(8,128)(2,1)} %bitcast.16, bf16[512,1024]{1,0:T(8,128)(2,1)} %copy-done.2, bf16[2048,128]{1,0:T(8,128)(2,1)} %collective-permute-done.11.refs_2_.o2, bf16[2048,128]{1,0:T(8,128)(2,1)} %copy-done.13, bf16[2048,128]{1,0:T(8,128)(2,1)} %copy-done.14, ...), custom_call_target="tpu_custom_call" | custom-call | flops 805306368 | bytes 5242880 | tf_op jit(solution)/shard_map/pallas_call | solution.py:243
  93.4 2.6 %all-to-all-done.1 = bf16[32,16,128]{2,1,0:T(8,128)(2,1)S(1)} async-done(((bf16[32,16,128]{2,1,0:T(8,128)(2,1)}), bf16[32,16,128]{2,1,0:T(8,128)(2,1)S(1)}, u32[]{:S(2)}, u32[]{:S(2)}) %all-to-all-start.1) | async-done | bytes 131104 | tf_op jit(solution)/shard_map/all_to_all | solution.py:266
  96.6 4.1 %shard_map.72 = bf16[512,1024]{1,0:T(8,128)(2,1)} custom-call(bf16[2,2,512,128]{3,2,1,0:T(8,128)(2,1)} %get-tuple-element.59.query_a, bf16[2,2,512,128]{3,2,1,0:T(8,128)(2,1)} %get-tuple-element.62.query_b, f32[2,2,512,128]{3,2,1,0:T(8,128)} %get-tuple-element.63.within_a, f32[2,2,512,128]{3,2,1,0:T(8,128)} %get-tuple-element.64.within_b, ...), custom_call_target="tpu_custom_call" | custom-call | flops 1342177280 | bytes 5242880 | tf_op jit(solution)/shard_map/pallas_call | solution.py:274
  100.7 7.9 %collective-permute-start.13 = (bf16[512,1024]{1,0:T(8,128)(2,1)}, bf16[512,1024]{1,0:T(8,128)(2,1)S(1)}, u32[]{:S(2)}, u32[]{:S(2)}) collective-permute-start(bf16[512,1024]{1,0:T(8,128)(2,1)} %shard_map.72), channel_id=1, source_target_pairs={{0,1},{1,0},{2,3},{3,2},{4,5},{5,4},{6,7},{7,6},{8,9},{9,8},{10,11... | collective-permute-start | bytes 3145736 | tf_op jit(solution)/shard_map/ppermute | solution.py:296
  108.6 4.1 %shard_map.71 = bf16[512,1024]{1,0:T(8,128)(2,1)} custom-call(bf16[2,2,512,128]{3,2,1,0:T(8,128)(2,1)} %get-tuple-element.59.query_a, bf16[2,2,512,128]{3,2,1,0:T(8,128)(2,1)} %get-tuple-element.62.query_b, f32[2,2,512,128]{3,2,1,0:T(8,128)} %get-tuple-element.63.within_a, f32[2,2,512,128]{3,2,1,0:T(8,128)} %get-tuple-element.64.within_b, ...), custom_call_target="tpu_custom_call" | custom-call | flops 1342177280 | bytes 5242880 | tf_op jit(solution)/shard_map/pallas_call | solution.py:274
  112.8 2.6 %fusion = bf16[1,512,1024]{2,1,0:T(8,128)(2,1)} fusion(bf16[512,1024]{1,0:T(8,128)(2,1)S(1)} %collective-permute-done.13, bf16[512,1024]{1,0:T(8,128)(2,1)} %shard_map.71), kind=kLoop, calls=%fused_computation.1 | loop fusion | flops 2097152 | bytes 3145728 | tf_op jit(solution)/shard_map/broadcast_in_dim | solution.py:297
  (54 shorter events, 20.9 us)
Async XLA Ops:
  0.0 25.1 %copy-start.1 = (bf16[1,512,1024]{2,1,0:T(8,128)(2,1)S(1)}, bf16[1,512,1024]{2,1,0:T(8,128)(2,1)}, u32[]{:S(2)}) copy-start(bf16[1,512,1024]{2,1,0:T(8,128)(2,1)} %param.6) | copy-start | bytes 3145732
  0.0 25.1 %collective-permute-start = (bf16[512,1024]{1,0:T(8,128)(2,1)}, bf16[512,1024]{1,0:T(8,128)(2,1)S(1)}, u32[]{:S(2)}, u32[]{:S(2)}) collective-permute-start(bf16[512,1024]{1,0:T(8,128)(2,1)} %bitcast.14), channel_id=1, source_target_pairs={{0,1},{1,0},{2,3},{3,2},{4,5},{5,4},{6,7},{7,6},{8,9},{9,8},{10,11... | collective-permute-start | bytes 3145736 | tf_op jit(solution)/shard_map/ppermute | solution.py:212
  8.9 8.5 %collective-permute-start.2 = (bf16[1024,128]{1,0:T(8,128)(2,1)}, bf16[1024,128]{1,0:T(8,128)(2,1)S(1)}, u32[]{:S(2)}, u32[]{:S(2)}) collective-permute-start(bf16[1024,128]{1,0:T(8,128)(2,1)} %wk.1), channel_id=1, source_target_pairs={{0,448},{1,65},{2,450},{3,67},{4,452},{5,69},{6,454},{7,71},{8,456... | collective-permute-start | bytes 786440 | tf_op jit(solution)/shard_map/ppermute | solution.py:34
  10.9 9.4 %collective-permute-start.4 = (bf16[1024,128]{1,0:T(8,128)(2,1)}, bf16[1024,128]{1,0:T(8,128)(2,1)S(1)}, u32[]{:S(2)}, u32[]{:S(2)}) collective-permute-start(bf16[1024,128]{1,0:T(8,128)(2,1)} %wv.1), channel_id=1, source_target_pairs={{0,448},{1,65},{2,450},{3,67},{4,452},{5,69},{6,454},{7,71},{8,456... | collective-permute-start | bytes 786440 | tf_op jit(solution)/shard_map/ppermute | solution.py:34
  17.5 9.3 %collective-permute-start.3 = (bf16[1024,128]{1,0:T(8,128)(2,1)S(1)}, bf16[1024,128]{1,0:T(8,128)(2,1)S(1)}, u32[]{:S(2)}, u32[]{:S(2)}) collective-permute-start(bf16[1024,128]{1,0:T(8,128)(2,1)S(1)} %collective-permute-done.2.wk), channel_id=1, source_target_pairs={{0,448},{1,65},{2,450},{3,67},{4,452},{5,69},{6,454},{7,71},{8,456... | collective-permute-start | bytes 786440 | tf_op jit(solution)/shard_map/ppermute | solution.py:34
  20.3 8.3 %collective-permute-start.5 = (bf16[1024,128]{1,0:T(8,128)(2,1)S(1)}, bf16[1024,128]{1,0:T(8,128)(2,1)S(1)}, u32[]{:S(2)}, u32[]{:S(2)}) collective-permute-start(bf16[1024,128]{1,0:T(8,128)(2,1)S(1)} %collective-permute-done.4.wv), channel_id=1, source_target_pairs={{0,448},{1,65},{2,450},{3,67},{4,452},{5,69},{6,454},{7,71},{8,456... | collective-permute-start | bytes 786440 | tf_op jit(solution)/shard_map/ppermute | solution.py:34
  23.2 11.1 %collective-permute-start.1 = (bf16[2048,128]{1,0:T(8,128)(2,1)S(1)}, bf16[2048,128]{1,0:T(8,128)(2,1)S(1)}, u32[]{:S(2)}, u32[]{:S(2)}) collective-permute-start(bf16[2048,128]{1,0:T(8,128)(2,1)S(1)} %pad_maximum_fusion.refs_3_.o_own), channel_id=1, source_target_pairs={{0,448},{1,65},{2,450},{3,67},{4,452},{5,69},{6,454},{7,71},{8,456... | collective-permute-start | bytes 1572872 | tf_op jit(solution)/shard_map/ppermute | solution.py:34
  25.1 31.7 %copy-start.2 = (bf16[512,1024]{1,0:T(8,128)(2,1)}, bf16[512,1024]{1,0:T(8,128)(2,1)S(1)}, u32[]{:S(2)}) copy-start(bf16[512,1024]{1,0:T(8,128)(2,1)S(1)} %collective-permute-done.other.refs_1_) | copy-start | bytes 3145732
  26.8 30.0 %copy-start.3 = (f32[2,128,128]{2,1,0:T(8,128)}, f32[2,128,128]{2,1,0:T(8,128)S(1)}, u32[]{:S(2)}) copy-start(f32[2,128,128]{2,1,0:T(8,128)S(1)} %get-tuple-element.51.s0) | copy-start | bytes 393220
  28.6 8.5 %collective-permute-start.6 = (bf16[1024,128]{1,0:T(8,128)(2,1)S(1)}, bf16[1024,128]{1,0:T(8,128)(2,1)S(1)}, u32[]{:S(2)}, u32[]{:S(2)}) collective-permute-start(bf16[1024,128]{1,0:T(8,128)(2,1)S(1)} %collective-permute-done.3.wk), channel_id=1, source_target_pairs={{0,448},{1,65},{2,450},{3,67},{4,452},{5,69},{6,454},{7,71},{8,456... | collective-permute-start | bytes 786440 | tf_op jit(solution)/shard_map/ppermute | solution.py:34
  30.5 9.4 %collective-permute-start.7 = (bf16[1024,128]{1,0:T(8,128)(2,1)S(1)}, bf16[1024,128]{1,0:T(8,128)(2,1)S(1)}, u32[]{:S(2)}, u32[]{:S(2)}) collective-permute-start(bf16[1024,128]{1,0:T(8,128)(2,1)S(1)} %collective-permute-done.5.wv), channel_id=1, source_target_pairs={{0,448},{1,65},{2,450},{3,67},{4,452},{5,69},{6,454},{7,71},{8,456... | collective-permute-start | bytes 786440 | tf_op jit(solution)/shard_map/ppermute | solution.py:34
  34.1 13.5 %copy-start.10 = (bf16[2,512,256]{2,1,0:T(8,128)(2,1)}, bf16[2,512,256]{2,1,0:T(8,128)(2,1)S(1)}, u32[]{:S(2)}) copy-start(bf16[2,512,256]{2,1,0:T(8,128)(2,1)S(1)} %get-tuple-element.57.refs_5_) | copy-start | bytes 1572868
  34.1 22.8 %copy-start.4 = (f32[2,128,128]{2,1,0:T(8,128)}, f32[2,128,128]{2,1,0:T(8,128)S(1)}, u32[]{:S(2)}) copy-start(f32[2,128,128]{2,1,0:T(8,128)S(1)} %get-tuple-element.52.s1) | copy-start | bytes 393220
  34.3 13.3 %copy-start.15 = (bf16[2048,128]{1,0:T(8,128)(2,1)}, bf16[2048,128]{1,0:T(8,128)(2,1)S(1)}, u32[]{:S(2)}) copy-start(bf16[2048,128]{1,0:T(8,128)(2,1)S(1)} %collective-permute-done.1.refs_2_.o0) | copy-start | bytes 1572868
  39.9 16.9 %copy-start.11 = (bf16[1024,128]{1,0:T(8,128)(2,1)S(1)}, bf16[1024,128]{1,0:T(8,128)(2,1)}, u32[]{:S(2)}) copy-start(bf16[1024,128]{1,0:T(8,128)(2,1)} %wk.1) | copy-start | bytes 786436
  39.9 16.9 %copy-start.12 = (bf16[1024,128]{1,0:T(8,128)(2,1)S(1)}, bf16[1024,128]{1,0:T(8,128)(2,1)}, u32[]{:S(2)}) copy-start(bf16[1024,128]{1,0:T(8,128)(2,1)} %wv.1) | copy-start | bytes 786436
  39.9 11.4 %collective-permute-start.8 = (bf16[2048,128]{1,0:T(8,128)(2,1)S(1)}, bf16[2048,128]{1,0:T(8,128)(2,1)}, u32[]{:S(2)}, u32[]{:S(2)}) collective-permute-start(bf16[2048,128]{1,0:T(8,128)(2,1)S(1)} %collective-permute-done.1.refs_2_.o0), channel_id=1, source_target_pairs={{0,448},{1,65},{2,450},{3,67},{4,452},{5,69},{6,454},{7,71},{8,456... | collective-permute-start | bytes 1572872 | tf_op jit(solution)/shard_map/ppermute | solution.py:34
  42.0 14.0 %collective-permute-start.9 = (bf16[1024,128]{1,0:T(8,128)(2,1)S(1)}, bf16[1024,128]{1,0:T(8,128)(2,1)S(1)}, u32[]{:S(2)}, u32[]{:S(2)}) collective-permute-start(bf16[1024,128]{1,0:T(8,128)(2,1)S(1)} %collective-permute-done.6.wk), channel_id=1, source_target_pairs={{0,448},{1,65},{2,450},{3,67},{4,452},{5,69},{6,454},{7,71},{8,456... | collective-permute-start | bytes 786440 | tf_op jit(solution)/shard_map/ppermute | solution.py:34
  43.9 12.9 %collective-permute-start.10 = (bf16[1024,128]{1,0:T(8,128)(2,1)S(1)}, bf16[1024,128]{1,0:T(8,128)(2,1)S(1)}, u32[]{:S(2)}, u32[]{:S(2)}) collective-permute-start(bf16[1024,128]{1,0:T(8,128)(2,1)S(1)} %collective-permute-done.7.wv), channel_id=1, source_target_pairs={{0,448},{1,65},{2,450},{3,67},{4,452},{5,69},{6,454},{7,71},{8,456... | collective-permute-start | bytes 786440 | tf_op jit(solution)/shard_map/ppermute | solution.py:34
  51.3 35.3 %collective-permute-start.12 = (bf16[2048,128]{1,0:T(8,128)(2,1)}, bf16[2048,128]{1,0:T(8,128)(2,1)S(1)}, u32[]{:S(2)}, u32[]{:S(2)}) collective-permute-start(bf16[2048,128]{1,0:T(8,128)(2,1)} %collective-permute-done.8.refs_3_.o1), channel_id=1, source_target_pairs={{0,384},{1,129},{2,386},{3,131},{4,388},{5,133},{6,390},{7,135},{8... | collective-permute-start | bytes 1572872 | tf_op jit(solution)/shard_map/ppermute | solution.py:34
  53.2 33.4 %collective-permute-start.11 = (bf16[2048,128]{1,0:T(8,128)(2,1)}, bf16[2048,128]{1,0:T(8,128)(2,1)}, u32[]{:S(2)}, u32[]{:S(2)}) collective-permute-start(bf16[2048,128]{1,0:T(8,128)(2,1)} %collective-permute-done.8.refs_3_.o1), channel_id=1, source_target_pairs={{0,448},{1,65},{2,450},{3,67},{4,452},{5,69},{6,454},{7,71},{8,456... | collective-permute-start | bytes 1572872 | tf_op jit(solution)/shard_map/ppermute | solution.py:34
  60.6 19.5 %all-to-all-start = ((bf16[32,16,128]{2,1,0:T(8,128)(2,1)}), bf16[32,16,128]{2,1,0:T(8,128)(2,1)S(1)}, u32[]{:S(2)}, u32[]{:S(2)}) async-start(bf16[32,16,128]{2,1,0:T(8,128)(2,1)} %bitcast.3), calls=%async_computation | async-start | bytes 262144 | tf_op jit(solution)/shard_map/all_to_all | solution.py:263
  80.8 15.2 %all-to-all-start.1 = ((bf16[32,16,128]{2,1,0:T(8,128)(2,1)}), bf16[32,16,128]{2,1,0:T(8,128)(2,1)S(1)}, u32[]{:S(2)}, u32[]{:S(2)}) async-start(bf16[32,16,128]{2,1,0:T(8,128)(2,1)} %shard_map.70), calls=%async_computation.1 | async-start | bytes 262144 | tf_op jit(solution)/shard_map/all_to_all | solution.py:266
  100.7 12.1 %collective-permute-start.13 = (bf16[512,1024]{1,0:T(8,128)(2,1)}, bf16[512,1024]{1,0:T(8,128)(2,1)S(1)}, u32[]{:S(2)}, u32[]{:S(2)}) collective-permute-start(bf16[512,1024]{1,0:T(8,128)(2,1)} %shard_map.72), channel_id=1, source_target_pairs={{0,1},{1,0},{2,3},{3,2},{4,5},{5,4},{6,7},{7,6},{8,9},{9,8},{10,11... | collective-permute-start | bytes 3145736 | tf_op jit(solution)/shard_map/ppermute | solution.py:296
  (9 other events, 49.6 us)
